TPU v7x, 32 devices: a whole 2x2x4 slice. The times are simulated.
32 devices in a mesh: depth: 4 (over y, x), freq: 8 (over z, core).
Axes of the slice: x: 2, y: 2, z: 4, core: 2. Of those that a mesh axis runs over, the one named last changes fastest.
Arguments:
- source: bfloat16 [8, 2, 1024, 256], P('freq'), may hold values from -6 to 6
- propagator: bfloat16 [4, 8, 2, 1024, 1024], P('depth', 'freq'), may hold values from -0.125 to 0.125
- transmission: float32 [4, 8, 1024], P('depth', 'freq'), may hold values from 0.5 to 1.5
- upgoing: bfloat16 [4, 8, 2, 1024, 256], P('depth', 'freq'), may hold values from -6 to 6
Outputs:
- gradient: float32 [4, 1024, 2, 1024], P('depth', 'freq')
All inputs are finite; a program needn't handle non-finite values.
Results may differ from a plain program's by a relative error of at most 0.013.
Values may be sent and summed in bfloat16 or wider, within the bound.
No kernel may reach another device: no remote copies, remote signals or barrier semaphores. Data moves between devices by JAX's collectives and lax.ppermute only.
A program may use at most 64 MiB of HBM per device.

v0:
```python
import jax
import jax.numpy as jnp
from jax import lax
from jax.sharding import PartitionSpec as P


def shifted(block, axis, distance):
    devices = range(lax.axis_size(axis))
    route = [(i - distance, i) for i in devices if i - distance in devices]
    return lax.ppermute(block, axis, route)


def advance(panel, weight, factor):
    shots = panel.shape[1] // 2
    real_part = jnp.dot(weight[0], panel, preferred_element_type=jnp.float32)
    imag_part = jnp.dot(weight[1], panel, preferred_element_type=jnp.float32)
    out_real = real_part[:, :shots] - imag_part[:, shots:]
    out_imag = real_part[:, shots:] + imag_part[:, :shots]
    joined = jnp.concatenate([out_real, out_imag], axis=1)
    return (joined * factor[:, None]).astype(jnp.bfloat16)


def shards(source, propagator, transmission, upgoing):
    weight = propagator[0, 0]
    factor = transmission[0, 0]
    upward = upgoing[0, 0]
    width = weight.shape[1]
    shots = source.shape[3]
    level = lax.axis_index("depth")
    levels = lax.axis_size("depth")
    freqs = lax.axis_size("freq")
    rows_own = width // freqs
    start_panel = jnp.concatenate([source[0, 0], source[0, 1]], axis=1)
    incoming = start_panel
    outgoing = advance(incoming, weight, factor)
    for tick in range(1, levels):
        arrived = shifted(outgoing, "depth", 1)
        incoming = jnp.where(level == 0, start_panel, arrived)
        outgoing = advance(incoming, weight, factor)
    up_pair = jnp.concatenate([upward[0], upward[1]], axis=1)
    dims = (((1,), (1,)), ((), ()))
    up_turn = jnp.concatenate([upward[1], -upward[0]], axis=1)
    real_part = lax.dot_general(up_pair, outgoing, dims, preferred_element_type=jnp.float32)
    imag_part = lax.dot_general(up_turn, outgoing, dims, preferred_element_type=jnp.float32)
    summed = lax.psum_scatter(
        jnp.stack([real_part, imag_part], axis=1), "freq", scatter_dimension=0, tiled=True
    )
    scale = (2.0 * shots * freqs) ** (-0.5)
    return (summed * scale).reshape(1, rows_own, 2, width)


def solution(mesh):
    return jax.shard_map(
        shards,
        mesh=mesh,
        in_specs=(
            P("freq", None, None, None),
            P("depth", "freq", None, None, None),
            P("depth", "freq", None),
            P("depth", "freq", None, None, None),
        ),
        out_specs=P("depth", "freq", None, None),
        check_vma=False,
    )
```

profile of v0, /device:TPU:4, one launch (start us, length us, event | category | flops | bytes accessed | tf_op | source)
XLA Modules:
  0.0 212.5 jit_solution(9129096174837874911)
XLA Ops:
  6.5 1.3 fusion.65
  8.2 3.0 %fusion.32 = f32[1024,512]{0,1:T(8,128)S(1)} fusion(bf16[1,1,2,1024,1024]{4,3,2,1,0:T(8,128)(2,1)} %param.5, bf16[1024,256]{0,1:T(8,128)(2,1)S(1)} %bitcast.73, bf16[1024,256]{0,1:T(8,128)(2,1)S(1)} %bitcast.65), kind=kOutput, calls=%fused_computation.31 | convolution fusion | flops 1075838976 | bytes 5242880 | tf_op jit(solution)/shard_map/dot_general | solution.py:16
  11.3 1.3 fusion.20
  12.6 0.6 slice_subtract_fusion.3
  13.6 3.4 %collective-permute-start = (bf16[1024,512]{0,1:T(8,128)(2,1)S(1)}, bf16[1024,512]{0,1:T(8,128)(2,1)S(1)}, u32[]{:S(2)}, u32[]{:S(2)}) collective-permute-start(bf16[1024,512]{0,1:T(8,128)(2,1)S(1)} %fusion), channel_id=1, source_target_pairs={{0,8},{8,16},{16,24},{1,9},{9,17},{17,25},{2,10},{10,18},{18,26},{... | collective-permute-start | bytes 3145736 | tf_op jit(solution)/shard_map/ppermute | solution.py:10
  17.0 24.3 %collective-permute-done = bf16[1024,512]{0,1:T(8,128)(2,1)S(1)} collective-permute-done((bf16[1024,512]{0,1:T(8,128)(2,1)S(1)}, bf16[1024,512]{0,1:T(8,128)(2,1)S(1)}, u32[]{:S(2)}, u32[]{:S(2)}) %collective-permute-start) | collective-permute-done | bytes 1048608 | tf_op jit(solution)/shard_map/ppermute | solution.py:10
  41.2 2.9 %fusion.35 = f32[1024,512]{0,1:T(8,128)S(1)} fusion(bf16[1,1,2,1024,1024]{4,3,2,1,0:T(8,128)(2,1)} %param.5, bf16[1024,512]{0,1:T(8,128)(2,1)S(1)} %collective-permute-done, pred[]{:T(512)S(6)} %eq.2, bf16[1024,256]{0,1:T(8,128)(2,1)S(1)} %bitcast.75, bf16[1024,256]{0,1:T(8,128)(2,1)S(1)} %bitcast.67), kind=kOutput, calls=%fused_computation.32 | convolution fusion | flops 1076363264 | bytes 6291457 | tf_op jit(solution)/shard_map/dot_general | solution.py:16
  44.1 1.3 fusion.23
  45.5 0.6 slice_subtract_fusion.2
  46.3 2.5 %collective-permute-start.1 = (bf16[1024,512]{0,1:T(8,128)(2,1)S(1)}, bf16[1024,512]{0,1:T(8,128)(2,1)S(1)}, u32[]{:S(2)}, u32[]{:S(2)}) collective-permute-start(bf16[1024,512]{0,1:T(8,128)(2,1)S(1)} %fusion.1), channel_id=1, source_target_pairs={{0,8},{8,16},{16,24},{1,9},{9,17},{17,25},{2,10},{10,18},{18,26},{... | collective-permute-start | bytes 3145736 | tf_op jit(solution)/shard_map/ppermute | solution.py:10
  48.8 24.3 %collective-permute-done.1 = bf16[1024,512]{0,1:T(8,128)(2,1)S(1)} collective-permute-done((bf16[1024,512]{0,1:T(8,128)(2,1)S(1)}, bf16[1024,512]{0,1:T(8,128)(2,1)S(1)}, u32[]{:S(2)}, u32[]{:S(2)}) %collective-permute-start.1) | collective-permute-done | bytes 1048608 | tf_op jit(solution)/shard_map/ppermute | solution.py:10
  73.1 1.3 fusion.38
  74.4 1.3 fusion.26
  75.8 0.6 slice_subtract_fusion.1
  76.6 2.2 %collective-permute-start.2 = (bf16[1024,512]{0,1:T(8,128)(2,1)S(1)}, bf16[1024,512]{0,1:T(8,128)(2,1)S(1)}, u32[]{:S(2)}, u32[]{:S(2)}) collective-permute-start(bf16[1024,512]{0,1:T(8,128)(2,1)S(1)} %fusion.2), channel_id=1, source_target_pairs={{0,8},{8,16},{16,24},{1,9},{9,17},{17,25},{2,10},{10,18},{18,26},{... | collective-permute-start | bytes 3145736 | tf_op jit(solution)/shard_map/ppermute | solution.py:10
  79.0 23.6 %collective-permute-done.2 = bf16[1024,512]{0,1:T(8,128)(2,1)S(1)} collective-permute-done((bf16[1024,512]{0,1:T(8,128)(2,1)S(1)}, bf16[1024,512]{0,1:T(8,128)(2,1)S(1)}, u32[]{:S(2)}, u32[]{:S(2)}) %collective-permute-start.2) | collective-permute-done | bytes 1048608 | tf_op jit(solution)/shard_map/ppermute | solution.py:10
  102.6 1.3 fusion.41
  104.0 1.3 fusion.29
  105.9 1.3 convolution_bitcast_fusion
  107.1 1.3 convolution_bitcast_fusion.1
  108.4 4.1 %pad_maximum_fusion = f32[1024,2,1024]{2,0,1:T(8,128)} fusion(f32[1024,1,1024]{2,0,1:T(8,128)S(1)} %convolution_bitcast_fusion, f32[1024,1,1024]{2,0,1:T(8,128)S(1)} %convolution_bitcast_fusion.1), kind=kLoop, calls=%fused_computation | loop fusion | flops 2097152 | bytes 16777216 | tf_op jit(solution)/shard_map/stack | solution.py:46
  112.5 90.1 %reduce-scatter.2.cloned.1.call-done = f32[128,2,1024]{2,0,1:T(8,128)} async-done(((f32[1024,2,1024]{2,0,1:T(8,128)}), f32[128,2,1024]{2,0,1:T(8,128)}) %reduce-scatter.2.cloned.1.call-update) | async-done | bytes 1048592 | tf_op jit(solution)/shard_map/reduce_scatter | solution.py:45
  202.6 1.3 multiply_bitcast_fusion
  203.9 1.8 copy.7
  (18 shorter events, 2.0 us)
Async XLA Ops:
  6.5 196.0 %reduce-scatter.2.cloned.1.call-start = ((), (), s32[]{:S(2)}) async-start(), calls=%async_computation.1 | async-start | bytes 9437184 | tf_op jit(solution)/shard_map/reduce_scatter | solution.py:45
  8.2 3.0 %copy-start.2 = (bf16[1,1,2,1024,1024]{4,3,2,1,0:T(8,128)(2,1)S(1)}, bf16[1,1,2,1024,1024]{4,3,2,1,0:T(8,128)(2,1)}, u32[]{:S(2)}) copy-start(bf16[1,1,2,1024,1024]{4,3,2,1,0:T(8,128)(2,1)} %param.5) | copy-start | bytes 12582916
  12.6 0.7 copy-start.1
  13.6 27.7 %collective-permute-start = (bf16[1024,512]{0,1:T(8,128)(2,1)S(1)}, bf16[1024,512]{0,1:T(8,128)(2,1)S(1)}, u32[]{:S(2)}, u32[]{:S(2)}) collective-permute-start(bf16[1024,512]{0,1:T(8,128)(2,1)S(1)} %fusion), channel_id=1, source_target_pairs={{0,8},{8,16},{16,24},{1,9},{9,17},{17,25},{2,10},{10,18},{18,26},{... | collective-permute-start | bytes 3145736 | tf_op jit(solution)/shard_map/ppermute | solution.py:10
  17.0 27.2 %copy-start.3 = (bf16[1,1,2,1024,1024]{4,3,2,1,0:T(8,128)(2,1)S(1)}, bf16[1,1,2,1024,1024]{4,3,2,1,0:T(8,128)(2,1)}, u32[]{:S(2)}) copy-start(bf16[1,1,2,1024,1024]{4,3,2,1,0:T(8,128)(2,1)} %param.5) | copy-start | bytes 12582916
  46.3 26.8 %collective-permute-start.1 = (bf16[1024,512]{0,1:T(8,128)(2,1)S(1)}, bf16[1024,512]{0,1:T(8,128)(2,1)S(1)}, u32[]{:S(2)}, u32[]{:S(2)}) collective-permute-start(bf16[1024,512]{0,1:T(8,128)(2,1)S(1)} %fusion.1), channel_id=1, source_target_pairs={{0,8},{8,16},{16,24},{1,9},{9,17},{17,25},{2,10},{10,18},{18,26},{... | collective-permute-start | bytes 3145736 | tf_op jit(solution)/shard_map/ppermute | solution.py:10
  76.3 2.5 %copy-start = (bf16[1,1,2,1024,256]{4,3,2,1,0:T(8,128)(2,1)S(1)}, bf16[1,1,2,1024,256]{4,3,2,1,0:T(8,128)(2,1)}, u32[]{:S(2)}) copy-start(bf16[1,1,2,1024,256]{4,3,2,1,0:T(8,128)(2,1)} %param.7) | copy-start | bytes 3145732
  76.6 26.0 %collective-permute-start.2 = (bf16[1024,512]{0,1:T(8,128)(2,1)S(1)}, bf16[1024,512]{0,1:T(8,128)(2,1)S(1)}, u32[]{:S(2)}, u32[]{:S(2)}) collective-permute-start(bf16[1024,512]{0,1:T(8,128)(2,1)S(1)} %fusion.2), channel_id=1, source_target_pairs={{0,8},{8,16},{16,24},{1,9},{9,17},{17,25},{2,10},{10,18},{18,26},{... | collective-permute-start | bytes 3145736 | tf_op jit(solution)/shard_map/ppermute | solution.py:10
Sparse Core Ops, SparseCore 0:
  112.6 89.9 reduce-scatter.1
where the time goes:
time: 214 us; the launch traced here: 213 us
  waiting for transfers between devices  162 us (76%)
  matrix products  16.4 us (8%)
  between operations  13.6 us (6%)
  other arithmetic  8.41 us (4%)
  starting transfers between devices  8.14 us (4%)
  local copies, waits for them, and re-layouts  3.67 us (2%)
    reduce_scatter x1, waiting for transfers between devices, shards(): lax.psum_scatter(jnp.stack([real_part, imag_part], axis=1), 'freq', scatt...  90.1 us
    ppermute x3, waiting for transfers between devices, shifted(): return lax.ppermute(block, axis, route)  72.2 us
    dot_general x4, matrix products, advance(): imag_part = jnp.dot(weight[1], panel, preferred_element_type=jnp.float32)  8.56 us
    ppermute x3, starting transfers between devices, shifted(): return lax.ppermute(block, axis, route)  8.14 us
    dot_general x4, matrix products, advance(): real_part = jnp.dot(weight[0], panel, preferred_element_type=jnp.float32)  5.3 us
  transfers between devices with their start and end apart: 4, of which 4 were waited for; matrix products, arithmetic and copies ran while one was open for 0% of the time, Pallas kernels for 0%

commit v1 on v0

--- a/solution.py
+++ b/solution.py
@@ -39,14 +39,14 @@
         outgoing = advance(incoming, weight, factor)
     up_pair = jnp.concatenate([upward[0], upward[1]], axis=1)
     dims = (((1,), (1,)), ((), ()))
-    up_turn = jnp.concatenate([upward[1], -upward[0]], axis=1)
-    real_part = lax.dot_general(up_pair, outgoing, dims, preferred_element_type=jnp.float32)
-    imag_part = lax.dot_general(up_turn, outgoing, dims, preferred_element_type=jnp.float32)
+    turned = jnp.concatenate([-outgoing[:, shots:], outgoing[:, :shots]], axis=1)
+    both = jnp.concatenate([outgoing, turned], axis=0)
+    term = lax.dot_general(up_pair, both, dims, preferred_element_type=jnp.float32)
     summed = lax.psum_scatter(
-        jnp.stack([real_part, imag_part], axis=1), "freq", scatter_dimension=0, tiled=True
+        term.astype(jnp.bfloat16), "freq", scatter_dimension=0, tiled=True
     )
     scale = (2.0 * shots * freqs) ** (-0.5)
-    return (summed * scale).reshape(1, rows_own, 2, width)
+    return (summed.astype(jnp.float32) * scale).reshape(1, rows_own, 2, width)
 
 
 def solution(mesh):

time: 214 us -> 173 us (0.81)
  waiting for transfers between devices: 162 us -> 123 us
  other arithmetic: 8.41 us -> 4.45 us
    reduce_scatter x1, waiting for transfers between devices: 90.1 us -> 50.4 us  [shards(): lax.psum_scatter(term.astype(jnp.bfloat16), 'freq', scatter_dimension=0,...]
    another operation x1 -> x0, other arithmetic: 4.08 us -> none  [shards(): jnp.stack([real_part, imag_part], axis=1)]
    dot_general x4, matrix products: 5.3 us -> 8.61 us  [advance(): real_part = jnp.dot(weight[0], panel, preferred_element_type=jnp.float32)]
    dot_general x4, matrix products: 8.56 us -> 5.3 us  [advance(): imag_part = jnp.dot(weight[1], panel, preferred_element_type=jnp.float32)]
    dot_general x2 -> x1, matrix products: 2.51 us -> 4.3 us  [shards(): lax.dot_general(up_pair, both, dims, preferred_element_type=jnp.float32)]
where the time goes in v1:
time: 173 us; the launch traced here: 171 us
  waiting for transfers between devices  123 us (71%)
  matrix products  18.2 us (11%)
  between operations  13.6 us (8%)
  starting transfers between devices  8.13 us (5%)
  other arithmetic  4.45 us (3%)
  local copies, waits for them, and re-layouts  3.75 us (2%)
    ppermute x3, waiting for transfers between devices, shifted(): return lax.ppermute(block, axis, route)  72.3 us
    reduce_scatter x1, waiting for transfers between devices, shards(): lax.psum_scatter(term.astype(jnp.bfloat16), 'freq', scatter_dimension=0,...  50.4 us
    dot_general x4, matrix products, advance(): real_part = jnp.dot(weight[0], panel, preferred_element_type=jnp.float32)  8.61 us
    ppermute x3, starting transfers between devices, shifted(): return lax.ppermute(block, axis, route)  8.13 us
    dot_general x4, matrix products, advance(): imag_part = jnp.dot(weight[1], panel, preferred_element_type=jnp.float32)  5.3 us
    dot_general x1, matrix products, shards(): lax.dot_general(up_pair, both, dims, preferred_element_type=jnp.float32)  4.3 us
  transfers between devices with their start and end apart: 4, of which 4 were waited for; matrix products, arithmetic and copies ran while one was open for 0% of the time, Pallas kernels for 0%

profile of v1, /device:TPU:4, one launch (start us, length us, event | category | flops | bytes accessed | tf_op | source)
XLA Modules:
  0.0 170.9 jit_solution(8382673671197064601)
XLA Ops:
  6.5 1.3 fusion.61
  8.2 3.0 %fusion.25 = f32[1024,512]{0,1:T(8,128)S(1)} fusion(bf16[1,1,2,1024,1024]{4,3,2,1,0:T(8,128)(2,1)} %param.5, bf16[1024,256]{0,1:T(8,128)(2,1)S(1)} %bitcast.65, bf16[1024,256]{0,1:T(8,128)(2,1)S(1)} %bitcast.57), kind=kOutput, calls=%fused_computation.30 | convolution fusion | flops 1075838976 | bytes 5242880 | tf_op jit(solution)/shard_map/dot_general | solution.py:15
  11.3 1.3 fusion.37
  12.6 0.6 slice_subtract_fusion.3
  13.5 3.4 %collective-permute-start = (bf16[1024,512]{0,1:T(8,128)(2,1)S(1)}, bf16[1024,512]{0,1:T(8,128)(2,1)S(1)}, u32[]{:S(2)}, u32[]{:S(2)}) collective-permute-start(bf16[1024,512]{0,1:T(8,128)(2,1)S(1)} %fusion), channel_id=1, source_target_pairs={{0,8},{8,16},{16,24},{1,9},{9,17},{17,25},{2,10},{10,18},{18,26},{... | collective-permute-start | bytes 3145736 | tf_op jit(solution)/shard_map/ppermute | solution.py:10
  17.0 24.3 %collective-permute-done = bf16[1024,512]{0,1:T(8,128)(2,1)S(1)} collective-permute-done((bf16[1024,512]{0,1:T(8,128)(2,1)S(1)}, bf16[1024,512]{0,1:T(8,128)(2,1)S(1)}, u32[]{:S(2)}, u32[]{:S(2)}) %collective-permute-start) | collective-permute-done | bytes 1048608 | tf_op jit(solution)/shard_map/ppermute | solution.py:10
  41.2 2.9 %fusion.28 = f32[1024,512]{0,1:T(8,128)S(1)} fusion(bf16[1,1,2,1024,1024]{4,3,2,1,0:T(8,128)(2,1)} %param.5, bf16[1024,512]{0,1:T(8,128)(2,1)S(1)} %collective-permute-done, pred[]{:T(512)S(6)} %eq.2, bf16[1024,256]{0,1:T(8,128)(2,1)S(1)} %bitcast.67, bf16[1024,256]{0,1:T(8,128)(2,1)S(1)} %bitcast.59), kind=kOutput, calls=%fused_computation.31 | convolution fusion | flops 1076363264 | bytes 6291457 | tf_op jit(solution)/shard_map/dot_general | solution.py:15
  44.2 1.3 fusion.40
  45.5 0.6 slice_subtract_fusion.2
  46.3 2.5 %collective-permute-start.1 = (bf16[1024,512]{0,1:T(8,128)(2,1)S(1)}, bf16[1024,512]{0,1:T(8,128)(2,1)S(1)}, u32[]{:S(2)}, u32[]{:S(2)}) collective-permute-start(bf16[1024,512]{0,1:T(8,128)(2,1)S(1)} %fusion.1), channel_id=1, source_target_pairs={{0,8},{8,16},{16,24},{1,9},{9,17},{17,25},{2,10},{10,18},{18,26},{... | collective-permute-start | bytes 3145736 | tf_op jit(solution)/shard_map/ppermute | solution.py:10
  48.8 24.3 %collective-permute-done.1 = bf16[1024,512]{0,1:T(8,128)(2,1)S(1)} collective-permute-done((bf16[1024,512]{0,1:T(8,128)(2,1)S(1)}, bf16[1024,512]{0,1:T(8,128)(2,1)S(1)}, u32[]{:S(2)}, u32[]{:S(2)}) %collective-permute-start.1) | collective-permute-done | bytes 1048608 | tf_op jit(solution)/shard_map/ppermute | solution.py:10
  73.1 1.3 fusion.31
  74.5 1.3 fusion.43
  75.8 0.6 slice_subtract_fusion.1
  76.7 2.2 %collective-permute-start.2 = (bf16[1024,512]{0,1:T(8,128)(2,1)S(1)}, bf16[1024,512]{0,1:T(8,128)(2,1)S(1)}, u32[]{:S(2)}, u32[]{:S(2)}) collective-permute-start(bf16[1024,512]{0,1:T(8,128)(2,1)S(1)} %fusion.2), channel_id=1, source_target_pairs={{0,8},{8,16},{16,24},{1,9},{9,17},{17,25},{2,10},{10,18},{18,26},{... | collective-permute-start | bytes 3145736 | tf_op jit(solution)/shard_map/ppermute | solution.py:10
  79.0 23.7 %collective-permute-done.2 = bf16[1024,512]{0,1:T(8,128)(2,1)S(1)} collective-permute-done((bf16[1024,512]{0,1:T(8,128)(2,1)S(1)}, bf16[1024,512]{0,1:T(8,128)(2,1)S(1)}, u32[]{:S(2)}, u32[]{:S(2)}) %collective-permute-start.2) | collective-permute-done | bytes 1048608 | tf_op jit(solution)/shard_map/ppermute | solution.py:10
  102.7 1.3 fusion.34
  104.0 1.3 fusion.46
  105.4 0.6 slice_subtract_fusion
  105.9 0.3 fusion.3
  106.3 4.3 %convolution_convert_fusion = bf16[1024,2048]{1,0:T(8,128)(2,1)} fusion(bf16[1024,256]{0,1:T(8,128)(2,1)S(1)} %get-tuple-element.16, bf16[1024,256]{0,1:T(8,128)(2,1)S(1)} %get-tuple-element.15, bf16[1024,512]{0,1:T(8,128)(2,1)S(1)} %fusion.3, bf16[1024,256]{1,0:T(8,128)(2,1)S(1)} %get-tuple-element.14, bf16[1024,256]{1,0:T(8,128)(2,1)S(1)} %get-tuple-element.13), kind=kOutput, calls=%fused_computation | convolution fusion | flops 2157969408 | bytes 7340032 | tf_op jit(solution)/shard_map/dot_general | solution.py:44
  110.6 50.4 %reduce-scatter.2.cloned.1.call-done = bf16[128,2048]{1,0:T(8,128)(2,1)} async-done(((bf16[1024,2048]{1,0:T(8,128)(2,1)}), bf16[128,2048]{1,0:T(8,128)(2,1)}) %reduce-scatter.2.cloned.1.call-update) | async-done | bytes 524304 | tf_op jit(solution)/shard_map/reduce_scatter | solution.py:45
  161.0 1.1 convert_multiply_fusion
  162.2 1.9 %reshape.12 = f32[1,128,2,1024]{3,2,1,0:T(2,128)} reshape(f32[128,2048]{1,0:T(8,128)S(1)} %convert_multiply_fusion) | data formatting | bytes 2097152 | tf_op jit(solution)/shard_map/reshape | solution.py:49
  (17 shorter events, 1.5 us)
Async XLA Ops:
  6.5 154.5 %reduce-scatter.2.cloned.1.call-start = ((), (), s32[]{:S(2)}) async-start(), calls=%async_computation.1 | async-start | bytes 4718592 | tf_op jit(solution)/shard_map/reduce_scatter | solution.py:45
  8.2 3.0 %copy-start.2 = (bf16[1,1,2,1024,1024]{4,3,2,1,0:T(8,128)(2,1)S(1)}, bf16[1,1,2,1024,1024]{4,3,2,1,0:T(8,128)(2,1)}, u32[]{:S(2)}) copy-start(bf16[1,1,2,1024,1024]{4,3,2,1,0:T(8,128)(2,1)} %param.5) | copy-start | bytes 12582916
  12.6 0.7 copy-start.1
  13.5 27.7 %collective-permute-start = (bf16[1024,512]{0,1:T(8,128)(2,1)S(1)}, bf16[1024,512]{0,1:T(8,128)(2,1)S(1)}, u32[]{:S(2)}, u32[]{:S(2)}) collective-permute-start(bf16[1024,512]{0,1:T(8,128)(2,1)S(1)} %fusion), channel_id=1, source_target_pairs={{0,8},{8,16},{16,24},{1,9},{9,17},{17,25},{2,10},{10,18},{18,26},{... | collective-permute-start | bytes 3145736 | tf_op jit(solution)/shard_map/ppermute | solution.py:10
  16.9 27.2 %copy-start.3 = (bf16[1,1,2,1024,1024]{4,3,2,1,0:T(8,128)(2,1)S(1)}, bf16[1,1,2,1024,1024]{4,3,2,1,0:T(8,128)(2,1)}, u32[]{:S(2)}) copy-start(bf16[1,1,2,1024,1024]{4,3,2,1,0:T(8,128)(2,1)} %param.5) | copy-start | bytes 12582916
  46.3 26.8 %collective-permute-start.1 = (bf16[1024,512]{0,1:T(8,128)(2,1)S(1)}, bf16[1024,512]{0,1:T(8,128)(2,1)S(1)}, u32[]{:S(2)}, u32[]{:S(2)}) collective-permute-start(bf16[1024,512]{0,1:T(8,128)(2,1)S(1)} %fusion.1), channel_id=1, source_target_pairs={{0,8},{8,16},{16,24},{1,9},{9,17},{17,25},{2,10},{10,18},{18,26},{... | collective-permute-start | bytes 3145736 | tf_op jit(solution)/shard_map/ppermute | solution.py:10
  76.4 2.5 %copy-start = (bf16[1,1,2,1024,256]{4,3,2,1,0:T(8,128)(2,1)S(1)}, bf16[1,1,2,1024,256]{4,3,2,1,0:T(8,128)(2,1)}, u32[]{:S(2)}) copy-start(bf16[1,1,2,1024,256]{4,3,2,1,0:T(8,128)(2,1)} %param.7) | copy-start | bytes 3145732
  76.7 26.0 %collective-permute-start.2 = (bf16[1024,512]{0,1:T(8,128)(2,1)S(1)}, bf16[1024,512]{0,1:T(8,128)(2,1)S(1)}, u32[]{:S(2)}, u32[]{:S(2)}) collective-permute-start(bf16[1024,512]{0,1:T(8,128)(2,1)S(1)} %fusion.2), channel_id=1, source_target_pairs={{0,8},{8,16},{16,24},{1,9},{9,17},{17,25},{2,10},{10,18},{18,26},{... | collective-permute-start | bytes 3145736 | tf_op jit(solution)/shard_map/ppermute | solution.py:10
Sparse Core Ops, SparseCore 0:
  110.7 50.2 reduce-scatter.1

commit v2 on v1

v2 whole, which is shorter than its diff:
```python
import jax
import jax.numpy as jnp
from jax import lax
from jax.sharding import PartitionSpec as P

CHUNKS = 4
DELAY = 2


def shifted(block, axis, distance):
    devices = range(lax.axis_size(axis))
    route = [(i - distance, i) for i in devices if i - distance in devices]
    return lax.ppermute(block, axis, route)


def advance(panel, weight, factor):
    shots = panel.shape[1] // 2
    turned = jnp.concatenate([-panel[:, shots:], panel[:, :shots]], axis=1)
    out = jnp.dot(weight[0], panel, preferred_element_type=jnp.float32) + jnp.dot(
        weight[1], turned, preferred_element_type=jnp.float32
    )
    return (out * factor[:, None]).astype(jnp.bfloat16)


def shards(source, propagator, transmission, upgoing):
    weight = propagator[0, 0]
    factor = transmission[0, 0]
    upward = upgoing[0, 0]
    width = weight.shape[1]
    shots = source.shape[3]
    level = lax.axis_index("depth")
    levels = lax.axis_size("depth")
    freqs = lax.axis_size("freq")
    rows_own = width // freqs
    part = shots // CHUNKS
    starts = [
        jnp.concatenate([source[0, 0, :, at : at + part], source[0, 1, :, at : at + part]], axis=1)
        for at in range(0, shots, part)
    ]
    first = lax.rem(DELAY * (levels - 1 - level), CHUNKS) * part
    rolled = lax.dynamic_slice_in_dim(jnp.concatenate([upward, upward], axis=2), first, shots, axis=2)
    up_pair = jnp.concatenate(
        [rolled[part_of, :, at : at + part] for at in range(0, shots, part) for part_of in range(2)], axis=1
    )
    ticks = CHUNKS + DELAY * (levels - 1)
    flying = []
    outs = []
    for tick in range(ticks):
        panel = starts[tick % CHUNKS]
        if tick >= DELAY:
            panel = jnp.where(level == 0, panel, flying[tick - DELAY])
        out = advance(panel, weight, factor)
        outs.append(out)
        if tick + DELAY < ticks:
            flying.append(shifted(out, "depth", 1))
    last = outs[-CHUNKS:]
    dims = (((1,), (1,)), ((), ()))
    panel = jnp.concatenate(last, axis=1)
    turned = jnp.concatenate([half for out in last for half in (-out[:, part:], out[:, :part])], axis=1)
    both = jnp.concatenate([panel, turned], axis=0)
    term = lax.dot_general(up_pair, both, dims, preferred_element_type=jnp.float32)
    summed = lax.psum_scatter(
        term.astype(jnp.bfloat16), "freq", scatter_dimension=0, tiled=True
    )
    scale = (2.0 * shots * freqs) ** (-0.5)
    return (summed.astype(jnp.float32) * scale).reshape(1, rows_own, 2, width)


def solution(mesh):
    return jax.shard_map(
        shards,
        mesh=mesh,
        in_specs=(
            P("freq", None, None, None),
            P("depth", "freq", None, None, None),
            P("depth", "freq", None),
            P("depth", "freq", None, None, None),
        ),
        out_specs=P("depth", "freq", None, None),
        check_vma=False,
    )
```

time: 173 us -> 147 us (0.85)
  waiting for transfers between devices: 123 us -> 67.9 us
  matrix products: 18.2 us -> 32.7 us
  starting transfers between devices: 8.13 us -> 17 us
  local copies, waits for them, and re-layouts: 3.75 us -> 8.61 us
    ppermute x3 -> x8, waiting for transfers between devices: 72.3 us -> 17.4 us  [shifted(): return lax.ppermute(block, axis, route)]
    dot_general x8 -> x20, matrix products: 13.9 us -> 26.3 us  [the longest x10 13.3 us: advance(): jnp.dot(weight[1], turned, preferred_element_type=jnp.float32)]
    ppermute x3 -> x8, starting transfers between devices: 8.13 us -> 17 us  [shifted(): return lax.ppermute(block, axis, route)]
    select_n x0 -> x8, other arithmetic: none -> 2.6 us  [shards(): panel = jnp.where(level == 0, panel, flying[tick - DELAY])]
    concatenate x0 -> x2, local copies, waits for them, and re-layouts: none -> 2.45 us  [the longest x1 2.44 us: shards(): jnp.concatenate([rolled[part_of, :, at:at + part] for at in range(0, shot...]
    sub x4 -> x0, other arithmetic: 2.21 us -> none  [advance(): out_real = real_part[:, :shots] - imag_part[:, shots:]]
    dot_general x1, matrix products: 4.3 us -> 6.44 us  [shards(): lax.dot_general(up_pair, both, dims, preferred_element_type=jnp.float32)]
  transfers between devices with their start and end apart: 4 -> 9, of which waited for: 4 -> 7; matrix products, arithmetic and copies ran while one was open for 0% -> 18% of each run, Pallas kernels for 0% -> 0%
where the time goes in v2:
time: 147 us; the launch traced here: 145 us
  waiting for transfers between devices  67.9 us (46%)
  matrix products  32.7 us (22%)
  starting transfers between devices  17 us (12%)
  between operations  13.9 us (9%)
  local copies, waits for them, and re-layouts  8.61 us (6%)
  other arithmetic  4.42 us (3%)
    reduce_scatter x1, waiting for transfers between devices, shards(): lax.psum_scatter(term.astype(jnp.bfloat16), 'freq', scatter_dimension=0,...  50.4 us
    ppermute x8, waiting for transfers between devices, shifted(): return lax.ppermute(block, axis, route)  17.4 us
    ppermute x8, starting transfers between devices, shifted(): return lax.ppermute(block, axis, route)  17 us
    dot_general x10, matrix products, advance(): jnp.dot(weight[1], turned, preferred_element_type=jnp.float32)  13.3 us
    dot_general x10, matrix products, advance(): jnp.dot(weight[0], panel, preferred_element_type=jnp.float32)  13 us
    dot_general x1, matrix products, shards(): lax.dot_general(up_pair, both, dims, preferred_element_type=jnp.float32)  6.44 us
  transfers between devices with their start and end apart: 9, of which 7 were waited for; matrix products, arithmetic and copies ran while one was open for 18% of the time, Pallas kernels for 0%

profile of v2, /device:TPU:4, one launch (start us, length us, event | category | flops | bytes accessed | tf_op | source)
XLA Modules:
  0.0 144.5 jit_solution(4390185320438206237)
XLA Ops:
  6.5 2.0 %fusion.237 = (bf16[1,1,1024,64]{3,2,1,0:T(8,128)(2,1)S(1)}, bf16[1,1,1024,64]{3,2,1,0:T(8,128)(2,1)S(1)}, bf16[1,1,1024,64]{3,2,1,0:T(8,128)(2,1)S(1)}, bf16[1,...) fusion(bf16[1,2,1024,256]{3,2,1,0:T(8,128)(2,1)} %param.4), kind=kLoop, calls=%fused_computation.199 | loop fusion | bytes 2097152 | tf_op jit(solution)/shard_map/slice | solution.py:37
  8.8 2.4 %fusion.27 = f32[128,1024]{1,0:T(8,128)S(1)} fusion(bf16[1024,64]{0,1:T(8,128)(2,1)S(1)} %bitcast.189, bf16[1024,64]{0,1:T(8,128)(2,1)S(1)} %bitcast_negate_fusion.1, bf16[1,1,2,1024,1024]{4,3,2,1,0:T(8,128)(2,1)} %param.5), kind=kOutput, calls=%fused_computation.30 | convolution fusion | flops 268959744 | bytes 2883584 | tf_op jit(solution)/shard_map/dot_general | solution.py:19
  11.2 3.1 %fusion.139 = bf16[1024,128]{0,1:T(8,128)(2,1)} fusion(f32[128,1024]{1,0:T(8,128)S(1)} %fusion.27, f32[1024]{0:T(1024)S(1)} %bitcast.202, bf16[1024,64]{0,1:T(8,128)(2,1)S(1)} %bitcast.182, bf16[1024,64]{0,1:T(8,128)(2,1)S(1)} %bitcast.190, bf16[1,1,2,1024,1024]{4,3,2,1,0:T(8,128)(2,1)} %param.5), kind=kOutput, calls=%fused_computation.82 | convolution fusion | flops 269352960 | bytes 3149824 | tf_op jit(solution)/shard_map/dot_general | solution.py:19
  14.4 3.4 %collective-permute-start = (bf16[1024,128]{0,1:T(8,128)(2,1)}, bf16[1024,128]{0,1:T(8,128)(2,1)}, u32[]{:S(2)}, u32[]{:S(2)}) collective-permute-start(bf16[1024,128]{0,1:T(8,128)(2,1)} %fusion.139), channel_id=1, source_target_pairs={{0,8},{8,16},{16,24},{1,9},{9,17},{17,25},{2,10},{10,18},{18,26},{... | collective-permute-start | bytes 786440 | tf_op jit(solution)/shard_map/ppermute | solution.py:13
  18.1 2.5 %fusion.19 = f32[128,1024]{1,0:T(8,128)S(1)} fusion(bf16[1024,64]{0,1:T(8,128)(2,1)S(1)} %bitcast.185, bf16[1024,64]{0,1:T(8,128)(2,1)S(1)} %bitcast_negate_fusion, bf16[1,1,2,1024,1024]{4,3,2,1,0:T(8,128)(2,1)} %param.5), kind=kOutput, calls=%fused_computation.22 | convolution fusion | flops 268959744 | bytes 2883584 | tf_op jit(solution)/shard_map/dot_general | solution.py:19
  20.6 3.1 %fusion.151 = bf16[1024,128]{0,1:T(8,128)(2,1)} fusion(f32[128,1024]{1,0:T(8,128)S(1)} %fusion.19, f32[1024]{0:T(1024)S(1)} %bitcast.203, bf16[1024,64]{0,1:T(8,128)(2,1)S(1)} %bitcast.179, bf16[1024,64]{0,1:T(8,128)(2,1)S(1)} %bitcast.186, bf16[1,1,2,1024,1024]{4,3,2,1,0:T(8,128)(2,1)} %param.5), kind=kOutput, calls=%fused_computation.86 | convolution fusion | flops 269352960 | bytes 3149824 | tf_op jit(solution)/shard_map/dot_general | solution.py:19
  23.7 1.9 %collective-permute-start.3 = (bf16[1024,128]{0,1:T(8,128)(2,1)}, bf16[1024,128]{0,1:T(8,128)(2,1)}, u32[]{:S(2)}, u32[]{:S(2)}) collective-permute-start(bf16[1024,128]{0,1:T(8,128)(2,1)} %fusion.151), channel_id=1, source_target_pairs={{0,8},{8,16},{16,24},{1,9},{9,17},{17,25},{2,10},{10,18},{18,26},{... | collective-permute-start | bytes 786440 | tf_op jit(solution)/shard_map/ppermute | solution.py:13
  26.6 1.3 slice_bitcast_fusion
  27.9 2.4 %concatenate.58 = bf16[1024,512]{1,0:T(8,128)(2,1)S(1)} concatenate(bf16[1024,64]{1,0:T(8,128)(2,1)} %get-tuple-element.20, bf16[1024,64]{1,0:T(8,128)(2,1)} %get-tuple-element.19, bf16[1024,64]{1,0:T(8,128)(2,1)} %get-tuple-element.18, bf16[1024,64]{1,0:T(8,128)(2,1)S(1)} %get-tuple-element.17, bf16[1024,64]{1,0:T(8,128)(2,1)S(1)} %get-tuple-element.16, ...), dimensions={1} | concatenate | bytes 2097152 | tf_op jit(solution)/shard_map/concatenate | solution.py:42
  30.3 1.2 broadcast_select_fusion.7
  31.5 2.5 %fusion.25 = f32[128,1024]{1,0:T(8,128)S(1)} fusion(bf16[1024,64]{0,1:T(8,128)(2,1)S(1)} %get-tuple-element.36, bf16[1024,64]{0,1:T(8,128)(2,1)S(1)} %get-tuple-element.35, bf16[1,1,2,1024,1024]{4,3,2,1,0:T(8,128)(2,1)} %param.5), kind=kOutput, calls=%fused_computation.28 | convolution fusion | flops 268959744 | bytes 2883584 | tf_op jit(solution)/shard_map/dot_general | solution.py:19
  34.9 1.9 %collective-permute-start.1 = (bf16[1024,128]{0,1:T(8,128)(2,1)S(1)}, bf16[1024,128]{0,1:T(8,128)(2,1)S(1)}, u32[]{:S(2)}, u32[]{:S(2)}) collective-permute-start(bf16[1024,128]{0,1:T(8,128)(2,1)S(1)} %fusion.142), channel_id=1, source_target_pairs={{0,8},{8,16},{16,24},{1,9},{9,17},{17,25},{2,10},{10,18},{18,26},{... | collective-permute-start | bytes 786440 | tf_op jit(solution)/shard_map/ppermute | solution.py:13
  39.6 1.9 %collective-permute-start.4 = (bf16[1024,128]{0,1:T(8,128)(2,1)S(1)}, bf16[1024,128]{0,1:T(8,128)(2,1)S(1)}, u32[]{:S(2)}, u32[]{:S(2)}) collective-permute-start(bf16[1024,128]{0,1:T(8,128)(2,1)S(1)} %fusion.154), channel_id=1, source_target_pairs={{0,8},{8,16},{16,24},{1,9},{9,17},{17,25},{2,10},{10,18},{18,26},{... | collective-permute-start | bytes 786440 | tf_op jit(solution)/shard_map/ppermute | solution.py:13
  41.5 4.8 %collective-permute-done.1 = bf16[1024,128]{0,1:T(8,128)(2,1)S(1)} collective-permute-done((bf16[1024,128]{0,1:T(8,128)(2,1)S(1)}, bf16[1024,128]{0,1:T(8,128)(2,1)S(1)}, u32[]{:S(2)}, u32[]{:S(2)}) %collective-permute-start.1) | collective-permute-done | bytes 262176 | tf_op jit(solution)/shard_map/ppermute | solution.py:13
  48.1 1.9 %collective-permute-start.2 = (bf16[1024,128]{0,1:T(8,128)(2,1)S(1)}, bf16[1024,128]{0,1:T(8,128)(2,1)S(1)}, u32[]{:S(2)}, u32[]{:S(2)}) collective-permute-start(bf16[1024,128]{0,1:T(8,128)(2,1)S(1)} %fusion.145), channel_id=1, source_target_pairs={{0,8},{8,16},{16,24},{1,9},{9,17},{17,25},{2,10},{10,18},{18,26},{... | collective-permute-start | bytes 786440 | tf_op jit(solution)/shard_map/ppermute | solution.py:13
  52.9 1.9 %collective-permute-start.5 = (bf16[1024,128]{0,1:T(8,128)(2,1)S(1)}, bf16[1024,128]{0,1:T(8,128)(2,1)S(1)}, u32[]{:S(2)}, u32[]{:S(2)}) collective-permute-start(bf16[1024,128]{0,1:T(8,128)(2,1)S(1)} %fusion.157), channel_id=1, source_target_pairs={{0,8},{8,16},{16,24},{1,9},{9,17},{17,25},{2,10},{10,18},{18,26},{... | collective-permute-start | bytes 786440 | tf_op jit(solution)/shard_map/ppermute | solution.py:13
  54.8 2.5 %collective-permute-done.2 = bf16[1024,128]{0,1:T(8,128)(2,1)S(1)} collective-permute-done((bf16[1024,128]{0,1:T(8,128)(2,1)S(1)}, bf16[1024,128]{0,1:T(8,128)(2,1)S(1)}, u32[]{:S(2)}, u32[]{:S(2)}) %collective-permute-start.2) | collective-permute-done | bytes 262176 | tf_op jit(solution)/shard_map/ppermute | solution.py:13
  59.1 2.1 %collective-permute-start.6 = (bf16[1024,128]{0,1:T(8,128)(2,1)S(1)}, bf16[1024,128]{0,1:T(8,128)(2,1)S(1)}, u32[]{:S(2)}, u32[]{:S(2)}) collective-permute-start(bf16[1024,128]{0,1:T(8,128)(2,1)S(1)} %fusion.148), channel_id=1, source_target_pairs={{0,8},{8,16},{16,24},{1,9},{9,17},{17,25},{2,10},{10,18},{18,26},{... | collective-permute-start | bytes 786440 | tf_op jit(solution)/shard_map/ppermute | solution.py:13
  61.2 3.7 %collective-permute-done.5 = bf16[1024,128]{0,1:T(8,128)(2,1)S(1)} collective-permute-done((bf16[1024,128]{0,1:T(8,128)(2,1)S(1)}, bf16[1024,128]{0,1:T(8,128)(2,1)S(1)}, u32[]{:S(2)}, u32[]{:S(2)}) %collective-permute-start.5) | collective-permute-done | bytes 262176 | tf_op jit(solution)/shard_map/ppermute | solution.py:13
  66.7 1.9 %collective-permute-start.7 = (bf16[1024,128]{0,1:T(8,128)(2,1)S(1)}, bf16[1024,128]{0,1:T(8,128)(2,1)S(1)}, u32[]{:S(2)}, u32[]{:S(2)}) collective-permute-start(bf16[1024,128]{0,1:T(8,128)(2,1)S(1)} %fusion.160), channel_id=1, source_target_pairs={{0,8},{8,16},{16,24},{1,9},{9,17},{17,25},{2,10},{10,18},{18,26},{... | collective-permute-start | bytes 786440 | tf_op jit(solution)/shard_map/ppermute | solution.py:13
  70.6 5.3 %collective-permute-done.7 = bf16[1024,128]{0,1:T(8,128)(2,1)S(1)} collective-permute-done((bf16[1024,128]{0,1:T(8,128)(2,1)S(1)}, bf16[1024,128]{0,1:T(8,128)(2,1)S(1)}, u32[]{:S(2)}, u32[]{:S(2)}) %collective-permute-start.7) | collective-permute-done | bytes 262176 | tf_op jit(solution)/shard_map/ppermute | solution.py:13
  77.8 6.4 %convolution_convert_fusion = bf16[1024,2048]{1,0:T(8,128)(2,1)} fusion(bf16[1024,512]{1,0:T(8,128)(2,1)S(1)} %concatenate.58, bf16[1024,512]{0,1:T(8,128)(2,1)S(1)} %slice_dynamic-update-slice_fusion, bf16[1024,128]{0,1:T(8,128)(2,1)S(1)} %fusion.166, bf16[1024,128]{0,1:T(8,128)(2,1)S(1)} %fusion.163, bf16[1024,128]{0,1:T(8,128)(2,1)S(1)} %fusion.160, ...), kind=kOutput, calls=%fused_computation | convolution fusion | flops 2160066560 | bytes 7340032 | tf_op jit(solution)/shard_map/dot_general | solution.py:61
  84.2 50.4 %reduce-scatter.2.cloned.1.call-done = bf16[128,2048]{1,0:T(8,128)(2,1)} async-done(((bf16[1024,2048]{1,0:T(8,128)(2,1)}), bf16[128,2048]{1,0:T(8,128)(2,1)}) %reduce-scatter.2.cloned.1.call-update) | async-done | bytes 524304 | tf_op jit(solution)/shard_map/reduce_scatter | solution.py:62
  135.8 1.9 %reshape.8 = f32[1,128,2,1024]{3,2,1,0:T(2,128)} reshape(f32[128,2048]{1,0:T(8,128)S(1)} %convert_multiply_fusion) | data formatting | bytes 2097152 | tf_op jit(solution)/shard_map/reshape | solution.py:66
  (62 shorter events, 18.1 us)
Async XLA Ops:
  6.5 4.7 %copy-start.2 = (f32[1,1,1024]{2,1,0:T(1,128)S(1)}, f32[1,1,1024]{2,1,0:T(1,128)}, u32[]{:S(2)}) copy-start(f32[1,1,1024]{2,1,0:T(1,128)} %param.6) | copy-start | bytes 12292
  6.5 128.2 %reduce-scatter.2.cloned.1.call-start = ((), (), s32[]{:S(2)}) async-start(), calls=%async_computation.1 | async-start | bytes 4718592 | tf_op jit(solution)/shard_map/reduce_scatter | solution.py:62
  14.4 16.0 %collective-permute-start = (bf16[1024,128]{0,1:T(8,128)(2,1)}, bf16[1024,128]{0,1:T(8,128)(2,1)}, u32[]{:S(2)}, u32[]{:S(2)}) collective-permute-start(bf16[1024,128]{0,1:T(8,128)(2,1)} %fusion.139), channel_id=1, source_target_pairs={{0,8},{8,16},{16,24},{1,9},{9,17},{17,25},{2,10},{10,18},{18,26},{... | collective-permute-start | bytes 786440 | tf_op jit(solution)/shard_map/ppermute | solution.py:13
  18.0 8.1 %copy-start = (bf16[1,1,2,1024,256]{4,3,2,1,0:T(8,128)(2,1)S(1)}, bf16[1,1,2,1024,256]{4,3,2,1,0:T(8,128)(2,1)}, u32[]{:S(2)}) copy-start(bf16[1,1,2,1024,256]{4,3,2,1,0:T(8,128)(2,1)} %param.7) | copy-start | bytes 3145732
  23.7 13.1 %collective-permute-start.3 = (bf16[1024,128]{0,1:T(8,128)(2,1)}, bf16[1024,128]{0,1:T(8,128)(2,1)}, u32[]{:S(2)}, u32[]{:S(2)}) collective-permute-start(bf16[1024,128]{0,1:T(8,128)(2,1)} %fusion.151), channel_id=1, source_target_pairs={{0,8},{8,16},{16,24},{1,9},{9,17},{17,25},{2,10},{10,18},{18,26},{... | collective-permute-start | bytes 786440 | tf_op jit(solution)/shard_map/ppermute | solution.py:13
  30.3 3.8 %copy-start.1 = (bf16[1,1,2,1024,1024]{4,3,2,1,0:T(8,128)(2,1)S(1)}, bf16[1,1,2,1024,1024]{4,3,2,1,0:T(8,128)(2,1)}, u32[]{:S(2)}) copy-start(bf16[1,1,2,1024,1024]{4,3,2,1,0:T(8,128)(2,1)} %param.5) | copy-start | bytes 12582916
  34.9 11.4 %collective-permute-start.1 = (bf16[1024,128]{0,1:T(8,128)(2,1)S(1)}, bf16[1024,128]{0,1:T(8,128)(2,1)S(1)}, u32[]{:S(2)}, u32[]{:S(2)}) collective-permute-start(bf16[1024,128]{0,1:T(8,128)(2,1)S(1)} %fusion.142), channel_id=1, source_target_pairs={{0,8},{8,16},{16,24},{1,9},{9,17},{17,25},{2,10},{10,18},{18,26},{... | collective-permute-start | bytes 786440 | tf_op jit(solution)/shard_map/ppermute | solution.py:13
  39.6 11.5 %collective-permute-start.4 = (bf16[1024,128]{0,1:T(8,128)(2,1)S(1)}, bf16[1024,128]{0,1:T(8,128)(2,1)S(1)}, u32[]{:S(2)}, u32[]{:S(2)}) collective-permute-start(bf16[1024,128]{0,1:T(8,128)(2,1)S(1)} %fusion.154), channel_id=1, source_target_pairs={{0,8},{8,16},{16,24},{1,9},{9,17},{17,25},{2,10},{10,18},{18,26},{... | collective-permute-start | bytes 786440 | tf_op jit(solution)/shard_map/ppermute | solution.py:13
  48.1 9.2 %collective-permute-start.2 = (bf16[1024,128]{0,1:T(8,128)(2,1)S(1)}, bf16[1024,128]{0,1:T(8,128)(2,1)S(1)}, u32[]{:S(2)}, u32[]{:S(2)}) collective-permute-start(bf16[1024,128]{0,1:T(8,128)(2,1)S(1)} %fusion.145), channel_id=1, source_target_pairs={{0,8},{8,16},{16,24},{1,9},{9,17},{17,25},{2,10},{10,18},{18,26},{... | collective-permute-start | bytes 786440 | tf_op jit(solution)/shard_map/ppermute | solution.py:13
  52.9 12.0 %collective-permute-start.5 = (bf16[1024,128]{0,1:T(8,128)(2,1)S(1)}, bf16[1024,128]{0,1:T(8,128)(2,1)S(1)}, u32[]{:S(2)}, u32[]{:S(2)}) collective-permute-start(bf16[1024,128]{0,1:T(8,128)(2,1)S(1)} %fusion.157), channel_id=1, source_target_pairs={{0,8},{8,16},{16,24},{1,9},{9,17},{17,25},{2,10},{10,18},{18,26},{... | collective-permute-start | bytes 786440 | tf_op jit(solution)/shard_map/ppermute | solution.py:13
  59.1 9.7 %collective-permute-start.6 = (bf16[1024,128]{0,1:T(8,128)(2,1)S(1)}, bf16[1024,128]{0,1:T(8,128)(2,1)S(1)}, u32[]{:S(2)}, u32[]{:S(2)}) collective-permute-start(bf16[1024,128]{0,1:T(8,128)(2,1)S(1)} %fusion.148), channel_id=1, source_target_pairs={{0,8},{8,16},{16,24},{1,9},{9,17},{17,25},{2,10},{10,18},{18,26},{... | collective-permute-start | bytes 786440 | tf_op jit(solution)/shard_map/ppermute | solution.py:13
  66.7 9.2 %collective-permute-start.7 = (bf16[1024,128]{0,1:T(8,128)(2,1)S(1)}, bf16[1024,128]{0,1:T(8,128)(2,1)S(1)}, u32[]{:S(2)}, u32[]{:S(2)}) collective-permute-start(bf16[1024,128]{0,1:T(8,128)(2,1)S(1)} %fusion.160), channel_id=1, source_target_pairs={{0,8},{8,16},{16,24},{1,9},{9,17},{17,25},{2,10},{10,18},{18,26},{... | collective-permute-start | bytes 786440 | tf_op jit(solution)/shard_map/ppermute | solution.py:13
Sparse Core Ops, SparseCore 0:
  84.4 50.2 reduce-scatter.1

commit v3 on v2

--- a/solution.py
+++ b/solution.py
@@ -8,8 +8,8 @@
 
 
 def shifted(block, axis, distance):
-    devices = range(lax.axis_size(axis))
-    route = [(i - distance, i) for i in devices if i - distance in devices]
+    size = lax.axis_size(axis)
+    route = [(i, (i + distance) % size) for i in range(size)]
     return lax.ppermute(block, axis, route)
 
 

time: 147 us -> 139 us (0.946)
  starting transfers between devices: 17 us -> 8.42 us
    ppermute x8, starting transfers between devices: 17 us -> 8.42 us  [shifted(): return lax.ppermute(block, axis, route)]
  transfers between devices with their start and end apart: 9 -> 9, of which waited for: 7 -> 7; matrix products, arithmetic and copies ran while one was open for 18% -> 19% of each run, Pallas kernels for 0% -> 0%
where the time goes in v3:
time: 139 us; the launch traced here: 137 us
  waiting for transfers between devices  68.9 us (50%)
  matrix products  32.7 us (24%)
  between operations  13.8 us (10%)
  local copies, waits for them, and re-layouts  8.61 us (6%)
  starting transfers between devices  8.42 us (6%)
  other arithmetic  4.41 us (3%)
    reduce_scatter x1, waiting for transfers between devices, shards(): lax.psum_scatter(term.astype(jnp.bfloat16), 'freq', scatter_dimension=0,...  50.8 us
    ppermute x8, waiting for transfers between devices, shifted(): return lax.ppermute(block, axis, route)  18.1 us
    dot_general x10, matrix products, advance(): jnp.dot(weight[1], turned, preferred_element_type=jnp.float32)  13.3 us
    dot_general x10, matrix products, advance(): jnp.dot(weight[0], panel, preferred_element_type=jnp.float32)  13 us
    ppermute x8, starting transfers between devices, shifted(): return lax.ppermute(block, axis, route)  8.42 us
    dot_general x1, matrix products, shards(): lax.dot_general(up_pair, both, dims, preferred_element_type=jnp.float32)  6.44 us
  transfers between devices with their start and end apart: 9, of which 7 were waited for; matrix products, arithmetic and copies ran while one was open for 19% of the time, Pallas kernels for 0%

profile of v3, /device:TPU:4, one launch (start us, length us, event | category | flops | bytes accessed | tf_op | source)
XLA Modules:
  0.0 136.9 jit_solution(6603272489064328048)
XLA Ops:
  6.5 2.0 %fusion.237 = (bf16[1,1,1024,64]{3,2,1,0:T(8,128)(2,1)S(1)}, bf16[1,1,1024,64]{3,2,1,0:T(8,128)(2,1)S(1)}, bf16[1,1,1024,64]{3,2,1,0:T(8,128)(2,1)S(1)}, bf16[1,...) fusion(bf16[1,2,1024,256]{3,2,1,0:T(8,128)(2,1)} %param.4), kind=kLoop, calls=%fused_computation.199 | loop fusion | bytes 2097152 | tf_op jit(solution)/shard_map/slice | solution.py:37
  8.8 2.4 %fusion.27 = f32[128,1024]{1,0:T(8,128)S(1)} fusion(bf16[1024,64]{0,1:T(8,128)(2,1)S(1)} %bitcast.189, bf16[1024,64]{0,1:T(8,128)(2,1)S(1)} %bitcast_negate_fusion.1, bf16[1,1,2,1024,1024]{4,3,2,1,0:T(8,128)(2,1)} %param.5), kind=kOutput, calls=%fused_computation.30 | convolution fusion | flops 268959744 | bytes 2883584 | tf_op jit(solution)/shard_map/dot_general | solution.py:19
  11.2 3.1 %fusion.139 = bf16[1024,128]{0,1:T(8,128)(2,1)} fusion(f32[128,1024]{1,0:T(8,128)S(1)} %fusion.27, f32[1024]{0:T(1024)S(1)} %bitcast.202, bf16[1024,64]{0,1:T(8,128)(2,1)S(1)} %bitcast.182, bf16[1024,64]{0,1:T(8,128)(2,1)S(1)} %bitcast.190, bf16[1,1,2,1024,1024]{4,3,2,1,0:T(8,128)(2,1)} %param.5), kind=kOutput, calls=%fused_computation.82 | convolution fusion | flops 269352960 | bytes 3149824 | tf_op jit(solution)/shard_map/dot_general | solution.py:19
  14.4 1.5 %collective-permute-start = (bf16[1024,128]{0,1:T(8,128)(2,1)}, bf16[1024,128]{0,1:T(8,128)(2,1)}, u32[]{:S(2)}, u32[]{:S(2)}) collective-permute-start(bf16[1024,128]{0,1:T(8,128)(2,1)} %fusion.139), channel_id=1, source_target_pairs={{0,8},{8,16},{16,24},{24,0},{1,9},{9,17},{17,25},{25,1},{2,10},{10... | collective-permute-start | bytes 786440 | tf_op jit(solution)/shard_map/ppermute | solution.py:13
  16.2 2.5 %fusion.19 = f32[128,1024]{1,0:T(8,128)S(1)} fusion(bf16[1024,64]{0,1:T(8,128)(2,1)S(1)} %bitcast.185, bf16[1024,64]{0,1:T(8,128)(2,1)S(1)} %bitcast_negate_fusion, bf16[1,1,2,1024,1024]{4,3,2,1,0:T(8,128)(2,1)} %param.5), kind=kOutput, calls=%fused_computation.22 | convolution fusion | flops 268959744 | bytes 2883584 | tf_op jit(solution)/shard_map/dot_general | solution.py:19
  18.7 3.1 %fusion.151 = bf16[1024,128]{0,1:T(8,128)(2,1)} fusion(f32[128,1024]{1,0:T(8,128)S(1)} %fusion.19, f32[1024]{0:T(1024)S(1)} %bitcast.203, bf16[1024,64]{0,1:T(8,128)(2,1)S(1)} %bitcast.179, bf16[1024,64]{0,1:T(8,128)(2,1)S(1)} %bitcast.186, bf16[1,1,2,1024,1024]{4,3,2,1,0:T(8,128)(2,1)} %param.5), kind=kOutput, calls=%fused_computation.86 | convolution fusion | flops 269352960 | bytes 3149824 | tf_op jit(solution)/shard_map/dot_general | solution.py:19
  22.8 1.3 slice_bitcast_fusion
  24.0 2.4 %concatenate.58 = bf16[1024,512]{1,0:T(8,128)(2,1)S(1)} concatenate(bf16[1024,64]{1,0:T(8,128)(2,1)} %get-tuple-element.20, bf16[1024,64]{1,0:T(8,128)(2,1)} %get-tuple-element.19, bf16[1024,64]{1,0:T(8,128)(2,1)} %get-tuple-element.18, bf16[1024,64]{1,0:T(8,128)(2,1)S(1)} %get-tuple-element.17, bf16[1024,64]{1,0:T(8,128)(2,1)S(1)} %get-tuple-element.16, ...), dimensions={1} | concatenate | bytes 2097152 | tf_op jit(solution)/shard_map/concatenate | solution.py:42
  26.5 1.2 broadcast_select_fusion.7
  27.7 2.5 %fusion.25 = f32[128,1024]{1,0:T(8,128)S(1)} fusion(bf16[1024,64]{0,1:T(8,128)(2,1)S(1)} %get-tuple-element.36, bf16[1024,64]{0,1:T(8,128)(2,1)S(1)} %get-tuple-element.35, bf16[1,1,2,1024,1024]{4,3,2,1,0:T(8,128)(2,1)} %param.5), kind=kOutput, calls=%fused_computation.28 | convolution fusion | flops 268959744 | bytes 2883584 | tf_op jit(solution)/shard_map/dot_general | solution.py:19
  31.1 2.0 %collective-permute-start.1 = (bf16[1024,128]{0,1:T(8,128)(2,1)S(1)}, bf16[1024,128]{0,1:T(8,128)(2,1)S(1)}, u32[]{:S(2)}, u32[]{:S(2)}) collective-permute-start(bf16[1024,128]{0,1:T(8,128)(2,1)S(1)} %fusion.142), channel_id=1, source_target_pairs={{0,8},{8,16},{16,24},{24,0},{1,9},{9,17},{17,25},{25,1},{2,10},{10... | collective-permute-start | bytes 786440 | tf_op jit(solution)/shard_map/ppermute | solution.py:13
  36.4 4.7 %collective-permute-done.1 = bf16[1024,128]{0,1:T(8,128)(2,1)S(1)} collective-permute-done((bf16[1024,128]{0,1:T(8,128)(2,1)S(1)}, bf16[1024,128]{0,1:T(8,128)(2,1)S(1)}, u32[]{:S(2)}, u32[]{:S(2)}) %collective-permute-start.1) | collective-permute-done | bytes 262176 | tf_op jit(solution)/shard_map/ppermute | solution.py:13
  42.9 1.2 collective-permute-start.2
  44.2 2.6 %collective-permute-done.4 = bf16[1024,128]{0,1:T(8,128)(2,1)S(1)} collective-permute-done((bf16[1024,128]{0,1:T(8,128)(2,1)S(1)}, bf16[1024,128]{0,1:T(8,128)(2,1)S(1)}, u32[]{:S(2)}, u32[]{:S(2)}) %collective-permute-start.4) | collective-permute-done | bytes 262176 | tf_op jit(solution)/shard_map/ppermute | solution.py:13
  48.6 1.2 collective-permute-start.5
  49.8 2.7 %collective-permute-done.2 = bf16[1024,128]{0,1:T(8,128)(2,1)S(1)} collective-permute-done((bf16[1024,128]{0,1:T(8,128)(2,1)S(1)}, bf16[1024,128]{0,1:T(8,128)(2,1)S(1)}, u32[]{:S(2)}, u32[]{:S(2)}) %collective-permute-start.2) | collective-permute-done | bytes 262176 | tf_op jit(solution)/shard_map/ppermute | solution.py:13
  54.3 1.3 collective-permute-start.6
  55.6 3.1 %collective-permute-done.5 = bf16[1024,128]{0,1:T(8,128)(2,1)S(1)} collective-permute-done((bf16[1024,128]{0,1:T(8,128)(2,1)S(1)}, bf16[1024,128]{0,1:T(8,128)(2,1)S(1)}, u32[]{:S(2)}, u32[]{:S(2)}) %collective-permute-start.5) | collective-permute-done | bytes 262176 | tf_op jit(solution)/shard_map/ppermute | solution.py:13
  61.1 3.5 %collective-permute-done.6 = bf16[1024,128]{0,1:T(8,128)(2,1)S(1)} collective-permute-done((bf16[1024,128]{0,1:T(8,128)(2,1)S(1)}, bf16[1024,128]{0,1:T(8,128)(2,1)S(1)}, u32[]{:S(2)}, u32[]{:S(2)}) %collective-permute-start.6) | collective-permute-done | bytes 262176 | tf_op jit(solution)/shard_map/ppermute | solution.py:13
  66.3 1.5 %collective-permute-done.7 = bf16[1024,128]{0,1:T(8,128)(2,1)S(1)} collective-permute-done((bf16[1024,128]{0,1:T(8,128)(2,1)S(1)}, bf16[1024,128]{0,1:T(8,128)(2,1)S(1)}, u32[]{:S(2)}, u32[]{:S(2)}) %collective-permute-start.7) | collective-permute-done | bytes 262176 | tf_op jit(solution)/shard_map/ppermute | solution.py:13
  69.8 6.4 %convolution_convert_fusion = bf16[1024,2048]{1,0:T(8,128)(2,1)} fusion(bf16[1024,512]{1,0:T(8,128)(2,1)S(1)} %concatenate.58, bf16[1024,512]{0,1:T(8,128)(2,1)S(1)} %slice_dynamic-update-slice_fusion, bf16[1024,128]{0,1:T(8,128)(2,1)S(1)} %fusion.166, bf16[1024,128]{0,1:T(8,128)(2,1)S(1)} %fusion.163, bf16[1024,128]{0,1:T(8,128)(2,1)S(1)} %fusion.160, ...), kind=kOutput, calls=%fused_computation | convolution fusion | flops 2160066560 | bytes 7340032 | tf_op jit(solution)/shard_map/dot_general | solution.py:61
  76.3 50.8 %reduce-scatter.2.cloned.1.call-done = bf16[128,2048]{1,0:T(8,128)(2,1)} async-done(((bf16[1024,2048]{1,0:T(8,128)(2,1)}), bf16[128,2048]{1,0:T(8,128)(2,1)}) %reduce-scatter.2.cloned.1.call-update) | async-done | bytes 524304 | tf_op jit(solution)/shard_map/reduce_scatter | solution.py:62
  127.1 1.1 convert_multiply_fusion
  128.2 1.9 %reshape.8 = f32[1,128,2,1024]{3,2,1,0:T(2,128)} reshape(f32[128,2048]{1,0:T(8,128)S(1)} %convert_multiply_fusion) | data formatting | bytes 2097152 | tf_op jit(solution)/shard_map/reshape | solution.py:66
  (62 shorter events, 16.9 us)
Async XLA Ops:
  6.5 4.7 %copy-start.2 = (f32[1,1,1024]{2,1,0:T(1,128)S(1)}, f32[1,1,1024]{2,1,0:T(1,128)}, u32[]{:S(2)}) copy-start(f32[1,1,1024]{2,1,0:T(1,128)} %param.6) | copy-start | bytes 12292
  6.5 120.5 %reduce-scatter.2.cloned.1.call-start = ((), (), s32[]{:S(2)}) async-start(), calls=%async_computation.1 | async-start | bytes 4718592 | tf_op jit(solution)/shard_map/reduce_scatter | solution.py:62
  14.4 12.1 %collective-permute-start = (bf16[1024,128]{0,1:T(8,128)(2,1)}, bf16[1024,128]{0,1:T(8,128)(2,1)}, u32[]{:S(2)}, u32[]{:S(2)}) collective-permute-start(bf16[1024,128]{0,1:T(8,128)(2,1)} %fusion.139), channel_id=1, source_target_pairs={{0,8},{8,16},{16,24},{24,0},{1,9},{9,17},{17,25},{25,1},{2,10},{10... | collective-permute-start | bytes 786440 | tf_op jit(solution)/shard_map/ppermute | solution.py:13
  16.1 6.2 %copy-start = (bf16[1,1,2,1024,256]{4,3,2,1,0:T(8,128)(2,1)S(1)}, bf16[1,1,2,1024,256]{4,3,2,1,0:T(8,128)(2,1)}, u32[]{:S(2)}) copy-start(bf16[1,1,2,1024,256]{4,3,2,1,0:T(8,128)(2,1)} %param.7) | copy-start | bytes 3145732
  21.8 11.3 %collective-permute-start.3 = (bf16[1024,128]{0,1:T(8,128)(2,1)}, bf16[1024,128]{0,1:T(8,128)(2,1)}, u32[]{:S(2)}, u32[]{:S(2)}) collective-permute-start(bf16[1024,128]{0,1:T(8,128)(2,1)} %fusion.151), channel_id=1, source_target_pairs={{0,8},{8,16},{16,24},{24,0},{1,9},{9,17},{17,25},{25,1},{2,10},{10... | collective-permute-start | bytes 786440 | tf_op jit(solution)/shard_map/ppermute | solution.py:13
  26.5 3.8 %copy-start.1 = (bf16[1,1,2,1024,1024]{4,3,2,1,0:T(8,128)(2,1)S(1)}, bf16[1,1,2,1024,1024]{4,3,2,1,0:T(8,128)(2,1)}, u32[]{:S(2)}) copy-start(bf16[1,1,2,1024,1024]{4,3,2,1,0:T(8,128)(2,1)} %param.5) | copy-start | bytes 12582916
  31.1 10.1 %collective-permute-start.1 = (bf16[1024,128]{0,1:T(8,128)(2,1)S(1)}, bf16[1024,128]{0,1:T(8,128)(2,1)S(1)}, u32[]{:S(2)}, u32[]{:S(2)}) collective-permute-start(bf16[1024,128]{0,1:T(8,128)(2,1)S(1)} %fusion.142), channel_id=1, source_target_pairs={{0,8},{8,16},{16,24},{24,0},{1,9},{9,17},{17,25},{25,1},{2,10},{10... | collective-permute-start | bytes 786440 | tf_op jit(solution)/shard_map/ppermute | solution.py:13
  35.8 10.9 %collective-permute-start.4 = (bf16[1024,128]{0,1:T(8,128)(2,1)S(1)}, bf16[1024,128]{0,1:T(8,128)(2,1)S(1)}, u32[]{:S(2)}, u32[]{:S(2)}) collective-permute-start(bf16[1024,128]{0,1:T(8,128)(2,1)S(1)} %fusion.154), channel_id=1, source_target_pairs={{0,8},{8,16},{16,24},{24,0},{1,9},{9,17},{17,25},{25,1},{2,10},{10... | collective-permute-start | bytes 786440 | tf_op jit(solution)/shard_map/ppermute | solution.py:13
  42.9 9.6 %collective-permute-start.2 = (bf16[1024,128]{0,1:T(8,128)(2,1)S(1)}, bf16[1024,128]{0,1:T(8,128)(2,1)S(1)}, u32[]{:S(2)}, u32[]{:S(2)}) collective-permute-start(bf16[1024,128]{0,1:T(8,128)(2,1)S(1)} %fusion.145), channel_id=1, source_target_pairs={{0,8},{8,16},{16,24},{24,0},{1,9},{9,17},{17,25},{25,1},{2,10},{10... | collective-permute-start | bytes 786440 | tf_op jit(solution)/shard_map/ppermute | solution.py:13
  48.6 10.1 %collective-permute-start.5 = (bf16[1024,128]{0,1:T(8,128)(2,1)S(1)}, bf16[1024,128]{0,1:T(8,128)(2,1)S(1)}, u32[]{:S(2)}, u32[]{:S(2)}) collective-permute-start(bf16[1024,128]{0,1:T(8,128)(2,1)S(1)} %fusion.157), channel_id=1, source_target_pairs={{0,8},{8,16},{16,24},{24,0},{1,9},{9,17},{17,25},{25,1},{2,10},{10... | collective-permute-start | bytes 786440 | tf_op jit(solution)/shard_map/ppermute | solution.py:13
  54.3 10.3 %collective-permute-start.6 = (bf16[1024,128]{0,1:T(8,128)(2,1)S(1)}, bf16[1024,128]{0,1:T(8,128)(2,1)S(1)}, u32[]{:S(2)}, u32[]{:S(2)}) collective-permute-start(bf16[1024,128]{0,1:T(8,128)(2,1)S(1)} %fusion.148), channel_id=1, source_target_pairs={{0,8},{8,16},{16,24},{24,0},{1,9},{9,17},{17,25},{25,1},{2,10},{10... | collective-permute-start | bytes 786440 | tf_op jit(solution)/shard_map/ppermute | solution.py:13
  60.5 7.4 %collective-permute-start.7 = (bf16[1024,128]{0,1:T(8,128)(2,1)S(1)}, bf16[1024,128]{0,1:T(8,128)(2,1)S(1)}, u32[]{:S(2)}, u32[]{:S(2)}) collective-permute-start(bf16[1024,128]{0,1:T(8,128)(2,1)S(1)} %fusion.160), channel_id=1, source_target_pairs={{0,8},{8,16},{16,24},{24,0},{1,9},{9,17},{17,25},{25,1},{2,10},{10... | collective-permute-start | bytes 786440 | tf_op jit(solution)/shard_map/ppermute | solution.py:13
Sparse Core Ops, SparseCore 0:
  76.4 50.6 reduce-scatter.1

commit v4 on v3

v4 whole, which is shorter than its diff:
```python
import functools
import math

import jax
import jax.numpy as jnp
from jax import lax
from jax.experimental import pallas as pl
from jax.experimental.pallas import tpu as pltpu
from jax.sharding import PartitionSpec as P

CHUNKS = 4
DELAY = 2
LIMIT = 48 * 1024 * 1024


def ring(block, axis, distance):
    size = lax.axis_size(axis)
    return lax.ppermute(block, axis, [(i, (i + distance) % size) for i in range(size)])


def swapped(block, axis, bit):
    return lax.ppermute(block, axis, [(i, i ^ bit) for i in range(lax.axis_size(axis))])


def first_kernel(part, source_ref, weight_ref, factor_ref, out_ref):
    chunks = out_ref.shape[0]
    dims = (((0,), (1,)), ((), ()))
    dot = functools.partial(lax.dot_general, dimension_numbers=dims, preferred_element_type=jnp.float32)
    real, imag = source_ref[0, 0], source_ref[0, 1]
    out_real = dot(real, weight_ref[0, 0, 0]) - dot(imag, weight_ref[0, 0, 1])
    out_imag = dot(real, weight_ref[0, 0, 1]) + dot(imag, weight_ref[0, 0, 0])
    out_real = (out_real * factor_ref[0]).astype(jnp.bfloat16)
    out_imag = (out_imag * factor_ref[0]).astype(jnp.bfloat16)
    for chunk in range(chunks):
        out_ref[chunk, :part] = out_real[chunk * part : (chunk + 1) * part]
        out_ref[chunk, part:] = out_imag[chunk * part : (chunk + 1) * part]


def first_advance(source, propagator, transmission, part):
    width = propagator.shape[3]
    shots = source.shape[3]
    wide = width // 4
    return pl.pallas_call(
        functools.partial(first_kernel, part),
        grid=(width // wide,),
        in_specs=[
            pl.BlockSpec((1, 2, width, shots), lambda n: (0, 0, 0, 0)),
            pl.BlockSpec((1, 1, 2, wide, width), lambda n: (0, 0, 0, n, 0)),
            pl.BlockSpec((1, 1, wide), lambda n: (0, 0, n)),
        ],
        out_specs=pl.BlockSpec((shots // part, 2 * part, wide), lambda n: (0, 0, n)),
        out_shape=jax.ShapeDtypeStruct((shots // part, 2 * part, width), jnp.bfloat16),
        compiler_params=pltpu.CompilerParams(vmem_limit_bytes=LIMIT),
        cost_estimate=pl.CostEstimate(
            flops=8 * width * width * shots, bytes_accessed=4 * width * (width + 2 * shots), transcendentals=0
        ),
    )(source, propagator, transmission)


def advance(panel, weight, factor):
    part = panel.shape[0] // 2
    dims = (((1,), (1,)), ((), ()))
    turned = jnp.concatenate([-panel[part:], panel[:part]], axis=0)
    out = lax.dot_general(panel, weight[0], dims, preferred_element_type=jnp.float32) + lax.dot_general(
        turned, weight[1], dims, preferred_element_type=jnp.float32
    )
    return (out * factor[None, :]).astype(jnp.bfloat16)


def operand_kernel(part, step, spot_ref, own_ref, got_ref, out_ref):
    rows = own_ref.shape[1]
    shots = own_ref.shape[2]
    chunks = shots // part
    for first in range(0, chunks, step):

        @pl.when(spot_ref[0] == first)
        def _():
            for which, ref in enumerate((own_ref, got_ref)):
                real, imag = ref[0], ref[1]
                minus = -real
                for at in range(chunks):
                    lo = (first + at) % chunks * part
                    left = (which * chunks + at) * 2 * part
                    out_ref[:rows, left : left + 2 * part] = jnp.concatenate(
                        [real[:, lo : lo + part], imag[:, lo : lo + part]], axis=1
                    )
                    out_ref[rows:, left : left + 2 * part] = jnp.concatenate(
                        [imag[:, lo : lo + part], minus[:, lo : lo + part]], axis=1
                    )


def operand(spots, own, got, rows, part, step):
    shots = own.shape[2]
    blocks = got.shape[1] // rows
    return pl.pallas_call(
        functools.partial(operand_kernel, part, step),
        grid_spec=pltpu.PrefetchScalarGridSpec(
            num_scalar_prefetch=1,
            grid=(blocks,),
            in_specs=[
                pl.BlockSpec((2, rows, shots), lambda i, spot: (0, spot[1 + i], 0)),
                pl.BlockSpec((2, rows, shots), lambda i, spot: (0, spot[1 + blocks + i], 0)),
            ],
            out_specs=pl.BlockSpec((2 * rows, 4 * shots), lambda i, spot: (i, 0)),
        ),
        out_shape=jax.ShapeDtypeStruct((2 * rows * blocks, 4 * shots), jnp.bfloat16),
        compiler_params=pltpu.CompilerParams(vmem_limit_bytes=LIMIT),
        cost_estimate=pl.CostEstimate(flops=0, bytes_accessed=24 * rows * blocks * shots, transcendentals=0),
    )(spots, own, got)


def term_kernel(rows, *refs):
    left_ref, panels, (keep_ref, send_ref, joined) = refs[0], refs[1:-3], refs[-3:]
    at = 0
    for panel in panels:
        joined[at : at + panel.shape[0]] = panel[...]
        at += panel.shape[0]
    out = jnp.dot(left_ref[...], joined[...], preferred_element_type=jnp.float32)
    groups = keep_ref.shape[0]
    for k in range(groups):
        for part in range(2):
            lo = (2 * k + part) * rows
            keep_ref[k, part] = out[lo : lo + rows]
            lo += 2 * groups * rows
            send_ref[k, part] = out[lo : lo + rows].astype(jnp.bfloat16)


def terms(left, panels, rows):
    deep = left.shape[1]
    width = panels[0].shape[1]
    groups = left.shape[0] // (4 * rows)
    wide = width // 4
    return pl.pallas_call(
        functools.partial(term_kernel, rows),
        grid=(width // wide,),
        in_specs=[pl.BlockSpec(left.shape, lambda n: (0, 0))]
        + [pl.BlockSpec((panel.shape[0], wide), lambda n: (0, n)) for panel in panels],
        out_specs=[pl.BlockSpec((groups, 2, rows, wide), lambda n: (0, 0, 0, n))] * 2,
        out_shape=[
            jax.ShapeDtypeStruct((groups, 2, rows, width), jnp.float32),
            jax.ShapeDtypeStruct((groups, 2, rows, width), jnp.bfloat16),
        ],
        scratch_shapes=[pltpu.VMEM((deep, wide), jnp.bfloat16)],
        compiler_params=pltpu.CompilerParams(vmem_limit_bytes=LIMIT),
        cost_estimate=pl.CostEstimate(
            flops=2 * left.shape[0] * deep * width,
            bytes_accessed=2 * deep * (left.shape[0] + width) + 12 * groups * rows * width,
            transcendentals=0,
        ),
    )(left, *panels)


def last_kernel(scale, *refs):
    *parts, out_ref = refs
    for part in range(2):
        total = parts[0][0, part]
        for ref in parts[1:]:
            total += ref[0, part].astype(jnp.float32)
        out_ref[0, :, part] = total * scale


def last_sum(parts, scale):
    rows, width = parts[0].shape[2:]
    return pl.pallas_call(
        functools.partial(last_kernel, scale),
        grid=(2,),
        in_specs=[pl.BlockSpec((1, 2, rows // 2, width), lambda n: (0, 0, n, 0)) for _ in parts],
        out_specs=pl.BlockSpec((1, rows // 2, 2, width), lambda n: (0, n, 0, 0)),
        out_shape=jax.ShapeDtypeStruct((1, rows, 2, width), jnp.float32),
        compiler_params=pltpu.CompilerParams(vmem_limit_bytes=LIMIT),
        cost_estimate=pl.CostEstimate(
            flops=2 * len(parts) * rows * width, bytes_accessed=16 * rows * width, transcendentals=0
        ),
    )(*parts)


def shards(source, propagator, transmission, upgoing):
    weight = propagator[0, 0]
    factor = transmission[0, 0]
    upward = upgoing[0, 0]
    width = weight.shape[1]
    shots = source.shape[3]
    level = lax.axis_index("depth")
    levels = lax.axis_size("depth")
    freqs = lax.axis_size("freq")
    mine = lax.axis_index("freq")
    groups = freqs // 4
    group, place, core = mine // 4, (mine // 2) % 2, mine % 2
    rows = width // freqs
    part = shots // CHUNKS
    ready = first_advance(source, propagator, transmission, part)
    by_place = upward.reshape(2, groups, 2, 2 * rows, shots)
    asked = lax.dynamic_index_in_dim(by_place, 1 - place, 2, keepdims=False).reshape(2, 2 * groups * rows, shots)
    got = swapped(asked, "freq", 2)
    order = [(s, k) for s in range(2) for k in range(groups)]
    spots = (
        [lax.rem(DELAY * (levels - 1 - level), CHUNKS)]
        + [4 * lax.rem(group + k, groups) + 2 * place + (core ^ s) for s, k in order]
        + [2 * lax.rem(group + k, groups) + (core ^ s) for s, k in order]
    )
    left = operand(jnp.stack(spots).astype(jnp.int32), upward, got, rows, part, math.gcd(DELAY, CHUNKS))

    ticks = CHUNKS + DELAY * (levels - 1)
    flying = []
    own = []
    other = []
    for tick in range(ticks):
        out = ready[tick % CHUNKS]
        if tick >= DELAY:
            arrived = flying[tick - DELAY]
            if tick == ticks // 2:
                arrived, left = lax.optimization_barrier((arrived, left))
            out = jnp.where(level == 0, out, advance(arrived, weight, factor))
        if tick + DELAY < ticks:
            flying.append(ring(out, "depth", 1))
        if tick >= ticks - CHUNKS:
            own.append(out)
            other.append(swapped(out, "freq", 2))
    keep, send = terms(left, own + other, rows)
    near = swapped(send, "freq", 1)
    parts = [keep, near]
    for k in range(1, groups):
        total = (keep[k : k + 1] + near[k : k + 1].astype(jnp.float32)).astype(jnp.bfloat16)
        parts.append(ring(total, "freq", 4 * k))
    return last_sum(parts, (2.0 * shots * freqs) ** (-0.5))


def solution(mesh):
    return jax.shard_map(
        shards,
        mesh=mesh,
        in_specs=(
            P("freq", None, None, None),
            P("depth", "freq", None, None, None),
            P("depth", "freq", None),
            P("depth", "freq", None, None, None),
        ),
        out_specs=P("depth", "freq", None, None),
        check_vma=False,
    )
```

time: 139 us -> 107 us (0.77)
  matrix products: 32.7 us -> 17.8 us
  between operations: 13.8 us -> 0.28 us
  Pallas kernels: 0 us -> 12.8 us
  waiting for transfers between devices: 68.9 us -> 56.7 us
  local copies, waits for them, and re-layouts: 8.61 us -> 2.88 us
  starting transfers between devices: 8.42 us -> 13.3 us
  other arithmetic: 4.41 us -> 1.28 us
    reduce_scatter x1 -> x0, waiting for transfers between devices: 50.8 us -> none  [shards(): lax.psum_scatter(term.astype(jnp.bfloat16), 'freq', scatter_dimension=0,...]
    ppermute x8 -> x15, waiting for transfers between devices: 18.1 us -> 56.7 us  [the longest x9 46.7 us: ring(): lax.ppermute(block, axis, [(i, (i + distance) % size) for i in range(size)])]
    dot_general x21 -> x16, matrix products: 32.7 us -> 17.8 us  [the longest x8 9.54 us: advance(): lax.dot_general(panel, weight[0], dims, preferred_element_type=jnp.float32)]
    pallas_call x0 -> x4, Pallas kernels: none -> 12.8 us  [the longest x1 4.98 us: first_advance(): pl.pallas_call(functools.partial(first_kernel, part), grid=(width // wide...]
    ppermute x8 -> x15, starting transfers between devices: 8.42 us -> 13.3 us  [the longest x6 6.98 us: swapped(): lax.ppermute(block, axis, [(i, i ^ bit) for i in range(lax.axis_size(axis...]
    select_n x8 -> x0, other arithmetic: 2.59 us -> none  [shards(): panel = jnp.where(level == 0, panel, flying[tick - DELAY])]
    concatenate x2 -> x0, local copies, waits for them, and re-layouts: 2.45 us -> none  [the longest x1 2.44 us: shards(): jnp.concatenate([rolled[part_of, :, at:at + part] for at in range(0, shot...]
    slice x1 -> x0, local copies, waits for them, and re-layouts: 1.96 us -> none  [shards(): source[0, 0, :, at:at + part]]
  transfers between devices with their start and end apart: 9 -> 15, of which waited for: 7 -> 11; matrix products, arithmetic and copies ran while one was open for 19% -> 18% of each run, Pallas kernels for 0% -> 1%
where the time goes in v4:
time: 107 us; the launch traced here: 105 us
  waiting for transfers between devices  56.7 us (53%)
  matrix products  17.8 us (17%)
  starting transfers between devices  13.3 us (12%)
  Pallas kernels  12.8 us (12%)
  local copies, waits for them, and re-layouts  2.88 us (3%)
  other arithmetic  1.28 us (1%)
    ppermute x9, waiting for transfers between devices, ring(): lax.ppermute(block, axis, [(i, (i + distance) % size) for i in range(size)])  46.7 us
    ppermute x6, waiting for transfers between devices, swapped(): lax.ppermute(block, axis, [(i, i ^ bit) for i in range(lax.axis_size(axis...  9.91 us
    dot_general x8, matrix products, advance(): lax.dot_general(panel, weight[0], dims, preferred_element_type=jnp.float32)  9.54 us
    dot_general x8, matrix products, advance(): lax.dot_general(turned, weight[1], dims, preferred_element_type=jnp.float32)  8.22 us
    ppermute x6, starting transfers between devices, swapped(): lax.ppermute(block, axis, [(i, i ^ bit) for i in range(lax.axis_size(axis...  6.98 us
    ppermute x9, starting transfers between devices, ring(): lax.ppermute(block, axis, [(i, (i + distance) % size) for i in range(size)])  6.27 us
    pallas_call x1, Pallas kernels, first_advance(): pl.pallas_call(functools.partial(first_kernel, part), grid=(width // wide...  4.98 us
    pallas_call x1, Pallas kernels, terms(): pl.pallas_call(functools.partial(term_kernel, rows), grid=(width // wide,...  4.94 us
  transfers between devices with their start and end apart: 15, of which 11 were waited for; matrix products, arithmetic and copies ran while one was open for 18% of the time, Pallas kernels for 1%

profile of v4, /device:TPU:4, one launch (start us, length us, event | category | flops | bytes accessed | tf_op | source)
XLA Modules:
  0.0 104.9 jit_solution(3564171943743728828)
XLA Ops:
  0.0 1.2 %copy-done.2 = bf16[1,2,1024,256]{3,2,1,0:T(8,128)(2,1)S(1)} copy-done((bf16[1,2,1024,256]{3,2,1,0:T(8,128)(2,1)S(1)}, bf16[1,2,1024,256]{3,2,1,0:T(8,128)(2,1)}, u32[]{:S(2)}) %copy-start.2) | copy-done | bytes 1048600
  1.9 5.0 %shard_map.46 = bf16[4,128,1024]{2,1,0:T(8,128)(2,1)S(1)} custom-call(bf16[1,2,1024,256]{3,2,1,0:T(8,128)(2,1)S(1)} %copy-done.2, bf16[1,1,2,1024,1024]{4,3,2,1,0:T(8,128)(2,1)} %weight_ref.1, f32[1,1,1024]{2,1,0:T(1,128)S(1)} %copy-done.3), custom_call_target="tpu_custom_call" | custom-call | flops 2147483648 | bytes 6291456 | tf_op jit(solution)/shard_map/pallas_call | solution.py:43
  7.7 1.5 %collective-permute-start.3 = (bf16[128,1024]{1,0:T(8,128)(2,1)}, bf16[128,1024]{1,0:T(8,128)(2,1)S(1)}, u32[]{:S(2)}, u32[]{:S(2)}) collective-permute-start(bf16[128,1024]{1,0:T(8,128)(2,1)} %get-tuple-element.13), channel_id=1, source_target_pairs={{0,8},{8,16},{16,24},{24,0},{1,9},{9,17},{17,25},{25,1},{2,10},{10... | collective-permute-start | bytes 786440 | tf_op jit(solution)/shard_map/ppermute | solution.py:18
  9.3 1.6 %collective-permute-start.2 = (bf16[2,512,256]{2,1,0:T(8,128)(2,1)S(1)}, bf16[2,512,256]{2,1,0:T(8,128)(2,1)S(1)}, u32[]{:S(2)}, u32[]{:S(2)}) collective-permute-start(bf16[2,512,256]{2,1,0:T(8,128)(2,1)S(1)} %bitcast.155), channel_id=1, source_target_pairs={{0,2},{1,3},{2,0},{3,1},{4,6},{5,7},{6,4},{7,5},{8,10},{9,11},{10,... | collective-permute-start | bytes 1572872 | tf_op jit(solution)/shard_map/ppermute | solution.py:22
  11.5 6.6 %collective-permute-done.3 = bf16[128,1024]{1,0:T(8,128)(2,1)S(1)} collective-permute-done((bf16[128,1024]{1,0:T(8,128)(2,1)}, bf16[128,1024]{1,0:T(8,128)(2,1)S(1)}, u32[]{:S(2)}, u32[]{:S(2)}) %collective-permute-start.3) | collective-permute-done | bytes 262176 | tf_op jit(solution)/shard_map/ppermute | solution.py:18
  18.1 2.4 %fusion.12 = f32[128,1024]{1,0:T(8,128)S(1)} fusion(bf16[1,1,2,1024,1024]{4,3,2,1,0:T(8,128)(2,1)} %weight_ref.1, bf16[64,1024]{1,0:T(8,128)(2,1)S(1)} %get-tuple-element.28, bf16[64,1024]{1,0:T(8,128)(2,1)S(1)} %get-tuple-element.27), kind=kOutput, calls=%fused_computation.12 | convolution fusion | flops 268959744 | bytes 2883584 | tf_op jit(solution)/shard_map/dot_general | solution.py:64
  20.5 2.6 %fusion.107 = bf16[128,1024]{1,0:T(8,128)(2,1)S(1)} fusion(f32[128,1024]{1,0:T(8,128)S(1)} %fusion.12, bf16[128,1024]{1,0:T(8,128)(2,1)S(1)} %collective-permute-done.3, bf16[1,1,2,1024,1024]{4,3,2,1,0:T(8,128)(2,1)} %weight_ref.1, f32[1024]{0:T(1024)S(1)} %bitcast.147, pred[]{:T(512)S(6)} %eq.5, bf16[4,128,1024]{2,1,0:T(8,128)(2,1)S(1)} %shard_map.46), kind=kOutput, calls=%fused_computation.57 | convolution fusion | flops 268959744 | bytes 3411969 | tf_op jit(solution)/shard_map/dot_general | solution.py:64
  25.6 1.8 %fusion.104 = bf16[128,1024]{1,0:T(8,128)(2,1)S(1)} fusion(f32[128,1024]{1,0:T(8,128)S(1)} %fusion.14, bf16[128,1024]{1,0:T(8,128)(2,1)} %collective-permute-done, bf16[1,1,2,1024,1024]{4,3,2,1,0:T(8,128)(2,1)S(1)} %copy-done.5, f32[1024]{0:T(1024)S(1)} %bitcast.148, pred[]{:T(512)S(6)} %eq.5, bf16[4,128,1024]{2,1,0:T(8,128)(2,1)S(1)} %shard_map.46), kind=kOutput, calls=%fused_computation.56 | convolution fusion | flops 268959744 | bytes 3411969 | tf_op jit(solution)/shard_map/dot_general | solution.py:64
  28.3 3.8 %collective-permute-done.4 = bf16[128,1024]{1,0:T(8,128)(2,1)S(1)} collective-permute-done((bf16[128,1024]{1,0:T(8,128)(2,1)S(1)}, bf16[128,1024]{1,0:T(8,128)(2,1)S(1)}, u32[]{:S(2)}, u32[]{:S(2)}) %collective-permute-start.4) | collective-permute-done | bytes 262176 | tf_op jit(solution)/shard_map/ppermute | solution.py:18
  33.9 1.5 %shard_map.47.refs_0_ = bf16[1024,1024]{1,0:T(8,128)(2,1)S(1)} custom-call(s32[9]{0:T(128)S(1)} %stack.39.spot_ref, bf16[2,1024,256]{2,1,0:T(8,128)(2,1)S(1)} %bitcast.146, bf16[2,512,256]{2,1,0:T(8,128)(2,1)S(1)} %collective-permute-done.2.got_ref), custom_call_target="tpu_custom_call" | custom-call | bytes 3145728 | tf_op jit(solution)/shard_map/pallas_call | solution.py:95
  35.4 2.3 %collective-permute-done.1 = bf16[128,1024]{1,0:T(8,128)(2,1)S(1)} collective-permute-done((bf16[128,1024]{1,0:T(8,128)(2,1)S(1)}, bf16[128,1024]{1,0:T(8,128)(2,1)S(1)}, u32[]{:S(2)}, u32[]{:S(2)}) %collective-permute-start.1) | collective-permute-done | bytes 262176 | tf_op jit(solution)/shard_map/ppermute | solution.py:18
  39.5 4.0 %collective-permute-done.5 = bf16[128,1024]{1,0:T(8,128)(2,1)S(1)} collective-permute-done((bf16[128,1024]{1,0:T(8,128)(2,1)S(1)}, bf16[128,1024]{1,0:T(8,128)(2,1)S(1)}, u32[]{:S(2)}, u32[]{:S(2)}) %collective-permute-start.5) | collective-permute-done | bytes 262176 | tf_op jit(solution)/shard_map/ppermute | solution.py:18
  45.2 1.6 %collective-permute-start.9 = (bf16[128,1024]{1,0:T(8,128)(2,1)S(1)}, bf16[128,1024]{1,0:T(8,128)(2,1)S(1)}, u32[]{:S(2)}, u32[]{:S(2)}) collective-permute-start(bf16[128,1024]{1,0:T(8,128)(2,1)S(1)} %fusion.113.refs_1_), channel_id=1, source_target_pairs={{0,2},{1,3},{2,0},{3,1},{4,6},{5,7},{6,4},{7,5},{8,10},{9,11},{10,... | collective-permute-start | bytes 786440 | tf_op jit(solution)/shard_map/ppermute | solution.py:22
  46.9 1.6 %collective-permute-done.6 = bf16[128,1024]{1,0:T(8,128)(2,1)S(1)} collective-permute-done((bf16[128,1024]{1,0:T(8,128)(2,1)S(1)}, bf16[128,1024]{1,0:T(8,128)(2,1)S(1)}, u32[]{:S(2)}, u32[]{:S(2)}) %collective-permute-start.6) | collective-permute-done | bytes 262176 | tf_op jit(solution)/shard_map/ppermute | solution.py:18
  50.2 2.8 %collective-permute-start.10 = (bf16[128,1024]{1,0:T(8,128)(2,1)S(1)}, bf16[128,1024]{1,0:T(8,128)(2,1)S(1)}, u32[]{:S(2)}, u32[]{:S(2)}) collective-permute-start(bf16[128,1024]{1,0:T(8,128)(2,1)S(1)} %fusion.119.refs_2_), channel_id=1, source_target_pairs={{0,2},{1,3},{2,0},{3,1},{4,6},{5,7},{6,4},{7,5},{8,10},{9,11},{10,... | collective-permute-start | bytes 786440 | tf_op jit(solution)/shard_map/ppermute | solution.py:22
  53.0 3.6 %collective-permute-done.7 = bf16[128,1024]{1,0:T(8,128)(2,1)S(1)} collective-permute-done((bf16[128,1024]{1,0:T(8,128)(2,1)S(1)}, bf16[128,1024]{1,0:T(8,128)(2,1)S(1)}, u32[]{:S(2)}, u32[]{:S(2)}) %collective-permute-start.7) | collective-permute-done | bytes 262176 | tf_op jit(solution)/shard_map/ppermute | solution.py:18
  58.9 1.4 %collective-permute-done.8 = bf16[128,1024]{1,0:T(8,128)(2,1)S(1)} collective-permute-done((bf16[128,1024]{1,0:T(8,128)(2,1)S(1)}, bf16[128,1024]{1,0:T(8,128)(2,1)S(1)}, u32[]{:S(2)}, u32[]{:S(2)}) %collective-permute-start.8) | collective-permute-done | bytes 262176 | tf_op jit(solution)/shard_map/ppermute | solution.py:18
  62.3 4.5 %collective-permute-done.11.refs_7_ = bf16[128,1024]{1,0:T(8,128)(2,1)S(1)} collective-permute-done((bf16[128,1024]{1,0:T(8,128)(2,1)S(1)}, bf16[128,1024]{1,0:T(8,128)(2,1)S(1)}, u32[]{:S(2)}, u32[]{:S(2)}) %collective-permute-start.11) | collective-permute-done | bytes 262176 | tf_op jit(solution)/shard_map/ppermute | solution.py:22
  66.8 2.8 %collective-permute-done.12.refs_8_ = bf16[128,1024]{1,0:T(8,128)(2,1)S(1)} collective-permute-done((bf16[128,1024]{1,0:T(8,128)(2,1)S(1)}, bf16[128,1024]{1,0:T(8,128)(2,1)S(1)}, u32[]{:S(2)}, u32[]{:S(2)}) %collective-permute-start.12) | collective-permute-done | bytes 262176 | tf_op jit(solution)/shard_map/ppermute | solution.py:22
  69.6 4.9 %shard_map.48 = (f32[2,2,128,1024]{3,2,1,0:T(8,128)S(1)}, bf16[2,2,128,1024]{3,2,1,0:T(8,128)(2,1)S(1)}) custom-call(bf16[1024,1024]{1,0:T(8,128)(2,1)} %copy-done.1, bf16[128,1024]{1,0:T(8,128)(2,1)S(1)} %fusion.113.refs_1_, bf16[128,1024]{1,0:T(8,128)(2,1)S(1)} %fusion.119.refs_2_, bf16[128,1024]{1,0:T(8,128)(2,1)S(1)} %fusion.122.refs_3_, ...), custom_call_target="tpu_custom_call" | custom-call | flops 2147483648 | bytes 7340032 | tf_op jit(solution)/shard_map/pallas_call | solution.py:133
  74.6 2.6 %collective-permute-done.13.refs_1_ = bf16[2,2,128,1024]{3,2,1,0:T(8,128)(2,1)S(1)} collective-permute-done((bf16[2,2,128,1024]{3,2,1,0:T(8,128)(2,1)S(1)}, bf16[2,2,128,1024]{3,2,1,0:T(8,128)(2,1)S(1)}, u32[]{:S(2)}, u32[]{:S(2)}) %collective-permute-start.13) | collective-permute-done | bytes 1048608 | tf_op jit(solution)/shard_map/ppermute | solution.py:22
  77.4 2.6 %collective-permute-start.14 = (bf16[1,2,128,1024]{3,2,1,0:T(8,128)(2,1)S(1)}, bf16[1,2,128,1024]{3,2,1,0:T(8,128)(2,1)S(1)}, u32[]{:S(2)}, u32[]{:S(2)}) collective-permute-start(bf16[1,2,128,1024]{3,2,1,0:T(8,128)(2,1)S(1)} %add_convert_fusion), channel_id=1, source_target_pairs={{0,4},{1,5},{2,6},{3,7},{4,0},{5,1},{6,2},{7,3},{8,12},{9,13},{10,... | collective-permute-start | bytes 1572872 | tf_op jit(solution)/shard_map/ppermute | solution.py:18
  80.0 23.5 %collective-permute-done.14.refs_2_ = bf16[1,2,128,1024]{3,2,1,0:T(8,128)(2,1)S(1)} collective-permute-done((bf16[1,2,128,1024]{3,2,1,0:T(8,128)(2,1)S(1)}, bf16[1,2,128,1024]{3,2,1,0:T(8,128)(2,1)S(1)}, u32[]{:S(2)}, u32[]{:S(2)}) %collective-permute-start.14) | collective-permute-done | bytes 524320 | tf_op jit(solution)/shard_map/ppermute | solution.py:18
  103.5 1.3 %shard_map.49 = f32[1,128,2,1024]{3,2,1,0:T(2,128)} custom-call(f32[2,2,128,1024]{3,2,1,0:T(8,128)S(1)} %get-tuple-element.11.refs_0_, bf16[2,2,128,1024]{3,2,1,0:T(8,128)(2,1)S(1)} %collective-permute-done.13.refs_1_, bf16[1,2,128,1024]{3,2,1,0:T(8,128)(2,1)S(1)} %collective-permute-done.14.refs_2_), custom_call_target="tpu_custom_call" | custom-call | flops 786432 | bytes 2097152 | tf_op jit(solution)/shard_map/pallas_call | solution.py:164
  (50 shorter events, 16.9 us)
Async XLA Ops:
  0.0 1.2 %copy-start.2 = (bf16[1,2,1024,256]{3,2,1,0:T(8,128)(2,1)S(1)}, bf16[1,2,1024,256]{3,2,1,0:T(8,128)(2,1)}, u32[]{:S(2)}) copy-start(bf16[1,2,1024,256]{3,2,1,0:T(8,128)(2,1)} %source_ref.1) | copy-start | bytes 3145732
  1.2 0.7 copy-start.3
  1.9 7.3 %copy-start = (bf16[1,1,2,1024,256]{4,3,2,1,0:T(8,128)(2,1)S(1)}, bf16[1,1,2,1024,256]{4,3,2,1,0:T(8,128)(2,1)}, u32[]{:S(2)}) copy-start(bf16[1,1,2,1024,256]{4,3,2,1,0:T(8,128)(2,1)} %param.7) | copy-start | bytes 3145732
  7.7 10.3 %collective-permute-start.3 = (bf16[128,1024]{1,0:T(8,128)(2,1)}, bf16[128,1024]{1,0:T(8,128)(2,1)S(1)}, u32[]{:S(2)}, u32[]{:S(2)}) collective-permute-start(bf16[128,1024]{1,0:T(8,128)(2,1)} %get-tuple-element.13), channel_id=1, source_target_pairs={{0,8},{8,16},{16,24},{24,0},{1,9},{9,17},{17,25},{25,1},{2,10},{10... | collective-permute-start | bytes 786440 | tf_op jit(solution)/shard_map/ppermute | solution.py:18
  9.3 11.2 %copy-start.4 = (f32[1,1,1024]{2,1,0:T(1,128)S(1)}, f32[1,1,1024]{2,1,0:T(1,128)}, u32[]{:S(2)}) copy-start(f32[1,1,1024]{2,1,0:T(1,128)} %factor_ref.1) | copy-start | bytes 12292
  9.3 24.6 %collective-permute-start.2 = (bf16[2,512,256]{2,1,0:T(8,128)(2,1)S(1)}, bf16[2,512,256]{2,1,0:T(8,128)(2,1)S(1)}, u32[]{:S(2)}, u32[]{:S(2)}) collective-permute-start(bf16[2,512,256]{2,1,0:T(8,128)(2,1)S(1)} %bitcast.155), channel_id=1, source_target_pairs={{0,2},{1,3},{2,0},{3,1},{4,6},{5,7},{6,4},{7,5},{8,10},{9,11},{10,... | collective-permute-start | bytes 1572872 | tf_op jit(solution)/shard_map/ppermute | solution.py:22
  10.9 12.8 %collective-permute-start = (bf16[128,1024]{1,0:T(8,128)(2,1)}, bf16[128,1024]{1,0:T(8,128)(2,1)}, u32[]{:S(2)}, u32[]{:S(2)}) collective-permute-start(bf16[128,1024]{1,0:T(8,128)(2,1)} %get-tuple-element.14), channel_id=1, source_target_pairs={{0,8},{8,16},{16,24},{24,0},{1,9},{9,17},{17,25},{25,1},{2,10},{10... | collective-permute-start | bytes 786440 | tf_op jit(solution)/shard_map/ppermute | solution.py:18
  20.5 4.3 %copy-start.5 = (bf16[1,1,2,1024,1024]{4,3,2,1,0:T(8,128)(2,1)S(1)}, bf16[1,1,2,1024,1024]{4,3,2,1,0:T(8,128)(2,1)}, u32[]{:S(2)}) copy-start(bf16[1,1,2,1024,1024]{4,3,2,1,0:T(8,128)(2,1)} %weight_ref.1) | copy-start | bytes 12582916
  23.1 9.0 %collective-permute-start.4 = (bf16[128,1024]{1,0:T(8,128)(2,1)S(1)}, bf16[128,1024]{1,0:T(8,128)(2,1)S(1)}, u32[]{:S(2)}, u32[]{:S(2)}) collective-permute-start(bf16[128,1024]{1,0:T(8,128)(2,1)S(1)} %fusion.107), channel_id=1, source_target_pairs={{0,8},{8,16},{16,24},{24,0},{1,9},{9,17},{17,25},{25,1},{2,10},{10... | collective-permute-start | bytes 786440 | tf_op jit(solution)/shard_map/ppermute | solution.py:18
  27.4 10.3 %collective-permute-start.1 = (bf16[128,1024]{1,0:T(8,128)(2,1)S(1)}, bf16[128,1024]{1,0:T(8,128)(2,1)S(1)}, u32[]{:S(2)}, u32[]{:S(2)}) collective-permute-start(bf16[128,1024]{1,0:T(8,128)(2,1)S(1)} %fusion.104), channel_id=1, source_target_pairs={{0,8},{8,16},{16,24},{24,0},{1,9},{9,17},{17,25},{25,1},{2,10},{10... | collective-permute-start | bytes 786440 | tf_op jit(solution)/shard_map/ppermute | solution.py:18
  33.8 9.7 %collective-permute-start.5 = (bf16[128,1024]{1,0:T(8,128)(2,1)S(1)}, bf16[128,1024]{1,0:T(8,128)(2,1)S(1)}, u32[]{:S(2)}, u32[]{:S(2)}) collective-permute-start(bf16[128,1024]{1,0:T(8,128)(2,1)S(1)} %fusion.110), channel_id=1, source_target_pairs={{0,8},{8,16},{16,24},{24,0},{1,9},{9,17},{17,25},{25,1},{2,10},{10... | collective-permute-start | bytes 786440 | tf_op jit(solution)/shard_map/ppermute | solution.py:18
  35.4 4.0 %copy-start.1 = (bf16[1024,1024]{1,0:T(8,128)(2,1)}, bf16[1024,1024]{1,0:T(8,128)(2,1)S(1)}, u32[]{:S(2)}) copy-start(bf16[1024,1024]{1,0:T(8,128)(2,1)S(1)} %shard_map.47.refs_0_) | copy-start | bytes 6291460
  39.4 9.0 %collective-permute-start.6 = (bf16[128,1024]{1,0:T(8,128)(2,1)S(1)}, bf16[128,1024]{1,0:T(8,128)(2,1)S(1)}, u32[]{:S(2)}, u32[]{:S(2)}) collective-permute-start(bf16[128,1024]{1,0:T(8,128)(2,1)S(1)} %fusion.116), channel_id=1, source_target_pairs={{0,8},{8,16},{16,24},{24,0},{1,9},{9,17},{17,25},{25,1},{2,10},{10... | collective-permute-start | bytes 786440 | tf_op jit(solution)/shard_map/ppermute | solution.py:18
  45.2 17.1 %collective-permute-start.9 = (bf16[128,1024]{1,0:T(8,128)(2,1)S(1)}, bf16[128,1024]{1,0:T(8,128)(2,1)S(1)}, u32[]{:S(2)}, u32[]{:S(2)}) collective-permute-start(bf16[128,1024]{1,0:T(8,128)(2,1)S(1)} %fusion.113.refs_1_), channel_id=1, source_target_pairs={{0,2},{1,3},{2,0},{3,1},{4,6},{5,7},{6,4},{7,5},{8,10},{9,11},{10,... | collective-permute-start | bytes 786440 | tf_op jit(solution)/shard_map/ppermute | solution.py:22
  46.9 9.8 %collective-permute-start.7 = (bf16[128,1024]{1,0:T(8,128)(2,1)S(1)}, bf16[128,1024]{1,0:T(8,128)(2,1)S(1)}, u32[]{:S(2)}, u32[]{:S(2)}) collective-permute-start(bf16[128,1024]{1,0:T(8,128)(2,1)S(1)} %fusion.113.refs_1_), channel_id=1, source_target_pairs={{0,8},{8,16},{16,24},{24,0},{1,9},{9,17},{17,25},{25,1},{2,10},{10... | collective-permute-start | bytes 786440 | tf_op jit(solution)/shard_map/ppermute | solution.py:18
  50.2 12.1 %collective-permute-start.10 = (bf16[128,1024]{1,0:T(8,128)(2,1)S(1)}, bf16[128,1024]{1,0:T(8,128)(2,1)S(1)}, u32[]{:S(2)}, u32[]{:S(2)}) collective-permute-start(bf16[128,1024]{1,0:T(8,128)(2,1)S(1)} %fusion.119.refs_2_), channel_id=1, source_target_pairs={{0,2},{1,3},{2,0},{3,1},{4,6},{5,7},{6,4},{7,5},{8,10},{9,11},{10,... | collective-permute-start | bytes 786440 | tf_op jit(solution)/shard_map/ppermute | solution.py:22
  53.0 7.3 %collective-permute-start.8 = (bf16[128,1024]{1,0:T(8,128)(2,1)S(1)}, bf16[128,1024]{1,0:T(8,128)(2,1)S(1)}, u32[]{:S(2)}, u32[]{:S(2)}) collective-permute-start(bf16[128,1024]{1,0:T(8,128)(2,1)S(1)} %fusion.119.refs_2_), channel_id=1, source_target_pairs={{0,8},{8,16},{16,24},{24,0},{1,9},{9,17},{17,25},{25,1},{2,10},{10... | collective-permute-start | bytes 786440 | tf_op jit(solution)/shard_map/ppermute | solution.py:18
  58.4 8.4 %collective-permute-start.11 = (bf16[128,1024]{1,0:T(8,128)(2,1)S(1)}, bf16[128,1024]{1,0:T(8,128)(2,1)S(1)}, u32[]{:S(2)}, u32[]{:S(2)}) collective-permute-start(bf16[128,1024]{1,0:T(8,128)(2,1)S(1)} %fusion.122.refs_3_), channel_id=1, source_target_pairs={{0,2},{1,3},{2,0},{3,1},{4,6},{5,7},{6,4},{7,5},{8,10},{9,11},{10,... | collective-permute-start | bytes 786440 | tf_op jit(solution)/shard_map/ppermute | solution.py:22
  62.0 7.6 %collective-permute-start.12 = (bf16[128,1024]{1,0:T(8,128)(2,1)S(1)}, bf16[128,1024]{1,0:T(8,128)(2,1)S(1)}, u32[]{:S(2)}, u32[]{:S(2)}) collective-permute-start(bf16[128,1024]{1,0:T(8,128)(2,1)S(1)} %fusion.125.refs_4_), channel_id=1, source_target_pairs={{0,2},{1,3},{2,0},{3,1},{4,6},{5,7},{6,4},{7,5},{8,10},{9,11},{10,... | collective-permute-start | bytes 786440 | tf_op jit(solution)/shard_map/ppermute | solution.py:22
  74.5 2.7 %collective-permute-start.13 = (bf16[2,2,128,1024]{3,2,1,0:T(8,128)(2,1)S(1)}, bf16[2,2,128,1024]{3,2,1,0:T(8,128)(2,1)S(1)}, u32[]{:S(2)}, u32[]{:S(2)}) collective-permute-start(bf16[2,2,128,1024]{3,2,1,0:T(8,128)(2,1)S(1)} %get-tuple-element.12), channel_id=1, source_target_pairs={{0,1},{1,0},{2,3},{3,2},{4,5},{5,4},{6,7},{7,6},{8,9},{9,8},{10,11... | collective-permute-start | bytes 3145736 | tf_op jit(solution)/shard_map/ppermute | solution.py:22
  77.4 26.1 %collective-permute-start.14 = (bf16[1,2,128,1024]{3,2,1,0:T(8,128)(2,1)S(1)}, bf16[1,2,128,1024]{3,2,1,0:T(8,128)(2,1)S(1)}, u32[]{:S(2)}, u32[]{:S(2)}) collective-permute-start(bf16[1,2,128,1024]{3,2,1,0:T(8,128)(2,1)S(1)} %add_convert_fusion), channel_id=1, source_target_pairs={{0,4},{1,5},{2,6},{3,7},{4,0},{5,1},{6,2},{7,3},{8,12},{9,13},{10,... | collective-permute-start | bytes 1572872 | tf_op jit(solution)/shard_map/ppermute | solution.py:18

commit v5 on v4

--- a/solution.py
+++ b/solution.py
@@ -10,7 +10,7 @@
 
 CHUNKS = 4
 DELAY = 2
-LIMIT = 48 * 1024 * 1024
+LIMIT = 32 * 1024 * 1024
 
 
 def ring(block, axis, distance):
@@ -22,48 +22,81 @@
     return lax.ppermute(block, axis, [(i, i ^ bit) for i in range(lax.axis_size(axis))])
 
 
-def first_kernel(part, source_ref, weight_ref, factor_ref, out_ref):
-    chunks = out_ref.shape[0]
-    dims = (((0,), (1,)), ((), ()))
-    dot = functools.partial(lax.dot_general, dimension_numbers=dims, preferred_element_type=jnp.float32)
-    real, imag = source_ref[0, 0], source_ref[0, 1]
-    out_real = dot(real, weight_ref[0, 0, 0]) - dot(imag, weight_ref[0, 0, 1])
-    out_imag = dot(real, weight_ref[0, 0, 1]) + dot(imag, weight_ref[0, 0, 0])
-    out_real = (out_real * factor_ref[0]).astype(jnp.bfloat16)
-    out_imag = (out_imag * factor_ref[0]).astype(jnp.bfloat16)
-    for chunk in range(chunks):
-        out_ref[chunk, :part] = out_real[chunk * part : (chunk + 1) * part]
-        out_ref[chunk, part:] = out_imag[chunk * part : (chunk + 1) * part]
+def first_kernel(part, source_ref, weight_ref, factor_ref, *refs):
+    *outs, joined_ref, source, factor, left, sem, sems = refs
+    width = joined_ref.shape[0]
+    blocks = sems.shape[0]
+    wide = width // blocks
+
+    def copies(n):
+        rows = pl.ds(n * wide, wide)
+        return [
+            pltpu.make_async_copy(
+                weight_ref.at[0, 0, half, rows], joined_ref.at[rows, pl.ds(half * width, width)], sems.at[n, half]
+            )
+            for half in range(2)
+        ]
+
+    begin = [
+        pltpu.make_async_copy(source_ref.at[0], source, sem.at[0]),
+        pltpu.make_async_copy(factor_ref.at[0], factor, sem.at[1]),
+    ]
+    for copy in begin:
+        copy.start()
+    for n in range(blocks):
+        for copy in copies(n):
+            copy.start()
+    for copy in begin:
+        copy.wait()
+    real, imag = source[0].T, source[1].T
+    for chunk in range(len(outs)):
+        lo, at = chunk * part, 2 * chunk * part
+        left[at : at + part, :width] = real[lo : lo + part]
+        left[at : at + part, width:] = -imag[lo : lo + part]
+        left[at + part : at + 2 * part, :width] = imag[lo : lo + part]
+        left[at + part : at + 2 * part, width:] = real[lo : lo + part]
+    for n in range(blocks):
+        for copy in copies(n):
+            copy.wait()
+        columns = slice(n * wide, (n + 1) * wide)
+        out = lax.dot_general(
+            left[...], joined_ref[columns], (((1,), (1,)), ((), ())), preferred_element_type=jnp.float32
+        )
+        out = (out * factor[:, columns]).astype(jnp.bfloat16)
+        for chunk in range(len(outs)):
+            outs[chunk][:, columns] = out[2 * chunk * part : 2 * (chunk + 1) * part]
 
 
 def first_advance(source, propagator, transmission, part):
     width = propagator.shape[3]
     shots = source.shape[3]
-    wide = width // 4
+    chunks = shots // part
+    whole = pl.BlockSpec(memory_space=pltpu.VMEM)
     return pl.pallas_call(
         functools.partial(first_kernel, part),
-        grid=(width // wide,),
-        in_specs=[
-            pl.BlockSpec((1, 2, width, shots), lambda n: (0, 0, 0, 0)),
-            pl.BlockSpec((1, 1, 2, wide, width), lambda n: (0, 0, 0, n, 0)),
-            pl.BlockSpec((1, 1, wide), lambda n: (0, 0, n)),
+        in_specs=[pl.BlockSpec(memory_space=pltpu.HBM)] * 3,
+        out_specs=[whole] * (chunks + 1),
+        out_shape=[jax.ShapeDtypeStruct((2 * part, width), jnp.bfloat16)] * chunks
+        + [jax.ShapeDtypeStruct((width, 2 * width), jnp.bfloat16)],
+        scratch_shapes=[
+            pltpu.VMEM((2, width, shots), jnp.bfloat16),
+            pltpu.VMEM((1, width), jnp.float32),
+            pltpu.VMEM((2 * shots, 2 * width), jnp.bfloat16),
+            pltpu.SemaphoreType.DMA((2,)),
+            pltpu.SemaphoreType.DMA((4, 2)),
         ],
-        out_specs=pl.BlockSpec((shots // part, 2 * part, wide), lambda n: (0, 0, n)),
-        out_shape=jax.ShapeDtypeStruct((shots // part, 2 * part, width), jnp.bfloat16),
         compiler_params=pltpu.CompilerParams(vmem_limit_bytes=LIMIT),
         cost_estimate=pl.CostEstimate(
             flops=8 * width * width * shots, bytes_accessed=4 * width * (width + 2 * shots), transcendentals=0
         ),
-    )(source, propagator, transmission)
-
-
-def advance(panel, weight, factor):
+    )(*(pltpu.with_memory_space_constraint(x, pltpu.HBM) for x in (source, propagator, transmission)))
+
+
+def advance(panel, joined, factor):
     part = panel.shape[0] // 2
-    dims = (((1,), (1,)), ((), ()))
     turned = jnp.concatenate([-panel[part:], panel[:part]], axis=0)
-    out = lax.dot_general(panel, weight[0], dims, preferred_element_type=jnp.float32) + lax.dot_general(
-        turned, weight[1], dims, preferred_element_type=jnp.float32
-    )
+    both = jnp.concatenate([panel, turned], axis=1)
+    out = lax.dot_general(both, joined, (((1,), (1,)), ((), ())), preferred_element_type=jnp.float32)
     return (out * factor[None, :]).astype(jnp.bfloat16)
 
 
@@ -109,45 +142,65 @@
     )(spots, own, got)
 
 
-def term_kernel(rows, *refs):
-    left_ref, panels, (keep_ref, send_ref, joined) = refs[0], refs[1:-3], refs[-3:]
-    at = 0
-    for panel in panels:
-        joined[at : at + panel.shape[0]] = panel[...]
-        at += panel.shape[0]
-    out = jnp.dot(left_ref[...], joined[...], preferred_element_type=jnp.float32)
-    groups = keep_ref.shape[0]
-    for k in range(groups):
-        for part in range(2):
-            lo = (2 * k + part) * rows
-            keep_ref[k, part] = out[lo : lo + rows]
-            lo += 2 * groups * rows
-            send_ref[k, part] = out[lo : lo + rows].astype(jnp.bfloat16)
-
-
-def terms(left, panels, rows):
-    deep = left.shape[1]
-    width = panels[0].shape[1]
-    groups = left.shape[0] // (4 * rows)
+def gathered(panels, columns):
+    return jnp.concatenate([panel[:, columns] for panel in panels], axis=0)
+
+
+def early_kernel(left_ref, *refs):
+    *panels, out_ref = refs
+    deep = sum(panel.shape[0] for panel in panels)
+    wide = out_ref.shape[1] // 4
+    for n in range(4):
+        columns = slice(n * wide, (n + 1) * wide)
+        out_ref[:, columns] = jnp.dot(
+            left_ref[:, :deep], gathered(panels, columns), preferred_element_type=jnp.float32
+        )
+
+
+def late_kernel(left_ref, early_ref, *refs):
+    *panels, keep_ref, send_ref = refs
+    deep = sum(panel.shape[0] for panel in panels)
+    start = left_ref.shape[1] - deep
+    groups, _, rows, width = keep_ref.shape
     wide = width // 4
-    return pl.pallas_call(
-        functools.partial(term_kernel, rows),
-        grid=(width // wide,),
-        in_specs=[pl.BlockSpec(left.shape, lambda n: (0, 0))]
-        + [pl.BlockSpec((panel.shape[0], wide), lambda n: (0, n)) for panel in panels],
-        out_specs=[pl.BlockSpec((groups, 2, rows, wide), lambda n: (0, 0, 0, n))] * 2,
-        out_shape=[
-            jax.ShapeDtypeStruct((groups, 2, rows, width), jnp.float32),
-            jax.ShapeDtypeStruct((groups, 2, rows, width), jnp.bfloat16),
-        ],
-        scratch_shapes=[pltpu.VMEM((deep, wide), jnp.bfloat16)],
-        compiler_params=pltpu.CompilerParams(vmem_limit_bytes=LIMIT),
-        cost_estimate=pl.CostEstimate(
-            flops=2 * left.shape[0] * deep * width,
-            bytes_accessed=2 * deep * (left.shape[0] + width) + 12 * groups * rows * width,
-            transcendentals=0,
-        ),
-    )(left, *panels)
+    for n in range(4):
+        columns = slice(n * wide, (n + 1) * wide)
+        out = early_ref[:, columns] + jnp.dot(
+            left_ref[:, start:], gathered(panels, columns), preferred_element_type=jnp.float32
+        )
+        for k in range(groups):
+            for part in range(2):
+                lo = (2 * k + part) * rows
+                keep_ref[k, part, :, columns] = out[lo : lo + rows]
+                lo += 2 * groups * rows
+                send_ref[k, part, :, columns] = out[lo : lo + rows].astype(jnp.bfloat16)
+
+
+def whole_call(kernel, args, outs, flops):
+    whole = pl.BlockSpec(memory_space=pltpu.VMEM)
+    size = sum(math.prod(x.shape) * x.dtype.itemsize for x in (*args, *outs))
+    return pl.pallas_call(
+        kernel,
+        in_specs=[whole] * len(args),
+        out_specs=[whole] * len(outs),
+        out_shape=outs,
+        compiler_params=pltpu.CompilerParams(vmem_limit_bytes=LIMIT),
+        cost_estimate=pl.CostEstimate(flops=flops, bytes_accessed=size, transcendentals=0),
+    )(*args)
+
+
+def early_terms(left, panels):
+    out = jax.ShapeDtypeStruct((left.shape[0], panels[0].shape[1]), jnp.float32)
+    deep = sum(panel.shape[0] for panel in panels)
+    return whole_call(early_kernel, (left, *panels), [out], 2 * deep * out.shape[0] * out.shape[1])[0]
+
+
+def late_terms(left, early, panels, rows):
+    width = early.shape[1]
+    deep = sum(panel.shape[0] for panel in panels)
+    shape = (left.shape[0] // (4 * rows), 2, rows, width)
+    outs = [jax.ShapeDtypeStruct(shape, jnp.float32), jax.ShapeDtypeStruct(shape, jnp.bfloat16)]
+    return whole_call(late_kernel, (left, early, *panels), outs, 2 * deep * left.shape[0] * width)
 
 
 def last_kernel(scale, *refs):
@@ -175,10 +228,9 @@
 
 
 def shards(source, propagator, transmission, upgoing):
-    weight = propagator[0, 0]
     factor = transmission[0, 0]
     upward = upgoing[0, 0]
-    width = weight.shape[1]
+    width = propagator.shape[3]
     shots = source.shape[3]
     level = lax.axis_index("depth")
     levels = lax.axis_size("depth")
@@ -188,7 +240,7 @@
     group, place, core = mine // 4, (mine // 2) % 2, mine % 2
     rows = width // freqs
     part = shots // CHUNKS
-    ready = first_advance(source, propagator, transmission, part)
+    *ready, joined = first_advance(source, propagator, transmission, part)
     by_place = upward.reshape(2, groups, 2, 2 * rows, shots)
     asked = lax.dynamic_index_in_dim(by_place, 1 - place, 2, keepdims=False).reshape(2, 2 * groups * rows, shots)
     got = swapped(asked, "freq", 2)
@@ -210,13 +262,14 @@
             arrived = flying[tick - DELAY]
             if tick == ticks // 2:
                 arrived, left = lax.optimization_barrier((arrived, left))
-            out = jnp.where(level == 0, out, advance(arrived, weight, factor))
+            out = jnp.where(level == 0, out, advance(arrived, joined, factor))
         if tick + DELAY < ticks:
             flying.append(ring(out, "depth", 1))
         if tick >= ticks - CHUNKS:
             own.append(out)
             other.append(swapped(out, "freq", 2))
-    keep, send = terms(left, own + other, rows)
+    early = early_terms(left, own + other[:-2])
+    keep, send = late_terms(left, early, other[-2:], rows)
     near = swapped(send, "freq", 1)
     parts = [keep, near]
     for k in range(1, groups):

time: 107 us -> 102 us (0.953)
  waiting for transfers between devices: 56.7 us -> 54.2 us
  matrix products: 17.8 us -> 15.4 us
    dot_general x16 -> x8, matrix products: 17.8 us -> 15.4 us  [advance(): lax.dot_general(both, joined, (((1,), (1,)), ((), ())), preferred_element...]
    ppermute x6, waiting for transfers between devices: 9.91 us -> 8.05 us  [swapped(): lax.ppermute(block, axis, [(i, i ^ bit) for i in range(lax.axis_size(axis...]
    ppermute x6, starting transfers between devices: 6.98 us -> 8.05 us  [swapped(): lax.ppermute(block, axis, [(i, i ^ bit) for i in range(lax.axis_size(axis...]
    pallas_call x2 -> x3, Pallas kernels: 9.92 us -> 10.2 us  [the longest x1 7.74 us: first_advance(): pl.pallas_call(functools.partial(first_kernel, part), in_specs=[pl.BlockS...]
  transfers between devices with their start and end apart: 15 -> 15, of which waited for: 11 -> 12; matrix products, arithmetic and copies ran while one was open for 18% -> 17% of each run, Pallas kernels for 1% -> 3%
where the time goes in v5:
time: 102 us; the launch traced here: 100 us
  waiting for transfers between devices  54.2 us (53%)
  matrix products  15.4 us (15%)
  starting transfers between devices  14.3 us (14%)
  Pallas kernels  13.1 us (13%)
  local copies, waits for them, and re-layouts  2.07 us (2%)
  other arithmetic  1.26 us (1%)
    ppermute x9, waiting for transfers between devices, ring(): lax.ppermute(block, axis, [(i, (i + distance) % size) for i in range(size)])  46.2 us
    dot_general x8, matrix products, advance(): lax.dot_general(both, joined, (((1,), (1,)), ((), ())), preferred_element...  15.4 us
    ppermute x6, starting transfers between devices, swapped(): lax.ppermute(block, axis, [(i, i ^ bit) for i in range(lax.axis_size(axis...  8.05 us
    ppermute x6, waiting for transfers between devices, swapped(): lax.ppermute(block, axis, [(i, i ^ bit) for i in range(lax.axis_size(axis...  8.05 us
    pallas_call x1, Pallas kernels, first_advance(): pl.pallas_call(functools.partial(first_kernel, part), in_specs=[pl.BlockS...  7.74 us
    ppermute x9, starting transfers between devices, ring(): lax.ppermute(block, axis, [(i, (i + distance) % size) for i in range(size)])  6.23 us
    pallas_call x2, Pallas kernels, whole_call(): pl.pallas_call(kernel, in_specs=[whole] * len(args), out_specs=[whole] *...  2.5 us
  transfers between devices with their start and end apart: 15, of which 12 were waited for; matrix products, arithmetic and copies ran while one was open for 17% of the time, Pallas kernels for 3%

profile of v5, /device:TPU:4, one launch (start us, length us, event | category | flops | bytes accessed | tf_op | source)
XLA Modules:
  0.0 100.5 jit_solution(17524428230501069728)
XLA Ops:
  0.0 7.7 %shard_map.46 = (bf16[128,1024]{1,0:T(8,128)(2,1)S(1)}, bf16[128,1024]{1,0:T(8,128)(2,1)S(1)}, bf16[128,1024]{1,0:T(8,128)(2,1)S(1)}, bf16[128,1024]{1,0:T(8,128)(2,1)S(1)}, bf16[1024,2048]{1,0:T(8,128)(2,1)S(1)}) custom-call(bf16[1,2,1024,256]{3,2,1,0:T(8,128)(2,1)} %source_ref.1, bf16[1,1,2,1024,1024]{4,3,2,1,0:T(8,128)(2,1)} %weight_ref.1, ...), custom_call_target="tpu_custom_call" | custom-call | flops 2147483648 | bytes 6291456 | tf_op jit(solution)/shard_map/pallas_call | solution.py:75
  7.8 1.9 %copy-done.1 = bf16[1024,2048]{1,0:T(8,128)(2,1)} copy-done((bf16[1024,2048]{1,0:T(8,128)(2,1)}, bf16[1024,2048]{1,0:T(8,128)(2,1)S(1)}, u32[]{:S(2)}) %copy-start.1) | copy-done | bytes 4194328
  11.2 1.6 %collective-permute-start.2 = (bf16[2,512,256]{2,1,0:T(8,128)(2,1)S(1)}, bf16[2,512,256]{2,1,0:T(8,128)(2,1)S(1)}, u32[]{:S(2)}, u32[]{:S(2)}) collective-permute-start(bf16[2,512,256]{2,1,0:T(8,128)(2,1)S(1)} %bitcast.25), channel_id=1, source_target_pairs={{0,2},{1,3},{2,0},{3,1},{4,6},{5,7},{6,4},{7,5},{8,10},{9,11},{10,... | collective-permute-start | bytes 1572872 | tf_op jit(solution)/shard_map/ppermute | solution.py:22
  13.4 6.4 %collective-permute-done = bf16[128,1024]{1,0:T(8,128)(2,1)S(1)} collective-permute-done((bf16[128,1024]{1,0:T(8,128)(2,1)S(1)}, bf16[128,1024]{1,0:T(8,128)(2,1)S(1)}, u32[]{:S(2)}, u32[]{:S(2)}) %collective-permute-start) | collective-permute-done | bytes 262176 | tf_op jit(solution)/shard_map/ppermute | solution.py:18
  19.8 3.7 %fusion.15 = bf16[128,1024]{1,0:T(8,128)(2,1)S(1)} fusion(bf16[128,1024]{1,0:T(8,128)(2,1)S(1)} %get-tuple-element.14, bf16[1024,2048]{1,0:T(8,128)(2,1)} %copy-done.1, bf16[64,1024]{1,0:T(8,128)(2,1)S(1)} %get-tuple-element.38, bf16[64,1024]{1,0:T(8,128)(2,1)S(1)} %get-tuple-element.37, bf16[128,1024]{1,0:T(8,128)(2,1)S(1)} %collective-permute-done, ...), kind=kOutput, calls=%fused_computation.23 | convolution fusion | flops 538836992 | bytes 5246977 | tf_op jit(solution)/shard_map/dot_general | solution.py:99
  25.4 2.5 %fusion.14 = bf16[128,1024]{1,0:T(8,128)(2,1)S(1)} fusion(bf16[128,1024]{1,0:T(8,128)(2,1)S(1)} %get-tuple-element.18, bf16[1024,2048]{1,0:T(8,128)(2,1)S(1)} %copy-done.2, bf16[64,1024]{1,0:T(8,128)(2,1)S(1)} %get-tuple-element.36, bf16[64,1024]{1,0:T(8,128)(2,1)S(1)} %get-tuple-element.35, bf16[128,1024]{1,0:T(8,128)(2,1)} %collective-permute-done.3, ...), kind=kOutput, calls=%fused_computation.22 | convolution fusion | flops 538836992 | bytes 5246977 | tf_op jit(solution)/shard_map/dot_general | solution.py:99
  28.6 1.5 %shard_map.47.left_ref = bf16[1024,1024]{1,0:T(8,128)(2,1)S(1)} custom-call(s32[9]{0:T(128)S(1)} %stack.39.spot_ref, bf16[2,1024,256]{2,1,0:T(8,128)(2,1)S(1)} %bitcast.24, bf16[2,512,256]{2,1,0:T(8,128)(2,1)S(1)} %collective-permute-done.2.got_ref), custom_call_target="tpu_custom_call" | custom-call | bytes 3145728 | tf_op jit(solution)/shard_map/pallas_call | solution.py:128
  31.4 1.5 %fusion.11 = bf16[128,1024]{1,0:T(8,128)(2,1)S(1)} fusion(bf16[128,1024]{1,0:T(8,128)(2,1)S(1)} %get-tuple-element.15, bf16[1024,2048]{1,0:T(8,128)(2,1)S(1)} %copy-done.2, bf16[64,1024]{1,0:T(8,128)(2,1)S(1)} %get-tuple-element.30, bf16[64,1024]{1,0:T(8,128)(2,1)S(1)} %get-tuple-element.29, bf16[128,1024]{1,0:T(8,128)(2,1)S(1)} %collective-permute-done.1, ...), kind=kOutput, calls=%fused_computation.19 | convolution fusion | flops 538836992 | bytes 5246977 | tf_op jit(solution)/shard_map/dot_general | solution.py:99
  33.0 5.0 %collective-permute-done.4 = bf16[128,1024]{1,0:T(8,128)(2,1)S(1)} collective-permute-done((bf16[128,1024]{1,0:T(8,128)(2,1)S(1)}, bf16[128,1024]{1,0:T(8,128)(2,1)S(1)}, u32[]{:S(2)}, u32[]{:S(2)}) %collective-permute-start.4) | collective-permute-done | bytes 262176 | tf_op jit(solution)/shard_map/ppermute | solution.py:18
  38.1 1.5 %fusion.13 = bf16[128,1024]{1,0:T(8,128)(2,1)S(1)} fusion(bf16[128,1024]{1,0:T(8,128)(2,1)S(1)} %get-tuple-element.19, bf16[1024,2048]{1,0:T(8,128)(2,1)S(1)} %copy-done.2, bf16[64,1024]{1,0:T(8,128)(2,1)S(1)} %get-tuple-element.34, bf16[64,1024]{1,0:T(8,128)(2,1)S(1)} %get-tuple-element.33, bf16[128,1024]{1,0:T(8,128)(2,1)S(1)} %collective-permute-done.4, ...), kind=kOutput, calls=%fused_computation.21 | convolution fusion | flops 538836992 | bytes 5246977 | tf_op jit(solution)/shard_map/dot_general | solution.py:99
  39.6 4.0 %collective-permute-done.6 = bf16[128,1024]{1,0:T(8,128)(2,1)S(1)} collective-permute-done((bf16[128,1024]{1,0:T(8,128)(2,1)S(1)}, bf16[128,1024]{1,0:T(8,128)(2,1)S(1)}, u32[]{:S(2)}, u32[]{:S(2)}) %collective-permute-start.6) | collective-permute-done | bytes 262176 | tf_op jit(solution)/shard_map/ppermute | solution.py:18
  43.7 1.5 %fusion.10.refs_1_ = bf16[128,1024]{1,0:T(8,128)(2,1)S(1)} fusion(bf16[128,1024]{1,0:T(8,128)(2,1)S(1)} %get-tuple-element.14, bf16[1024,2048]{1,0:T(8,128)(2,1)S(1)} %copy-done.2, bf16[64,1024]{1,0:T(8,128)(2,1)S(1)} %get-tuple-element.28, bf16[64,1024]{1,0:T(8,128)(2,1)S(1)} %get-tuple-element.27, bf16[128,1024]{1,0:T(8,128)(2,1)S(1)} %collective-permute-done.6, ...), kind=kOutput, calls=%fused_computation.18 | convolution fusion | flops 538836992 | bytes 5246977 | tf_op jit(solution)/shard_map/dot_general | solution.py:99
  45.2 1.6 %collective-permute-start.10 = (bf16[128,1024]{1,0:T(8,128)(2,1)S(1)}, bf16[128,1024]{1,0:T(8,128)(2,1)S(1)}, u32[]{:S(2)}, u32[]{:S(2)}) collective-permute-start(bf16[128,1024]{1,0:T(8,128)(2,1)S(1)} %fusion.10.refs_1_), channel_id=1, source_target_pairs={{0,2},{1,3},{2,0},{3,1},{4,6},{5,7},{6,4},{7,5},{8,10},{9,11},{10,... | collective-permute-start | bytes 786440 | tf_op jit(solution)/shard_map/ppermute | solution.py:22
  48.3 1.5 %fusion.12.refs_0_ = bf16[128,1024]{1,0:T(8,128)(2,1)S(1)} fusion(bf16[128,1024]{1,0:T(8,128)(2,1)S(1)} %get-tuple-element.18, bf16[1024,2048]{1,0:T(8,128)(2,1)S(1)} %copy-done.2, bf16[64,1024]{1,0:T(8,128)(2,1)S(1)} %get-tuple-element.32, bf16[64,1024]{1,0:T(8,128)(2,1)S(1)} %get-tuple-element.31, bf16[128,1024]{1,0:T(8,128)(2,1)S(1)} %collective-permute-done.5, ...), kind=kOutput, calls=%fused_computation.20 | convolution fusion | flops 538836992 | bytes 5246977 | tf_op jit(solution)/shard_map/dot_general | solution.py:99
  49.9 2.8 %collective-permute-start.9 = (bf16[128,1024]{1,0:T(8,128)(2,1)S(1)}, bf16[128,1024]{1,0:T(8,128)(2,1)S(1)}, u32[]{:S(2)}, u32[]{:S(2)}) collective-permute-start(bf16[128,1024]{1,0:T(8,128)(2,1)S(1)} %fusion.12.refs_0_), channel_id=1, source_target_pairs={{0,2},{1,3},{2,0},{3,1},{4,6},{5,7},{6,4},{7,5},{8,10},{9,11},{10,... | collective-permute-start | bytes 786440 | tf_op jit(solution)/shard_map/ppermute | solution.py:22
  52.6 3.4 %collective-permute-done.8 = bf16[128,1024]{1,0:T(8,128)(2,1)S(1)} collective-permute-done((bf16[128,1024]{1,0:T(8,128)(2,1)S(1)}, bf16[128,1024]{1,0:T(8,128)(2,1)S(1)}, u32[]{:S(2)}, u32[]{:S(2)}) %collective-permute-start.8) | collective-permute-done | bytes 262176 | tf_op jit(solution)/shard_map/ppermute | solution.py:18
  56.0 1.5 %fusion.8.refs_3_ = bf16[128,1024]{1,0:T(8,128)(2,1)S(1)} fusion(bf16[128,1024]{1,0:T(8,128)(2,1)S(1)} %get-tuple-element.15, bf16[1024,2048]{1,0:T(8,128)(2,1)S(1)} %copy-done.2, bf16[64,1024]{1,0:T(8,128)(2,1)S(1)} %get-tuple-element.24, bf16[64,1024]{1,0:T(8,128)(2,1)S(1)} %get-tuple-element.23, bf16[128,1024]{1,0:T(8,128)(2,1)S(1)} %collective-permute-done.8, ...), kind=kOutput, calls=%fused_computation.16 | convolution fusion | flops 538836992 | bytes 5246977 | tf_op jit(solution)/shard_map/dot_general | solution.py:99
  59.9 1.6 %fusion.9.refs_2_ = bf16[128,1024]{1,0:T(8,128)(2,1)S(1)} fusion(bf16[128,1024]{1,0:T(8,128)(2,1)S(1)} %get-tuple-element.19, bf16[1024,2048]{1,0:T(8,128)(2,1)S(1)} %copy-done.2, bf16[64,1024]{1,0:T(8,128)(2,1)S(1)} %get-tuple-element.26, bf16[64,1024]{1,0:T(8,128)(2,1)S(1)} %get-tuple-element.25, bf16[128,1024]{1,0:T(8,128)(2,1)S(1)} %collective-permute-done.7, ...), kind=kOutput, calls=%fused_computation.17 | convolution fusion | flops 538836992 | bytes 5246977 | tf_op jit(solution)/shard_map/dot_general | solution.py:99
  62.2 1.8 %shard_map.48.early_ref = f32[1024,1024]{1,0:T(8,128)S(1)} custom-call(bf16[1024,1024]{1,0:T(8,128)(2,1)S(1)} %shard_map.47.left_ref, bf16[128,1024]{1,0:T(8,128)(2,1)S(1)} %fusion.12.refs_0_, bf16[128,1024]{1,0:T(8,128)(2,1)S(1)} %fusion.10.refs_1_, bf16[128,1024]{1,0:T(8,128)(2,1)S(1)} %fusion.9.refs_2_, bf16[128,1024]{1,0:T(8,128)(2,1)S(1)} %fusion.8.refs_3_, ...), custom_call_target="tpu_custom_call" | custom-call | flops 1610612736 | bytes 7864320 | tf_op jit(solution)/shard_map/pallas_call | solution.py:182
  64.0 2.6 %collective-permute-done.12.refs_1_ = bf16[128,1024]{1,0:T(8,128)(2,1)S(1)} collective-permute-done((bf16[128,1024]{1,0:T(8,128)(2,1)S(1)}, bf16[128,1024]{1,0:T(8,128)(2,1)S(1)}, u32[]{:S(2)}, u32[]{:S(2)}) %collective-permute-start.12) | collective-permute-done | bytes 262176 | tf_op jit(solution)/shard_map/ppermute | solution.py:22
  66.6 2.8 %collective-permute-done.11.refs_0_ = bf16[128,1024]{1,0:T(8,128)(2,1)S(1)} collective-permute-done((bf16[128,1024]{1,0:T(8,128)(2,1)S(1)}, bf16[128,1024]{1,0:T(8,128)(2,1)S(1)}, u32[]{:S(2)}, u32[]{:S(2)}) %collective-permute-start.11) | collective-permute-done | bytes 262176 | tf_op jit(solution)/shard_map/ppermute | solution.py:22
  70.2 2.6 %collective-permute-done.13.refs_1_ = bf16[2,2,128,1024]{3,2,1,0:T(8,128)(2,1)S(1)} collective-permute-done((bf16[2,2,128,1024]{3,2,1,0:T(8,128)(2,1)S(1)}, bf16[2,2,128,1024]{3,2,1,0:T(8,128)(2,1)S(1)}, u32[]{:S(2)}, u32[]{:S(2)}) %collective-permute-start.13) | collective-permute-done | bytes 1048608 | tf_op jit(solution)/shard_map/ppermute | solution.py:22
  73.0 2.7 %collective-permute-start.14 = (bf16[1,2,128,1024]{3,2,1,0:T(8,128)(2,1)S(1)}, bf16[1,2,128,1024]{3,2,1,0:T(8,128)(2,1)S(1)}, u32[]{:S(2)}, u32[]{:S(2)}) collective-permute-start(bf16[1,2,128,1024]{3,2,1,0:T(8,128)(2,1)S(1)} %add_convert_fusion), channel_id=1, source_target_pairs={{0,4},{1,5},{2,6},{3,7},{4,0},{5,1},{6,2},{7,3},{8,12},{9,13},{10,... | collective-permute-start | bytes 1572872 | tf_op jit(solution)/shard_map/ppermute | solution.py:18
  75.7 23.5 %collective-permute-done.14.refs_2_ = bf16[1,2,128,1024]{3,2,1,0:T(8,128)(2,1)S(1)} collective-permute-done((bf16[1,2,128,1024]{3,2,1,0:T(8,128)(2,1)S(1)}, bf16[1,2,128,1024]{3,2,1,0:T(8,128)(2,1)S(1)}, u32[]{:S(2)}, u32[]{:S(2)}) %collective-permute-start.14) | collective-permute-done | bytes 524320 | tf_op jit(solution)/shard_map/ppermute | solution.py:18
  (38 shorter events, 12.9 us)
Async XLA Ops:
  0.0 19.8 %copy-start.3 = (f32[1,1,1024]{2,1,0:T(1,128)S(1)}, f32[1,1,1024]{2,1,0:T(1,128)}, u32[]{:S(2)}) copy-start(f32[1,1,1024]{2,1,0:T(1,128)} %factor_ref.1) | copy-start | bytes 12292
  0.0 11.2 %copy-start = (bf16[1,1,2,1024,256]{4,3,2,1,0:T(8,128)(2,1)S(1)}, bf16[1,1,2,1024,256]{4,3,2,1,0:T(8,128)(2,1)}, u32[]{:S(2)}) copy-start(bf16[1,1,2,1024,256]{4,3,2,1,0:T(8,128)(2,1)} %param.7) | copy-start | bytes 3145732
  7.8 1.9 %copy-start.1 = (bf16[1024,2048]{1,0:T(8,128)(2,1)}, bf16[1024,2048]{1,0:T(8,128)(2,1)S(1)}, u32[]{:S(2)}) copy-start(bf16[1024,2048]{1,0:T(8,128)(2,1)S(1)} %get-tuple-element.16) | copy-start | bytes 12582916
  9.7 10.1 %collective-permute-start = (bf16[128,1024]{1,0:T(8,128)(2,1)S(1)}, bf16[128,1024]{1,0:T(8,128)(2,1)S(1)}, u32[]{:S(2)}, u32[]{:S(2)}) collective-permute-start(bf16[128,1024]{1,0:T(8,128)(2,1)S(1)} %get-tuple-element.15), channel_id=1, source_target_pairs={{0,8},{8,16},{16,24},{24,0},{1,9},{9,17},{17,25},{25,1},{2,10},{10... | collective-permute-start | bytes 786440 | tf_op jit(solution)/shard_map/ppermute | solution.py:18
  11.2 17.4 %collective-permute-start.2 = (bf16[2,512,256]{2,1,0:T(8,128)(2,1)S(1)}, bf16[2,512,256]{2,1,0:T(8,128)(2,1)S(1)}, u32[]{:S(2)}, u32[]{:S(2)}) collective-permute-start(bf16[2,512,256]{2,1,0:T(8,128)(2,1)S(1)} %bitcast.25), channel_id=1, source_target_pairs={{0,2},{1,3},{2,0},{3,1},{4,6},{5,7},{6,4},{7,5},{8,10},{9,11},{10,... | collective-permute-start | bytes 1572872 | tf_op jit(solution)/shard_map/ppermute | solution.py:22
  12.9 11.5 %collective-permute-start.3 = (bf16[128,1024]{1,0:T(8,128)(2,1)S(1)}, bf16[128,1024]{1,0:T(8,128)(2,1)}, u32[]{:S(2)}, u32[]{:S(2)}) collective-permute-start(bf16[128,1024]{1,0:T(8,128)(2,1)S(1)} %get-tuple-element.19), channel_id=1, source_target_pairs={{0,8},{8,16},{16,24},{24,0},{1,9},{9,17},{17,25},{25,1},{2,10},{10... | collective-permute-start | bytes 786440 | tf_op jit(solution)/shard_map/ppermute | solution.py:18
  13.4 11.9 %copy-start.2 = (bf16[1024,2048]{1,0:T(8,128)(2,1)S(1)}, bf16[1024,2048]{1,0:T(8,128)(2,1)}, u32[]{:S(2)}) copy-start(bf16[1024,2048]{1,0:T(8,128)(2,1)} %copy-done.1) | copy-start | bytes 12582916
  23.6 7.8 %collective-permute-start.1 = (bf16[128,1024]{1,0:T(8,128)(2,1)S(1)}, bf16[128,1024]{1,0:T(8,128)(2,1)S(1)}, u32[]{:S(2)}, u32[]{:S(2)}) collective-permute-start(bf16[128,1024]{1,0:T(8,128)(2,1)S(1)} %fusion.15), channel_id=1, source_target_pairs={{0,8},{8,16},{16,24},{24,0},{1,9},{9,17},{17,25},{25,1},{2,10},{10... | collective-permute-start | bytes 786440 | tf_op jit(solution)/shard_map/ppermute | solution.py:18
  27.8 10.2 %collective-permute-start.4 = (bf16[128,1024]{1,0:T(8,128)(2,1)S(1)}, bf16[128,1024]{1,0:T(8,128)(2,1)S(1)}, u32[]{:S(2)}, u32[]{:S(2)}) collective-permute-start(bf16[128,1024]{1,0:T(8,128)(2,1)S(1)} %fusion.14), channel_id=1, source_target_pairs={{0,8},{8,16},{16,24},{24,0},{1,9},{9,17},{17,25},{25,1},{2,10},{10... | collective-permute-start | bytes 786440 | tf_op jit(solution)/shard_map/ppermute | solution.py:18
  32.9 10.7 %collective-permute-start.6 = (bf16[128,1024]{1,0:T(8,128)(2,1)S(1)}, bf16[128,1024]{1,0:T(8,128)(2,1)S(1)}, u32[]{:S(2)}, u32[]{:S(2)}) collective-permute-start(bf16[128,1024]{1,0:T(8,128)(2,1)S(1)} %fusion.11), channel_id=1, source_target_pairs={{0,8},{8,16},{16,24},{24,0},{1,9},{9,17},{17,25},{25,1},{2,10},{10... | collective-permute-start | bytes 786440 | tf_op jit(solution)/shard_map/ppermute | solution.py:18
  39.6 8.7 %collective-permute-start.5 = (bf16[128,1024]{1,0:T(8,128)(2,1)S(1)}, bf16[128,1024]{1,0:T(8,128)(2,1)S(1)}, u32[]{:S(2)}, u32[]{:S(2)}) collective-permute-start(bf16[128,1024]{1,0:T(8,128)(2,1)S(1)} %fusion.13), channel_id=1, source_target_pairs={{0,8},{8,16},{16,24},{24,0},{1,9},{9,17},{17,25},{25,1},{2,10},{10... | collective-permute-start | bytes 786440 | tf_op jit(solution)/shard_map/ppermute | solution.py:18
  45.2 17.0 %collective-permute-start.10 = (bf16[128,1024]{1,0:T(8,128)(2,1)S(1)}, bf16[128,1024]{1,0:T(8,128)(2,1)S(1)}, u32[]{:S(2)}, u32[]{:S(2)}) collective-permute-start(bf16[128,1024]{1,0:T(8,128)(2,1)S(1)} %fusion.10.refs_1_), channel_id=1, source_target_pairs={{0,2},{1,3},{2,0},{3,1},{4,6},{5,7},{6,4},{7,5},{8,10},{9,11},{10,... | collective-permute-start | bytes 786440 | tf_op jit(solution)/shard_map/ppermute | solution.py:22
  46.8 9.2 %collective-permute-start.8 = (bf16[128,1024]{1,0:T(8,128)(2,1)S(1)}, bf16[128,1024]{1,0:T(8,128)(2,1)S(1)}, u32[]{:S(2)}, u32[]{:S(2)}) collective-permute-start(bf16[128,1024]{1,0:T(8,128)(2,1)S(1)} %fusion.10.refs_1_), channel_id=1, source_target_pairs={{0,8},{8,16},{16,24},{24,0},{1,9},{9,17},{17,25},{25,1},{2,10},{10... | collective-permute-start | bytes 786440 | tf_op jit(solution)/shard_map/ppermute | solution.py:18
  49.9 12.4 %collective-permute-start.9 = (bf16[128,1024]{1,0:T(8,128)(2,1)S(1)}, bf16[128,1024]{1,0:T(8,128)(2,1)S(1)}, u32[]{:S(2)}, u32[]{:S(2)}) collective-permute-start(bf16[128,1024]{1,0:T(8,128)(2,1)S(1)} %fusion.12.refs_0_), channel_id=1, source_target_pairs={{0,2},{1,3},{2,0},{3,1},{4,6},{5,7},{6,4},{7,5},{8,10},{9,11},{10,... | collective-permute-start | bytes 786440 | tf_op jit(solution)/shard_map/ppermute | solution.py:22
  52.6 7.3 %collective-permute-start.7 = (bf16[128,1024]{1,0:T(8,128)(2,1)S(1)}, bf16[128,1024]{1,0:T(8,128)(2,1)S(1)}, u32[]{:S(2)}, u32[]{:S(2)}) collective-permute-start(bf16[128,1024]{1,0:T(8,128)(2,1)S(1)} %fusion.12.refs_0_), channel_id=1, source_target_pairs={{0,8},{8,16},{16,24},{24,0},{1,9},{9,17},{17,25},{25,1},{2,10},{10... | collective-permute-start | bytes 786440 | tf_op jit(solution)/shard_map/ppermute | solution.py:18
  57.6 9.0 %collective-permute-start.12 = (bf16[128,1024]{1,0:T(8,128)(2,1)S(1)}, bf16[128,1024]{1,0:T(8,128)(2,1)S(1)}, u32[]{:S(2)}, u32[]{:S(2)}) collective-permute-start(bf16[128,1024]{1,0:T(8,128)(2,1)S(1)} %fusion.8.refs_3_), channel_id=1, source_target_pairs={{0,2},{1,3},{2,0},{3,1},{4,6},{5,7},{6,4},{7,5},{8,10},{9,11},{10,... | collective-permute-start | bytes 786440 | tf_op jit(solution)/shard_map/ppermute | solution.py:22
  61.5 7.9 %collective-permute-start.11 = (bf16[128,1024]{1,0:T(8,128)(2,1)S(1)}, bf16[128,1024]{1,0:T(8,128)(2,1)S(1)}, u32[]{:S(2)}, u32[]{:S(2)}) collective-permute-start(bf16[128,1024]{1,0:T(8,128)(2,1)S(1)} %fusion.9.refs_2_), channel_id=1, source_target_pairs={{0,2},{1,3},{2,0},{3,1},{4,6},{5,7},{6,4},{7,5},{8,10},{9,11},{10,... | collective-permute-start | bytes 786440 | tf_op jit(solution)/shard_map/ppermute | solution.py:22
  70.1 2.7 %collective-permute-start.13 = (bf16[2,2,128,1024]{3,2,1,0:T(8,128)(2,1)S(1)}, bf16[2,2,128,1024]{3,2,1,0:T(8,128)(2,1)S(1)}, u32[]{:S(2)}, u32[]{:S(2)}) collective-permute-start(bf16[2,2,128,1024]{3,2,1,0:T(8,128)(2,1)S(1)} %get-tuple-element.22), channel_id=1, source_target_pairs={{0,1},{1,0},{2,3},{3,2},{4,5},{5,4},{6,7},{7,6},{8,9},{9,8},{10,11... | collective-permute-start | bytes 3145736 | tf_op jit(solution)/shard_map/ppermute | solution.py:22
  73.0 26.2 %collective-permute-start.14 = (bf16[1,2,128,1024]{3,2,1,0:T(8,128)(2,1)S(1)}, bf16[1,2,128,1024]{3,2,1,0:T(8,128)(2,1)S(1)}, u32[]{:S(2)}, u32[]{:S(2)}) collective-permute-start(bf16[1,2,128,1024]{3,2,1,0:T(8,128)(2,1)S(1)} %add_convert_fusion), channel_id=1, source_target_pairs={{0,4},{1,5},{2,6},{3,7},{4,0},{5,1},{6,2},{7,3},{8,12},{9,13},{10,... | collective-permute-start | bytes 1572872 | tf_op jit(solution)/shard_map/ppermute | solution.py:18

commit v6 on v5

--- a/solution.py
+++ b/solution.py
@@ -10,7 +10,7 @@
 
 CHUNKS = 4
 DELAY = 2
-LIMIT = 32 * 1024 * 1024
+LIMIT = 16 * 1024 * 1024
 
 
 def ring(block, axis, distance):
@@ -23,7 +23,7 @@
 
 
 def first_kernel(part, source_ref, weight_ref, factor_ref, *refs):
-    *outs, joined_ref, source, factor, left, sem, sems = refs
+    *outs, joined_ref, source, factor, right, sem, sems = refs
     width = joined_ref.shape[0]
     blocks = sems.shape[0]
     wide = width // blocks
@@ -48,23 +48,20 @@
             copy.start()
     for copy in begin:
         copy.wait()
-    real, imag = source[0].T, source[1].T
-    for chunk in range(len(outs)):
-        lo, at = chunk * part, 2 * chunk * part
-        left[at : at + part, :width] = real[lo : lo + part]
-        left[at : at + part, width:] = -imag[lo : lo + part]
-        left[at + part : at + 2 * part, :width] = imag[lo : lo + part]
-        left[at + part : at + 2 * part, width:] = real[lo : lo + part]
+    shots = source.shape[2]
+    for half, (re, im) in enumerate(((source[0], source[1]), (-source[1], source[0]))):
+        right[half * width : (half + 1) * width, :shots] = re
+        right[half * width : (half + 1) * width, shots:] = im
     for n in range(blocks):
         for copy in copies(n):
             copy.wait()
         columns = slice(n * wide, (n + 1) * wide)
-        out = lax.dot_general(
-            left[...], joined_ref[columns], (((1,), (1,)), ((), ())), preferred_element_type=jnp.float32
-        )
-        out = (out * factor[:, columns]).astype(jnp.bfloat16)
+        out = jnp.dot(joined_ref[columns], right[...], preferred_element_type=jnp.float32)
+        out = (out.T * factor[:, columns]).astype(jnp.bfloat16)
         for chunk in range(len(outs)):
-            outs[chunk][:, columns] = out[2 * chunk * part : 2 * (chunk + 1) * part]
+            lo = chunk * part
+            outs[chunk][:part, columns] = out[lo : lo + part]
+            outs[chunk][part:, columns] = out[shots + lo : shots + lo + part]
 
 
 def first_advance(source, propagator, transmission, part):
@@ -77,11 +74,11 @@
         in_specs=[pl.BlockSpec(memory_space=pltpu.HBM)] * 3,
         out_specs=[whole] * (chunks + 1),
         out_shape=[jax.ShapeDtypeStruct((2 * part, width), jnp.bfloat16)] * chunks
-        + [jax.ShapeDtypeStruct((width, 2 * width), jnp.bfloat16)],
+        + [pltpu.VMEM((width, 2 * width), jnp.bfloat16)],
         scratch_shapes=[
             pltpu.VMEM((2, width, shots), jnp.bfloat16),
             pltpu.VMEM((1, width), jnp.float32),
-            pltpu.VMEM((2 * shots, 2 * width), jnp.bfloat16),
+            pltpu.VMEM((2 * width, 2 * shots), jnp.bfloat16),
             pltpu.SemaphoreType.DMA((2,)),
             pltpu.SemaphoreType.DMA((4, 2)),
         ],
@@ -92,12 +89,42 @@
     )(*(pltpu.with_memory_space_constraint(x, pltpu.HBM) for x in (source, propagator, transmission)))
 
 
-def advance(panel, joined, factor):
-    part = panel.shape[0] // 2
-    turned = jnp.concatenate([-panel[part:], panel[:part]], axis=0)
-    both = jnp.concatenate([panel, turned], axis=1)
-    out = lax.dot_general(both, joined, (((1,), (1,)), ((), ())), preferred_element_type=jnp.float32)
-    return (out * factor[None, :]).astype(jnp.bfloat16)
+def advance_kernel(level_ref, arrived_ref, ready_ref, joined_ref, factor_ref, out_ref, both):
+    part = arrived_ref.shape[0] // 2
+    width = arrived_ref.shape[1]
+    wide = width // 4
+
+    @pl.when(level_ref[0] == 0)
+    def _():
+        out_ref[...] = ready_ref[...]
+
+    @pl.when(level_ref[0] != 0)
+    def _():
+        both[:, :width] = arrived_ref[...]
+        both[:part, width:] = -arrived_ref[part:]
+        both[part:, width:] = arrived_ref[:part]
+        for n in range(4):
+            columns = slice(n * wide, (n + 1) * wide)
+            out = lax.dot_general(
+                joined_ref[columns], both[...], (((1,), (1,)), ((), ())), preferred_element_type=jnp.float32
+            )
+            out_ref[:, columns] = (out.T * factor_ref[:, columns]).astype(jnp.bfloat16)
+
+
+def advance(level, arrived, ready, joined, factor):
+    rows, width = arrived.shape
+    whole = pl.BlockSpec(memory_space=pltpu.VMEM)
+    return pl.pallas_call(
+        advance_kernel,
+        in_specs=[pl.BlockSpec(memory_space=pltpu.SMEM)] + [whole] * 4,
+        out_specs=whole,
+        out_shape=jax.ShapeDtypeStruct((rows, width), jnp.bfloat16),
+        scratch_shapes=[pltpu.VMEM((rows, 2 * width), jnp.bfloat16)],
+        compiler_params=pltpu.CompilerParams(vmem_limit_bytes=LIMIT),
+        cost_estimate=pl.CostEstimate(
+            flops=4 * rows * width * width, bytes_accessed=4 * width * width + 6 * rows * width, transcendentals=0
+        ),
+    )(level, arrived, ready, pltpu.with_memory_space_constraint(joined, pltpu.VMEM), factor)
 
 
 def operand_kernel(part, step, spot_ref, own_ref, got_ref, out_ref):
@@ -228,12 +255,13 @@
 
 
 def shards(source, propagator, transmission, upgoing):
-    factor = transmission[0, 0]
+    factor = transmission[0]
     upward = upgoing[0, 0]
     width = propagator.shape[3]
     shots = source.shape[3]
     level = lax.axis_index("depth")
     levels = lax.axis_size("depth")
+    level_at = level.astype(jnp.int32).reshape(1)
     freqs = lax.axis_size("freq")
     mine = lax.axis_index("freq")
     groups = freqs // 4
@@ -262,7 +290,7 @@
             arrived = flying[tick - DELAY]
             if tick == ticks // 2:
                 arrived, left = lax.optimization_barrier((arrived, left))
-            out = jnp.where(level == 0, out, advance(arrived, joined, factor))
+            out = advance(level_at, arrived, out, joined, factor)
         if tick + DELAY < ticks:
             flying.append(ring(out, "depth", 1))
         if tick >= ticks - CHUNKS:

time: 102 us -> 103 us (level)
  matrix products: 15.4 us -> 0 us
  Pallas kernels: 13.1 us -> 22.9 us
  local copies, waits for them, and re-layouts: 2.07 us -> 8.88 us
  waiting for transfers between devices: 54.2 us -> 56.2 us
  other arithmetic: 1.26 us -> 0.14 us
    dot_general x8 -> x0, matrix products: 15.4 us -> none  [advance(): lax.dot_general(both, joined, (((1,), (1,)), ((), ())), preferred_element...]
    pallas_call x0 -> x8, Pallas kernels: none -> 11.7 us  [advance(): pl.pallas_call(advance_kernel, in_specs=[pl.BlockSpec(memory_space=pltpu....]
    unnamed x8 -> x14, local copies, waits for them, and re-layouts: 1.95 us -> 7.97 us
    ppermute x6, waiting for transfers between devices: 8.05 us -> 11.5 us  [swapped(): lax.ppermute(block, axis, [(i, i ^ bit) for i in range(lax.axis_size(axis...]
    pallas_call x1, Pallas kernels: 7.74 us -> 5.8 us  [first_advance(): pl.pallas_call(functools.partial(first_kernel, part), in_specs=[pl.BlockS...]
    ppermute x9, waiting for transfers between devices: 46.2 us -> 44.7 us  [ring(): lax.ppermute(block, axis, [(i, (i + distance) % size) for i in range(size)])]
    neg x8 -> x0, other arithmetic: 1.11 us -> none  [advance(): turned = jnp.concatenate([-panel[part:], panel[:part]], axis=0)]
  transfers between devices with their start and end apart: 15 -> 15, of which waited for: 12 -> 13; matrix products, arithmetic and copies ran while one was open for 17% -> 1% of each run, Pallas kernels for 3% -> 15%
where the time goes in v6:
time: 103 us; the launch traced here: 102 us
  waiting for transfers between devices  56.2 us (55%)
  Pallas kernels  22.9 us (22%)
  starting transfers between devices  13.7 us (13%)
  local copies, waits for them, and re-layouts  8.88 us (9%)
    ppermute x9, waiting for transfers between devices, ring(): lax.ppermute(block, axis, [(i, (i + distance) % size) for i in range(size)])  44.7 us
    pallas_call x8, Pallas kernels, advance(): pl.pallas_call(advance_kernel, in_specs=[pl.BlockSpec(memory_space=pltpu....  11.7 us
    ppermute x6, waiting for transfers between devices, swapped(): lax.ppermute(block, axis, [(i, i ^ bit) for i in range(lax.axis_size(axis...  11.5 us
    unnamed x14, local copies, waits for them, and re-layouts  7.97 us
    ppermute x6, starting transfers between devices, swapped(): lax.ppermute(block, axis, [(i, i ^ bit) for i in range(lax.axis_size(axis...  7.02 us
    ppermute x9, starting transfers between devices, ring(): lax.ppermute(block, axis, [(i, (i + distance) % size) for i in range(size)])  6.67 us
    pallas_call x1, Pallas kernels, first_advance(): pl.pallas_call(functools.partial(first_kernel, part), in_specs=[pl.BlockS...  5.8 us
    pallas_call x2, Pallas kernels, whole_call(): pl.pallas_call(kernel, in_specs=[whole] * len(args), out_specs=[whole] *...  2.52 us
  transfers between devices with their start and end apart: 15, of which 13 were waited for; matrix products, arithmetic and copies ran while one was open for 1% of the time, Pallas kernels for 15%

profile of v6, /device:TPU:4, one launch (start us, length us, event | category | flops | bytes accessed | tf_op | source)
XLA Modules:
  0.0 101.9 jit_solution(4964635791985782179)
XLA Ops:
  0.0 5.8 %shard_map.46 = (bf16[128,1024]{1,0:T(8,128)(2,1)S(1)}, bf16[128,1024]{1,0:T(8,128)(2,1)S(1)}, bf16[128,1024]{1,0:T(8,128)(2,1)S(1)}, bf16[128,1024]{1,0:T(8,128)(2,1)S(1)}, bf16[1024,2048]{1,0:T(8,128)(2,1)S(1)}) custom-call(bf16[1,2,1024,256]{3,2,1,0:T(8,128)(2,1)} %source_ref.1, bf16[1,1,2,1024,1024]{4,3,2,1,0:T(8,128)(2,1)} %weight_ref.1, ...), custom_call_target="tpu_custom_call" | custom-call | flops 2147483648 | bytes 6291456 | tf_op jit(solution)/shard_map/pallas_call | solution.py:72
  5.8 1.9 %copy-done = bf16[1024,2048]{1,0:T(8,128)(2,1)} copy-done((bf16[1024,2048]{1,0:T(8,128)(2,1)}, bf16[1024,2048]{1,0:T(8,128)(2,1)S(1)}, u32[]{:S(2)}) %copy-start) | copy-done | bytes 4194328
  7.7 1.5 %collective-permute-start = (bf16[128,1024]{1,0:T(8,128)(2,1)S(1)}, bf16[128,1024]{1,0:T(8,128)(2,1)S(1)}, u32[]{:S(2)}, u32[]{:S(2)}) collective-permute-start(bf16[128,1024]{1,0:T(8,128)(2,1)S(1)} %get-tuple-element.14.ready_ref), channel_id=1, source_target_pairs={{0,8},{8,16},{16,24},{24,0},{1,9},{9,17},{17,25},{25,1},{2,10},{10... | collective-permute-start | bytes 786440 | tf_op jit(solution)/shard_map/ppermute | solution.py:18
  10.1 1.6 %collective-permute-start.2 = (bf16[2,512,256]{2,1,0:T(8,128)(2,1)}, bf16[2,512,256]{2,1,0:T(8,128)(2,1)S(1)}, u32[]{:S(2)}, u32[]{:S(2)}) collective-permute-start(bf16[2,512,256]{2,1,0:T(8,128)(2,1)} %bitcast.13), channel_id=1, source_target_pairs={{0,2},{1,3},{2,0},{3,1},{4,6},{5,7},{6,4},{7,5},{8,10},{9,11},{10,... | collective-permute-start | bytes 1572872 | tf_op jit(solution)/shard_map/ppermute | solution.py:22
  12.1 5.7 %collective-permute-done.arrived_ref = bf16[128,1024]{1,0:T(8,128)(2,1)S(1)} collective-permute-done((bf16[128,1024]{1,0:T(8,128)(2,1)S(1)}, bf16[128,1024]{1,0:T(8,128)(2,1)S(1)}, u32[]{:S(2)}, u32[]{:S(2)}) %collective-permute-start) | collective-permute-done | bytes 262176 | tf_op jit(solution)/shard_map/ppermute | solution.py:18
  17.8 2.2 %copy-done.1 = bf16[1024,2048]{1,0:T(8,128)(2,1)S(1)} copy-done((bf16[1024,2048]{1,0:T(8,128)(2,1)S(1)}, bf16[1024,2048]{1,0:T(8,128)(2,1)}, u32[]{:S(2)}) %copy-start.1) | copy-done | bytes 4194328
  26.4 1.5 %shard_map.48.left_ref = bf16[1024,1024]{1,0:T(8,128)(2,1)S(1)} custom-call(s32[9]{0:T(128)S(1)} %stack.39.spot_ref, bf16[2,1024,256]{2,1,0:T(8,128)(2,1)S(1)} %bitcast.17, bf16[2,512,256]{2,1,0:T(8,128)(2,1)S(1)} %collective-permute-done.2.got_ref), custom_call_target="tpu_custom_call" | custom-call | bytes 3145728 | tf_op jit(solution)/shard_map/pallas_call | solution.py:155
  28.0 1.6 %collective-permute-done.1.arrived_ref = bf16[128,1024]{1,0:T(8,128)(2,1)S(1)} collective-permute-done((bf16[128,1024]{1,0:T(8,128)(2,1)S(1)}, bf16[128,1024]{1,0:T(8,128)(2,1)S(1)}, u32[]{:S(2)}, u32[]{:S(2)}) %collective-permute-start.1) | collective-permute-done | bytes 262176 | tf_op jit(solution)/shard_map/ppermute | solution.py:18
  29.5 2.2 %copy-done.2 = bf16[1024,2048]{1,0:T(8,128)(2,1)S(1)} copy-done((bf16[1024,2048]{1,0:T(8,128)(2,1)S(1)}, bf16[1024,2048]{1,0:T(8,128)(2,1)}, u32[]{:S(2)}) %copy-start.2) | copy-done | bytes 4194328
  33.1 2.2 %collective-permute-done.4.arrived_ref = bf16[128,1024]{1,0:T(8,128)(2,1)} collective-permute-done((bf16[128,1024]{1,0:T(8,128)(2,1)S(1)}, bf16[128,1024]{1,0:T(8,128)(2,1)}, u32[]{:S(2)}, u32[]{:S(2)}) %collective-permute-start.4) | collective-permute-done | bytes 262176 | tf_op jit(solution)/shard_map/ppermute | solution.py:18
  35.3 2.3 %shard_map.50 = bf16[128,1024]{1,0:T(8,128)(2,1)S(1)} custom-call(s32[1]{0:T(128)} %bitcast.level_ref, bf16[128,1024]{1,0:T(8,128)(2,1)} %collective-permute-done.4.arrived_ref, bf16[128,1024]{1,0:T(8,128)(2,1)S(1)} %get-tuple-element.18.ready_ref, bf16[1024,2048]{1,0:T(8,128)(2,1)S(1)} %copy-done.2, f32[1,1024]{1,0:T(1,128)S(1)} %bitcast.21), custom_call_target="tpu_custom_call" | custom-call | flops 536870912 | bytes 4980736 | tf_op jit(solution)/shard_map/pallas_call | solution.py:117
  37.9 3.7 %collective-permute-done.6.arrived_ref = bf16[128,1024]{1,0:T(8,128)(2,1)S(1)} collective-permute-done((bf16[128,1024]{1,0:T(8,128)(2,1)S(1)}, bf16[128,1024]{1,0:T(8,128)(2,1)S(1)}, u32[]{:S(2)}, u32[]{:S(2)}) %collective-permute-start.6) | collective-permute-done | bytes 262176 | tf_op jit(solution)/shard_map/ppermute | solution.py:18
  42.9 4.9 %collective-permute-done.5.arrived_ref = bf16[128,1024]{1,0:T(8,128)(2,1)S(1)} collective-permute-done((bf16[128,1024]{1,0:T(8,128)(2,1)S(1)}, bf16[128,1024]{1,0:T(8,128)(2,1)S(1)}, u32[]{:S(2)}, u32[]{:S(2)}) %collective-permute-start.5) | collective-permute-done | bytes 262176 | tf_op jit(solution)/shard_map/ppermute | solution.py:18
  49.3 1.6 %collective-permute-start.10 = (bf16[128,1024]{1,0:T(8,128)(2,1)S(1)}, bf16[128,1024]{1,0:T(8,128)(2,1)S(1)}, u32[]{:S(2)}, u32[]{:S(2)}) collective-permute-start(bf16[128,1024]{1,0:T(8,128)(2,1)S(1)} %shard_map.53.refs_1_), channel_id=1, source_target_pairs={{0,2},{1,3},{2,0},{3,1},{4,6},{5,7},{6,4},{7,5},{8,10},{9,11},{10,... | collective-permute-start | bytes 786440 | tf_op jit(solution)/shard_map/ppermute | solution.py:22
  51.3 2.1 %collective-permute-done.8.arrived_ref = bf16[128,1024]{1,0:T(8,128)(2,1)S(1)} collective-permute-done((bf16[128,1024]{1,0:T(8,128)(2,1)S(1)}, bf16[128,1024]{1,0:T(8,128)(2,1)S(1)}, u32[]{:S(2)}, u32[]{:S(2)}) %collective-permute-start.8) | collective-permute-done | bytes 262176 | tf_op jit(solution)/shard_map/ppermute | solution.py:18
  54.8 1.6 %collective-permute-start.12 = (bf16[128,1024]{1,0:T(8,128)(2,1)S(1)}, bf16[128,1024]{1,0:T(8,128)(2,1)S(1)}, u32[]{:S(2)}, u32[]{:S(2)}) collective-permute-start(bf16[128,1024]{1,0:T(8,128)(2,1)S(1)} %shard_map.55.refs_3_), channel_id=1, source_target_pairs={{0,2},{1,3},{2,0},{3,1},{4,6},{5,7},{6,4},{7,5},{8,10},{9,11},{10,... | collective-permute-start | bytes 786440 | tf_op jit(solution)/shard_map/ppermute | solution.py:22
  58.6 1.6 %collective-permute-start.11 = (bf16[128,1024]{1,0:T(8,128)(2,1)S(1)}, bf16[128,1024]{1,0:T(8,128)(2,1)S(1)}, u32[]{:S(2)}, u32[]{:S(2)}) collective-permute-start(bf16[128,1024]{1,0:T(8,128)(2,1)S(1)} %shard_map.54.refs_2_), channel_id=1, source_target_pairs={{0,2},{1,3},{2,0},{3,1},{4,6},{5,7},{6,4},{7,5},{8,10},{9,11},{10,... | collective-permute-start | bytes 786440 | tf_op jit(solution)/shard_map/ppermute | solution.py:22
  60.2 3.9 %collective-permute-done.9.refs_4_ = bf16[128,1024]{1,0:T(8,128)(2,1)S(1)} collective-permute-done((bf16[128,1024]{1,0:T(8,128)(2,1)S(1)}, bf16[128,1024]{1,0:T(8,128)(2,1)S(1)}, u32[]{:S(2)}, u32[]{:S(2)}) %collective-permute-start.9) | collective-permute-done | bytes 262176 | tf_op jit(solution)/shard_map/ppermute | solution.py:22
  64.2 1.8 %shard_map.56.early_ref = f32[1024,1024]{1,0:T(8,128)S(1)} custom-call(bf16[1024,1024]{1,0:T(8,128)(2,1)S(1)} %shard_map.48.left_ref, bf16[128,1024]{1,0:T(8,128)(2,1)S(1)} %shard_map.51.refs_0_, bf16[128,1024]{1,0:T(8,128)(2,1)S(1)} %shard_map.53.refs_1_, bf16[128,1024]{1,0:T(8,128)(2,1)S(1)} %shard_map.54.refs_2_, ...), custom_call_target="tpu_custom_call" | custom-call | flops 1610612736 | bytes 7864320 | tf_op jit(solution)/shard_map/pallas_call | solution.py:209
  66.0 2.1 %collective-permute-done.12.refs_1_ = bf16[128,1024]{1,0:T(8,128)(2,1)S(1)} collective-permute-done((bf16[128,1024]{1,0:T(8,128)(2,1)S(1)}, bf16[128,1024]{1,0:T(8,128)(2,1)S(1)}, u32[]{:S(2)}, u32[]{:S(2)}) %collective-permute-start.12) | collective-permute-done | bytes 262176 | tf_op jit(solution)/shard_map/ppermute | solution.py:22
  68.0 2.8 %collective-permute-done.11.refs_0_ = bf16[128,1024]{1,0:T(8,128)(2,1)S(1)} collective-permute-done((bf16[128,1024]{1,0:T(8,128)(2,1)S(1)}, bf16[128,1024]{1,0:T(8,128)(2,1)S(1)}, u32[]{:S(2)}, u32[]{:S(2)}) %collective-permute-start.11) | collective-permute-done | bytes 262176 | tf_op jit(solution)/shard_map/ppermute | solution.py:22
  71.7 2.6 %collective-permute-done.13.refs_1_ = bf16[2,2,128,1024]{3,2,1,0:T(8,128)(2,1)S(1)} collective-permute-done((bf16[2,2,128,1024]{3,2,1,0:T(8,128)(2,1)S(1)}, bf16[2,2,128,1024]{3,2,1,0:T(8,128)(2,1)S(1)}, u32[]{:S(2)}, u32[]{:S(2)}) %collective-permute-start.13) | collective-permute-done | bytes 1048608 | tf_op jit(solution)/shard_map/ppermute | solution.py:22
  74.5 2.6 %collective-permute-start.14 = (bf16[1,2,128,1024]{3,2,1,0:T(8,128)(2,1)S(1)}, bf16[1,2,128,1024]{3,2,1,0:T(8,128)(2,1)S(1)}, u32[]{:S(2)}, u32[]{:S(2)}) collective-permute-start(bf16[1,2,128,1024]{3,2,1,0:T(8,128)(2,1)S(1)} %add_convert_fusion), channel_id=1, source_target_pairs={{0,4},{1,5},{2,6},{3,7},{4,0},{5,1},{6,2},{7,3},{8,12},{9,13},{10,... | collective-permute-start | bytes 1572872 | tf_op jit(solution)/shard_map/ppermute | solution.py:18
  77.1 23.5 %collective-permute-done.14.refs_2_ = bf16[1,2,128,1024]{3,2,1,0:T(8,128)(2,1)S(1)} collective-permute-done((bf16[1,2,128,1024]{3,2,1,0:T(8,128)(2,1)S(1)}, bf16[1,2,128,1024]{3,2,1,0:T(8,128)(2,1)S(1)}, u32[]{:S(2)}, u32[]{:S(2)}) %collective-permute-start.14) | collective-permute-done | bytes 524320 | tf_op jit(solution)/shard_map/ppermute | solution.py:18
  (36 shorter events, 18.3 us)
Async XLA Ops:
  0.0 17.8 %copy-start.6 = (f32[1,1,1024]{2,1,0:T(1,128)S(1)}, f32[1,1,1024]{2,1,0:T(1,128)}, u32[]{:S(2)}) copy-start(f32[1,1,1024]{2,1,0:T(1,128)} %factor_ref.1) | copy-start | bytes 12292
  0.0 9.2 %copy-start.3 = (bf16[1,1,2,1024,256]{4,3,2,1,0:T(8,128)(2,1)S(1)}, bf16[1,1,2,1024,256]{4,3,2,1,0:T(8,128)(2,1)}, u32[]{:S(2)}) copy-start(bf16[1,1,2,1024,256]{4,3,2,1,0:T(8,128)(2,1)} %param.7) | copy-start | bytes 3145732
  5.8 1.9 %copy-start = (bf16[1024,2048]{1,0:T(8,128)(2,1)}, bf16[1024,2048]{1,0:T(8,128)(2,1)S(1)}, u32[]{:S(2)}) copy-start(bf16[1024,2048]{1,0:T(8,128)(2,1)S(1)} %get-tuple-element.16.joined_ref) | copy-start | bytes 12582916
  7.7 10.1 %collective-permute-start = (bf16[128,1024]{1,0:T(8,128)(2,1)S(1)}, bf16[128,1024]{1,0:T(8,128)(2,1)S(1)}, u32[]{:S(2)}, u32[]{:S(2)}) collective-permute-start(bf16[128,1024]{1,0:T(8,128)(2,1)S(1)} %get-tuple-element.14.ready_ref), channel_id=1, source_target_pairs={{0,8},{8,16},{16,24},{24,0},{1,9},{9,17},{17,25},{25,1},{2,10},{10... | collective-permute-start | bytes 786440 | tf_op jit(solution)/shard_map/ppermute | solution.py:18
  10.1 16.4 %collective-permute-start.2 = (bf16[2,512,256]{2,1,0:T(8,128)(2,1)}, bf16[2,512,256]{2,1,0:T(8,128)(2,1)S(1)}, u32[]{:S(2)}, u32[]{:S(2)}) collective-permute-start(bf16[2,512,256]{2,1,0:T(8,128)(2,1)} %bitcast.13), channel_id=1, source_target_pairs={{0,2},{1,3},{2,0},{3,1},{4,6},{5,7},{6,4},{7,5},{8,10},{9,11},{10,... | collective-permute-start | bytes 1572872 | tf_op jit(solution)/shard_map/ppermute | solution.py:22
  11.6 10.7 %collective-permute-start.3 = (bf16[128,1024]{1,0:T(8,128)(2,1)S(1)}, bf16[128,1024]{1,0:T(8,128)(2,1)S(1)}, u32[]{:S(2)}, u32[]{:S(2)}) collective-permute-start(bf16[128,1024]{1,0:T(8,128)(2,1)S(1)} %get-tuple-element.18.ready_ref), channel_id=1, source_target_pairs={{0,8},{8,16},{16,24},{24,0},{1,9},{9,17},{17,25},{25,1},{2,10},{10... | collective-permute-start | bytes 786440 | tf_op jit(solution)/shard_map/ppermute | solution.py:18
  17.8 2.2 %copy-start.1 = (bf16[1024,2048]{1,0:T(8,128)(2,1)S(1)}, bf16[1024,2048]{1,0:T(8,128)(2,1)}, u32[]{:S(2)}) copy-start(bf16[1024,2048]{1,0:T(8,128)(2,1)} %copy-done) | copy-start | bytes 12582916
  21.4 8.1 %collective-permute-start.1 = (bf16[128,1024]{1,0:T(8,128)(2,1)S(1)}, bf16[128,1024]{1,0:T(8,128)(2,1)S(1)}, u32[]{:S(2)}, u32[]{:S(2)}) collective-permute-start(bf16[128,1024]{1,0:T(8,128)(2,1)S(1)} %shard_map.47), channel_id=1, source_target_pairs={{0,8},{8,16},{16,24},{24,0},{1,9},{9,17},{17,25},{25,1},{2,10},{10... | collective-permute-start | bytes 786440 | tf_op jit(solution)/shard_map/ppermute | solution.py:18
  22.3 0.7 copy-start.4
  23.0 0.9 copy-start.5
  25.3 10.0 %collective-permute-start.4 = (bf16[128,1024]{1,0:T(8,128)(2,1)S(1)}, bf16[128,1024]{1,0:T(8,128)(2,1)}, u32[]{:S(2)}, u32[]{:S(2)}) collective-permute-start(bf16[128,1024]{1,0:T(8,128)(2,1)S(1)} %shard_map.49), channel_id=1, source_target_pairs={{0,8},{8,16},{16,24},{24,0},{1,9},{9,17},{17,25},{25,1},{2,10},{10... | collective-permute-start | bytes 786440 | tf_op jit(solution)/shard_map/ppermute | solution.py:18
  29.5 2.2 %copy-start.2 = (bf16[1024,2048]{1,0:T(8,128)(2,1)S(1)}, bf16[1024,2048]{1,0:T(8,128)(2,1)}, u32[]{:S(2)}) copy-start(bf16[1024,2048]{1,0:T(8,128)(2,1)} %copy-done) | copy-start | bytes 12582916
  33.1 8.5 %collective-permute-start.6 = (bf16[128,1024]{1,0:T(8,128)(2,1)S(1)}, bf16[128,1024]{1,0:T(8,128)(2,1)S(1)}, u32[]{:S(2)}, u32[]{:S(2)}) collective-permute-start(bf16[128,1024]{1,0:T(8,128)(2,1)S(1)} %shard_map.52), channel_id=1, source_target_pairs={{0,8},{8,16},{16,24},{24,0},{1,9},{9,17},{17,25},{25,1},{2,10},{10... | collective-permute-start | bytes 786440 | tf_op jit(solution)/shard_map/ppermute | solution.py:18
  37.6 10.2 %collective-permute-start.5 = (bf16[128,1024]{1,0:T(8,128)(2,1)S(1)}, bf16[128,1024]{1,0:T(8,128)(2,1)S(1)}, u32[]{:S(2)}, u32[]{:S(2)}) collective-permute-start(bf16[128,1024]{1,0:T(8,128)(2,1)S(1)} %shard_map.50), channel_id=1, source_target_pairs={{0,8},{8,16},{16,24},{24,0},{1,9},{9,17},{17,25},{25,1},{2,10},{10... | collective-permute-start | bytes 786440 | tf_op jit(solution)/shard_map/ppermute | solution.py:18
  42.9 10.6 %collective-permute-start.8 = (bf16[128,1024]{1,0:T(8,128)(2,1)S(1)}, bf16[128,1024]{1,0:T(8,128)(2,1)S(1)}, u32[]{:S(2)}, u32[]{:S(2)}) collective-permute-start(bf16[128,1024]{1,0:T(8,128)(2,1)S(1)} %shard_map.53.refs_1_), channel_id=1, source_target_pairs={{0,8},{8,16},{16,24},{24,0},{1,9},{9,17},{17,25},{25,1},{2,10},{10... | collective-permute-start | bytes 786440 | tf_op jit(solution)/shard_map/ppermute | solution.py:18
  49.2 8.1 %collective-permute-start.7 = (bf16[128,1024]{1,0:T(8,128)(2,1)S(1)}, bf16[128,1024]{1,0:T(8,128)(2,1)S(1)}, u32[]{:S(2)}, u32[]{:S(2)}) collective-permute-start(bf16[128,1024]{1,0:T(8,128)(2,1)S(1)} %shard_map.51.refs_0_), channel_id=1, source_target_pairs={{0,8},{8,16},{16,24},{24,0},{1,9},{9,17},{17,25},{25,1},{2,10},{10... | collective-permute-start | bytes 786440 | tf_op jit(solution)/shard_map/ppermute | solution.py:18
  49.3 11.0 %collective-permute-start.10 = (bf16[128,1024]{1,0:T(8,128)(2,1)S(1)}, bf16[128,1024]{1,0:T(8,128)(2,1)S(1)}, u32[]{:S(2)}, u32[]{:S(2)}) collective-permute-start(bf16[128,1024]{1,0:T(8,128)(2,1)S(1)} %shard_map.53.refs_1_), channel_id=1, source_target_pairs={{0,2},{1,3},{2,0},{3,1},{4,6},{5,7},{6,4},{7,5},{8,10},{9,11},{10,... | collective-permute-start | bytes 786440 | tf_op jit(solution)/shard_map/ppermute | solution.py:22
  50.9 13.3 %collective-permute-start.9 = (bf16[128,1024]{1,0:T(8,128)(2,1)S(1)}, bf16[128,1024]{1,0:T(8,128)(2,1)S(1)}, u32[]{:S(2)}, u32[]{:S(2)}) collective-permute-start(bf16[128,1024]{1,0:T(8,128)(2,1)S(1)} %shard_map.51.refs_0_), channel_id=1, source_target_pairs={{0,2},{1,3},{2,0},{3,1},{4,6},{5,7},{6,4},{7,5},{8,10},{9,11},{10,... | collective-permute-start | bytes 786440 | tf_op jit(solution)/shard_map/ppermute | solution.py:22
  54.8 13.2 %collective-permute-start.12 = (bf16[128,1024]{1,0:T(8,128)(2,1)S(1)}, bf16[128,1024]{1,0:T(8,128)(2,1)S(1)}, u32[]{:S(2)}, u32[]{:S(2)}) collective-permute-start(bf16[128,1024]{1,0:T(8,128)(2,1)S(1)} %shard_map.55.refs_3_), channel_id=1, source_target_pairs={{0,2},{1,3},{2,0},{3,1},{4,6},{5,7},{6,4},{7,5},{8,10},{9,11},{10,... | collective-permute-start | bytes 786440 | tf_op jit(solution)/shard_map/ppermute | solution.py:22
  58.6 12.2 %collective-permute-start.11 = (bf16[128,1024]{1,0:T(8,128)(2,1)S(1)}, bf16[128,1024]{1,0:T(8,128)(2,1)S(1)}, u32[]{:S(2)}, u32[]{:S(2)}) collective-permute-start(bf16[128,1024]{1,0:T(8,128)(2,1)S(1)} %shard_map.54.refs_2_), channel_id=1, source_target_pairs={{0,2},{1,3},{2,0},{3,1},{4,6},{5,7},{6,4},{7,5},{8,10},{9,11},{10,... | collective-permute-start | bytes 786440 | tf_op jit(solution)/shard_map/ppermute | solution.py:22
  71.6 2.7 %collective-permute-start.13 = (bf16[2,2,128,1024]{3,2,1,0:T(8,128)(2,1)S(1)}, bf16[2,2,128,1024]{3,2,1,0:T(8,128)(2,1)S(1)}, u32[]{:S(2)}, u32[]{:S(2)}) collective-permute-start(bf16[2,2,128,1024]{3,2,1,0:T(8,128)(2,1)S(1)} %get-tuple-element.22), channel_id=1, source_target_pairs={{0,1},{1,0},{2,3},{3,2},{4,5},{5,4},{6,7},{7,6},{8,9},{9,8},{10,11... | collective-permute-start | bytes 3145736 | tf_op jit(solution)/shard_map/ppermute | solution.py:22
  74.5 26.2 %collective-permute-start.14 = (bf16[1,2,128,1024]{3,2,1,0:T(8,128)(2,1)S(1)}, bf16[1,2,128,1024]{3,2,1,0:T(8,128)(2,1)S(1)}, u32[]{:S(2)}, u32[]{:S(2)}) collective-permute-start(bf16[1,2,128,1024]{3,2,1,0:T(8,128)(2,1)S(1)} %add_convert_fusion), channel_id=1, source_target_pairs={{0,4},{1,5},{2,6},{3,7},{4,0},{5,1},{6,2},{7,3},{8,12},{9,13},{10,... | collective-permute-start | bytes 1572872 | tf_op jit(solution)/shard_map/ppermute | solution.py:18

commit v7 on v6

--- a/solution.py
+++ b/solution.py
@@ -22,11 +22,20 @@
     return lax.ppermute(block, axis, [(i, i ^ bit) for i in range(lax.axis_size(axis))])
 
 
-def first_kernel(part, source_ref, weight_ref, factor_ref, *refs):
-    *outs, joined_ref, source, factor, right, sem, sems = refs
+def places(ids_ref):
+    mine = ids_ref[1]
+    return lax.div(mine, 4), lax.rem(lax.div(mine, 2), 2), lax.rem(mine, 2)
+
+
+def first_kernel(part, ids_ref, source_ref, weight_ref, factor_ref, upward_ref, *refs):
+    *outs, joined_ref, asked_ref, source, factor, sem, sems, asked_sems = refs
     width = joined_ref.shape[0]
+    shots = source.shape[2]
     blocks = sems.shape[0]
     wide = width // blocks
+    groups = asked_sems.shape[0]
+    tall = asked_ref.shape[1] // groups
+    _, place, _ = places(ids_ref)
 
     def copies(n):
         rows = pl.ds(n * wide, wide)
@@ -41,64 +50,80 @@
         pltpu.make_async_copy(source_ref.at[0], source, sem.at[0]),
         pltpu.make_async_copy(factor_ref.at[0], factor, sem.at[1]),
     ]
+    asked = []
+    for k in range(groups):
+        row = pl.multiple_of((2 * k + 1 - place) * tall, tall)
+        asked.append(
+            pltpu.make_async_copy(
+                upward_ref.at[0, 0, :, pl.ds(row, tall)], asked_ref.at[:, pl.ds(k * tall, tall)], asked_sems.at[k]
+            )
+        )
+    for copy in begin + copies(0):
+        copy.start()
     for copy in begin:
-        copy.start()
-    for n in range(blocks):
+        copy.wait()
+    for n in range(1, blocks):
         for copy in copies(n):
             copy.start()
-    for copy in begin:
-        copy.wait()
-    shots = source.shape[2]
-    for half, (re, im) in enumerate(((source[0], source[1]), (-source[1], source[0]))):
-        right[half * width : (half + 1) * width, :shots] = re
-        right[half * width : (half + 1) * width, shots:] = im
+    for copy in asked:
+        copy.start()
+    dot = functools.partial(jnp.dot, preferred_element_type=jnp.float32)
     for n in range(blocks):
         for copy in copies(n):
             copy.wait()
         columns = slice(n * wide, (n + 1) * wide)
-        out = jnp.dot(joined_ref[columns], right[...], preferred_element_type=jnp.float32)
-        out = (out.T * factor[:, columns]).astype(jnp.bfloat16)
+        real, imag = joined_ref[columns, :width], joined_ref[columns, width:]
+        out_real = dot(real, source[0]) - dot(imag, source[1])
+        out_imag = dot(real, source[1]) + dot(imag, source[0])
+        out_real = (out_real.T * factor[:, columns]).astype(jnp.bfloat16)
+        out_imag = (out_imag.T * factor[:, columns]).astype(jnp.bfloat16)
         for chunk in range(len(outs)):
             lo = chunk * part
-            outs[chunk][:part, columns] = out[lo : lo + part]
-            outs[chunk][part:, columns] = out[shots + lo : shots + lo + part]
-
-
-def first_advance(source, propagator, transmission, part):
+            outs[chunk][:part, columns] = out_real[lo : lo + part]
+            outs[chunk][part:, columns] = out_imag[lo : lo + part]
+    for copy in asked:
+        copy.wait()
+
+
+def first_advance(ids, source, propagator, transmission, upgoing, part, groups):
     width = propagator.shape[3]
     shots = source.shape[3]
     chunks = shots // part
     whole = pl.BlockSpec(memory_space=pltpu.VMEM)
+    pinned = [pltpu.with_memory_space_constraint(x, pltpu.HBM) for x in (source, propagator, transmission, upgoing)]
     return pl.pallas_call(
         functools.partial(first_kernel, part),
-        in_specs=[pl.BlockSpec(memory_space=pltpu.HBM)] * 3,
-        out_specs=[whole] * (chunks + 1),
+        in_specs=[pl.BlockSpec(memory_space=pltpu.SMEM)] + [pl.BlockSpec(memory_space=pltpu.HBM)] * 4,
+        out_specs=[whole] * (chunks + 2),
         out_shape=[jax.ShapeDtypeStruct((2 * part, width), jnp.bfloat16)] * chunks
-        + [pltpu.VMEM((width, 2 * width), jnp.bfloat16)],
+        + [
+            pltpu.VMEM((width, 2 * width), jnp.bfloat16),
+            jax.ShapeDtypeStruct((2, width // 2, shots), jnp.bfloat16),
+        ],
         scratch_shapes=[
             pltpu.VMEM((2, width, shots), jnp.bfloat16),
             pltpu.VMEM((1, width), jnp.float32),
-            pltpu.VMEM((2 * width, 2 * shots), jnp.bfloat16),
             pltpu.SemaphoreType.DMA((2,)),
             pltpu.SemaphoreType.DMA((4, 2)),
+            pltpu.SemaphoreType.DMA((groups,)),
         ],
         compiler_params=pltpu.CompilerParams(vmem_limit_bytes=LIMIT),
         cost_estimate=pl.CostEstimate(
             flops=8 * width * width * shots, bytes_accessed=4 * width * (width + 2 * shots), transcendentals=0
         ),
-    )(*(pltpu.with_memory_space_constraint(x, pltpu.HBM) for x in (source, propagator, transmission)))
-
-
-def advance_kernel(level_ref, arrived_ref, ready_ref, joined_ref, factor_ref, out_ref, both):
+    )(ids, *pinned)
+
+
+def advance_kernel(ids_ref, arrived_ref, ready_ref, joined_ref, factor_ref, out_ref, both):
     part = arrived_ref.shape[0] // 2
     width = arrived_ref.shape[1]
     wide = width // 4
 
-    @pl.when(level_ref[0] == 0)
+    @pl.when(ids_ref[0] == 0)
     def _():
         out_ref[...] = ready_ref[...]
 
-    @pl.when(level_ref[0] != 0)
+    @pl.when(ids_ref[0] != 0)
     def _():
         both[:, :width] = arrived_ref[...]
         both[:part, width:] = -arrived_ref[part:]
@@ -111,7 +136,7 @@
             out_ref[:, columns] = (out.T * factor_ref[:, columns]).astype(jnp.bfloat16)
 
 
-def advance(level, arrived, ready, joined, factor):
+def advance(ids, arrived, ready, joined, factor):
     rows, width = arrived.shape
     whole = pl.BlockSpec(memory_space=pltpu.VMEM)
     return pl.pallas_call(
@@ -124,16 +149,17 @@
         cost_estimate=pl.CostEstimate(
             flops=4 * rows * width * width, bytes_accessed=4 * width * width + 6 * rows * width, transcendentals=0
         ),
-    )(level, arrived, ready, pltpu.with_memory_space_constraint(joined, pltpu.VMEM), factor)
-
-
-def operand_kernel(part, step, spot_ref, own_ref, got_ref, out_ref):
+    )(ids, arrived, ready, pltpu.with_memory_space_constraint(joined, pltpu.VMEM), factor)
+
+
+def operand_kernel(part, levels, ids_ref, own_ref, got_ref, out_ref):
     rows = own_ref.shape[1]
     shots = own_ref.shape[2]
     chunks = shots // part
-    for first in range(0, chunks, step):
-
-        @pl.when(spot_ref[0] == first)
+    turn = lax.rem(DELAY * (levels - 1 - ids_ref[0]), chunks)
+    for first in range(0, chunks, math.gcd(DELAY, chunks)):
+
+        @pl.when(turn == first)
         def _():
             for which, ref in enumerate((own_ref, got_ref)):
                 real, imag = ref[0], ref[1]
@@ -149,24 +175,32 @@
                     )
 
 
-def operand(spots, own, got, rows, part, step):
+def operand(ids, own, got, rows, part, levels):
     shots = own.shape[2]
     blocks = got.shape[1] // rows
-    return pl.pallas_call(
-        functools.partial(operand_kernel, part, step),
+    groups = blocks // 2
+
+    def spot(i, ids_ref, stride):
+        group, place, core = places(ids_ref)
+        other = lax.rem(lax.div(i, groups) + core, 2)
+        block = stride * lax.rem(group + lax.rem(i, groups), groups) + other
+        return block + 2 * place if stride == 4 else block
+
+    return pl.pallas_call(
+        functools.partial(operand_kernel, part, levels),
         grid_spec=pltpu.PrefetchScalarGridSpec(
             num_scalar_prefetch=1,
             grid=(blocks,),
             in_specs=[
-                pl.BlockSpec((2, rows, shots), lambda i, spot: (0, spot[1 + i], 0)),
-                pl.BlockSpec((2, rows, shots), lambda i, spot: (0, spot[1 + blocks + i], 0)),
+                pl.BlockSpec((2, rows, shots), lambda i, ids_ref: (0, spot(i, ids_ref, 4), 0)),
+                pl.BlockSpec((2, rows, shots), lambda i, ids_ref: (0, spot(i, ids_ref, 2), 0)),
             ],
-            out_specs=pl.BlockSpec((2 * rows, 4 * shots), lambda i, spot: (i, 0)),
+            out_specs=pl.BlockSpec((2 * rows, 4 * shots), lambda i, ids_ref: (i, 0)),
         ),
         out_shape=jax.ShapeDtypeStruct((2 * rows * blocks, 4 * shots), jnp.bfloat16),
         compiler_params=pltpu.CompilerParams(vmem_limit_bytes=LIMIT),
         cost_estimate=pl.CostEstimate(flops=0, bytes_accessed=24 * rows * blocks * shots, transcendentals=0),
-    )(spots, own, got)
+    )(ids, own, got)
 
 
 def gathered(panels, columns):
@@ -259,26 +293,15 @@
     upward = upgoing[0, 0]
     width = propagator.shape[3]
     shots = source.shape[3]
-    level = lax.axis_index("depth")
     levels = lax.axis_size("depth")
-    level_at = level.astype(jnp.int32).reshape(1)
     freqs = lax.axis_size("freq")
-    mine = lax.axis_index("freq")
     groups = freqs // 4
-    group, place, core = mine // 4, (mine // 2) % 2, mine % 2
     rows = width // freqs
     part = shots // CHUNKS
-    *ready, joined = first_advance(source, propagator, transmission, part)
-    by_place = upward.reshape(2, groups, 2, 2 * rows, shots)
-    asked = lax.dynamic_index_in_dim(by_place, 1 - place, 2, keepdims=False).reshape(2, 2 * groups * rows, shots)
+    ids = jnp.stack([lax.axis_index("depth"), lax.axis_index("freq")]).astype(jnp.int32)
+    *ready, joined, asked = first_advance(ids, source, propagator, transmission, upgoing, part, groups)
     got = swapped(asked, "freq", 2)
-    order = [(s, k) for s in range(2) for k in range(groups)]
-    spots = (
-        [lax.rem(DELAY * (levels - 1 - level), CHUNKS)]
-        + [4 * lax.rem(group + k, groups) + 2 * place + (core ^ s) for s, k in order]
-        + [2 * lax.rem(group + k, groups) + (core ^ s) for s, k in order]
-    )
-    left = operand(jnp.stack(spots).astype(jnp.int32), upward, got, rows, part, math.gcd(DELAY, CHUNKS))
+    left = operand(ids, upward, got, rows, part, levels)
 
     ticks = CHUNKS + DELAY * (levels - 1)
     flying = []
@@ -290,7 +313,7 @@
             arrived = flying[tick - DELAY]
             if tick == ticks // 2:
                 arrived, left = lax.optimization_barrier((arrived, left))
-            out = advance(level_at, arrived, out, joined, factor)
+            out = advance(ids, arrived, out, joined, factor)
         if tick + DELAY < ticks:
             flying.append(ring(out, "depth", 1))
         if tick >= ticks - CHUNKS:

time: 103 us -> 102 us (level)
  local copies, waits for them, and re-layouts: 8.88 us -> 0.01 us
  waiting for transfers between devices: 56.2 us -> 60 us
  Pallas kernels: 22.9 us -> 26.5 us
    unnamed x14 -> x4, local copies, waits for them, and re-layouts: 7.97 us -> 0.01 us
    pallas_call x8, Pallas kernels: 11.7 us -> 15.2 us  [advance(): pl.pallas_call(advance_kernel, in_specs=[pl.BlockSpec(memory_space=pltpu....]
    ppermute x9, waiting for transfers between devices: 44.7 us -> 48 us  [ring(): lax.ppermute(block, axis, [(i, (i + distance) % size) for i in range(size)])]
  transfers between devices with their start and end apart: 15 -> 15, of which waited for: 13 -> 12; matrix products, arithmetic and copies ran while one was open for 1% -> 0% of each run, Pallas kernels for 15% -> 19%
where the time goes in v7:
time: 102 us; the launch traced here: 100 us
  waiting for transfers between devices  60 us (59%)
  Pallas kernels  26.5 us (26%)
  starting transfers between devices  13.2 us (13%)
    ppermute x9, waiting for transfers between devices, ring(): lax.ppermute(block, axis, [(i, (i + distance) % size) for i in range(size)])  48 us
    pallas_call x8, Pallas kernels, advance(): pl.pallas_call(advance_kernel, in_specs=[pl.BlockSpec(memory_space=pltpu....  15.2 us
    ppermute x6, waiting for transfers between devices, swapped(): lax.ppermute(block, axis, [(i, i ^ bit) for i in range(lax.axis_size(axis...  12 us
    ppermute x6, starting transfers between devices, swapped(): lax.ppermute(block, axis, [(i, i ^ bit) for i in range(lax.axis_size(axis...  6.8 us
    ppermute x9, starting transfers between devices, ring(): lax.ppermute(block, axis, [(i, (i + distance) % size) for i in range(size)])  6.38 us
    pallas_call x1, Pallas kernels, first_advance(): pl.pallas_call(functools.partial(first_kernel, part), in_specs=[pl.BlockS...  5.8 us
    pallas_call x2, Pallas kernels, whole_call(): pl.pallas_call(kernel, in_specs=[whole] * len(args), out_specs=[whole] *...  2.5 us
  transfers between devices with their start and end apart: 15, of which 12 were waited for; matrix products, arithmetic and copies ran while one was open for 0% of the time, Pallas kernels for 19%

profile of v7, /device:TPU:4, one launch (start us, length us, event | category | flops | bytes accessed | tf_op | source)
XLA Modules:
  0.0 100.1 jit_solution(51889328226798769)
XLA Ops:
  0.1 5.8 %shard_map.46 = (bf16[128,1024]{1,0:T(8,128)(2,1)S(1)}, bf16[128,1024]{1,0:T(8,128)(2,1)S(1)}, bf16[128,1024]{1,0:T(8,128)(2,1)S(1)}, bf16[128,1024]{1,0:T(8,128...) custom-call(s32[2]{0:T(128)S(1)} %pad_add_fusion.ids_ref, ...), custom_call_target="tpu_custom_call" | custom-call | flops 2147483648 | bytes 6291456 | tf_op jit(solution)/shard_map/pallas_call | solution.py:94
  7.5 2.0 %collective-permute-start.2 = (bf16[2,512,256]{2,1,0:T(8,128)(2,1)S(1)}, bf16[2,512,256]{2,1,0:T(8,128)(2,1)S(1)}, u32[]{:S(2)}, u32[]{:S(2)}) collective-permute-start(bf16[2,512,256]{2,1,0:T(8,128)(2,1)S(1)} %get-tuple-element.18), channel_id=1, source_target_pairs={{0,2},{1,3},{2,0},{3,1},{4,6},{5,7},{6,4},{7,5},{8,10},{9,11},{10,... | collective-permute-start | bytes 1572872 | tf_op jit(solution)/shard_map/ppermute | solution.py:22
  9.5 6.5 %collective-permute-done.3.arrived_ref = bf16[128,1024]{1,0:T(8,128)(2,1)S(1)} collective-permute-done((bf16[128,1024]{1,0:T(8,128)(2,1)S(1)}, bf16[128,1024]{1,0:T(8,128)(2,1)S(1)}, u32[]{:S(2)}, u32[]{:S(2)}) %collective-permute-start.3) | collective-permute-done | bytes 262176 | tf_op jit(solution)/shard_map/ppermute | solution.py:18
  16.0 1.9 %shard_map.49 = bf16[128,1024]{1,0:T(8,128)(2,1)S(1)} custom-call(s32[2]{0:T(128)S(1)} %pad_add_fusion.ids_ref, bf16[128,1024]{1,0:T(8,128)(2,1)S(1)} %collective-permute-done.3.arrived_ref, bf16[128,1024]{1,0:T(8,128)(2,1)S(1)} %get-tuple-element.21.ready_ref, bf16[1024,2048]{1,0:T(8,128)(2,1)S(1)} %get-tuple-element.17.joined_ref, f32[1,1024]{1,0:T(1,128)S(1)} %bitcast.5), custom_call_target="tpu_custom_call" | custom-call | flops 536870912 | bytes 4980736 | tf_op jit(solution)/shard_map/pallas_call | solution.py:142
  18.6 3.1 %collective-permute-done.arrived_ref = bf16[128,1024]{1,0:T(8,128)(2,1)S(1)} collective-permute-done((bf16[128,1024]{1,0:T(8,128)(2,1)S(1)}, bf16[128,1024]{1,0:T(8,128)(2,1)S(1)}, u32[]{:S(2)}, u32[]{:S(2)}) %collective-permute-start) | collective-permute-done | bytes 262176 | tf_op jit(solution)/shard_map/ppermute | solution.py:18
  21.7 1.9 %shard_map.47 = bf16[128,1024]{1,0:T(8,128)(2,1)S(1)} custom-call(s32[2]{0:T(128)S(1)} %pad_add_fusion.ids_ref, bf16[128,1024]{1,0:T(8,128)(2,1)S(1)} %collective-permute-done.arrived_ref, bf16[128,1024]{1,0:T(8,128)(2,1)S(1)} %get-tuple-element.16.ready_ref, bf16[1024,2048]{1,0:T(8,128)(2,1)S(1)} %get-tuple-element.17.joined_ref, f32[1,1024]{1,0:T(1,128)S(1)} %bitcast.6), custom_call_target="tpu_custom_call" | custom-call | flops 536870912 | bytes 4980736 | tf_op jit(solution)/shard_map/pallas_call | solution.py:142
  24.2 3.1 %collective-permute-done.4.arrived_ref = bf16[128,1024]{1,0:T(8,128)(2,1)S(1)} collective-permute-done((bf16[128,1024]{1,0:T(8,128)(2,1)S(1)}, bf16[128,1024]{1,0:T(8,128)(2,1)S(1)}, u32[]{:S(2)}, u32[]{:S(2)}) %collective-permute-start.4) | collective-permute-done | bytes 262176 | tf_op jit(solution)/shard_map/ppermute | solution.py:18
  27.3 1.9 %shard_map.50 = bf16[128,1024]{1,0:T(8,128)(2,1)S(1)} custom-call(s32[2]{0:T(128)S(1)} %pad_add_fusion.ids_ref, bf16[128,1024]{1,0:T(8,128)(2,1)S(1)} %collective-permute-done.4.arrived_ref, bf16[128,1024]{1,0:T(8,128)(2,1)S(1)} %get-tuple-element.20.ready_ref, bf16[1024,2048]{1,0:T(8,128)(2,1)S(1)} %get-tuple-element.17.joined_ref, f32[1,1024]{1,0:T(1,128)S(1)} %bitcast.7), custom_call_target="tpu_custom_call" | custom-call | flops 536870912 | bytes 4980736 | tf_op jit(solution)/shard_map/pallas_call | solution.py:142
  31.5 2.2 %collective-permute-done.1.arrived_ref = bf16[128,1024]{1,0:T(8,128)(2,1)S(1)} collective-permute-done((bf16[128,1024]{1,0:T(8,128)(2,1)S(1)}, bf16[128,1024]{1,0:T(8,128)(2,1)S(1)}, u32[]{:S(2)}, u32[]{:S(2)}) %collective-permute-start.1) | collective-permute-done | bytes 262176 | tf_op jit(solution)/shard_map/ppermute | solution.py:18
  33.8 1.9 %shard_map.52 = bf16[128,1024]{1,0:T(8,128)(2,1)S(1)} custom-call(s32[2]{0:T(128)S(1)} %pad_add_fusion.ids_ref, bf16[128,1024]{1,0:T(8,128)(2,1)S(1)} %collective-permute-done.1.arrived_ref, bf16[128,1024]{1,0:T(8,128)(2,1)S(1)} %get-tuple-element.15.ready_ref, bf16[1024,2048]{1,0:T(8,128)(2,1)S(1)} %get-tuple-element.17.joined_ref, f32[1,1024]{1,0:T(1,128)S(1)} %bitcast.8), custom_call_target="tpu_custom_call" | custom-call | flops 536870912 | bytes 4980736 | tf_op jit(solution)/shard_map/pallas_call | solution.py:142
  35.7 3.6 %collective-permute-done.5.arrived_ref = bf16[128,1024]{1,0:T(8,128)(2,1)S(1)} collective-permute-done((bf16[128,1024]{1,0:T(8,128)(2,1)S(1)}, bf16[128,1024]{1,0:T(8,128)(2,1)S(1)}, u32[]{:S(2)}, u32[]{:S(2)}) %collective-permute-start.5) | collective-permute-done | bytes 262176 | tf_op jit(solution)/shard_map/ppermute | solution.py:18
  39.4 1.9 %shard_map.51.refs_0_ = bf16[128,1024]{1,0:T(8,128)(2,1)S(1)} custom-call(s32[2]{0:T(128)S(1)} %pad_add_fusion.ids_ref, bf16[128,1024]{1,0:T(8,128)(2,1)S(1)} %collective-permute-done.5.arrived_ref, bf16[128,1024]{1,0:T(8,128)(2,1)S(1)} %get-tuple-element.21.ready_ref, bf16[1024,2048]{1,0:T(8,128)(2,1)S(1)} %get-tuple-element.17.joined_ref, ...), custom_call_target="tpu_custom_call" | custom-call | flops 536870912 | bytes 4980736 | tf_op jit(solution)/shard_map/pallas_call | solution.py:142
  41.3 3.8 %collective-permute-done.6.arrived_ref = bf16[128,1024]{1,0:T(8,128)(2,1)S(1)} collective-permute-done((bf16[128,1024]{1,0:T(8,128)(2,1)S(1)}, bf16[128,1024]{1,0:T(8,128)(2,1)S(1)}, u32[]{:S(2)}, u32[]{:S(2)}) %collective-permute-start.6) | collective-permute-done | bytes 262176 | tf_op jit(solution)/shard_map/ppermute | solution.py:18
  45.1 1.9 %shard_map.53.refs_1_ = bf16[128,1024]{1,0:T(8,128)(2,1)S(1)} custom-call(s32[2]{0:T(128)S(1)} %pad_add_fusion.ids_ref, bf16[128,1024]{1,0:T(8,128)(2,1)S(1)} %collective-permute-done.6.arrived_ref, bf16[128,1024]{1,0:T(8,128)(2,1)S(1)} %get-tuple-element.16.ready_ref, bf16[1024,2048]{1,0:T(8,128)(2,1)S(1)} %get-tuple-element.17.joined_ref, ...), custom_call_target="tpu_custom_call" | custom-call | flops 536870912 | bytes 4980736 | tf_op jit(solution)/shard_map/pallas_call | solution.py:142
  49.2 2.2 %collective-permute-done.7.arrived_ref = bf16[128,1024]{1,0:T(8,128)(2,1)S(1)} collective-permute-done((bf16[128,1024]{1,0:T(8,128)(2,1)S(1)}, bf16[128,1024]{1,0:T(8,128)(2,1)S(1)}, u32[]{:S(2)}, u32[]{:S(2)}) %collective-permute-start.7) | collective-permute-done | bytes 262176 | tf_op jit(solution)/shard_map/ppermute | solution.py:18
  51.4 1.9 %shard_map.54.refs_2_ = bf16[128,1024]{1,0:T(8,128)(2,1)S(1)} custom-call(s32[2]{0:T(128)S(1)} %pad_add_fusion.ids_ref, bf16[128,1024]{1,0:T(8,128)(2,1)S(1)} %collective-permute-done.7.arrived_ref, bf16[128,1024]{1,0:T(8,128)(2,1)S(1)} %get-tuple-element.20.ready_ref, bf16[1024,2048]{1,0:T(8,128)(2,1)S(1)} %get-tuple-element.17.joined_ref, ...), custom_call_target="tpu_custom_call" | custom-call | flops 536870912 | bytes 4980736 | tf_op jit(solution)/shard_map/pallas_call | solution.py:142
  55.0 1.9 %shard_map.55.refs_3_ = bf16[128,1024]{1,0:T(8,128)(2,1)S(1)} custom-call(s32[2]{0:T(128)S(1)} %pad_add_fusion.ids_ref, bf16[128,1024]{1,0:T(8,128)(2,1)S(1)} %collective-permute-done.8.arrived_ref, bf16[128,1024]{1,0:T(8,128)(2,1)S(1)} %get-tuple-element.15.ready_ref, bf16[1024,2048]{1,0:T(8,128)(2,1)S(1)} %get-tuple-element.17.joined_ref, ...), custom_call_target="tpu_custom_call" | custom-call | flops 536870912 | bytes 4980736 | tf_op jit(solution)/shard_map/pallas_call | solution.py:142
  57.9 4.1 %collective-permute-done.10.refs_5_ = bf16[128,1024]{1,0:T(8,128)(2,1)S(1)} collective-permute-done((bf16[128,1024]{1,0:T(8,128)(2,1)S(1)}, bf16[128,1024]{1,0:T(8,128)(2,1)S(1)}, u32[]{:S(2)}, u32[]{:S(2)}) %collective-permute-start.10) | collective-permute-done | bytes 262176 | tf_op jit(solution)/shard_map/ppermute | solution.py:22
  62.0 1.8 %shard_map.56.early_ref = f32[1024,1024]{1,0:T(8,128)S(1)} custom-call(bf16[1024,1024]{1,0:T(8,128)(2,1)S(1)} %shard_map.48.left_ref, bf16[128,1024]{1,0:T(8,128)(2,1)S(1)} %shard_map.51.refs_0_, bf16[128,1024]{1,0:T(8,128)(2,1)S(1)} %shard_map.53.refs_1_, bf16[128,1024]{1,0:T(8,128)(2,1)S(1)} %shard_map.54.refs_2_, ...), custom_call_target="tpu_custom_call" | custom-call | flops 1610612736 | bytes 7864320 | tf_op jit(solution)/shard_map/pallas_call | solution.py:243
  63.8 2.4 %collective-permute-done.11.refs_0_ = bf16[128,1024]{1,0:T(8,128)(2,1)S(1)} collective-permute-done((bf16[128,1024]{1,0:T(8,128)(2,1)S(1)}, bf16[128,1024]{1,0:T(8,128)(2,1)S(1)}, u32[]{:S(2)}, u32[]{:S(2)}) %collective-permute-start.11) | collective-permute-done | bytes 262176 | tf_op jit(solution)/shard_map/ppermute | solution.py:22
  66.2 2.8 %collective-permute-done.12.refs_1_ = bf16[128,1024]{1,0:T(8,128)(2,1)S(1)} collective-permute-done((bf16[128,1024]{1,0:T(8,128)(2,1)S(1)}, bf16[128,1024]{1,0:T(8,128)(2,1)S(1)}, u32[]{:S(2)}, u32[]{:S(2)}) %collective-permute-start.12) | collective-permute-done | bytes 262176 | tf_op jit(solution)/shard_map/ppermute | solution.py:22
  69.8 2.6 %collective-permute-done.13.refs_1_ = bf16[2,2,128,1024]{3,2,1,0:T(8,128)(2,1)S(1)} collective-permute-done((bf16[2,2,128,1024]{3,2,1,0:T(8,128)(2,1)S(1)}, bf16[2,2,128,1024]{3,2,1,0:T(8,128)(2,1)S(1)}, u32[]{:S(2)}, u32[]{:S(2)}) %collective-permute-start.13) | collective-permute-done | bytes 1048608 | tf_op jit(solution)/shard_map/ppermute | solution.py:22
  72.6 2.7 %collective-permute-start.14 = (bf16[1,2,128,1024]{3,2,1,0:T(8,128)(2,1)S(1)}, bf16[1,2,128,1024]{3,2,1,0:T(8,128)(2,1)S(1)}, u32[]{:S(2)}, u32[]{:S(2)}) collective-permute-start(bf16[1,2,128,1024]{3,2,1,0:T(8,128)(2,1)S(1)} %add_convert_fusion), channel_id=1, source_target_pairs={{0,4},{1,5},{2,6},{3,7},{4,0},{5,1},{6,2},{7,3},{8,12},{9,13},{10,... | collective-permute-start | bytes 1572872 | tf_op jit(solution)/shard_map/ppermute | solution.py:18
  75.3 23.5 %collective-permute-done.14.refs_2_ = bf16[1,2,128,1024]{3,2,1,0:T(8,128)(2,1)S(1)} collective-permute-done((bf16[1,2,128,1024]{3,2,1,0:T(8,128)(2,1)S(1)}, bf16[1,2,128,1024]{3,2,1,0:T(8,128)(2,1)S(1)}, u32[]{:S(2)}, u32[]{:S(2)}) %collective-permute-start.14) | collective-permute-done | bytes 524320 | tf_op jit(solution)/shard_map/ppermute | solution.py:18
  (25 shorter events, 12.5 us)
Async XLA Ops:
  0.0 16.0 %copy-start.1 = (f32[1,1,1024]{2,1,0:T(1,128)S(1)}, f32[1,1,1024]{2,1,0:T(1,128)}, u32[]{:S(2)}) copy-start(f32[1,1,1024]{2,1,0:T(1,128)} %factor_ref.1) | copy-start | bytes 12292
  5.9 10.1 %collective-permute-start.3 = (bf16[128,1024]{1,0:T(8,128)(2,1)S(1)}, bf16[128,1024]{1,0:T(8,128)(2,1)S(1)}, u32[]{:S(2)}, u32[]{:S(2)}) collective-permute-start(bf16[128,1024]{1,0:T(8,128)(2,1)S(1)} %get-tuple-element.20.ready_ref), channel_id=1, source_target_pairs={{0,8},{8,16},{16,24},{24,0},{1,9},{9,17},{17,25},{25,1},{2,10},{10... | collective-permute-start | bytes 786440 | tf_op jit(solution)/shard_map/ppermute | solution.py:18
  7.4 14.2 %collective-permute-start = (bf16[128,1024]{1,0:T(8,128)(2,1)S(1)}, bf16[128,1024]{1,0:T(8,128)(2,1)S(1)}, u32[]{:S(2)}, u32[]{:S(2)}) collective-permute-start(bf16[128,1024]{1,0:T(8,128)(2,1)S(1)} %get-tuple-element.15.ready_ref), channel_id=1, source_target_pairs={{0,8},{8,16},{16,24},{24,0},{1,9},{9,17},{17,25},{25,1},{2,10},{10... | collective-permute-start | bytes 786440 | tf_op jit(solution)/shard_map/ppermute | solution.py:18
  7.5 22.3 %collective-permute-start.2 = (bf16[2,512,256]{2,1,0:T(8,128)(2,1)S(1)}, bf16[2,512,256]{2,1,0:T(8,128)(2,1)S(1)}, u32[]{:S(2)}, u32[]{:S(2)}) collective-permute-start(bf16[2,512,256]{2,1,0:T(8,128)(2,1)S(1)} %get-tuple-element.18), channel_id=1, source_target_pairs={{0,2},{1,3},{2,0},{3,1},{4,6},{5,7},{6,4},{7,5},{8,10},{9,11},{10,... | collective-permute-start | bytes 1572872 | tf_op jit(solution)/shard_map/ppermute | solution.py:22
  17.9 9.3 %collective-permute-start.4 = (bf16[128,1024]{1,0:T(8,128)(2,1)S(1)}, bf16[128,1024]{1,0:T(8,128)(2,1)S(1)}, u32[]{:S(2)}, u32[]{:S(2)}) collective-permute-start(bf16[128,1024]{1,0:T(8,128)(2,1)S(1)} %shard_map.49), channel_id=1, source_target_pairs={{0,8},{8,16},{16,24},{24,0},{1,9},{9,17},{17,25},{25,1},{2,10},{10... | collective-permute-start | bytes 786440 | tf_op jit(solution)/shard_map/ppermute | solution.py:18
  21.7 8.2 %copy-start = (bf16[1,1,2,1024,256]{4,3,2,1,0:T(8,128)(2,1)S(1)}, bf16[1,1,2,1024,256]{4,3,2,1,0:T(8,128)(2,1)}, u32[]{:S(2)}) copy-start(bf16[1,1,2,1024,256]{4,3,2,1,0:T(8,128)(2,1)} %upward_ref.1) | copy-start | bytes 3145732
  23.6 10.2 %collective-permute-start.1 = (bf16[128,1024]{1,0:T(8,128)(2,1)S(1)}, bf16[128,1024]{1,0:T(8,128)(2,1)S(1)}, u32[]{:S(2)}, u32[]{:S(2)}) collective-permute-start(bf16[128,1024]{1,0:T(8,128)(2,1)S(1)} %shard_map.47), channel_id=1, source_target_pairs={{0,8},{8,16},{16,24},{24,0},{1,9},{9,17},{17,25},{25,1},{2,10},{10... | collective-permute-start | bytes 786440 | tf_op jit(solution)/shard_map/ppermute | solution.py:18
  29.2 10.2 %collective-permute-start.5 = (bf16[128,1024]{1,0:T(8,128)(2,1)S(1)}, bf16[128,1024]{1,0:T(8,128)(2,1)S(1)}, u32[]{:S(2)}, u32[]{:S(2)}) collective-permute-start(bf16[128,1024]{1,0:T(8,128)(2,1)S(1)} %shard_map.50), channel_id=1, source_target_pairs={{0,8},{8,16},{16,24},{24,0},{1,9},{9,17},{17,25},{25,1},{2,10},{10... | collective-permute-start | bytes 786440 | tf_op jit(solution)/shard_map/ppermute | solution.py:18
  35.7 9.4 %collective-permute-start.6 = (bf16[128,1024]{1,0:T(8,128)(2,1)S(1)}, bf16[128,1024]{1,0:T(8,128)(2,1)S(1)}, u32[]{:S(2)}, u32[]{:S(2)}) collective-permute-start(bf16[128,1024]{1,0:T(8,128)(2,1)S(1)} %shard_map.52), channel_id=1, source_target_pairs={{0,8},{8,16},{16,24},{24,0},{1,9},{9,17},{17,25},{25,1},{2,10},{10... | collective-permute-start | bytes 786440 | tf_op jit(solution)/shard_map/ppermute | solution.py:18
  41.3 10.1 %collective-permute-start.7 = (bf16[128,1024]{1,0:T(8,128)(2,1)S(1)}, bf16[128,1024]{1,0:T(8,128)(2,1)S(1)}, u32[]{:S(2)}, u32[]{:S(2)}) collective-permute-start(bf16[128,1024]{1,0:T(8,128)(2,1)S(1)} %shard_map.51.refs_0_), channel_id=1, source_target_pairs={{0,8},{8,16},{16,24},{24,0},{1,9},{9,17},{17,25},{25,1},{2,10},{10... | collective-permute-start | bytes 786440 | tf_op jit(solution)/shard_map/ppermute | solution.py:18
  47.0 8.0 %collective-permute-start.8 = (bf16[128,1024]{1,0:T(8,128)(2,1)S(1)}, bf16[128,1024]{1,0:T(8,128)(2,1)S(1)}, u32[]{:S(2)}, u32[]{:S(2)}) collective-permute-start(bf16[128,1024]{1,0:T(8,128)(2,1)S(1)} %shard_map.53.refs_1_), channel_id=1, source_target_pairs={{0,8},{8,16},{16,24},{24,0},{1,9},{9,17},{17,25},{25,1},{2,10},{10... | collective-permute-start | bytes 786440 | tf_op jit(solution)/shard_map/ppermute | solution.py:18
  47.1 10.8 %collective-permute-start.9 = (bf16[128,1024]{1,0:T(8,128)(2,1)S(1)}, bf16[128,1024]{1,0:T(8,128)(2,1)S(1)}, u32[]{:S(2)}, u32[]{:S(2)}) collective-permute-start(bf16[128,1024]{1,0:T(8,128)(2,1)S(1)} %shard_map.51.refs_0_), channel_id=1, source_target_pairs={{0,2},{1,3},{2,0},{3,1},{4,6},{5,7},{6,4},{7,5},{8,10},{9,11},{10,... | collective-permute-start | bytes 786440 | tf_op jit(solution)/shard_map/ppermute | solution.py:22
  48.7 13.3 %collective-permute-start.10 = (bf16[128,1024]{1,0:T(8,128)(2,1)S(1)}, bf16[128,1024]{1,0:T(8,128)(2,1)S(1)}, u32[]{:S(2)}, u32[]{:S(2)}) collective-permute-start(bf16[128,1024]{1,0:T(8,128)(2,1)S(1)} %shard_map.53.refs_1_), channel_id=1, source_target_pairs={{0,2},{1,3},{2,0},{3,1},{4,6},{5,7},{6,4},{7,5},{8,10},{9,11},{10,... | collective-permute-start | bytes 786440 | tf_op jit(solution)/shard_map/ppermute | solution.py:22
  53.3 12.9 %collective-permute-start.11 = (bf16[128,1024]{1,0:T(8,128)(2,1)S(1)}, bf16[128,1024]{1,0:T(8,128)(2,1)S(1)}, u32[]{:S(2)}, u32[]{:S(2)}) collective-permute-start(bf16[128,1024]{1,0:T(8,128)(2,1)S(1)} %shard_map.54.refs_2_), channel_id=1, source_target_pairs={{0,2},{1,3},{2,0},{3,1},{4,6},{5,7},{6,4},{7,5},{8,10},{9,11},{10,... | collective-permute-start | bytes 786440 | tf_op jit(solution)/shard_map/ppermute | solution.py:22
  56.9 12.1 %collective-permute-start.12 = (bf16[128,1024]{1,0:T(8,128)(2,1)S(1)}, bf16[128,1024]{1,0:T(8,128)(2,1)S(1)}, u32[]{:S(2)}, u32[]{:S(2)}) collective-permute-start(bf16[128,1024]{1,0:T(8,128)(2,1)S(1)} %shard_map.55.refs_3_), channel_id=1, source_target_pairs={{0,2},{1,3},{2,0},{3,1},{4,6},{5,7},{6,4},{7,5},{8,10},{9,11},{10,... | collective-permute-start | bytes 786440 | tf_op jit(solution)/shard_map/ppermute | solution.py:22
  69.7 2.7 %collective-permute-start.13 = (bf16[2,2,128,1024]{3,2,1,0:T(8,128)(2,1)S(1)}, bf16[2,2,128,1024]{3,2,1,0:T(8,128)(2,1)S(1)}, u32[]{:S(2)}, u32[]{:S(2)}) collective-permute-start(bf16[2,2,128,1024]{3,2,1,0:T(8,128)(2,1)S(1)} %get-tuple-element.24), channel_id=1, source_target_pairs={{0,1},{1,0},{2,3},{3,2},{4,5},{5,4},{6,7},{7,6},{8,9},{9,8},{10,11... | collective-permute-start | bytes 3145736 | tf_op jit(solution)/shard_map/ppermute | solution.py:22
  72.6 26.2 %collective-permute-start.14 = (bf16[1,2,128,1024]{3,2,1,0:T(8,128)(2,1)S(1)}, bf16[1,2,128,1024]{3,2,1,0:T(8,128)(2,1)S(1)}, u32[]{:S(2)}, u32[]{:S(2)}) collective-permute-start(bf16[1,2,128,1024]{3,2,1,0:T(8,128)(2,1)S(1)} %add_convert_fusion), channel_id=1, source_target_pairs={{0,4},{1,5},{2,6},{3,7},{4,0},{5,1},{6,2},{7,3},{8,12},{9,13},{10,... | collective-permute-start | bytes 1572872 | tf_op jit(solution)/shard_map/ppermute | solution.py:18

commit v8 on v7

--- a/solution.py
+++ b/solution.py
@@ -22,12 +22,12 @@
     return lax.ppermute(block, axis, [(i, i ^ bit) for i in range(lax.axis_size(axis))])
 
 
-def places(ids_ref):
-    mine = ids_ref[1]
+def places(mine_ref):
+    mine = mine_ref[0]
     return lax.div(mine, 4), lax.rem(lax.div(mine, 2), 2), lax.rem(mine, 2)
 
 
-def first_kernel(part, ids_ref, source_ref, weight_ref, factor_ref, upward_ref, *refs):
+def first_kernel(part, level_ref, mine_ref, source_ref, weight_ref, factor_ref, upward_ref, *refs):
     *outs, joined_ref, asked_ref, source, factor, sem, sems, asked_sems = refs
     width = joined_ref.shape[0]
     shots = source.shape[2]
@@ -35,7 +35,7 @@
     wide = width // blocks
     groups = asked_sems.shape[0]
     tall = asked_ref.shape[1] // groups
-    _, place, _ = places(ids_ref)
+    _, place, _ = places(mine_ref)
 
     def copies(n):
         rows = pl.ds(n * wide, wide)
@@ -85,7 +85,7 @@
         copy.wait()
 
 
-def first_advance(ids, source, propagator, transmission, upgoing, part, groups):
+def first_advance(level, mine, source, propagator, transmission, upgoing, part, groups):
     width = propagator.shape[3]
     shots = source.shape[3]
     chunks = shots // part
@@ -93,7 +93,7 @@
     pinned = [pltpu.with_memory_space_constraint(x, pltpu.HBM) for x in (source, propagator, transmission, upgoing)]
     return pl.pallas_call(
         functools.partial(first_kernel, part),
-        in_specs=[pl.BlockSpec(memory_space=pltpu.SMEM)] + [pl.BlockSpec(memory_space=pltpu.HBM)] * 4,
+        in_specs=[pl.BlockSpec(memory_space=pltpu.SMEM)] * 2 + [pl.BlockSpec(memory_space=pltpu.HBM)] * 4,
         out_specs=[whole] * (chunks + 2),
         out_shape=[jax.ShapeDtypeStruct((2 * part, width), jnp.bfloat16)] * chunks
         + [
@@ -111,19 +111,19 @@
         cost_estimate=pl.CostEstimate(
             flops=8 * width * width * shots, bytes_accessed=4 * width * (width + 2 * shots), transcendentals=0
         ),
-    )(ids, *pinned)
-
-
-def advance_kernel(ids_ref, arrived_ref, ready_ref, joined_ref, factor_ref, out_ref, both):
+    )(level, mine, *pinned)
+
+
+def advance_kernel(level_ref, arrived_ref, ready_ref, joined_ref, factor_ref, out_ref, both):
     part = arrived_ref.shape[0] // 2
     width = arrived_ref.shape[1]
     wide = width // 4
 
-    @pl.when(ids_ref[0] == 0)
+    @pl.when(level_ref[0] == 0)
     def _():
         out_ref[...] = ready_ref[...]
 
-    @pl.when(ids_ref[0] != 0)
+    @pl.when(level_ref[0] != 0)
     def _():
         both[:, :width] = arrived_ref[...]
         both[:part, width:] = -arrived_ref[part:]
@@ -136,7 +136,7 @@
             out_ref[:, columns] = (out.T * factor_ref[:, columns]).astype(jnp.bfloat16)
 
 
-def advance(ids, arrived, ready, joined, factor):
+def advance(level, arrived, ready, joined, factor):
     rows, width = arrived.shape
     whole = pl.BlockSpec(memory_space=pltpu.VMEM)
     return pl.pallas_call(
@@ -149,14 +149,14 @@
         cost_estimate=pl.CostEstimate(
             flops=4 * rows * width * width, bytes_accessed=4 * width * width + 6 * rows * width, transcendentals=0
         ),
-    )(ids, arrived, ready, pltpu.with_memory_space_constraint(joined, pltpu.VMEM), factor)
-
-
-def operand_kernel(part, levels, ids_ref, own_ref, got_ref, out_ref):
+    )(level, arrived, ready, pltpu.with_memory_space_constraint(joined, pltpu.VMEM), factor)
+
+
+def operand_kernel(part, levels, level_ref, mine_ref, own_ref, got_ref, out_ref):
     rows = own_ref.shape[1]
     shots = own_ref.shape[2]
     chunks = shots // part
-    turn = lax.rem(DELAY * (levels - 1 - ids_ref[0]), chunks)
+    turn = lax.rem(DELAY * (levels - 1 - level_ref[0]), chunks)
     for first in range(0, chunks, math.gcd(DELAY, chunks)):
 
         @pl.when(turn == first)
@@ -175,13 +175,13 @@
                     )
 
 
-def operand(ids, own, got, rows, part, levels):
+def operand(level, mine, own, got, rows, part, levels):
     shots = own.shape[2]
     blocks = got.shape[1] // rows
     groups = blocks // 2
 
-    def spot(i, ids_ref, stride):
-        group, place, core = places(ids_ref)
+    def spot(i, mine_ref, stride):
+        group, place, core = places(mine_ref)
         other = lax.rem(lax.div(i, groups) + core, 2)
         block = stride * lax.rem(group + lax.rem(i, groups), groups) + other
         return block + 2 * place if stride == 4 else block
@@ -189,18 +189,18 @@
     return pl.pallas_call(
         functools.partial(operand_kernel, part, levels),
         grid_spec=pltpu.PrefetchScalarGridSpec(
-            num_scalar_prefetch=1,
+            num_scalar_prefetch=2,
             grid=(blocks,),
             in_specs=[
-                pl.BlockSpec((2, rows, shots), lambda i, ids_ref: (0, spot(i, ids_ref, 4), 0)),
-                pl.BlockSpec((2, rows, shots), lambda i, ids_ref: (0, spot(i, ids_ref, 2), 0)),
+                pl.BlockSpec((2, rows, shots), lambda i, _, mine_ref: (0, spot(i, mine_ref, 4), 0)),
+                pl.BlockSpec((2, rows, shots), lambda i, _, mine_ref: (0, spot(i, mine_ref, 2), 0)),
             ],
-            out_specs=pl.BlockSpec((2 * rows, 4 * shots), lambda i, ids_ref: (i, 0)),
+            out_specs=pl.BlockSpec((2 * rows, 4 * shots), lambda i, *_: (i, 0)),
         ),
         out_shape=jax.ShapeDtypeStruct((2 * rows * blocks, 4 * shots), jnp.bfloat16),
         compiler_params=pltpu.CompilerParams(vmem_limit_bytes=LIMIT),
         cost_estimate=pl.CostEstimate(flops=0, bytes_accessed=24 * rows * blocks * shots, transcendentals=0),
-    )(ids, own, got)
+    )(level, mine, own, got)
 
 
 def gathered(panels, columns):
@@ -298,10 +298,10 @@
     groups = freqs // 4
     rows = width // freqs
     part = shots // CHUNKS
-    ids = jnp.stack([lax.axis_index("depth"), lax.axis_index("freq")]).astype(jnp.int32)
-    *ready, joined, asked = first_advance(ids, source, propagator, transmission, upgoing, part, groups)
+    level, mine = (lax.axis_index(axis).astype(jnp.int32).reshape(1) for axis in ("depth", "freq"))
+    *ready, joined, asked = first_advance(level, mine, source, propagator, transmission, upgoing, part, groups)
     got = swapped(asked, "freq", 2)
-    left = operand(ids, upward, got, rows, part, levels)
+    left = operand(level, mine, upward, got, rows, part, levels)
 
     ticks = CHUNKS + DELAY * (levels - 1)
     flying = []
@@ -313,7 +313,9 @@
             arrived = flying[tick - DELAY]
             if tick == ticks // 2:
                 arrived, left = lax.optimization_barrier((arrived, left))
-            out = advance(ids, arrived, out, joined, factor)
+            if len(other) >= DELAY:
+                arrived, other[-DELAY] = lax.optimization_barrier((arrived, other[-DELAY]))
+            out = advance(level, arrived, out, joined, factor)
         if tick + DELAY < ticks:
             flying.append(ring(out, "depth", 1))
         if tick >= ticks - CHUNKS:

time: 102 us -> 95.1 us (0.932); the launches traced: 100 us -> 94.9 us
  Pallas kernels: 26.5 us -> 21 us
  starting transfers between devices: 13.2 us -> 15.3 us
  waiting for transfers between devices: 60 us -> 58.4 us
    pallas_call x8, Pallas kernels: 15.2 us -> 10.7 us  [advance(): pl.pallas_call(advance_kernel, in_specs=[pl.BlockSpec(memory_space=pltpu....]
    ppermute x6, waiting for transfers between devices: 12 us -> 9.25 us  [swapped(): lax.ppermute(block, axis, [(i, i ^ bit) for i in range(lax.axis_size(axis...]
    ppermute x6, starting transfers between devices: 6.8 us -> 8.99 us  [swapped(): lax.ppermute(block, axis, [(i, i ^ bit) for i in range(lax.axis_size(axis...]
    ppermute x9, waiting for transfers between devices: 48 us -> 49.1 us  [ring(): lax.ppermute(block, axis, [(i, (i + distance) % size) for i in range(size)])]
  transfers between devices with their start and end apart: 15 -> 15, of which waited for: 12 -> 13; matrix products, arithmetic and copies ran while one was open for 0% -> 0% of each run, Pallas kernels for 19% -> 14%
where the time goes in v8:
time: 95.1 us; the launch traced here: 94.9 us
  waiting for transfers between devices  58.4 us (61%)
  Pallas kernels  21 us (22%)
  starting transfers between devices  15.3 us (16%)
    ppermute x9, waiting for transfers between devices, ring(): lax.ppermute(block, axis, [(i, (i + distance) % size) for i in range(size)])  49.1 us
    pallas_call x8, Pallas kernels, advance(): pl.pallas_call(advance_kernel, in_specs=[pl.BlockSpec(memory_space=pltpu....  10.7 us
    ppermute x6, waiting for transfers between devices, swapped(): lax.ppermute(block, axis, [(i, i ^ bit) for i in range(lax.axis_size(axis...  9.25 us
    ppermute x6, starting transfers between devices, swapped(): lax.ppermute(block, axis, [(i, i ^ bit) for i in range(lax.axis_size(axis...  8.99 us
    ppermute x9, starting transfers between devices, ring(): lax.ppermute(block, axis, [(i, (i + distance) % size) for i in range(size)])  6.35 us
    pallas_call x1, Pallas kernels, first_advance(): pl.pallas_call(functools.partial(first_kernel, part), in_specs=[pl.BlockS...  5.28 us
    pallas_call x2, Pallas kernels, whole_call(): pl.pallas_call(kernel, in_specs=[whole] * len(args), out_specs=[whole] *...  2.5 us
  transfers between devices with their start and end apart: 15, of which 13 were waited for; matrix products, arithmetic and copies ran while one was open for 0% of the time, Pallas kernels for 14%

profile of v8, /device:TPU:4, one launch (start us, length us, event | category | flops | bytes accessed | tf_op | source)
XLA Modules:
  0.0 94.9 jit_solution(8476034261235700749)
XLA Ops:
  0.0 5.3 %shard_map.46 = (bf16[128,1024]{1,0:T(8,128)(2,1)S(1)}, bf16[128,1024]{1,0:T(8,128)(2,1)S(1)}, bf16[128,1024]{1,0:T(8,128)(2,1)S(1)}, bf16[128,1024]{1,0:T(8,128...) custom-call(s32[1]{0:T(128)} %bitcast.level_ref, s32[1]{0:T(128)} %bitcast.1.mine_ref, ...), custom_call_target="tpu_custom_call" | custom-call | flops 2147483648 | bytes 6291456 | tf_op jit(solution)/shard_map/pallas_call | solution.py:94
  5.3 1.6 %collective-permute-start.3 = (bf16[128,1024]{1,0:T(8,128)(2,1)S(1)}, bf16[128,1024]{1,0:T(8,128)(2,1)S(1)}, u32[]{:S(2)}, u32[]{:S(2)}) collective-permute-start(bf16[128,1024]{1,0:T(8,128)(2,1)S(1)} %get-tuple-element.24.ready_ref), channel_id=1, source_target_pairs={{0,8},{8,16},{16,24},{24,0},{1,9},{9,17},{17,25},{25,1},{2,10},{10... | collective-permute-start | bytes 786440 | tf_op jit(solution)/shard_map/ppermute | solution.py:18
  6.9 2.0 %collective-permute-start.2 = (bf16[2,512,256]{2,1,0:T(8,128)(2,1)S(1)}, bf16[2,512,256]{2,1,0:T(8,128)(2,1)S(1)}, u32[]{:S(2)}, u32[]{:S(2)}) collective-permute-start(bf16[2,512,256]{2,1,0:T(8,128)(2,1)S(1)} %get-tuple-element.22), channel_id=1, source_target_pairs={{0,2},{1,3},{2,0},{3,1},{4,6},{5,7},{6,4},{7,5},{8,10},{9,11},{10,... | collective-permute-start | bytes 1572872 | tf_op jit(solution)/shard_map/ppermute | solution.py:22
  8.9 6.5 %collective-permute-done.3.arrived_ref = bf16[128,1024]{1,0:T(8,128)(2,1)S(1)} collective-permute-done((bf16[128,1024]{1,0:T(8,128)(2,1)S(1)}, bf16[128,1024]{1,0:T(8,128)(2,1)S(1)}, u32[]{:S(2)}, u32[]{:S(2)}) %collective-permute-start.3) | collective-permute-done | bytes 262176 | tf_op jit(solution)/shard_map/ppermute | solution.py:18
  15.4 1.3 %shard_map.49 = bf16[128,1024]{1,0:T(8,128)(2,1)S(1)} custom-call(s32[1]{0:T(128)} %bitcast.level_ref, bf16[128,1024]{1,0:T(8,128)(2,1)S(1)} %collective-permute-done.3.arrived_ref, bf16[128,1024]{1,0:T(8,128)(2,1)S(1)} %get-tuple-element.25.ready_ref, bf16[1024,2048]{1,0:T(8,128)(2,1)S(1)} %get-tuple-element.21.joined_ref, f32[1,1024]{1,0:T(1,128)S(1)} %bitcast.5), custom_call_target="tpu_custom_call" | custom-call | flops 536870912 | bytes 4980736 | tf_op jit(solution)/shard_map/pallas_call | solution.py:142
  17.5 3.6 %collective-permute-done.arrived_ref = bf16[128,1024]{1,0:T(8,128)(2,1)S(1)} collective-permute-done((bf16[128,1024]{1,0:T(8,128)(2,1)S(1)}, bf16[128,1024]{1,0:T(8,128)(2,1)S(1)}, u32[]{:S(2)}, u32[]{:S(2)}) %collective-permute-start) | collective-permute-done | bytes 262176 | tf_op jit(solution)/shard_map/ppermute | solution.py:18
  23.1 3.9 %collective-permute-done.4.arrived_ref = bf16[128,1024]{1,0:T(8,128)(2,1)S(1)} collective-permute-done((bf16[128,1024]{1,0:T(8,128)(2,1)S(1)}, bf16[128,1024]{1,0:T(8,128)(2,1)S(1)}, u32[]{:S(2)}, u32[]{:S(2)}) %collective-permute-start.4) | collective-permute-done | bytes 262176 | tf_op jit(solution)/shard_map/ppermute | solution.py:18
  29.8 2.8 %collective-permute-done.1.arrived_ref = bf16[128,1024]{1,0:T(8,128)(2,1)S(1)} collective-permute-done((bf16[128,1024]{1,0:T(8,128)(2,1)S(1)}, bf16[128,1024]{1,0:T(8,128)(2,1)S(1)}, u32[]{:S(2)}, u32[]{:S(2)}) %collective-permute-start.1) | collective-permute-done | bytes 262176 | tf_op jit(solution)/shard_map/ppermute | solution.py:18
  32.6 1.3 %shard_map.52 = bf16[128,1024]{1,0:T(8,128)(2,1)S(1)} custom-call(s32[1]{0:T(128)} %bitcast.level_ref, bf16[128,1024]{1,0:T(8,128)(2,1)S(1)} %collective-permute-done.1.arrived_ref, bf16[128,1024]{1,0:T(8,128)(2,1)S(1)} %get-tuple-element.19.ready_ref, bf16[1024,2048]{1,0:T(8,128)(2,1)S(1)} %get-tuple-element.21.joined_ref, f32[1,1024]{1,0:T(1,128)S(1)} %bitcast.8), custom_call_target="tpu_custom_call" | custom-call | flops 536870912 | bytes 4980736 | tf_op jit(solution)/shard_map/pallas_call | solution.py:142
  34.3 4.2 %collective-permute-done.5.arrived_ref = bf16[128,1024]{1,0:T(8,128)(2,1)S(1)} collective-permute-done((bf16[128,1024]{1,0:T(8,128)(2,1)S(1)}, bf16[128,1024]{1,0:T(8,128)(2,1)S(1)}, u32[]{:S(2)}, u32[]{:S(2)}) %collective-permute-start.5) | collective-permute-done | bytes 262176 | tf_op jit(solution)/shard_map/ppermute | solution.py:18
  38.5 1.3 %shard_map.51.refs_0_ = bf16[128,1024]{1,0:T(8,128)(2,1)S(1)} custom-call(s32[1]{0:T(128)} %bitcast.level_ref, bf16[128,1024]{1,0:T(8,128)(2,1)S(1)} %collective-permute-done.5.arrived_ref, bf16[128,1024]{1,0:T(8,128)(2,1)S(1)} %get-tuple-element.25.ready_ref, bf16[1024,2048]{1,0:T(8,128)(2,1)S(1)} %get-tuple-element.21.joined_ref, f32[1,1024]{1,0:T(1,128)S(1)} %bitcast.9), custom_call_target="tpu_custom_call" | custom-call | flops 536870912 | bytes 4980736 | tf_op jit(solution)/shard_map/pallas_call | solution.py:142
  39.9 1.6 %collective-permute-start.8 = (bf16[128,1024]{1,0:T(8,128)(2,1)S(1)}, bf16[128,1024]{1,0:T(8,128)(2,1)S(1)}, u32[]{:S(2)}, u32[]{:S(2)}) collective-permute-start(bf16[128,1024]{1,0:T(8,128)(2,1)S(1)} %shard_map.51.refs_0_), channel_id=1, source_target_pairs={{0,2},{1,3},{2,0},{3,1},{4,6},{5,7},{6,4},{7,5},{8,10},{9,11},{10,... | collective-permute-start | bytes 786440 | tf_op jit(solution)/shard_map/ppermute | solution.py:22
  41.5 1.8 %collective-permute-done.6.arrived_ref = bf16[128,1024]{1,0:T(8,128)(2,1)S(1)} collective-permute-done((bf16[128,1024]{1,0:T(8,128)(2,1)S(1)}, bf16[128,1024]{1,0:T(8,128)(2,1)S(1)}, u32[]{:S(2)}, u32[]{:S(2)}) %collective-permute-start.6) | collective-permute-done | bytes 262176 | tf_op jit(solution)/shard_map/ppermute | solution.py:18
  43.3 1.3 %shard_map.53.refs_1_ = bf16[128,1024]{1,0:T(8,128)(2,1)S(1)} custom-call(s32[1]{0:T(128)} %bitcast.level_ref, bf16[128,1024]{1,0:T(8,128)(2,1)S(1)} %collective-permute-done.6.arrived_ref, bf16[128,1024]{1,0:T(8,128)(2,1)S(1)} %get-tuple-element.20.ready_ref, bf16[1024,2048]{1,0:T(8,128)(2,1)S(1)} %get-tuple-element.21.joined_ref, f32[1,1024]{1,0:T(1,128)S(1)} %bitcast.10), custom_call_target="tpu_custom_call" | custom-call | flops 536870912 | bytes 4980736 | tf_op jit(solution)/shard_map/pallas_call | solution.py:142
  44.7 2.5 %collective-permute-start.10 = (bf16[128,1024]{1,0:T(8,128)(2,1)S(1)}, bf16[128,1024]{1,0:T(8,128)(2,1)S(1)}, u32[]{:S(2)}, u32[]{:S(2)}) collective-permute-start(bf16[128,1024]{1,0:T(8,128)(2,1)S(1)} %shard_map.53.refs_1_), channel_id=1, source_target_pairs={{0,2},{1,3},{2,0},{3,1},{4,6},{5,7},{6,4},{7,5},{8,10},{9,11},{10,... | collective-permute-start | bytes 786440 | tf_op jit(solution)/shard_map/ppermute | solution.py:22
  47.9 2.7 %collective-permute-done.7.arrived_ref = bf16[128,1024]{1,0:T(8,128)(2,1)S(1)} collective-permute-done((bf16[128,1024]{1,0:T(8,128)(2,1)S(1)}, bf16[128,1024]{1,0:T(8,128)(2,1)S(1)}, u32[]{:S(2)}, u32[]{:S(2)}) %collective-permute-start.7) | collective-permute-done | bytes 262176 | tf_op jit(solution)/shard_map/ppermute | solution.py:18
  50.6 1.3 %shard_map.54.refs_2_ = bf16[128,1024]{1,0:T(8,128)(2,1)S(1)} custom-call(s32[1]{0:T(128)} %bitcast.level_ref, bf16[128,1024]{1,0:T(8,128)(2,1)S(1)} %collective-permute-done.7.arrived_ref, bf16[128,1024]{1,0:T(8,128)(2,1)S(1)} %get-tuple-element.24.ready_ref, bf16[1024,2048]{1,0:T(8,128)(2,1)S(1)} %get-tuple-element.21.joined_ref, f32[1,1024]{1,0:T(1,128)S(1)} %bitcast.11), custom_call_target="tpu_custom_call" | custom-call | flops 536870912 | bytes 4980736 | tf_op jit(solution)/shard_map/pallas_call | solution.py:142
  55.8 1.5 %collective-permute-start.12 = (bf16[128,1024]{1,0:T(8,128)(2,1)S(1)}, bf16[128,1024]{1,0:T(8,128)(2,1)S(1)}, u32[]{:S(2)}, u32[]{:S(2)}) collective-permute-start(bf16[128,1024]{1,0:T(8,128)(2,1)S(1)} %shard_map.55.refs_3_), channel_id=1, source_target_pairs={{0,2},{1,3},{2,0},{3,1},{4,6},{5,7},{6,4},{7,5},{8,10},{9,11},{10,... | collective-permute-start | bytes 786440 | tf_op jit(solution)/shard_map/ppermute | solution.py:22
  57.3 1.8 %shard_map.56.early_ref = f32[1024,1024]{1,0:T(8,128)S(1)} custom-call(bf16[1024,1024]{1,0:T(8,128)(2,1)S(1)} %shard_map.48.left_ref, bf16[128,1024]{1,0:T(8,128)(2,1)S(1)} %shard_map.51.refs_0_, bf16[128,1024]{1,0:T(8,128)(2,1)S(1)} %shard_map.53.refs_1_, bf16[128,1024]{1,0:T(8,128)(2,1)S(1)} %shard_map.54.refs_2_, ...), custom_call_target="tpu_custom_call" | custom-call | flops 1610612736 | bytes 7864320 | tf_op jit(solution)/shard_map/pallas_call | solution.py:243
  59.1 2.0 %collective-permute-done.11.refs_0_ = bf16[128,1024]{1,0:T(8,128)(2,1)S(1)} collective-permute-done((bf16[128,1024]{1,0:T(8,128)(2,1)S(1)}, bf16[128,1024]{1,0:T(8,128)(2,1)S(1)}, u32[]{:S(2)}, u32[]{:S(2)}) %collective-permute-start.11) | collective-permute-done | bytes 262176 | tf_op jit(solution)/shard_map/ppermute | solution.py:22
  61.1 2.8 %collective-permute-done.12.refs_1_ = bf16[128,1024]{1,0:T(8,128)(2,1)S(1)} collective-permute-done((bf16[128,1024]{1,0:T(8,128)(2,1)S(1)}, bf16[128,1024]{1,0:T(8,128)(2,1)S(1)}, u32[]{:S(2)}, u32[]{:S(2)}) %collective-permute-start.12) | collective-permute-done | bytes 262176 | tf_op jit(solution)/shard_map/ppermute | solution.py:22
  64.7 2.6 %collective-permute-done.13.refs_1_ = bf16[2,2,128,1024]{3,2,1,0:T(8,128)(2,1)S(1)} collective-permute-done((bf16[2,2,128,1024]{3,2,1,0:T(8,128)(2,1)S(1)}, bf16[2,2,128,1024]{3,2,1,0:T(8,128)(2,1)S(1)}, u32[]{:S(2)}, u32[]{:S(2)}) %collective-permute-start.13) | collective-permute-done | bytes 1048608 | tf_op jit(solution)/shard_map/ppermute | solution.py:22
  67.5 2.7 %collective-permute-start.14 = (bf16[1,2,128,1024]{3,2,1,0:T(8,128)(2,1)S(1)}, bf16[1,2,128,1024]{3,2,1,0:T(8,128)(2,1)S(1)}, u32[]{:S(2)}, u32[]{:S(2)}) collective-permute-start(bf16[1,2,128,1024]{3,2,1,0:T(8,128)(2,1)S(1)} %add_convert_fusion), channel_id=1, source_target_pairs={{0,4},{1,5},{2,6},{3,7},{4,0},{5,1},{6,2},{7,3},{8,12},{9,13},{10,... | collective-permute-start | bytes 1572872 | tf_op jit(solution)/shard_map/ppermute | solution.py:18
  70.1 23.5 %collective-permute-done.14.refs_2_ = bf16[1,2,128,1024]{3,2,1,0:T(8,128)(2,1)S(1)} collective-permute-done((bf16[1,2,128,1024]{3,2,1,0:T(8,128)(2,1)S(1)}, bf16[1,2,128,1024]{3,2,1,0:T(8,128)(2,1)S(1)}, u32[]{:S(2)}, u32[]{:S(2)}) %collective-permute-start.14) | collective-permute-done | bytes 524320 | tf_op jit(solution)/shard_map/ppermute | solution.py:18
  (24 shorter events, 12.7 us)
Async XLA Ops:
  0.0 15.4 %copy-start.1 = (f32[1,1,1024]{2,1,0:T(1,128)S(1)}, f32[1,1,1024]{2,1,0:T(1,128)}, u32[]{:S(2)}) copy-start(f32[1,1,1024]{2,1,0:T(1,128)} %factor_ref.1) | copy-start | bytes 12292
  5.3 10.1 %collective-permute-start.3 = (bf16[128,1024]{1,0:T(8,128)(2,1)S(1)}, bf16[128,1024]{1,0:T(8,128)(2,1)S(1)}, u32[]{:S(2)}, u32[]{:S(2)}) collective-permute-start(bf16[128,1024]{1,0:T(8,128)(2,1)S(1)} %get-tuple-element.24.ready_ref), channel_id=1, source_target_pairs={{0,8},{8,16},{16,24},{24,0},{1,9},{9,17},{17,25},{25,1},{2,10},{10... | collective-permute-start | bytes 786440 | tf_op jit(solution)/shard_map/ppermute | solution.py:18
  6.8 14.2 %collective-permute-start = (bf16[128,1024]{1,0:T(8,128)(2,1)S(1)}, bf16[128,1024]{1,0:T(8,128)(2,1)S(1)}, u32[]{:S(2)}, u32[]{:S(2)}) collective-permute-start(bf16[128,1024]{1,0:T(8,128)(2,1)S(1)} %get-tuple-element.19.ready_ref), channel_id=1, source_target_pairs={{0,8},{8,16},{16,24},{24,0},{1,9},{9,17},{17,25},{25,1},{2,10},{10... | collective-permute-start | bytes 786440 | tf_op jit(solution)/shard_map/ppermute | solution.py:18
  6.9 21.8 %collective-permute-start.2 = (bf16[2,512,256]{2,1,0:T(8,128)(2,1)S(1)}, bf16[2,512,256]{2,1,0:T(8,128)(2,1)S(1)}, u32[]{:S(2)}, u32[]{:S(2)}) collective-permute-start(bf16[2,512,256]{2,1,0:T(8,128)(2,1)S(1)} %get-tuple-element.22), channel_id=1, source_target_pairs={{0,2},{1,3},{2,0},{3,1},{4,6},{5,7},{6,4},{7,5},{8,10},{9,11},{10,... | collective-permute-start | bytes 1572872 | tf_op jit(solution)/shard_map/ppermute | solution.py:22
  16.8 10.2 %collective-permute-start.4 = (bf16[128,1024]{1,0:T(8,128)(2,1)S(1)}, bf16[128,1024]{1,0:T(8,128)(2,1)S(1)}, u32[]{:S(2)}, u32[]{:S(2)}) collective-permute-start(bf16[128,1024]{1,0:T(8,128)(2,1)S(1)} %shard_map.49), channel_id=1, source_target_pairs={{0,8},{8,16},{16,24},{24,0},{1,9},{9,17},{17,25},{25,1},{2,10},{10... | collective-permute-start | bytes 786440 | tf_op jit(solution)/shard_map/ppermute | solution.py:18
  21.1 7.6 %copy-start = (bf16[1,1,2,1024,256]{4,3,2,1,0:T(8,128)(2,1)S(1)}, bf16[1,1,2,1024,256]{4,3,2,1,0:T(8,128)(2,1)}, u32[]{:S(2)}) copy-start(bf16[1,1,2,1024,256]{4,3,2,1,0:T(8,128)(2,1)} %upward_ref.1) | copy-start | bytes 3145732
  22.4 10.2 %collective-permute-start.1 = (bf16[128,1024]{1,0:T(8,128)(2,1)S(1)}, bf16[128,1024]{1,0:T(8,128)(2,1)S(1)}, u32[]{:S(2)}, u32[]{:S(2)}) collective-permute-start(bf16[128,1024]{1,0:T(8,128)(2,1)S(1)} %shard_map.47), channel_id=1, source_target_pairs={{0,8},{8,16},{16,24},{24,0},{1,9},{9,17},{17,25},{25,1},{2,10},{10... | collective-permute-start | bytes 786440 | tf_op jit(solution)/shard_map/ppermute | solution.py:18
  28.3 10.2 %collective-permute-start.5 = (bf16[128,1024]{1,0:T(8,128)(2,1)S(1)}, bf16[128,1024]{1,0:T(8,128)(2,1)S(1)}, u32[]{:S(2)}, u32[]{:S(2)}) collective-permute-start(bf16[128,1024]{1,0:T(8,128)(2,1)S(1)} %shard_map.50), channel_id=1, source_target_pairs={{0,8},{8,16},{16,24},{24,0},{1,9},{9,17},{17,25},{25,1},{2,10},{10... | collective-permute-start | bytes 786440 | tf_op jit(solution)/shard_map/ppermute | solution.py:18
  34.0 9.4 %collective-permute-start.6 = (bf16[128,1024]{1,0:T(8,128)(2,1)S(1)}, bf16[128,1024]{1,0:T(8,128)(2,1)S(1)}, u32[]{:S(2)}, u32[]{:S(2)}) collective-permute-start(bf16[128,1024]{1,0:T(8,128)(2,1)S(1)} %shard_map.52), channel_id=1, source_target_pairs={{0,8},{8,16},{16,24},{24,0},{1,9},{9,17},{17,25},{25,1},{2,10},{10... | collective-permute-start | bytes 786440 | tf_op jit(solution)/shard_map/ppermute | solution.py:18
  39.9 8.0 %collective-permute-start.8 = (bf16[128,1024]{1,0:T(8,128)(2,1)S(1)}, bf16[128,1024]{1,0:T(8,128)(2,1)S(1)}, u32[]{:S(2)}, u32[]{:S(2)}) collective-permute-start(bf16[128,1024]{1,0:T(8,128)(2,1)S(1)} %shard_map.51.refs_0_), channel_id=1, source_target_pairs={{0,2},{1,3},{2,0},{3,1},{4,6},{5,7},{6,4},{7,5},{8,10},{9,11},{10,... | collective-permute-start | bytes 786440 | tf_op jit(solution)/shard_map/ppermute | solution.py:22
  41.5 9.1 %collective-permute-start.7 = (bf16[128,1024]{1,0:T(8,128)(2,1)S(1)}, bf16[128,1024]{1,0:T(8,128)(2,1)S(1)}, u32[]{:S(2)}, u32[]{:S(2)}) collective-permute-start(bf16[128,1024]{1,0:T(8,128)(2,1)S(1)} %shard_map.51.refs_0_), channel_id=1, source_target_pairs={{0,8},{8,16},{16,24},{24,0},{1,9},{9,17},{17,25},{25,1},{2,10},{10... | collective-permute-start | bytes 786440 | tf_op jit(solution)/shard_map/ppermute | solution.py:18
  44.7 9.7 %collective-permute-start.10 = (bf16[128,1024]{1,0:T(8,128)(2,1)S(1)}, bf16[128,1024]{1,0:T(8,128)(2,1)S(1)}, u32[]{:S(2)}, u32[]{:S(2)}) collective-permute-start(bf16[128,1024]{1,0:T(8,128)(2,1)S(1)} %shard_map.53.refs_1_), channel_id=1, source_target_pairs={{0,2},{1,3},{2,0},{3,1},{4,6},{5,7},{6,4},{7,5},{8,10},{9,11},{10,... | collective-permute-start | bytes 786440 | tf_op jit(solution)/shard_map/ppermute | solution.py:22
  47.1 7.3 %collective-permute-start.9 = (bf16[128,1024]{1,0:T(8,128)(2,1)S(1)}, bf16[128,1024]{1,0:T(8,128)(2,1)S(1)}, u32[]{:S(2)}, u32[]{:S(2)}) collective-permute-start(bf16[128,1024]{1,0:T(8,128)(2,1)S(1)} %shard_map.53.refs_1_), channel_id=1, source_target_pairs={{0,8},{8,16},{16,24},{24,0},{1,9},{9,17},{17,25},{25,1},{2,10},{10... | collective-permute-start | bytes 786440 | tf_op jit(solution)/shard_map/ppermute | solution.py:18
  52.0 9.1 %collective-permute-start.11 = (bf16[128,1024]{1,0:T(8,128)(2,1)S(1)}, bf16[128,1024]{1,0:T(8,128)(2,1)S(1)}, u32[]{:S(2)}, u32[]{:S(2)}) collective-permute-start(bf16[128,1024]{1,0:T(8,128)(2,1)S(1)} %shard_map.54.refs_2_), channel_id=1, source_target_pairs={{0,2},{1,3},{2,0},{3,1},{4,6},{5,7},{6,4},{7,5},{8,10},{9,11},{10,... | collective-permute-start | bytes 786440 | tf_op jit(solution)/shard_map/ppermute | solution.py:22
  55.8 8.1 %collective-permute-start.12 = (bf16[128,1024]{1,0:T(8,128)(2,1)S(1)}, bf16[128,1024]{1,0:T(8,128)(2,1)S(1)}, u32[]{:S(2)}, u32[]{:S(2)}) collective-permute-start(bf16[128,1024]{1,0:T(8,128)(2,1)S(1)} %shard_map.55.refs_3_), channel_id=1, source_target_pairs={{0,2},{1,3},{2,0},{3,1},{4,6},{5,7},{6,4},{7,5},{8,10},{9,11},{10,... | collective-permute-start | bytes 786440 | tf_op jit(solution)/shard_map/ppermute | solution.py:22
  64.6 2.7 %collective-permute-start.13 = (bf16[2,2,128,1024]{3,2,1,0:T(8,128)(2,1)S(1)}, bf16[2,2,128,1024]{3,2,1,0:T(8,128)(2,1)S(1)}, u32[]{:S(2)}, u32[]{:S(2)}) collective-permute-start(bf16[2,2,128,1024]{3,2,1,0:T(8,128)(2,1)S(1)} %get-tuple-element.32), channel_id=1, source_target_pairs={{0,1},{1,0},{2,3},{3,2},{4,5},{5,4},{6,7},{7,6},{8,9},{9,8},{10,11... | collective-permute-start | bytes 3145736 | tf_op jit(solution)/shard_map/ppermute | solution.py:22
  67.5 26.2 %collective-permute-start.14 = (bf16[1,2,128,1024]{3,2,1,0:T(8,128)(2,1)S(1)}, bf16[1,2,128,1024]{3,2,1,0:T(8,128)(2,1)S(1)}, u32[]{:S(2)}, u32[]{:S(2)}) collective-permute-start(bf16[1,2,128,1024]{3,2,1,0:T(8,128)(2,1)S(1)} %add_convert_fusion), channel_id=1, source_target_pairs={{0,4},{1,5},{2,6},{3,7},{4,0},{5,1},{6,2},{7,3},{8,12},{9,13},{10,... | collective-permute-start | bytes 1572872 | tf_op jit(solution)/shard_map/ppermute | solution.py:18

commit v9 on v8

--- a/solution.py
+++ b/solution.py
@@ -8,7 +8,7 @@
 from jax.experimental.pallas import tpu as pltpu
 from jax.sharding import PartitionSpec as P
 
-CHUNKS = 4
+CHUNKS = 8
 DELAY = 2
 LIMIT = 16 * 1024 * 1024
 

time: 95.1 us -> 102 us (1.073)
  Pallas kernels: 21 us -> 31.5 us
  waiting for transfers between devices: 58.4 us -> 55.9 us
  starting transfers between devices: 15.3 us -> 14.1 us
    pallas_call x1, Pallas kernels: 1.12 us -> 6.14 us  [operand(): pl.pallas_call(functools.partial(operand_kernel, part, levels), grid_spec...]
    pallas_call x8 -> x12, Pallas kernels: 10.7 us -> 15.7 us  [advance(): pl.pallas_call(advance_kernel, in_specs=[pl.BlockSpec(memory_space=pltpu....]
    ppermute x9 -> x13, waiting for transfers between devices: 49.1 us -> 45.3 us  [ring(): lax.ppermute(block, axis, [(i, (i + distance) % size) for i in range(size)])]
    ppermute x6 -> x10, waiting for transfers between devices: 9.25 us -> 10.6 us  [swapped(): lax.ppermute(block, axis, [(i, i ^ bit) for i in range(lax.axis_size(axis...]
    ppermute x6 -> x10, starting transfers between devices: 8.99 us -> 7.91 us  [swapped(): lax.ppermute(block, axis, [(i, i ^ bit) for i in range(lax.axis_size(axis...]
    ppermute x9 -> x13, starting transfers between devices: 6.35 us -> 6.2 us  [ring(): lax.ppermute(block, axis, [(i, (i + distance) % size) for i in range(size)])]
  transfers between devices with their start and end apart: 15 -> 23, of which waited for: 13 -> 14; matrix products, arithmetic and copies ran while one was open for 0% -> 0% of each run, Pallas kernels for 14% -> 24%
where the time goes in v9:
time: 102 us
  waiting for transfers between devices  55.9 us (55%)
  Pallas kernels  31.5 us (31%)
  starting transfers between devices  14.1 us (14%)
    ppermute x13, waiting for transfers between devices, ring(): lax.ppermute(block, axis, [(i, (i + distance) % size) for i in range(size)])  45.3 us
    pallas_call x12, Pallas kernels, advance(): pl.pallas_call(advance_kernel, in_specs=[pl.BlockSpec(memory_space=pltpu....  15.7 us
    ppermute x10, waiting for transfers between devices, swapped(): lax.ppermute(block, axis, [(i, i ^ bit) for i in range(lax.axis_size(axis...  10.6 us
    ppermute x10, starting transfers between devices, swapped(): lax.ppermute(block, axis, [(i, i ^ bit) for i in range(lax.axis_size(axis...  7.91 us
    ppermute x13, starting transfers between devices, ring(): lax.ppermute(block, axis, [(i, (i + distance) % size) for i in range(size)])  6.2 us
    pallas_call x1, Pallas kernels, operand(): pl.pallas_call(functools.partial(operand_kernel, part, levels), grid_spec...  6.14 us
    pallas_call x1, Pallas kernels, first_advance(): pl.pallas_call(functools.partial(first_kernel, part), in_specs=[pl.BlockS...  5.28 us
    pallas_call x2, Pallas kernels, whole_call(): pl.pallas_call(kernel, in_specs=[whole] * len(args), out_specs=[whole] *...  3.02 us
  transfers between devices with their start and end apart: 23, of which 14 were waited for; matrix products, arithmetic and copies ran while one was open for 0% of the time, Pallas kernels for 24%

profile of v9, /device:TPU:4, one launch (start us, length us, event | category | flops | bytes accessed | tf_op | source)
XLA Modules:
  0.0 101.8 jit_solution(894337620584195510)
XLA Ops:
  0.0 5.3 %shard_map.46 = (bf16[64,1024]{1,0:T(8,128)(2,1)S(1)}, bf16[64,1024]{1,0:T(8,128)(2,1)S(1)}, bf16[64,1024]{1,0:T(8,128)(2,1)S(1)}, bf16[64,1024]{1,0:T(8,128)(2,...) custom-call(s32[1]{0:T(128)} %bitcast.level_ref, ...), custom_call_target="tpu_custom_call" | custom-call | flops 2147483648 | bytes 6291456 | tf_op jit(solution)/shard_map/pallas_call | solution.py:94
  5.3 1.6 %collective-permute-start.3 = (bf16[2,512,256]{2,1,0:T(8,128)(2,1)S(1)}, bf16[2,512,256]{2,1,0:T(8,128)(2,1)S(1)}, u32[]{:S(2)}, u32[]{:S(2)}) collective-permute-start(bf16[2,512,256]{2,1,0:T(8,128)(2,1)S(1)} %get-tuple-element.35), channel_id=1, source_target_pairs={{0,2},{1,3},{2,0},{3,1},{4,6},{5,7},{6,4},{7,5},{8,10},{9,11},{10,... | collective-permute-start | bytes 1572872 | tf_op jit(solution)/shard_map/ppermute | solution.py:22
  6.9 1.5 %collective-permute-start.4 = (bf16[64,1024]{1,0:T(8,128)(2,1)S(1)}, bf16[64,1024]{1,0:T(8,128)(2,1)S(1)}, u32[]{:S(2)}, u32[]{:S(2)}) collective-permute-start(bf16[64,1024]{1,0:T(8,128)(2,1)S(1)} %get-tuple-element.37.ready_ref), channel_id=1, source_target_pairs={{0,8},{8,16},{16,24},{24,0},{1,9},{9,17},{17,25},{25,1},{2,10},{10... | collective-permute-start | bytes 393224 | tf_op jit(solution)/shard_map/ppermute | solution.py:18
  8.9 5.3 %collective-permute-done.4.arrived_ref = bf16[64,1024]{1,0:T(8,128)(2,1)S(1)} collective-permute-done((bf16[64,1024]{1,0:T(8,128)(2,1)S(1)}, bf16[64,1024]{1,0:T(8,128)(2,1)S(1)}, u32[]{:S(2)}, u32[]{:S(2)}) %collective-permute-start.4) | collective-permute-done | bytes 131104 | tf_op jit(solution)/shard_map/ppermute | solution.py:18
  17.6 4.3 %collective-permute-done.5.arrived_ref = bf16[64,1024]{1,0:T(8,128)(2,1)S(1)} collective-permute-done((bf16[64,1024]{1,0:T(8,128)(2,1)S(1)}, bf16[64,1024]{1,0:T(8,128)(2,1)S(1)}, u32[]{:S(2)}, u32[]{:S(2)}) %collective-permute-start.5) | collective-permute-done | bytes 131104 | tf_op jit(solution)/shard_map/ppermute | solution.py:18
  23.3 1.4 %collective-permute-done.1.arrived_ref = bf16[64,1024]{1,0:T(8,128)(2,1)S(1)} collective-permute-done((bf16[64,1024]{1,0:T(8,128)(2,1)S(1)}, bf16[64,1024]{1,0:T(8,128)(2,1)S(1)}, u32[]{:S(2)}, u32[]{:S(2)}) %collective-permute-start.1) | collective-permute-done | bytes 131104 | tf_op jit(solution)/shard_map/ppermute | solution.py:18
  26.1 3.1 %collective-permute-done.6.arrived_ref = bf16[64,1024]{1,0:T(8,128)(2,1)S(1)} collective-permute-done((bf16[64,1024]{1,0:T(8,128)(2,1)S(1)}, bf16[64,1024]{1,0:T(8,128)(2,1)S(1)}, u32[]{:S(2)}, u32[]{:S(2)}) %collective-permute-start.6) | collective-permute-done | bytes 131104 | tf_op jit(solution)/shard_map/ppermute | solution.py:18
  31.0 6.1 %shard_map.49.left_ref = bf16[1024,1024]{1,0:T(8,128)(2,1)S(1)} custom-call(s32[1]{0:T(128)} %bitcast.level_ref, s32[1]{0:T(128)} %bitcast.1.mine_ref, bf16[2,1024,256]{2,1,0:T(8,128)(2,1)S(1)} %bitcast.4, bf16[2,512,256]{2,1,0:T(8,128)(2,1)S(1)} %collective-permute-done.3.got_ref), custom_call_target="tpu_custom_call" | custom-call | bytes 3145728 | tf_op jit(solution)/shard_map/pallas_call | solution.py:189
  37.2 1.3 %shard_map.53.refs_1_ = bf16[64,1024]{1,0:T(8,128)(2,1)S(1)} custom-call(s32[1]{0:T(128)} %bitcast.level_ref, bf16[64,1024]{1,0:T(8,128)(2,1)S(1)} %collective-permute-done.2.arrived_ref, bf16[64,1024]{1,0:T(8,128)(2,1)S(1)} %get-tuple-element.42.ready_ref, bf16[1024,2048]{1,0:T(8,128)(2,1)S(1)} %get-tuple-element.33.joined_ref, f32[1,1024]{1,0:T(1,128)S(1)} %bitcast.10), custom_call_target="tpu_custom_call" | custom-call | flops 268435456 | bytes 4587520 | tf_op jit(solution)/shard_map/pallas_call | solution.py:142
  38.5 1.6 %collective-permute-start.10 = (bf16[64,1024]{1,0:T(8,128)(2,1)S(1)}, bf16[64,1024]{1,0:T(8,128)(2,1)S(1)}, u32[]{:S(2)}, u32[]{:S(2)}) collective-permute-start(bf16[64,1024]{1,0:T(8,128)(2,1)S(1)} %shard_map.53.refs_1_), channel_id=1, source_target_pairs={{0,2},{1,3},{2,0},{3,1},{4,6},{5,7},{6,4},{7,5},{8,10},{9,11},{10,... | collective-permute-start | bytes 393224 | tf_op jit(solution)/shard_map/ppermute | solution.py:22
  40.1 1.3 %shard_map.54.refs_2_ = bf16[64,1024]{1,0:T(8,128)(2,1)S(1)} custom-call(s32[1]{0:T(128)} %bitcast.level_ref, bf16[64,1024]{1,0:T(8,128)(2,1)S(1)} %collective-permute-done.7.arrived_ref, bf16[64,1024]{1,0:T(8,128)(2,1)S(1)} %get-tuple-element.37.ready_ref, bf16[1024,2048]{1,0:T(8,128)(2,1)S(1)} %get-tuple-element.33.joined_ref, f32[1,1024]{1,0:T(1,128)S(1)} %bitcast.11), custom_call_target="tpu_custom_call" | custom-call | flops 268435456 | bytes 4587520 | tf_op jit(solution)/shard_map/pallas_call | solution.py:142
  43.5 3.6 %collective-permute-done.9.arrived_ref = bf16[64,1024]{1,0:T(8,128)(2,1)S(1)} collective-permute-done((bf16[64,1024]{1,0:T(8,128)(2,1)S(1)}, bf16[64,1024]{1,0:T(8,128)(2,1)S(1)}, u32[]{:S(2)}, u32[]{:S(2)}) %collective-permute-start.9) | collective-permute-done | bytes 131104 | tf_op jit(solution)/shard_map/ppermute | solution.py:18
  47.2 1.3 %shard_map.55.refs_3_ = bf16[64,1024]{1,0:T(8,128)(2,1)S(1)} custom-call(s32[1]{0:T(128)} %bitcast.level_ref, bf16[64,1024]{1,0:T(8,128)(2,1)S(1)} %collective-permute-done.9.arrived_ref, bf16[64,1024]{1,0:T(8,128)(2,1)S(1)} %get-tuple-element.31.ready_ref, bf16[1024,2048]{1,0:T(8,128)(2,1)S(1)} %get-tuple-element.33.joined_ref, f32[1,1024]{1,0:T(1,128)S(1)} %bitcast.12), custom_call_target="tpu_custom_call" | custom-call | flops 268435456 | bytes 4587520 | tf_op jit(solution)/shard_map/pallas_call | solution.py:142
  52.2 2.8 %collective-permute-done.14.refs_11_ = bf16[64,1024]{1,0:T(8,128)(2,1)S(1)} collective-permute-done((bf16[64,1024]{1,0:T(8,128)(2,1)S(1)}, bf16[64,1024]{1,0:T(8,128)(2,1)S(1)}, u32[]{:S(2)}, u32[]{:S(2)}) %collective-permute-start.14) | collective-permute-done | bytes 131104 | tf_op jit(solution)/shard_map/ppermute | solution.py:22
  57.0 1.8 %collective-permute-start.18 = (bf16[64,1024]{1,0:T(8,128)(2,1)S(1)}, bf16[64,1024]{1,0:T(8,128)(2,1)S(1)}, u32[]{:S(2)}, u32[]{:S(2)}) collective-permute-start(bf16[64,1024]{1,0:T(8,128)(2,1)S(1)} %shard_map.57.refs_5_), channel_id=1, source_target_pairs={{0,2},{1,3},{2,0},{3,1},{4,6},{5,7},{6,4},{7,5},{8,10},{9,11},{10,... | collective-permute-start | bytes 393224 | tf_op jit(solution)/shard_map/ppermute | solution.py:22
  58.8 1.3 %shard_map.58.refs_6_ = bf16[64,1024]{1,0:T(8,128)(2,1)S(1)} custom-call(s32[1]{0:T(128)} %bitcast.level_ref, bf16[64,1024]{1,0:T(8,128)(2,1)S(1)} %collective-permute-done.15.arrived_ref, bf16[64,1024]{1,0:T(8,128)(2,1)S(1)} %get-tuple-element.39.ready_ref, bf16[1024,2048]{1,0:T(8,128)(2,1)S(1)} %get-tuple-element.33.joined_ref, f32[1,1024]{1,0:T(1,128)S(1)} %bitcast.15), custom_call_target="tpu_custom_call" | custom-call | flops 268435456 | bytes 4587520 | tf_op jit(solution)/shard_map/pallas_call | solution.py:142
  60.6 1.7 %collective-permute-done.18.refs_13_ = bf16[64,1024]{1,0:T(8,128)(2,1)S(1)} collective-permute-done((bf16[64,1024]{1,0:T(8,128)(2,1)S(1)}, bf16[64,1024]{1,0:T(8,128)(2,1)S(1)}, u32[]{:S(2)}, u32[]{:S(2)}) %collective-permute-start.18) | collective-permute-done | bytes 131104 | tf_op jit(solution)/shard_map/ppermute | solution.py:22
  62.4 2.2 %collective-permute-done.17.arrived_ref = bf16[64,1024]{1,0:T(8,128)(2,1)S(1)} collective-permute-done((bf16[64,1024]{1,0:T(8,128)(2,1)S(1)}, bf16[64,1024]{1,0:T(8,128)(2,1)S(1)}, u32[]{:S(2)}, u32[]{:S(2)}) %collective-permute-start.17) | collective-permute-done | bytes 131104 | tf_op jit(solution)/shard_map/ppermute | solution.py:18
  66.3 2.3 %shard_map.60.early_ref = f32[1024,1024]{1,0:T(8,128)S(1)} custom-call(bf16[1024,1024]{1,0:T(8,128)(2,1)S(1)} %shard_map.49.left_ref, bf16[64,1024]{1,0:T(8,128)(2,1)S(1)} %shard_map.52.refs_0_, bf16[64,1024]{1,0:T(8,128)(2,1)S(1)} %shard_map.53.refs_1_, bf16[64,1024]{1,0:T(8,128)(2,1)S(1)} %shard_map.54.refs_2_, bf16[64,1024]{1,0:T(8,128)(2,1)S(1)} %shard_map.55.refs_3_, ...), custom_call_target="tpu_custom_call" | custom-call | flops 1879048192 | bytes 8126464 | tf_op jit(solution)/shard_map/pallas_call | solution.py:243
  68.7 2.3 %collective-permute-done.20.refs_1_ = bf16[64,1024]{1,0:T(8,128)(2,1)S(1)} collective-permute-done((bf16[64,1024]{1,0:T(8,128)(2,1)S(1)}, bf16[64,1024]{1,0:T(8,128)(2,1)S(1)}, u32[]{:S(2)}, u32[]{:S(2)}) %collective-permute-start.20) | collective-permute-done | bytes 131104 | tf_op jit(solution)/shard_map/ppermute | solution.py:22
  71.7 2.6 %collective-permute-done.21.refs_1_ = bf16[2,2,128,1024]{3,2,1,0:T(8,128)(2,1)S(1)} collective-permute-done((bf16[2,2,128,1024]{3,2,1,0:T(8,128)(2,1)S(1)}, bf16[2,2,128,1024]{3,2,1,0:T(8,128)(2,1)S(1)}, u32[]{:S(2)}, u32[]{:S(2)}) %collective-permute-start.21) | collective-permute-done | bytes 1048608 | tf_op jit(solution)/shard_map/ppermute | solution.py:22
  74.5 2.6 %collective-permute-start.22 = (bf16[1,2,128,1024]{3,2,1,0:T(8,128)(2,1)S(1)}, bf16[1,2,128,1024]{3,2,1,0:T(8,128)(2,1)S(1)}, u32[]{:S(2)}, u32[]{:S(2)}) collective-permute-start(bf16[1,2,128,1024]{3,2,1,0:T(8,128)(2,1)S(1)} %add_convert_fusion), channel_id=1, source_target_pairs={{0,4},{1,5},{2,6},{3,7},{4,0},{5,1},{6,2},{7,3},{8,12},{9,13},{10,... | collective-permute-start | bytes 1572872 | tf_op jit(solution)/shard_map/ppermute | solution.py:18
  77.2 23.3 %collective-permute-done.22.refs_2_ = bf16[1,2,128,1024]{3,2,1,0:T(8,128)(2,1)S(1)} collective-permute-done((bf16[1,2,128,1024]{3,2,1,0:T(8,128)(2,1)S(1)}, bf16[1,2,128,1024]{3,2,1,0:T(8,128)(2,1)S(1)}, u32[]{:S(2)}, u32[]{:S(2)}) %collective-permute-start.22) | collective-permute-done | bytes 524320 | tf_op jit(solution)/shard_map/ppermute | solution.py:18
  100.5 1.3 %shard_map.62 = f32[1,128,2,1024]{3,2,1,0:T(2,128)} custom-call(f32[2,2,128,1024]{3,2,1,0:T(8,128)S(1)} %get-tuple-element.55.refs_0_, bf16[2,2,128,1024]{3,2,1,0:T(8,128)(2,1)S(1)} %collective-permute-done.21.refs_1_, bf16[1,2,128,1024]{3,2,1,0:T(8,128)(2,1)S(1)} %collective-permute-done.22.refs_2_), custom_call_target="tpu_custom_call" | custom-call | flops 786432 | bytes 2097152 | tf_op jit(solution)/shard_map/pallas_call | solution.py:278
  (44 shorter events, 19.5 us)
Async XLA Ops:
  0.0 14.2 %copy-start.1 = (f32[1,1,1024]{2,1,0:T(1,128)S(1)}, f32[1,1,1024]{2,1,0:T(1,128)}, u32[]{:S(2)}) copy-start(f32[1,1,1024]{2,1,0:T(1,128)} %factor_ref.1) | copy-start | bytes 12292
  5.3 25.7 %collective-permute-start.3 = (bf16[2,512,256]{2,1,0:T(8,128)(2,1)S(1)}, bf16[2,512,256]{2,1,0:T(8,128)(2,1)S(1)}, u32[]{:S(2)}, u32[]{:S(2)}) collective-permute-start(bf16[2,512,256]{2,1,0:T(8,128)(2,1)S(1)} %get-tuple-element.35), channel_id=1, source_target_pairs={{0,2},{1,3},{2,0},{3,1},{4,6},{5,7},{6,4},{7,5},{8,10},{9,11},{10,... | collective-permute-start | bytes 1572872 | tf_op jit(solution)/shard_map/ppermute | solution.py:22
  6.9 7.3 %collective-permute-start.4 = (bf16[64,1024]{1,0:T(8,128)(2,1)S(1)}, bf16[64,1024]{1,0:T(8,128)(2,1)S(1)}, u32[]{:S(2)}, u32[]{:S(2)}) collective-permute-start(bf16[64,1024]{1,0:T(8,128)(2,1)S(1)} %get-tuple-element.37.ready_ref), channel_id=1, source_target_pairs={{0,8},{8,16},{16,24},{24,0},{1,9},{9,17},{17,25},{25,1},{2,10},{10... | collective-permute-start | bytes 393224 | tf_op jit(solution)/shard_map/ppermute | solution.py:18
  8.4 7.8 %collective-permute-start = (bf16[64,1024]{1,0:T(8,128)(2,1)S(1)}, bf16[64,1024]{1,0:T(8,128)(2,1)S(1)}, u32[]{:S(2)}, u32[]{:S(2)}) collective-permute-start(bf16[64,1024]{1,0:T(8,128)(2,1)S(1)} %get-tuple-element.31.ready_ref), channel_id=1, source_target_pairs={{0,8},{8,16},{16,24},{24,0},{1,9},{9,17},{17,25},{25,1},{2,10},{10... | collective-permute-start | bytes 393224 | tf_op jit(solution)/shard_map/ppermute | solution.py:18
  15.5 6.4 %collective-permute-start.5 = (bf16[64,1024]{1,0:T(8,128)(2,1)S(1)}, bf16[64,1024]{1,0:T(8,128)(2,1)S(1)}, u32[]{:S(2)}, u32[]{:S(2)}) collective-permute-start(bf16[64,1024]{1,0:T(8,128)(2,1)S(1)} %shard_map.50), channel_id=1, source_target_pairs={{0,8},{8,16},{16,24},{24,0},{1,9},{9,17},{17,25},{25,1},{2,10},{10... | collective-permute-start | bytes 393224 | tf_op jit(solution)/shard_map/ppermute | solution.py:18
  17.5 7.2 %collective-permute-start.1 = (bf16[64,1024]{1,0:T(8,128)(2,1)S(1)}, bf16[64,1024]{1,0:T(8,128)(2,1)S(1)}, u32[]{:S(2)}, u32[]{:S(2)}) collective-permute-start(bf16[64,1024]{1,0:T(8,128)(2,1)S(1)} %shard_map.47), channel_id=1, source_target_pairs={{0,8},{8,16},{16,24},{24,0},{1,9},{9,17},{17,25},{25,1},{2,10},{10... | collective-permute-start | bytes 393224 | tf_op jit(solution)/shard_map/ppermute | solution.py:18
  23.2 5.9 %collective-permute-start.6 = (bf16[64,1024]{1,0:T(8,128)(2,1)S(1)}, bf16[64,1024]{1,0:T(8,128)(2,1)S(1)}, u32[]{:S(2)}, u32[]{:S(2)}) collective-permute-start(bf16[64,1024]{1,0:T(8,128)(2,1)S(1)} %shard_map.51), channel_id=1, source_target_pairs={{0,8},{8,16},{16,24},{24,0},{1,9},{9,17},{17,25},{25,1},{2,10},{10... | collective-permute-start | bytes 393224 | tf_op jit(solution)/shard_map/ppermute | solution.py:18
  26.0 11.2 %collective-permute-start.2 = (bf16[64,1024]{1,0:T(8,128)(2,1)S(1)}, bf16[64,1024]{1,0:T(8,128)(2,1)S(1)}, u32[]{:S(2)}, u32[]{:S(2)}) collective-permute-start(bf16[64,1024]{1,0:T(8,128)(2,1)S(1)} %shard_map.48), channel_id=1, source_target_pairs={{0,8},{8,16},{16,24},{24,0},{1,9},{9,17},{17,25},{25,1},{2,10},{10... | collective-permute-start | bytes 393224 | tf_op jit(solution)/shard_map/ppermute | solution.py:18
  30.4 9.7 %collective-permute-start.8 = (bf16[64,1024]{1,0:T(8,128)(2,1)S(1)}, bf16[64,1024]{1,0:T(8,128)(2,1)S(1)}, u32[]{:S(2)}, u32[]{:S(2)}) collective-permute-start(bf16[64,1024]{1,0:T(8,128)(2,1)S(1)} %shard_map.52.refs_0_), channel_id=1, source_target_pairs={{0,2},{1,3},{2,0},{3,1},{4,6},{5,7},{6,4},{7,5},{8,10},{9,11},{10,... | collective-permute-start | bytes 393224 | tf_op jit(solution)/shard_map/ppermute | solution.py:22
  31.0 9.1 %collective-permute-start.7 = (bf16[64,1024]{1,0:T(8,128)(2,1)S(1)}, bf16[64,1024]{1,0:T(8,128)(2,1)S(1)}, u32[]{:S(2)}, u32[]{:S(2)}) collective-permute-start(bf16[64,1024]{1,0:T(8,128)(2,1)S(1)} %shard_map.52.refs_0_), channel_id=1, source_target_pairs={{0,8},{8,16},{16,24},{24,0},{1,9},{9,17},{17,25},{25,1},{2,10},{10... | collective-permute-start | bytes 393224 | tf_op jit(solution)/shard_map/ppermute | solution.py:18
  38.5 5.0 %collective-permute-start.10 = (bf16[64,1024]{1,0:T(8,128)(2,1)S(1)}, bf16[64,1024]{1,0:T(8,128)(2,1)S(1)}, u32[]{:S(2)}, u32[]{:S(2)}) collective-permute-start(bf16[64,1024]{1,0:T(8,128)(2,1)S(1)} %shard_map.53.refs_1_), channel_id=1, source_target_pairs={{0,2},{1,3},{2,0},{3,1},{4,6},{5,7},{6,4},{7,5},{8,10},{9,11},{10,... | collective-permute-start | bytes 393224 | tf_op jit(solution)/shard_map/ppermute | solution.py:22
  40.1 7.1 %collective-permute-start.9 = (bf16[64,1024]{1,0:T(8,128)(2,1)S(1)}, bf16[64,1024]{1,0:T(8,128)(2,1)S(1)}, u32[]{:S(2)}, u32[]{:S(2)}) collective-permute-start(bf16[64,1024]{1,0:T(8,128)(2,1)S(1)} %shard_map.53.refs_1_), channel_id=1, source_target_pairs={{0,8},{8,16},{16,24},{24,0},{1,9},{9,17},{17,25},{25,1},{2,10},{10... | collective-permute-start | bytes 393224 | tf_op jit(solution)/shard_map/ppermute | solution.py:18
  41.4 7.3 %collective-permute-start.12 = (bf16[64,1024]{1,0:T(8,128)(2,1)S(1)}, bf16[64,1024]{1,0:T(8,128)(2,1)S(1)}, u32[]{:S(2)}, u32[]{:S(2)}) collective-permute-start(bf16[64,1024]{1,0:T(8,128)(2,1)S(1)} %shard_map.54.refs_2_), channel_id=1, source_target_pairs={{0,2},{1,3},{2,0},{3,1},{4,6},{5,7},{6,4},{7,5},{8,10},{9,11},{10,... | collective-permute-start | bytes 393224 | tf_op jit(solution)/shard_map/ppermute | solution.py:22
  42.0 8.0 %collective-permute-start.11 = (bf16[64,1024]{1,0:T(8,128)(2,1)S(1)}, bf16[64,1024]{1,0:T(8,128)(2,1)S(1)}, u32[]{:S(2)}, u32[]{:S(2)}) collective-permute-start(bf16[64,1024]{1,0:T(8,128)(2,1)S(1)} %shard_map.54.refs_2_), channel_id=1, source_target_pairs={{0,8},{8,16},{16,24},{24,0},{1,9},{9,17},{17,25},{25,1},{2,10},{10... | collective-permute-start | bytes 393224 | tf_op jit(solution)/shard_map/ppermute | solution.py:18
  48.5 6.4 %collective-permute-start.14 = (bf16[64,1024]{1,0:T(8,128)(2,1)S(1)}, bf16[64,1024]{1,0:T(8,128)(2,1)S(1)}, u32[]{:S(2)}, u32[]{:S(2)}) collective-permute-start(bf16[64,1024]{1,0:T(8,128)(2,1)S(1)} %shard_map.55.refs_3_), channel_id=1, source_target_pairs={{0,2},{1,3},{2,0},{3,1},{4,6},{5,7},{6,4},{7,5},{8,10},{9,11},{10,... | collective-permute-start | bytes 393224 | tf_op jit(solution)/shard_map/ppermute | solution.py:22
  48.6 7.1 %collective-permute-start.13 = (bf16[64,1024]{1,0:T(8,128)(2,1)S(1)}, bf16[64,1024]{1,0:T(8,128)(2,1)S(1)}, u32[]{:S(2)}, u32[]{:S(2)}) collective-permute-start(bf16[64,1024]{1,0:T(8,128)(2,1)S(1)} %shard_map.55.refs_3_), channel_id=1, source_target_pairs={{0,8},{8,16},{16,24},{24,0},{1,9},{9,17},{17,25},{25,1},{2,10},{10... | collective-permute-start | bytes 393224 | tf_op jit(solution)/shard_map/ppermute | solution.py:18
  51.3 7.5 %collective-permute-start.16 = (bf16[64,1024]{1,0:T(8,128)(2,1)S(1)}, bf16[64,1024]{1,0:T(8,128)(2,1)S(1)}, u32[]{:S(2)}, u32[]{:S(2)}) collective-permute-start(bf16[64,1024]{1,0:T(8,128)(2,1)S(1)} %shard_map.56.refs_4_), channel_id=1, source_target_pairs={{0,2},{1,3},{2,0},{3,1},{4,6},{5,7},{6,4},{7,5},{8,10},{9,11},{10,... | collective-permute-start | bytes 393224 | tf_op jit(solution)/shard_map/ppermute | solution.py:22
  52.0 6.8 %collective-permute-start.15 = (bf16[64,1024]{1,0:T(8,128)(2,1)S(1)}, bf16[64,1024]{1,0:T(8,128)(2,1)S(1)}, u32[]{:S(2)}, u32[]{:S(2)}) collective-permute-start(bf16[64,1024]{1,0:T(8,128)(2,1)S(1)} %shard_map.56.refs_4_), channel_id=1, source_target_pairs={{0,8},{8,16},{16,24},{24,0},{1,9},{9,17},{17,25},{25,1},{2,10},{10... | collective-permute-start | bytes 393224 | tf_op jit(solution)/shard_map/ppermute | solution.py:18
  57.0 5.4 %collective-permute-start.18 = (bf16[64,1024]{1,0:T(8,128)(2,1)S(1)}, bf16[64,1024]{1,0:T(8,128)(2,1)S(1)}, u32[]{:S(2)}, u32[]{:S(2)}) collective-permute-start(bf16[64,1024]{1,0:T(8,128)(2,1)S(1)} %shard_map.57.refs_5_), channel_id=1, source_target_pairs={{0,2},{1,3},{2,0},{3,1},{4,6},{5,7},{6,4},{7,5},{8,10},{9,11},{10,... | collective-permute-start | bytes 393224 | tf_op jit(solution)/shard_map/ppermute | solution.py:22
  58.8 5.9 %collective-permute-start.17 = (bf16[64,1024]{1,0:T(8,128)(2,1)S(1)}, bf16[64,1024]{1,0:T(8,128)(2,1)S(1)}, u32[]{:S(2)}, u32[]{:S(2)}) collective-permute-start(bf16[64,1024]{1,0:T(8,128)(2,1)S(1)} %shard_map.57.refs_5_), channel_id=1, source_target_pairs={{0,8},{8,16},{16,24},{24,0},{1,9},{9,17},{17,25},{25,1},{2,10},{10... | collective-permute-start | bytes 393224 | tf_op jit(solution)/shard_map/ppermute | solution.py:18
  60.1 8.6 %collective-permute-start.19 = (bf16[64,1024]{1,0:T(8,128)(2,1)S(1)}, bf16[64,1024]{1,0:T(8,128)(2,1)S(1)}, u32[]{:S(2)}, u32[]{:S(2)}) collective-permute-start(bf16[64,1024]{1,0:T(8,128)(2,1)S(1)} %shard_map.58.refs_6_), channel_id=1, source_target_pairs={{0,2},{1,3},{2,0},{3,1},{4,6},{5,7},{6,4},{7,5},{8,10},{9,11},{10,... | collective-permute-start | bytes 393224 | tf_op jit(solution)/shard_map/ppermute | solution.py:22
  65.9 5.0 %collective-permute-start.20 = (bf16[64,1024]{1,0:T(8,128)(2,1)S(1)}, bf16[64,1024]{1,0:T(8,128)(2,1)S(1)}, u32[]{:S(2)}, u32[]{:S(2)}) collective-permute-start(bf16[64,1024]{1,0:T(8,128)(2,1)S(1)} %shard_map.59.refs_7_), channel_id=1, source_target_pairs={{0,2},{1,3},{2,0},{3,1},{4,6},{5,7},{6,4},{7,5},{8,10},{9,11},{10,... | collective-permute-start | bytes 393224 | tf_op jit(solution)/shard_map/ppermute | solution.py:22
  71.7 2.7 %collective-permute-start.21 = (bf16[2,2,128,1024]{3,2,1,0:T(8,128)(2,1)S(1)}, bf16[2,2,128,1024]{3,2,1,0:T(8,128)(2,1)S(1)}, u32[]{:S(2)}, u32[]{:S(2)}) collective-permute-start(bf16[2,2,128,1024]{3,2,1,0:T(8,128)(2,1)S(1)} %get-tuple-element.56), channel_id=1, source_target_pairs={{0,1},{1,0},{2,3},{3,2},{4,5},{5,4},{6,7},{7,6},{8,9},{9,8},{10,11... | collective-permute-start | bytes 3145736 | tf_op jit(solution)/shard_map/ppermute | solution.py:22
  74.5 25.9 %collective-permute-start.22 = (bf16[1,2,128,1024]{3,2,1,0:T(8,128)(2,1)S(1)}, bf16[1,2,128,1024]{3,2,1,0:T(8,128)(2,1)S(1)}, u32[]{:S(2)}, u32[]{:S(2)}) collective-permute-start(bf16[1,2,128,1024]{3,2,1,0:T(8,128)(2,1)S(1)} %add_convert_fusion), channel_id=1, source_target_pairs={{0,4},{1,5},{2,6},{3,7},{4,0},{5,1},{6,2},{7,3},{8,12},{9,13},{10,... | collective-permute-start | bytes 1572872 | tf_op jit(solution)/shard_map/ppermute | solution.py:18
  (1 other events, 6.3 us)

commit v10 on v8

--- a/solution.py
+++ b/solution.py
@@ -27,10 +27,22 @@
     return lax.div(mine, 4), lax.rem(lax.div(mine, 2), 2), lax.rem(mine, 2)
 
 
+def start_panels(part, real, imag, right, factor, outs, columns):
+    dot = functools.partial(jnp.dot, preferred_element_type=jnp.float32)
+    shots = right.shape[1] // 2
+    first, second = dot(real, right), dot(imag, right)
+    out_real = ((first[:, :shots] - second[:, shots:]).T * factor).astype(jnp.bfloat16)
+    out_imag = ((first[:, shots:] + second[:, :shots]).T * factor).astype(jnp.bfloat16)
+    for chunk, out in enumerate(outs):
+        lo = chunk * part
+        out[:part, columns] = out_real[lo : lo + part]
+        out[part:, columns] = out_imag[lo : lo + part]
+
+
 def first_kernel(part, level_ref, mine_ref, source_ref, weight_ref, factor_ref, upward_ref, *refs):
-    *outs, joined_ref, asked_ref, source, factor, sem, sems, asked_sems = refs
+    *outs, joined_ref, later_ref, asked_ref, right, factor, sem, sems, asked_sems = refs
     width = joined_ref.shape[0]
-    shots = source.shape[2]
+    shots = later_ref.shape[1] // 2
     blocks = sems.shape[0]
     wide = width // blocks
     groups = asked_sems.shape[0]
@@ -46,72 +58,88 @@
             for half in range(2)
         ]
 
-    begin = [
-        pltpu.make_async_copy(source_ref.at[0], source, sem.at[0]),
-        pltpu.make_async_copy(factor_ref.at[0], factor, sem.at[1]),
-    ]
-    asked = []
+    def columns_of(start, to_ref, first_sem):
+        return [
+            pltpu.make_async_copy(
+                source_ref.at[0, half, :, pl.ds(start, shots)],
+                to_ref.at[:, pl.ds(half * shots, shots)],
+                sem.at[first_sem + half],
+            )
+            for half in range(2)
+        ]
+
+    begin = columns_of(0, right, 0) + [pltpu.make_async_copy(factor_ref.at[0], factor, sem.at[4])]
+    rest = columns_of(shots, later_ref, 2)
     for k in range(groups):
         row = pl.multiple_of((2 * k + 1 - place) * tall, tall)
-        asked.append(
+        rest.append(
             pltpu.make_async_copy(
                 upward_ref.at[0, 0, :, pl.ds(row, tall)], asked_ref.at[:, pl.ds(k * tall, tall)], asked_sems.at[k]
             )
         )
-    for copy in begin + copies(0):
+    for copy in begin:
+        copy.start()
+    for n in range(blocks):
+        for copy in copies(n):
+            copy.start()
+    for copy in rest:
         copy.start()
     for copy in begin:
         copy.wait()
-    for n in range(1, blocks):
-        for copy in copies(n):
-            copy.start()
-    for copy in asked:
-        copy.start()
-    dot = functools.partial(jnp.dot, preferred_element_type=jnp.float32)
     for n in range(blocks):
         for copy in copies(n):
             copy.wait()
         columns = slice(n * wide, (n + 1) * wide)
         real, imag = joined_ref[columns, :width], joined_ref[columns, width:]
-        out_real = dot(real, source[0]) - dot(imag, source[1])
-        out_imag = dot(real, source[1]) + dot(imag, source[0])
-        out_real = (out_real.T * factor[:, columns]).astype(jnp.bfloat16)
-        out_imag = (out_imag.T * factor[:, columns]).astype(jnp.bfloat16)
-        for chunk in range(len(outs)):
-            lo = chunk * part
-            outs[chunk][:part, columns] = out_real[lo : lo + part]
-            outs[chunk][part:, columns] = out_imag[lo : lo + part]
-    for copy in asked:
+        start_panels(part, real, imag, right[...], factor[:, columns], outs, columns)
+    for copy in rest:
         copy.wait()
 
 
 def first_advance(level, mine, source, propagator, transmission, upgoing, part, groups):
     width = propagator.shape[3]
     shots = source.shape[3]
-    chunks = shots // part
+    chunks = shots // 2 // part
     whole = pl.BlockSpec(memory_space=pltpu.VMEM)
     pinned = [pltpu.with_memory_space_constraint(x, pltpu.HBM) for x in (source, propagator, transmission, upgoing)]
     return pl.pallas_call(
         functools.partial(first_kernel, part),
         in_specs=[pl.BlockSpec(memory_space=pltpu.SMEM)] * 2 + [pl.BlockSpec(memory_space=pltpu.HBM)] * 4,
-        out_specs=[whole] * (chunks + 2),
+        out_specs=[whole] * (chunks + 3),
         out_shape=[jax.ShapeDtypeStruct((2 * part, width), jnp.bfloat16)] * chunks
         + [
             pltpu.VMEM((width, 2 * width), jnp.bfloat16),
+            jax.ShapeDtypeStruct((width, shots), jnp.bfloat16),
             jax.ShapeDtypeStruct((2, width // 2, shots), jnp.bfloat16),
         ],
         scratch_shapes=[
-            pltpu.VMEM((2, width, shots), jnp.bfloat16),
+            pltpu.VMEM((width, shots), jnp.bfloat16),
             pltpu.VMEM((1, width), jnp.float32),
-            pltpu.SemaphoreType.DMA((2,)),
+            pltpu.SemaphoreType.DMA((5,)),
             pltpu.SemaphoreType.DMA((4, 2)),
             pltpu.SemaphoreType.DMA((groups,)),
         ],
         compiler_params=pltpu.CompilerParams(vmem_limit_bytes=LIMIT),
         cost_estimate=pl.CostEstimate(
-            flops=8 * width * width * shots, bytes_accessed=4 * width * (width + 2 * shots), transcendentals=0
+            flops=4 * width * width * shots, bytes_accessed=4 * width * (width + 2 * shots), transcendentals=0
         ),
     )(level, mine, *pinned)
+
+
+def second_kernel(part, joined_ref, right_ref, factor_ref, *outs):
+    width = joined_ref.shape[0]
+    wide = width // 4
+    for n in range(4):
+        columns = slice(n * wide, (n + 1) * wide)
+        real, imag = joined_ref[columns, :width], joined_ref[columns, width:]
+        start_panels(part, real, imag, right_ref[...], factor_ref[:, columns], outs, columns)
+
+
+def second_advance(joined, right, factor, part):
+    width, shots = right.shape
+    outs = [jax.ShapeDtypeStruct((2 * part, width), jnp.bfloat16)] * (shots // 2 // part)
+    joined = pltpu.with_memory_space_constraint(joined, pltpu.VMEM)
+    return whole_call(functools.partial(second_kernel, part), (joined, right, factor), outs, 4 * width * width * shots)
 
 
 def advance_kernel(level_ref, arrived_ref, ready_ref, joined_ref, factor_ref, out_ref, both):
@@ -275,17 +303,8 @@
 
 def last_sum(parts, scale):
     rows, width = parts[0].shape[2:]
-    return pl.pallas_call(
-        functools.partial(last_kernel, scale),
-        grid=(2,),
-        in_specs=[pl.BlockSpec((1, 2, rows // 2, width), lambda n: (0, 0, n, 0)) for _ in parts],
-        out_specs=pl.BlockSpec((1, rows // 2, 2, width), lambda n: (0, n, 0, 0)),
-        out_shape=jax.ShapeDtypeStruct((1, rows, 2, width), jnp.float32),
-        compiler_params=pltpu.CompilerParams(vmem_limit_bytes=LIMIT),
-        cost_estimate=pl.CostEstimate(
-            flops=2 * len(parts) * rows * width, bytes_accessed=16 * rows * width, transcendentals=0
-        ),
-    )(*parts)
+    out = jax.ShapeDtypeStruct((1, rows, 2, width), jnp.float32)
+    return whole_call(functools.partial(last_kernel, scale), parts, [out], 2 * len(parts) * rows * width)[0]
 
 
 def shards(source, propagator, transmission, upgoing):
@@ -299,7 +318,8 @@
     rows = width // freqs
     part = shots // CHUNKS
     level, mine = (lax.axis_index(axis).astype(jnp.int32).reshape(1) for axis in ("depth", "freq"))
-    *ready, joined, asked = first_advance(level, mine, source, propagator, transmission, upgoing, part, groups)
+    *ready, joined, later, asked = first_advance(level, mine, source, propagator, transmission, upgoing, part, groups)
+    ready += second_advance(joined, later, factor, part)
     got = swapped(asked, "freq", 2)
     left = operand(level, mine, upward, got, rows, part, levels)
 

time: 95.1 us -> 94.7 us (level)
  waiting for transfers between devices: 58.4 us -> 57.2 us
    pallas_call x2 -> x4, Pallas kernels: 2.5 us -> 5.16 us  [whole_call(): pl.pallas_call(kernel, in_specs=[whole] * len(args), out_specs=[whole] *...]
    pallas_call x1 -> x0, Pallas kernels: 1.32 us -> none  [last_sum(): pl.pallas_call(functools.partial(last_kernel, scale), grid=(2,), in_specs...]
    ppermute x9, waiting for transfers between devices: 49.1 us -> 47.9 us  [ring(): lax.ppermute(block, axis, [(i, (i + distance) % size) for i in range(size)])]
  transfers between devices with their start and end apart: 15 -> 15, of which waited for: 13 -> 13; matrix products, arithmetic and copies ran while one was open for 0% -> 0% of each run, Pallas kernels for 14% -> 16%
where the time goes in v10:
time: 94.7 us; the launch traced here: 94.5 us
  waiting for transfers between devices  57.2 us (60%)
  Pallas kernels  21.9 us (23%)
  starting transfers between devices  15.1 us (16%)
    ppermute x9, waiting for transfers between devices, ring(): lax.ppermute(block, axis, [(i, (i + distance) % size) for i in range(size)])  47.9 us
    pallas_call x8, Pallas kernels, advance(): pl.pallas_call(advance_kernel, in_specs=[pl.BlockSpec(memory_space=pltpu....  10.9 us
    ppermute x6, waiting for transfers between devices, swapped(): lax.ppermute(block, axis, [(i, i ^ bit) for i in range(lax.axis_size(axis...  9.27 us
    ppermute x6, starting transfers between devices, swapped(): lax.ppermute(block, axis, [(i, i ^ bit) for i in range(lax.axis_size(axis...  8.94 us
    ppermute x9, starting transfers between devices, ring(): lax.ppermute(block, axis, [(i, (i + distance) % size) for i in range(size)])  6.19 us
    pallas_call x4, Pallas kernels, whole_call(): pl.pallas_call(kernel, in_specs=[whole] * len(args), out_specs=[whole] *...  5.16 us
    pallas_call x1, Pallas kernels, first_advance(): pl.pallas_call(functools.partial(first_kernel, part), in_specs=[pl.BlockS...  4.72 us
  transfers between devices with their start and end apart: 15, of which 13 were waited for; matrix products, arithmetic and copies ran while one was open for 0% of the time, Pallas kernels for 16%

profile of v10, /device:TPU:4, one launch (start us, length us, event | category | flops | bytes accessed | tf_op | source)
XLA Modules:
  0.0 94.5 jit_solution(7477464506380057918)
XLA Ops:
  0.0 4.7 %shard_map.46 = (bf16[128,1024]{1,0:T(8,128)(2,1)S(1)}, bf16[128,1024]{1,0:T(8,128)(2,1)S(1)}, bf16[1024,2048]{1,0:T(8,128)(2,1)S(1)}, bf16[1024,256]{1,0:T(8,128)(2,1)S(1)}, bf16[2,512,256]{2,1,0:T(8,128)(2,1)S(1)}) custom-call(s32[1]{0:T(128)} %bitcast.level_ref, s32[1]{0:T(128)} %bitcast.1.mine_ref, bf16[1,2,1024,256]{3,2,1,0:T(8,128)(2,1)} %source_ref.1, ...), custom_call_target="tpu_custom_call" | custom-call | flops 1073741824 | bytes 6291456 | tf_op jit(solution)/shard_map/pallas_call | solution.py:105
  4.7 1.5 %collective-permute-start.3 = (bf16[128,1024]{1,0:T(8,128)(2,1)S(1)}, bf16[128,1024]{1,0:T(8,128)(2,1)S(1)}, u32[]{:S(2)}, u32[]{:S(2)}) collective-permute-start(bf16[128,1024]{1,0:T(8,128)(2,1)S(1)} %get-tuple-element.26.ready_ref), channel_id=1, source_target_pairs={{0,8},{8,16},{16,24},{24,0},{1,9},{9,17},{17,25},{25,1},{2,10},{10... | collective-permute-start | bytes 786440 | tf_op jit(solution)/shard_map/ppermute | solution.py:18
  6.3 2.0 %collective-permute-start.2 = (bf16[2,512,256]{2,1,0:T(8,128)(2,1)S(1)}, bf16[2,512,256]{2,1,0:T(8,128)(2,1)S(1)}, u32[]{:S(2)}, u32[]{:S(2)}) collective-permute-start(bf16[2,512,256]{2,1,0:T(8,128)(2,1)S(1)} %get-tuple-element.24), channel_id=1, source_target_pairs={{0,2},{1,3},{2,0},{3,1},{4,6},{5,7},{6,4},{7,5},{8,10},{9,11},{10,... | collective-permute-start | bytes 1572872 | tf_op jit(solution)/shard_map/ppermute | solution.py:22
  8.3 1.3 %shard_map.47 = (bf16[128,1024]{1,0:T(8,128)(2,1)S(1)}, bf16[128,1024]{1,0:T(8,128)(2,1)S(1)}) custom-call(bf16[1024,2048]{1,0:T(8,128)(2,1)S(1)} %get-tuple-element.21.joined_ref, bf16[1024,256]{1,0:T(8,128)(2,1)S(1)} %get-tuple-element.22.right_ref, f32[1,1024]{1,0:T(1,128)S(1)} %bitcast.5), custom_call_target="tpu_custom_call" | custom-call | flops 1073741824 | bytes 5246976 | tf_op jit(solution)/shard_map/pallas_call | solution.py:271
  9.7 5.2 %collective-permute-done.3.arrived_ref = bf16[128,1024]{1,0:T(8,128)(2,1)S(1)} collective-permute-done((bf16[128,1024]{1,0:T(8,128)(2,1)S(1)}, bf16[128,1024]{1,0:T(8,128)(2,1)S(1)}, u32[]{:S(2)}, u32[]{:S(2)}) %collective-permute-start.3) | collective-permute-done | bytes 262176 | tf_op jit(solution)/shard_map/ppermute | solution.py:18
  14.9 1.3 %shard_map.50 = bf16[128,1024]{1,0:T(8,128)(2,1)S(1)} custom-call(s32[1]{0:T(128)} %bitcast.level_ref, bf16[128,1024]{1,0:T(8,128)(2,1)S(1)} %collective-permute-done.3.arrived_ref, bf16[128,1024]{1,0:T(8,128)(2,1)S(1)} %get-tuple-element.27.ready_ref, bf16[1024,2048]{1,0:T(8,128)(2,1)S(1)} %get-tuple-element.21.joined_ref, f32[1,1024]{1,0:T(1,128)S(1)} %bitcast.6), custom_call_target="tpu_custom_call" | custom-call | flops 536870912 | bytes 4980736 | tf_op jit(solution)/shard_map/pallas_call | solution.py:170
  16.9 3.6 %collective-permute-done.arrived_ref = bf16[128,1024]{1,0:T(8,128)(2,1)S(1)} collective-permute-done((bf16[128,1024]{1,0:T(8,128)(2,1)S(1)}, bf16[128,1024]{1,0:T(8,128)(2,1)S(1)}, u32[]{:S(2)}, u32[]{:S(2)}) %collective-permute-start) | collective-permute-done | bytes 262176 | tf_op jit(solution)/shard_map/ppermute | solution.py:18
  22.5 3.9 %collective-permute-done.4.arrived_ref = bf16[128,1024]{1,0:T(8,128)(2,1)S(1)} collective-permute-done((bf16[128,1024]{1,0:T(8,128)(2,1)S(1)}, bf16[128,1024]{1,0:T(8,128)(2,1)S(1)}, u32[]{:S(2)}, u32[]{:S(2)}) %collective-permute-start.4) | collective-permute-done | bytes 262176 | tf_op jit(solution)/shard_map/ppermute | solution.py:18
  26.4 1.3 %shard_map.51 = bf16[128,1024]{1,0:T(8,128)(2,1)S(1)} custom-call(s32[1]{0:T(128)} %bitcast.level_ref, bf16[128,1024]{1,0:T(8,128)(2,1)S(1)} %collective-permute-done.4.arrived_ref, bf16[128,1024]{1,0:T(8,128)(2,1)S(1)} %get-tuple-element.26.ready_ref, bf16[1024,2048]{1,0:T(8,128)(2,1)S(1)} %get-tuple-element.21.joined_ref, f32[1,1024]{1,0:T(1,128)S(1)} %bitcast.8), custom_call_target="tpu_custom_call" | custom-call | flops 536870912 | bytes 4980736 | tf_op jit(solution)/shard_map/pallas_call | solution.py:170
  29.2 2.8 %collective-permute-done.1.arrived_ref = bf16[128,1024]{1,0:T(8,128)(2,1)S(1)} collective-permute-done((bf16[128,1024]{1,0:T(8,128)(2,1)S(1)}, bf16[128,1024]{1,0:T(8,128)(2,1)S(1)}, u32[]{:S(2)}, u32[]{:S(2)}) %collective-permute-start.1) | collective-permute-done | bytes 262176 | tf_op jit(solution)/shard_map/ppermute | solution.py:18
  33.7 4.3 %collective-permute-done.5.arrived_ref = bf16[128,1024]{1,0:T(8,128)(2,1)S(1)} collective-permute-done((bf16[128,1024]{1,0:T(8,128)(2,1)S(1)}, bf16[128,1024]{1,0:T(8,128)(2,1)S(1)}, u32[]{:S(2)}, u32[]{:S(2)}) %collective-permute-start.5) | collective-permute-done | bytes 262176 | tf_op jit(solution)/shard_map/ppermute | solution.py:18
  38.0 1.3 %shard_map.52.refs_0_ = bf16[128,1024]{1,0:T(8,128)(2,1)S(1)} custom-call(s32[1]{0:T(128)} %bitcast.level_ref, bf16[128,1024]{1,0:T(8,128)(2,1)S(1)} %collective-permute-done.5.arrived_ref, bf16[128,1024]{1,0:T(8,128)(2,1)S(1)} %get-tuple-element.27.ready_ref, bf16[1024,2048]{1,0:T(8,128)(2,1)S(1)} %get-tuple-element.21.joined_ref, f32[1,1024]{1,0:T(1,128)S(1)} %bitcast.10), custom_call_target="tpu_custom_call" | custom-call | flops 536870912 | bytes 4980736 | tf_op jit(solution)/shard_map/pallas_call | solution.py:170
  39.3 1.6 %collective-permute-start.8 = (bf16[128,1024]{1,0:T(8,128)(2,1)S(1)}, bf16[128,1024]{1,0:T(8,128)(2,1)S(1)}, u32[]{:S(2)}, u32[]{:S(2)}) collective-permute-start(bf16[128,1024]{1,0:T(8,128)(2,1)S(1)} %shard_map.52.refs_0_), channel_id=1, source_target_pairs={{0,2},{1,3},{2,0},{3,1},{4,6},{5,7},{6,4},{7,5},{8,10},{9,11},{10,... | collective-permute-start | bytes 786440 | tf_op jit(solution)/shard_map/ppermute | solution.py:22
  41.0 1.8 %collective-permute-done.6.arrived_ref = bf16[128,1024]{1,0:T(8,128)(2,1)S(1)} collective-permute-done((bf16[128,1024]{1,0:T(8,128)(2,1)S(1)}, bf16[128,1024]{1,0:T(8,128)(2,1)S(1)}, u32[]{:S(2)}, u32[]{:S(2)}) %collective-permute-start.6) | collective-permute-done | bytes 262176 | tf_op jit(solution)/shard_map/ppermute | solution.py:18
  44.2 2.4 %collective-permute-start.10 = (bf16[128,1024]{1,0:T(8,128)(2,1)S(1)}, bf16[128,1024]{1,0:T(8,128)(2,1)S(1)}, u32[]{:S(2)}, u32[]{:S(2)}) collective-permute-start(bf16[128,1024]{1,0:T(8,128)(2,1)S(1)} %shard_map.54.refs_1_), channel_id=1, source_target_pairs={{0,2},{1,3},{2,0},{3,1},{4,6},{5,7},{6,4},{7,5},{8,10},{9,11},{10,... | collective-permute-start | bytes 786440 | tf_op jit(solution)/shard_map/ppermute | solution.py:22
  47.4 2.7 %collective-permute-done.7.arrived_ref = bf16[128,1024]{1,0:T(8,128)(2,1)S(1)} collective-permute-done((bf16[128,1024]{1,0:T(8,128)(2,1)S(1)}, bf16[128,1024]{1,0:T(8,128)(2,1)S(1)}, u32[]{:S(2)}, u32[]{:S(2)}) %collective-permute-start.7) | collective-permute-done | bytes 262176 | tf_op jit(solution)/shard_map/ppermute | solution.py:18
  53.8 1.5 %shard_map.56.refs_3_ = bf16[128,1024]{1,0:T(8,128)(2,1)S(1)} custom-call(s32[1]{0:T(128)} %bitcast.level_ref, bf16[128,1024]{1,0:T(8,128)(2,1)S(1)} %collective-permute-done.9.arrived_ref, bf16[128,1024]{1,0:T(8,128)(2,1)S(1)} %get-tuple-element.20.ready_ref, bf16[1024,2048]{1,0:T(8,128)(2,1)S(1)} %get-tuple-element.21.joined_ref, f32[1,1024]{1,0:T(1,128)S(1)} %bitcast.13), custom_call_target="tpu_custom_call" | custom-call | flops 536870912 | bytes 4980736 | tf_op jit(solution)/shard_map/pallas_call | solution.py:170
  55.4 1.6 %collective-permute-start.12 = (bf16[128,1024]{1,0:T(8,128)(2,1)S(1)}, bf16[128,1024]{1,0:T(8,128)(2,1)S(1)}, u32[]{:S(2)}, u32[]{:S(2)}) collective-permute-start(bf16[128,1024]{1,0:T(8,128)(2,1)S(1)} %shard_map.56.refs_3_), channel_id=1, source_target_pairs={{0,2},{1,3},{2,0},{3,1},{4,6},{5,7},{6,4},{7,5},{8,10},{9,11},{10,... | collective-permute-start | bytes 786440 | tf_op jit(solution)/shard_map/ppermute | solution.py:22
  57.0 1.8 %shard_map.57.early_ref = f32[1024,1024]{1,0:T(8,128)S(1)} custom-call(bf16[1024,1024]{1,0:T(8,128)(2,1)S(1)} %shard_map.49.left_ref, bf16[128,1024]{1,0:T(8,128)(2,1)S(1)} %shard_map.52.refs_0_, bf16[128,1024]{1,0:T(8,128)(2,1)S(1)} %shard_map.54.refs_1_, bf16[128,1024]{1,0:T(8,128)(2,1)S(1)} %shard_map.55.refs_2_, ...), custom_call_target="tpu_custom_call" | custom-call | flops 1610612736 | bytes 7864320 | tf_op jit(solution)/shard_map/pallas_call | solution.py:271
  58.8 1.9 %collective-permute-done.11.refs_0_ = bf16[128,1024]{1,0:T(8,128)(2,1)S(1)} collective-permute-done((bf16[128,1024]{1,0:T(8,128)(2,1)S(1)}, bf16[128,1024]{1,0:T(8,128)(2,1)S(1)}, u32[]{:S(2)}, u32[]{:S(2)}) %collective-permute-start.11) | collective-permute-done | bytes 262176 | tf_op jit(solution)/shard_map/ppermute | solution.py:22
  60.7 2.8 %collective-permute-done.12.refs_1_ = bf16[128,1024]{1,0:T(8,128)(2,1)S(1)} collective-permute-done((bf16[128,1024]{1,0:T(8,128)(2,1)S(1)}, bf16[128,1024]{1,0:T(8,128)(2,1)S(1)}, u32[]{:S(2)}, u32[]{:S(2)}) %collective-permute-start.12) | collective-permute-done | bytes 262176 | tf_op jit(solution)/shard_map/ppermute | solution.py:22
  64.3 2.6 %collective-permute-done.13.refs_1_ = bf16[2,2,128,1024]{3,2,1,0:T(8,128)(2,1)S(1)} collective-permute-done((bf16[2,2,128,1024]{3,2,1,0:T(8,128)(2,1)S(1)}, bf16[2,2,128,1024]{3,2,1,0:T(8,128)(2,1)S(1)}, u32[]{:S(2)}, u32[]{:S(2)}) %collective-permute-start.13) | collective-permute-done | bytes 1048608 | tf_op jit(solution)/shard_map/ppermute | solution.py:22
  67.1 2.7 %collective-permute-start.14 = (bf16[1,2,128,1024]{3,2,1,0:T(8,128)(2,1)S(1)}, bf16[1,2,128,1024]{3,2,1,0:T(8,128)(2,1)S(1)}, u32[]{:S(2)}, u32[]{:S(2)}) collective-permute-start(bf16[1,2,128,1024]{3,2,1,0:T(8,128)(2,1)S(1)} %add_convert_fusion), channel_id=1, source_target_pairs={{0,4},{1,5},{2,6},{3,7},{4,0},{5,1},{6,2},{7,3},{8,12},{9,13},{10,... | collective-permute-start | bytes 1572872 | tf_op jit(solution)/shard_map/ppermute | solution.py:18
  69.7 23.5 %collective-permute-done.14.refs_2_ = bf16[1,2,128,1024]{3,2,1,0:T(8,128)(2,1)S(1)} collective-permute-done((bf16[1,2,128,1024]{3,2,1,0:T(8,128)(2,1)S(1)}, bf16[1,2,128,1024]{3,2,1,0:T(8,128)(2,1)S(1)}, u32[]{:S(2)}, u32[]{:S(2)}) %collective-permute-start.14) | collective-permute-done | bytes 524320 | tf_op jit(solution)/shard_map/ppermute | solution.py:18
  (25 shorter events, 13.9 us)
Async XLA Ops:
  0.0 8.3 %copy-start.1 = (f32[1,1,1024]{2,1,0:T(1,128)S(1)}, f32[1,1,1024]{2,1,0:T(1,128)}, u32[]{:S(2)}) copy-start(f32[1,1,1024]{2,1,0:T(1,128)} %factor_ref.1) | copy-start | bytes 12292
  4.7 10.1 %collective-permute-start.3 = (bf16[128,1024]{1,0:T(8,128)(2,1)S(1)}, bf16[128,1024]{1,0:T(8,128)(2,1)S(1)}, u32[]{:S(2)}, u32[]{:S(2)}) collective-permute-start(bf16[128,1024]{1,0:T(8,128)(2,1)S(1)} %get-tuple-element.26.ready_ref), channel_id=1, source_target_pairs={{0,8},{8,16},{16,24},{24,0},{1,9},{9,17},{17,25},{25,1},{2,10},{10... | collective-permute-start | bytes 786440 | tf_op jit(solution)/shard_map/ppermute | solution.py:18
  6.3 14.2 %collective-permute-start = (bf16[128,1024]{1,0:T(8,128)(2,1)S(1)}, bf16[128,1024]{1,0:T(8,128)(2,1)S(1)}, u32[]{:S(2)}, u32[]{:S(2)}) collective-permute-start(bf16[128,1024]{1,0:T(8,128)(2,1)S(1)} %get-tuple-element.20.ready_ref), channel_id=1, source_target_pairs={{0,8},{8,16},{16,24},{24,0},{1,9},{9,17},{17,25},{25,1},{2,10},{10... | collective-permute-start | bytes 786440 | tf_op jit(solution)/shard_map/ppermute | solution.py:18
  6.3 21.8 %collective-permute-start.2 = (bf16[2,512,256]{2,1,0:T(8,128)(2,1)S(1)}, bf16[2,512,256]{2,1,0:T(8,128)(2,1)S(1)}, u32[]{:S(2)}, u32[]{:S(2)}) collective-permute-start(bf16[2,512,256]{2,1,0:T(8,128)(2,1)S(1)} %get-tuple-element.24), channel_id=1, source_target_pairs={{0,2},{1,3},{2,0},{3,1},{4,6},{5,7},{6,4},{7,5},{8,10},{9,11},{10,... | collective-permute-start | bytes 1572872 | tf_op jit(solution)/shard_map/ppermute | solution.py:22
  16.2 10.2 %collective-permute-start.4 = (bf16[128,1024]{1,0:T(8,128)(2,1)S(1)}, bf16[128,1024]{1,0:T(8,128)(2,1)S(1)}, u32[]{:S(2)}, u32[]{:S(2)}) collective-permute-start(bf16[128,1024]{1,0:T(8,128)(2,1)S(1)} %shard_map.50), channel_id=1, source_target_pairs={{0,8},{8,16},{16,24},{24,0},{1,9},{9,17},{17,25},{25,1},{2,10},{10... | collective-permute-start | bytes 786440 | tf_op jit(solution)/shard_map/ppermute | solution.py:18
  20.5 7.6 %copy-start = (bf16[1,1,2,1024,256]{4,3,2,1,0:T(8,128)(2,1)S(1)}, bf16[1,1,2,1024,256]{4,3,2,1,0:T(8,128)(2,1)}, u32[]{:S(2)}) copy-start(bf16[1,1,2,1024,256]{4,3,2,1,0:T(8,128)(2,1)} %upward_ref.1) | copy-start | bytes 3145732
  21.8 10.2 %collective-permute-start.1 = (bf16[128,1024]{1,0:T(8,128)(2,1)S(1)}, bf16[128,1024]{1,0:T(8,128)(2,1)S(1)}, u32[]{:S(2)}, u32[]{:S(2)}) collective-permute-start(bf16[128,1024]{1,0:T(8,128)(2,1)S(1)} %shard_map.48), channel_id=1, source_target_pairs={{0,8},{8,16},{16,24},{24,0},{1,9},{9,17},{17,25},{25,1},{2,10},{10... | collective-permute-start | bytes 786440 | tf_op jit(solution)/shard_map/ppermute | solution.py:18
  27.8 10.2 %collective-permute-start.5 = (bf16[128,1024]{1,0:T(8,128)(2,1)S(1)}, bf16[128,1024]{1,0:T(8,128)(2,1)S(1)}, u32[]{:S(2)}, u32[]{:S(2)}) collective-permute-start(bf16[128,1024]{1,0:T(8,128)(2,1)S(1)} %shard_map.51), channel_id=1, source_target_pairs={{0,8},{8,16},{16,24},{24,0},{1,9},{9,17},{17,25},{25,1},{2,10},{10... | collective-permute-start | bytes 786440 | tf_op jit(solution)/shard_map/ppermute | solution.py:18
  33.4 9.4 %collective-permute-start.6 = (bf16[128,1024]{1,0:T(8,128)(2,1)S(1)}, bf16[128,1024]{1,0:T(8,128)(2,1)S(1)}, u32[]{:S(2)}, u32[]{:S(2)}) collective-permute-start(bf16[128,1024]{1,0:T(8,128)(2,1)S(1)} %shard_map.53), channel_id=1, source_target_pairs={{0,8},{8,16},{16,24},{24,0},{1,9},{9,17},{17,25},{25,1},{2,10},{10... | collective-permute-start | bytes 786440 | tf_op jit(solution)/shard_map/ppermute | solution.py:18
  39.3 8.0 %collective-permute-start.8 = (bf16[128,1024]{1,0:T(8,128)(2,1)S(1)}, bf16[128,1024]{1,0:T(8,128)(2,1)S(1)}, u32[]{:S(2)}, u32[]{:S(2)}) collective-permute-start(bf16[128,1024]{1,0:T(8,128)(2,1)S(1)} %shard_map.52.refs_0_), channel_id=1, source_target_pairs={{0,2},{1,3},{2,0},{3,1},{4,6},{5,7},{6,4},{7,5},{8,10},{9,11},{10,... | collective-permute-start | bytes 786440 | tf_op jit(solution)/shard_map/ppermute | solution.py:22
  41.0 9.1 %collective-permute-start.7 = (bf16[128,1024]{1,0:T(8,128)(2,1)S(1)}, bf16[128,1024]{1,0:T(8,128)(2,1)S(1)}, u32[]{:S(2)}, u32[]{:S(2)}) collective-permute-start(bf16[128,1024]{1,0:T(8,128)(2,1)S(1)} %shard_map.52.refs_0_), channel_id=1, source_target_pairs={{0,8},{8,16},{16,24},{24,0},{1,9},{9,17},{17,25},{25,1},{2,10},{10... | collective-permute-start | bytes 786440 | tf_op jit(solution)/shard_map/ppermute | solution.py:18
  44.2 9.6 %collective-permute-start.10 = (bf16[128,1024]{1,0:T(8,128)(2,1)S(1)}, bf16[128,1024]{1,0:T(8,128)(2,1)S(1)}, u32[]{:S(2)}, u32[]{:S(2)}) collective-permute-start(bf16[128,1024]{1,0:T(8,128)(2,1)S(1)} %shard_map.54.refs_1_), channel_id=1, source_target_pairs={{0,2},{1,3},{2,0},{3,1},{4,6},{5,7},{6,4},{7,5},{8,10},{9,11},{10,... | collective-permute-start | bytes 786440 | tf_op jit(solution)/shard_map/ppermute | solution.py:22
  46.6 7.3 %collective-permute-start.9 = (bf16[128,1024]{1,0:T(8,128)(2,1)S(1)}, bf16[128,1024]{1,0:T(8,128)(2,1)S(1)}, u32[]{:S(2)}, u32[]{:S(2)}) collective-permute-start(bf16[128,1024]{1,0:T(8,128)(2,1)S(1)} %shard_map.54.refs_1_), channel_id=1, source_target_pairs={{0,8},{8,16},{16,24},{24,0},{1,9},{9,17},{17,25},{25,1},{2,10},{10... | collective-permute-start | bytes 786440 | tf_op jit(solution)/shard_map/ppermute | solution.py:18
  51.4 9.2 %collective-permute-start.11 = (bf16[128,1024]{1,0:T(8,128)(2,1)S(1)}, bf16[128,1024]{1,0:T(8,128)(2,1)S(1)}, u32[]{:S(2)}, u32[]{:S(2)}) collective-permute-start(bf16[128,1024]{1,0:T(8,128)(2,1)S(1)} %shard_map.55.refs_2_), channel_id=1, source_target_pairs={{0,2},{1,3},{2,0},{3,1},{4,6},{5,7},{6,4},{7,5},{8,10},{9,11},{10,... | collective-permute-start | bytes 786440 | tf_op jit(solution)/shard_map/ppermute | solution.py:22
  55.4 8.1 %collective-permute-start.12 = (bf16[128,1024]{1,0:T(8,128)(2,1)S(1)}, bf16[128,1024]{1,0:T(8,128)(2,1)S(1)}, u32[]{:S(2)}, u32[]{:S(2)}) collective-permute-start(bf16[128,1024]{1,0:T(8,128)(2,1)S(1)} %shard_map.56.refs_3_), channel_id=1, source_target_pairs={{0,2},{1,3},{2,0},{3,1},{4,6},{5,7},{6,4},{7,5},{8,10},{9,11},{10,... | collective-permute-start | bytes 786440 | tf_op jit(solution)/shard_map/ppermute | solution.py:22
  64.2 2.7 %collective-permute-start.13 = (bf16[2,2,128,1024]{3,2,1,0:T(8,128)(2,1)S(1)}, bf16[2,2,128,1024]{3,2,1,0:T(8,128)(2,1)S(1)}, u32[]{:S(2)}, u32[]{:S(2)}) collective-permute-start(bf16[2,2,128,1024]{3,2,1,0:T(8,128)(2,1)S(1)} %get-tuple-element.34), channel_id=1, source_target_pairs={{0,1},{1,0},{2,3},{3,2},{4,5},{5,4},{6,7},{7,6},{8,9},{9,8},{10,11... | collective-permute-start | bytes 3145736 | tf_op jit(solution)/shard_map/ppermute | solution.py:22
  67.1 26.2 %collective-permute-start.14 = (bf16[1,2,128,1024]{3,2,1,0:T(8,128)(2,1)S(1)}, bf16[1,2,128,1024]{3,2,1,0:T(8,128)(2,1)S(1)}, u32[]{:S(2)}, u32[]{:S(2)}) collective-permute-start(bf16[1,2,128,1024]{3,2,1,0:T(8,128)(2,1)S(1)} %add_convert_fusion), channel_id=1, source_target_pairs={{0,4},{1,5},{2,6},{3,7},{4,0},{5,1},{6,2},{7,3},{8,12},{9,13},{10,... | collective-permute-start | bytes 1572872 | tf_op jit(solution)/shard_map/ppermute | solution.py:18

commit v11 on v10

--- a/solution.py
+++ b/solution.py
@@ -8,8 +8,9 @@
 from jax.experimental.pallas import tpu as pltpu
 from jax.sharding import PartitionSpec as P
 
-CHUNKS = 4
-DELAY = 2
+STEPS = 4
+STREAMS = 2
+BEHIND = 2
 LIMIT = 16 * 1024 * 1024
 
 
@@ -180,30 +181,22 @@
     )(level, arrived, ready, pltpu.with_memory_space_constraint(joined, pltpu.VMEM), factor)
 
 
-def operand_kernel(part, levels, level_ref, mine_ref, own_ref, got_ref, out_ref):
-    rows = own_ref.shape[1]
-    shots = own_ref.shape[2]
-    chunks = shots // part
-    turn = lax.rem(DELAY * (levels - 1 - level_ref[0]), chunks)
-    for first in range(0, chunks, math.gcd(DELAY, chunks)):
-
-        @pl.when(turn == first)
-        def _():
-            for which, ref in enumerate((own_ref, got_ref)):
-                real, imag = ref[0], ref[1]
-                minus = -real
-                for at in range(chunks):
-                    lo = (first + at) % chunks * part
-                    left = (which * chunks + at) * 2 * part
-                    out_ref[:rows, left : left + 2 * part] = jnp.concatenate(
-                        [real[:, lo : lo + part], imag[:, lo : lo + part]], axis=1
-                    )
-                    out_ref[rows:, left : left + 2 * part] = jnp.concatenate(
-                        [imag[:, lo : lo + part], minus[:, lo : lo + part]], axis=1
-                    )
-
-
-def operand(level, mine, own, got, rows, part, levels):
+def operand_kernel(own_ref, got_ref, out_ref):
+    rows, shots = own_ref.shape[1:]
+    half = shots // STREAMS
+    for which, ref in enumerate((own_ref, got_ref)):
+        real, imag = ref[0], ref[1]
+        minus = -real
+        for stream in range(STREAMS):
+            lanes = slice(stream * half, (stream + 1) * half)
+            left = 2 * (which * shots + stream * half)
+            out_ref[:rows, left : left + half] = real[:, lanes]
+            out_ref[:rows, left + half : left + 2 * half] = imag[:, lanes]
+            out_ref[rows:, left : left + half] = imag[:, lanes]
+            out_ref[rows:, left + half : left + 2 * half] = minus[:, lanes]
+
+
+def operand(mine, own, got, rows):
     shots = own.shape[2]
     blocks = got.shape[1] // rows
     groups = blocks // 2
@@ -215,47 +208,53 @@
         return block + 2 * place if stride == 4 else block
 
     return pl.pallas_call(
-        functools.partial(operand_kernel, part, levels),
+        lambda _, *refs: operand_kernel(*refs),
         grid_spec=pltpu.PrefetchScalarGridSpec(
-            num_scalar_prefetch=2,
+            num_scalar_prefetch=1,
             grid=(blocks,),
             in_specs=[
-                pl.BlockSpec((2, rows, shots), lambda i, _, mine_ref: (0, spot(i, mine_ref, 4), 0)),
-                pl.BlockSpec((2, rows, shots), lambda i, _, mine_ref: (0, spot(i, mine_ref, 2), 0)),
+                pl.BlockSpec((2, rows, shots), lambda i, mine_ref: (0, spot(i, mine_ref, 4), 0)),
+                pl.BlockSpec((2, rows, shots), lambda i, mine_ref: (0, spot(i, mine_ref, 2), 0)),
             ],
-            out_specs=pl.BlockSpec((2 * rows, 4 * shots), lambda i, *_: (i, 0)),
+            out_specs=pl.BlockSpec((2 * rows, 4 * shots), lambda i, mine_ref: (i, 0)),
         ),
         out_shape=jax.ShapeDtypeStruct((2 * rows * blocks, 4 * shots), jnp.bfloat16),
         compiler_params=pltpu.CompilerParams(vmem_limit_bytes=LIMIT),
         cost_estimate=pl.CostEstimate(flops=0, bytes_accessed=24 * rows * blocks * shots, transcendentals=0),
-    )(level, mine, own, got)
-
-
-def gathered(panels, columns):
-    return jnp.concatenate([panel[:, columns] for panel in panels], axis=0)
-
-
-def early_kernel(left_ref, *refs):
-    *panels, out_ref = refs
-    deep = sum(panel.shape[0] for panel in panels)
+    )(mine, own, got)
+
+
+def gather(levels, level_ref, panels, joined):
+    part = panels[0].shape[0] // 2
+    half = STEPS * part
+    first = lax.rem(levels - 1 - level_ref[0], STEPS)
+    for at, panel in enumerate(panels):
+        base = at // STEPS * 2 * half
+        row = pl.multiple_of(lax.rem(first + at, STEPS) * part, part)
+        joined[pl.ds(base + row, part)] = panel[:part]
+        joined[pl.ds(base + half + row, part)] = panel[part:]
+
+
+def early_kernel(levels, level_ref, left_ref, *refs):
+    *panels, out_ref, joined = refs
+    gather(levels, level_ref, panels, joined)
+    deep = joined.shape[0]
     wide = out_ref.shape[1] // 4
     for n in range(4):
         columns = slice(n * wide, (n + 1) * wide)
-        out_ref[:, columns] = jnp.dot(
-            left_ref[:, :deep], gathered(panels, columns), preferred_element_type=jnp.float32
-        )
-
-
-def late_kernel(left_ref, early_ref, *refs):
-    *panels, keep_ref, send_ref = refs
-    deep = sum(panel.shape[0] for panel in panels)
-    start = left_ref.shape[1] - deep
+        out_ref[:, columns] = jnp.dot(left_ref[:, :deep], joined[:, columns], preferred_element_type=jnp.float32)
+
+
+def late_kernel(levels, level_ref, left_ref, early_ref, *refs):
+    *panels, keep_ref, send_ref, joined = refs
+    gather(levels, level_ref, panels, joined)
+    start = left_ref.shape[1] - joined.shape[0]
     groups, _, rows, width = keep_ref.shape
     wide = width // 4
     for n in range(4):
         columns = slice(n * wide, (n + 1) * wide)
         out = early_ref[:, columns] + jnp.dot(
-            left_ref[:, start:], gathered(panels, columns), preferred_element_type=jnp.float32
+            left_ref[:, start:], joined[:, columns], preferred_element_type=jnp.float32
         )
         for k in range(groups):
             for part in range(2):
@@ -265,31 +264,37 @@
                 send_ref[k, part, :, columns] = out[lo : lo + rows].astype(jnp.bfloat16)
 
 
-def whole_call(kernel, args, outs, flops):
+def whole_call(kernel, args, outs, flops, scalars=(), scratch=()):
     whole = pl.BlockSpec(memory_space=pltpu.VMEM)
     size = sum(math.prod(x.shape) * x.dtype.itemsize for x in (*args, *outs))
     return pl.pallas_call(
         kernel,
-        in_specs=[whole] * len(args),
+        in_specs=[pl.BlockSpec(memory_space=pltpu.SMEM)] * len(scalars) + [whole] * len(args),
         out_specs=[whole] * len(outs),
         out_shape=outs,
+        scratch_shapes=scratch,
         compiler_params=pltpu.CompilerParams(vmem_limit_bytes=LIMIT),
         cost_estimate=pl.CostEstimate(flops=flops, bytes_accessed=size, transcendentals=0),
-    )(*args)
-
-
-def early_terms(left, panels):
-    out = jax.ShapeDtypeStruct((left.shape[0], panels[0].shape[1]), jnp.float32)
+    )(*scalars, *args)
+
+
+def early_terms(level, left, panels, levels):
+    width = panels[0].shape[1]
     deep = sum(panel.shape[0] for panel in panels)
-    return whole_call(early_kernel, (left, *panels), [out], 2 * deep * out.shape[0] * out.shape[1])[0]
-
-
-def late_terms(left, early, panels, rows):
+    out = jax.ShapeDtypeStruct((left.shape[0], width), jnp.float32)
+    kernel = functools.partial(early_kernel, levels)
+    scratch = [pltpu.VMEM((deep, width), jnp.bfloat16)]
+    return whole_call(kernel, (left, *panels), [out], 2 * deep * left.shape[0] * width, (level,), scratch)[0]
+
+
+def late_terms(level, left, early, panels, rows, levels):
     width = early.shape[1]
     deep = sum(panel.shape[0] for panel in panels)
     shape = (left.shape[0] // (4 * rows), 2, rows, width)
     outs = [jax.ShapeDtypeStruct(shape, jnp.float32), jax.ShapeDtypeStruct(shape, jnp.bfloat16)]
-    return whole_call(late_kernel, (left, early, *panels), outs, 2 * deep * left.shape[0] * width)
+    kernel = functools.partial(late_kernel, levels)
+    scratch = [pltpu.VMEM((deep, width), jnp.bfloat16)]
+    return whole_call(kernel, (left, early, *panels), outs, 2 * deep * left.shape[0] * width, (level,), scratch)
 
 
 def last_kernel(scale, *refs):
@@ -316,33 +321,44 @@
     freqs = lax.axis_size("freq")
     groups = freqs // 4
     rows = width // freqs
-    part = shots // CHUNKS
+    part = shots // STREAMS // STEPS
     level, mine = (lax.axis_index(axis).astype(jnp.int32).reshape(1) for axis in ("depth", "freq"))
     *ready, joined, later, asked = first_advance(level, mine, source, propagator, transmission, upgoing, part, groups)
-    ready += second_advance(joined, later, factor, part)
+    ready = [ready, second_advance(joined, later, factor, part)]
     got = swapped(asked, "freq", 2)
-    left = operand(level, mine, upward, got, rows, part, levels)
-
-    ticks = CHUNKS + DELAY * (levels - 1)
-    flying = []
-    own = []
-    other = []
-    for tick in range(ticks):
-        out = ready[tick % CHUNKS]
-        if tick >= DELAY:
-            arrived = flying[tick - DELAY]
-            if tick == ticks // 2:
+    left = operand(mine, upward, got, rows)
+
+    steps = STEPS + levels - 1
+    flying = [None] * STREAMS
+    own = [[] for _ in range(STREAMS)]
+    other = [[] for _ in range(STREAMS)]
+    waiting = []
+    crossing = []
+    for event in range(STREAMS * steps):
+        step, stream = divmod(event, STREAMS)
+        out = ready[stream][step % STEPS]
+        if step >= 1:
+            arrived = flying[stream]
+            if event == steps:
                 arrived, left = lax.optimization_barrier((arrived, left))
-            if len(other) >= DELAY:
-                arrived, other[-DELAY] = lax.optimization_barrier((arrived, other[-DELAY]))
+            if waiting:
+                which, panel = waiting.pop()
+                panel, arrived = lax.optimization_barrier((panel, arrived))
+                crossing.append((which, len(other[which])))
+                other[which].append(swapped(panel, "freq", 2))
+            if len(crossing) > BEHIND:
+                which, at = crossing.pop(0)
+                arrived, other[which][at] = lax.optimization_barrier((arrived, other[which][at]))
             out = advance(level, arrived, out, joined, factor)
-        if tick + DELAY < ticks:
-            flying.append(ring(out, "depth", 1))
-        if tick >= ticks - CHUNKS:
-            own.append(out)
-            other.append(swapped(out, "freq", 2))
-    early = early_terms(left, own + other[:-2])
-    keep, send = late_terms(left, early, other[-2:], rows)
+        if step + 1 < steps:
+            flying[stream] = ring(out, "depth", 1)
+        if step >= levels - 1:
+            own[stream].append(out)
+            waiting.append((stream, out))
+    which, panel = waiting.pop()
+    other[which].append(swapped(panel, "freq", 2))
+    early = early_terms(level, left, own[0] + own[1] + other[0], levels)
+    keep, send = late_terms(level, left, early, other[1], rows, levels)
     near = swapped(send, "freq", 1)
     parts = [keep, near]
     for k in range(1, groups):

time: 94.7 us -> 95.6 us (level); the launches traced: 94.5 us -> 94.4 us
  waiting for transfers between devices: 57.2 us -> 51.6 us
  Pallas kernels: 21.9 us -> 26.5 us
    pallas_call x8 -> x12, Pallas kernels: 10.9 us -> 15.7 us  [advance(): pl.pallas_call(advance_kernel, in_specs=[pl.BlockSpec(memory_space=pltpu....]
    ppermute x6 -> x10, waiting for transfers between devices: 9.27 us -> 5.19 us  [swapped(): lax.ppermute(block, axis, [(i, i ^ bit) for i in range(lax.axis_size(axis...]
    ppermute x9 -> x13, waiting for transfers between devices: 47.9 us -> 46.5 us  [ring(): lax.ppermute(block, axis, [(i, (i + distance) % size) for i in range(size)])]
    ppermute x9 -> x13, starting transfers between devices: 6.19 us -> 7.09 us  [ring(): lax.ppermute(block, axis, [(i, (i + distance) % size) for i in range(size)])]
    ppermute x6 -> x10, starting transfers between devices: 8.94 us -> 8.81 us  [swapped(): lax.ppermute(block, axis, [(i, i ^ bit) for i in range(lax.axis_size(axis...]
  transfers between devices with their start and end apart: 15 -> 23, of which waited for: 13 -> 16; matrix products, arithmetic and copies ran while one was open for 0% -> 0% of each run, Pallas kernels for 16% -> 21%
where the time goes in v11:
time: 95.6 us; the launch traced here: 94.4 us
  waiting for transfers between devices  51.6 us (54%)
  Pallas kernels  26.5 us (28%)
  starting transfers between devices  15.9 us (17%)
    ppermute x13, waiting for transfers between devices, ring(): lax.ppermute(block, axis, [(i, (i + distance) % size) for i in range(size)])  46.5 us
    pallas_call x12, Pallas kernels, advance(): pl.pallas_call(advance_kernel, in_specs=[pl.BlockSpec(memory_space=pltpu....  15.7 us
    ppermute x10, starting transfers between devices, swapped(): lax.ppermute(block, axis, [(i, i ^ bit) for i in range(lax.axis_size(axis...  8.81 us
    ppermute x13, starting transfers between devices, ring(): lax.ppermute(block, axis, [(i, (i + distance) % size) for i in range(size)])  7.09 us
    pallas_call x4, Pallas kernels, whole_call(): pl.pallas_call(kernel, in_specs=[pl.BlockSpec(memory_space=pltpu.SMEM)] *...  5.33 us
    ppermute x10, waiting for transfers between devices, swapped(): lax.ppermute(block, axis, [(i, i ^ bit) for i in range(lax.axis_size(axis...  5.19 us
    pallas_call x1, Pallas kernels, first_advance(): pl.pallas_call(functools.partial(first_kernel, part), in_specs=[pl.BlockS...  4.72 us
  transfers between devices with their start and end apart: 23, of which 16 were waited for; matrix products, arithmetic and copies ran while one was open for 0% of the time, Pallas kernels for 21%

profile of v11, /device:TPU:4, one launch (start us, length us, event | category | flops | bytes accessed | tf_op | source)
XLA Modules:
  0.0 94.4 jit_solution(119204420906231254)
XLA Ops:
  0.0 4.7 %shard_map.46 = (bf16[64,1024]{1,0:T(8,128)(2,1)S(1)}, bf16[64,1024]{1,0:T(8,128)(2,1)S(1)}, bf16[64,1024]{1,0:T(8,128)(2,1)S(1)}, bf16[64,1024]{1,0:T(8,128)(2,...) custom-call(s32[1]{0:T(128)} %bitcast.level_ref, ...), custom_call_target="tpu_custom_call" | custom-call | flops 1073741824 | bytes 6291456 | tf_op jit(solution)/shard_map/pallas_call | solution.py:106
  4.7 1.5 %collective-permute-start.4 = (bf16[64,1024]{1,0:T(8,128)(2,1)S(1)}, bf16[64,1024]{1,0:T(8,128)(2,1)S(1)}, u32[]{:S(2)}, u32[]{:S(2)}) collective-permute-start(bf16[64,1024]{1,0:T(8,128)(2,1)S(1)} %get-tuple-element.51.ready_ref), channel_id=1, source_target_pairs={{0,8},{8,16},{16,24},{24,0},{1,9},{9,17},{17,25},{25,1},{2,10},{10... | collective-permute-start | bytes 393224 | tf_op jit(solution)/shard_map/ppermute | solution.py:19
  6.3 1.6 %collective-permute-start.3 = (bf16[2,512,256]{2,1,0:T(8,128)(2,1)S(1)}, bf16[2,512,256]{2,1,0:T(8,128)(2,1)S(1)}, u32[]{:S(2)}, u32[]{:S(2)}) collective-permute-start(bf16[2,512,256]{2,1,0:T(8,128)(2,1)S(1)} %get-tuple-element.49), channel_id=1, source_target_pairs={{0,2},{1,3},{2,0},{3,1},{4,6},{5,7},{6,4},{7,5},{8,10},{9,11},{10,... | collective-permute-start | bytes 1572872 | tf_op jit(solution)/shard_map/ppermute | solution.py:23
  7.9 1.4 %shard_map.47 = (bf16[64,1024]{1,0:T(8,128)(2,1)S(1)}, bf16[64,1024]{1,0:T(8,128)(2,1)S(1)}, bf16[64,1024]{1,0:T(8,128)(2,1)S(1)}, bf16[64,1024]{1,0:T(8,128)(2,1)S(1)}) custom-call(bf16[1024,2048]{1,0:T(8,128)(2,1)S(1)} %get-tuple-element.44.joined_ref, bf16[1024,256]{1,0:T(8,128)(2,1)S(1)} %get-tuple-element.45.right_ref, f32[1,1024]{1,0:T(1,128)S(1)} %bitcast.5), custom_call_target="tpu_custom_call" | custom-call | flops 1073741824 | bytes 5246976 | tf_op jit(solution)/shard_map/pallas_call | solution.py:270
  12.9 2.7 %collective-permute-done.arrived_ref = bf16[64,1024]{1,0:T(8,128)(2,1)S(1)} collective-permute-done((bf16[64,1024]{1,0:T(8,128)(2,1)S(1)}, bf16[64,1024]{1,0:T(8,128)(2,1)S(1)}, u32[]{:S(2)}, u32[]{:S(2)}) %collective-permute-start) | collective-permute-done | bytes 131104 | tf_op jit(solution)/shard_map/ppermute | solution.py:19
  15.6 1.3 %shard_map.48 = bf16[64,1024]{1,0:T(8,128)(2,1)S(1)} custom-call(s32[1]{0:T(128)} %bitcast.level_ref, bf16[64,1024]{1,0:T(8,128)(2,1)S(1)} %collective-permute-done.arrived_ref, bf16[64,1024]{1,0:T(8,128)(2,1)S(1)} %get-tuple-element.47.ready_ref, bf16[1024,2048]{1,0:T(8,128)(2,1)S(1)} %get-tuple-element.44.joined_ref, f32[1,1024]{1,0:T(1,128)S(1)} %bitcast.7), custom_call_target="tpu_custom_call" | custom-call | flops 268435456 | bytes 4587520 | tf_op jit(solution)/shard_map/pallas_call | solution.py:171
  19.9 4.2 %collective-permute-done.1.arrived_ref = bf16[64,1024]{1,0:T(8,128)(2,1)S(1)} collective-permute-done((bf16[64,1024]{1,0:T(8,128)(2,1)S(1)}, bf16[64,1024]{1,0:T(8,128)(2,1)S(1)}, u32[]{:S(2)}, u32[]{:S(2)}) %collective-permute-start.1) | collective-permute-done | bytes 131104 | tf_op jit(solution)/shard_map/ppermute | solution.py:19
  28.8 2.9 %collective-permute-done.2.arrived_ref = bf16[64,1024]{1,0:T(8,128)(2,1)S(1)} collective-permute-done((bf16[64,1024]{1,0:T(8,128)(2,1)S(1)}, bf16[64,1024]{1,0:T(8,128)(2,1)S(1)}, u32[]{:S(2)}, u32[]{:S(2)}) %collective-permute-start.2) | collective-permute-done | bytes 131104 | tf_op jit(solution)/shard_map/ppermute | solution.py:19
  31.7 1.3 %shard_map.54.refs_4_ = bf16[64,1024]{1,0:T(8,128)(2,1)S(1)} custom-call(s32[1]{0:T(128)} %bitcast.level_ref, bf16[64,1024]{1,0:T(8,128)(2,1)S(1)} %collective-permute-done.2.arrived_ref, bf16[64,1024]{1,0:T(8,128)(2,1)S(1)} %get-tuple-element.57.ready_ref, bf16[1024,2048]{1,0:T(8,128)(2,1)S(1)} %get-tuple-element.44.joined_ref, f32[1,1024]{1,0:T(1,128)S(1)} %bitcast.11), custom_call_target="tpu_custom_call" | custom-call | flops 268435456 | bytes 4587520 | tf_op jit(solution)/shard_map/pallas_call | solution.py:171
  34.5 1.3 %shard_map.55.refs_1_ = bf16[64,1024]{1,0:T(8,128)(2,1)S(1)} custom-call(s32[1]{0:T(128)} %bitcast.level_ref, bf16[64,1024]{1,0:T(8,128)(2,1)S(1)} %collective-permute-done.7.arrived_ref, bf16[64,1024]{1,0:T(8,128)(2,1)S(1)} %get-tuple-element.51.ready_ref, bf16[1024,2048]{1,0:T(8,128)(2,1)S(1)} %get-tuple-element.44.joined_ref, f32[1,1024]{1,0:T(1,128)S(1)} %bitcast.12), custom_call_target="tpu_custom_call" | custom-call | flops 268435456 | bytes 4587520 | tf_op jit(solution)/shard_map/pallas_call | solution.py:171
  35.8 1.5 %collective-permute-start.11 = (bf16[64,1024]{1,0:T(8,128)(2,1)S(1)}, bf16[64,1024]{1,0:T(8,128)(2,1)S(1)}, u32[]{:S(2)}, u32[]{:S(2)}) collective-permute-start(bf16[64,1024]{1,0:T(8,128)(2,1)S(1)} %shard_map.54.refs_4_), channel_id=1, source_target_pairs={{0,2},{1,3},{2,0},{3,1},{4,6},{5,7},{6,4},{7,5},{8,10},{9,11},{10,... | collective-permute-start | bytes 393224 | tf_op jit(solution)/shard_map/ppermute | solution.py:23
  37.3 1.8 %collective-permute-done.8.arrived_ref = bf16[64,1024]{1,0:T(8,128)(2,1)S(1)} collective-permute-done((bf16[64,1024]{1,0:T(8,128)(2,1)S(1)}, bf16[64,1024]{1,0:T(8,128)(2,1)S(1)}, u32[]{:S(2)}, u32[]{:S(2)}) %collective-permute-start.8) | collective-permute-done | bytes 131104 | tf_op jit(solution)/shard_map/ppermute | solution.py:19
  39.1 1.3 %shard_map.56.refs_5_ = bf16[64,1024]{1,0:T(8,128)(2,1)S(1)} custom-call(s32[1]{0:T(128)} %bitcast.level_ref, bf16[64,1024]{1,0:T(8,128)(2,1)S(1)} %collective-permute-done.8.arrived_ref, bf16[64,1024]{1,0:T(8,128)(2,1)S(1)} %get-tuple-element.46.ready_ref, bf16[1024,2048]{1,0:T(8,128)(2,1)S(1)} %get-tuple-element.44.joined_ref, f32[1,1024]{1,0:T(1,128)S(1)} %bitcast.13), custom_call_target="tpu_custom_call" | custom-call | flops 268435456 | bytes 4587520 | tf_op jit(solution)/shard_map/pallas_call | solution.py:171
  41.7 1.3 %shard_map.57.refs_2_ = bf16[64,1024]{1,0:T(8,128)(2,1)S(1)} custom-call(s32[1]{0:T(128)} %bitcast.level_ref, bf16[64,1024]{1,0:T(8,128)(2,1)S(1)} %collective-permute-done.10.arrived_ref, bf16[64,1024]{1,0:T(8,128)(2,1)S(1)} %get-tuple-element.52.ready_ref, bf16[1024,2048]{1,0:T(8,128)(2,1)S(1)} %get-tuple-element.44.joined_ref, f32[1,1024]{1,0:T(1,128)S(1)} %bitcast.14), custom_call_target="tpu_custom_call" | custom-call | flops 268435456 | bytes 4587520 | tf_op jit(solution)/shard_map/pallas_call | solution.py:171
  44.9 2.8 %collective-permute-done.12.arrived_ref = bf16[64,1024]{1,0:T(8,128)(2,1)S(1)} collective-permute-done((bf16[64,1024]{1,0:T(8,128)(2,1)S(1)}, bf16[64,1024]{1,0:T(8,128)(2,1)S(1)}, u32[]{:S(2)}, u32[]{:S(2)}) %collective-permute-start.12) | collective-permute-done | bytes 131104 | tf_op jit(solution)/shard_map/ppermute | solution.py:19
  47.7 1.3 %shard_map.58.refs_6_ = bf16[64,1024]{1,0:T(8,128)(2,1)S(1)} custom-call(s32[1]{0:T(128)} %bitcast.level_ref, bf16[64,1024]{1,0:T(8,128)(2,1)S(1)} %collective-permute-done.12.arrived_ref, bf16[64,1024]{1,0:T(8,128)(2,1)S(1)} %get-tuple-element.47.ready_ref, bf16[1024,2048]{1,0:T(8,128)(2,1)S(1)} %get-tuple-element.44.joined_ref, f32[1,1024]{1,0:T(1,128)S(1)} %bitcast.15), custom_call_target="tpu_custom_call" | custom-call | flops 268435456 | bytes 4587520 | tf_op jit(solution)/shard_map/pallas_call | solution.py:171
  51.7 3.2 %collective-permute-done.16.arrived_ref = bf16[64,1024]{1,0:T(8,128)(2,1)S(1)} collective-permute-done((bf16[64,1024]{1,0:T(8,128)(2,1)S(1)}, bf16[64,1024]{1,0:T(8,128)(2,1)S(1)}, u32[]{:S(2)}, u32[]{:S(2)}) %collective-permute-start.16) | collective-permute-done | bytes 131104 | tf_op jit(solution)/shard_map/ppermute | solution.py:19
  55.5 1.5 %collective-permute-start.19 = (bf16[64,1024]{1,0:T(8,128)(2,1)S(1)}, bf16[64,1024]{1,0:T(8,128)(2,1)S(1)}, u32[]{:S(2)}, u32[]{:S(2)}) collective-permute-start(bf16[64,1024]{1,0:T(8,128)(2,1)S(1)} %shard_map.58.refs_6_), channel_id=1, source_target_pairs={{0,2},{1,3},{2,0},{3,1},{4,6},{5,7},{6,4},{7,5},{8,10},{9,11},{10,... | collective-permute-start | bytes 393224 | tf_op jit(solution)/shard_map/ppermute | solution.py:23
  59.9 1.9 %shard_map.61.early_ref = f32[1024,1024]{1,0:T(8,128)S(1)} custom-call(s32[1]{0:T(128)} %bitcast.level_ref, bf16[1024,1024]{1,0:T(8,128)(2,1)S(1)} %shard_map.50.left_ref, bf16[64,1024]{1,0:T(8,128)(2,1)S(1)} %shard_map.53.refs_0_, bf16[64,1024]{1,0:T(8,128)(2,1)S(1)} %shard_map.55.refs_1_, bf16[64,1024]{1,0:T(8,128)(2,1)S(1)} %shard_map.57.refs_2_, ...), custom_call_target="tpu_custom_call" | custom-call | flops 1610612736 | bytes 7864320 | tf_op jit(solution)/shard_map/pallas_call | solution.py:270
  61.8 1.5 %collective-permute-done.20.refs_3_ = bf16[64,1024]{1,0:T(8,128)(2,1)S(1)} collective-permute-done((bf16[64,1024]{1,0:T(8,128)(2,1)S(1)}, bf16[64,1024]{1,0:T(8,128)(2,1)S(1)}, u32[]{:S(2)}, u32[]{:S(2)}) %collective-permute-start.20) | collective-permute-done | bytes 131104 | tf_op jit(solution)/shard_map/ppermute | solution.py:23
  64.1 2.6 %collective-permute-done.21.refs_1_ = bf16[2,2,128,1024]{3,2,1,0:T(8,128)(2,1)S(1)} collective-permute-done((bf16[2,2,128,1024]{3,2,1,0:T(8,128)(2,1)S(1)}, bf16[2,2,128,1024]{3,2,1,0:T(8,128)(2,1)S(1)}, u32[]{:S(2)}, u32[]{:S(2)}) %collective-permute-start.21) | collective-permute-done | bytes 1048608 | tf_op jit(solution)/shard_map/ppermute | solution.py:23
  67.0 2.7 %collective-permute-start.22 = (bf16[1,2,128,1024]{3,2,1,0:T(8,128)(2,1)S(1)}, bf16[1,2,128,1024]{3,2,1,0:T(8,128)(2,1)S(1)}, u32[]{:S(2)}, u32[]{:S(2)}) collective-permute-start(bf16[1,2,128,1024]{3,2,1,0:T(8,128)(2,1)S(1)} %add_convert_fusion), channel_id=1, source_target_pairs={{0,4},{1,5},{2,6},{3,7},{4,0},{5,1},{6,2},{7,3},{8,12},{9,13},{10,... | collective-permute-start | bytes 1572872 | tf_op jit(solution)/shard_map/ppermute | solution.py:19
  69.7 23.5 %collective-permute-done.22.refs_2_ = bf16[1,2,128,1024]{3,2,1,0:T(8,128)(2,1)S(1)} collective-permute-done((bf16[1,2,128,1024]{3,2,1,0:T(8,128)(2,1)S(1)}, bf16[1,2,128,1024]{3,2,1,0:T(8,128)(2,1)S(1)}, u32[]{:S(2)}, u32[]{:S(2)}) %collective-permute-start.22) | collective-permute-done | bytes 524320 | tf_op jit(solution)/shard_map/ppermute | solution.py:19
  93.1 1.3 %shard_map.63 = f32[1,128,2,1024]{3,2,1,0:T(2,128)} custom-call(f32[2,2,128,1024]{3,2,1,0:T(8,128)S(1)} %get-tuple-element.81.refs_0_, bf16[2,2,128,1024]{3,2,1,0:T(8,128)(2,1)S(1)} %collective-permute-done.21.refs_1_, bf16[1,2,128,1024]{3,2,1,0:T(8,128)(2,1)S(1)} %collective-permute-done.22.refs_2_), custom_call_target="tpu_custom_call" | custom-call | flops 786432 | bytes 4718592 | tf_op jit(solution)/shard_map/pallas_call | solution.py:270
  (45 shorter events, 23.1 us)
Async XLA Ops:
  0.0 7.9 %copy-start.1 = (f32[1,1,1024]{2,1,0:T(1,128)S(1)}, f32[1,1,1024]{2,1,0:T(1,128)}, u32[]{:S(2)}) copy-start(f32[1,1,1024]{2,1,0:T(1,128)} %factor_ref.1) | copy-start | bytes 12292
  4.7 6.2 %collective-permute-start.4 = (bf16[64,1024]{1,0:T(8,128)(2,1)S(1)}, bf16[64,1024]{1,0:T(8,128)(2,1)S(1)}, u32[]{:S(2)}, u32[]{:S(2)}) collective-permute-start(bf16[64,1024]{1,0:T(8,128)(2,1)S(1)} %get-tuple-element.51.ready_ref), channel_id=1, source_target_pairs={{0,8},{8,16},{16,24},{24,0},{1,9},{9,17},{17,25},{25,1},{2,10},{10... | collective-permute-start | bytes 393224 | tf_op jit(solution)/shard_map/ppermute | solution.py:19
  6.3 21.7 %collective-permute-start.3 = (bf16[2,512,256]{2,1,0:T(8,128)(2,1)S(1)}, bf16[2,512,256]{2,1,0:T(8,128)(2,1)S(1)}, u32[]{:S(2)}, u32[]{:S(2)}) collective-permute-start(bf16[2,512,256]{2,1,0:T(8,128)(2,1)S(1)} %get-tuple-element.49), channel_id=1, source_target_pairs={{0,2},{1,3},{2,0},{3,1},{4,6},{5,7},{6,4},{7,5},{8,10},{9,11},{10,... | collective-permute-start | bytes 1572872 | tf_op jit(solution)/shard_map/ppermute | solution.py:23
  9.2 6.3 %collective-permute-start = (bf16[64,1024]{1,0:T(8,128)(2,1)S(1)}, bf16[64,1024]{1,0:T(8,128)(2,1)S(1)}, u32[]{:S(2)}, u32[]{:S(2)}) collective-permute-start(bf16[64,1024]{1,0:T(8,128)(2,1)S(1)} %get-tuple-element.46.ready_ref), channel_id=1, source_target_pairs={{0,8},{8,16},{16,24},{24,0},{1,9},{9,17},{17,25},{25,1},{2,10},{10... | collective-permute-start | bytes 393224 | tf_op jit(solution)/shard_map/ppermute | solution.py:19
  12.2 5.9 %collective-permute-start.5 = (bf16[64,1024]{1,0:T(8,128)(2,1)S(1)}, bf16[64,1024]{1,0:T(8,128)(2,1)S(1)}, u32[]{:S(2)}, u32[]{:S(2)}) collective-permute-start(bf16[64,1024]{1,0:T(8,128)(2,1)S(1)} %shard_map.51), channel_id=1, source_target_pairs={{0,8},{8,16},{16,24},{24,0},{1,9},{9,17},{17,25},{25,1},{2,10},{10... | collective-permute-start | bytes 393224 | tf_op jit(solution)/shard_map/ppermute | solution.py:19
  16.9 7.1 %collective-permute-start.1 = (bf16[64,1024]{1,0:T(8,128)(2,1)S(1)}, bf16[64,1024]{1,0:T(8,128)(2,1)S(1)}, u32[]{:S(2)}, u32[]{:S(2)}) collective-permute-start(bf16[64,1024]{1,0:T(8,128)(2,1)S(1)} %shard_map.48), channel_id=1, source_target_pairs={{0,8},{8,16},{16,24},{24,0},{1,9},{9,17},{17,25},{25,1},{2,10},{10... | collective-permute-start | bytes 393224 | tf_op jit(solution)/shard_map/ppermute | solution.py:19
  19.5 7.1 %collective-permute-start.6 = (bf16[64,1024]{1,0:T(8,128)(2,1)S(1)}, bf16[64,1024]{1,0:T(8,128)(2,1)S(1)}, u32[]{:S(2)}, u32[]{:S(2)}) collective-permute-start(bf16[64,1024]{1,0:T(8,128)(2,1)S(1)} %shard_map.52), channel_id=1, source_target_pairs={{0,8},{8,16},{16,24},{24,0},{1,9},{9,17},{17,25},{25,1},{2,10},{10... | collective-permute-start | bytes 393224 | tf_op jit(solution)/shard_map/ppermute | solution.py:19
  25.4 6.3 %collective-permute-start.2 = (bf16[64,1024]{1,0:T(8,128)(2,1)S(1)}, bf16[64,1024]{1,0:T(8,128)(2,1)S(1)}, u32[]{:S(2)}, u32[]{:S(2)}) collective-permute-start(bf16[64,1024]{1,0:T(8,128)(2,1)S(1)} %shard_map.49), channel_id=1, source_target_pairs={{0,8},{8,16},{16,24},{24,0},{1,9},{9,17},{17,25},{25,1},{2,10},{10... | collective-permute-start | bytes 393224 | tf_op jit(solution)/shard_map/ppermute | solution.py:19
  27.9 6.6 %collective-permute-start.7 = (bf16[64,1024]{1,0:T(8,128)(2,1)S(1)}, bf16[64,1024]{1,0:T(8,128)(2,1)S(1)}, u32[]{:S(2)}, u32[]{:S(2)}) collective-permute-start(bf16[64,1024]{1,0:T(8,128)(2,1)S(1)} %shard_map.53.refs_0_), channel_id=1, source_target_pairs={{0,8},{8,16},{16,24},{24,0},{1,9},{9,17},{17,25},{25,1},{2,10},{10... | collective-permute-start | bytes 393224 | tf_op jit(solution)/shard_map/ppermute | solution.py:19
  33.0 6.1 %collective-permute-start.8 = (bf16[64,1024]{1,0:T(8,128)(2,1)S(1)}, bf16[64,1024]{1,0:T(8,128)(2,1)S(1)}, u32[]{:S(2)}, u32[]{:S(2)}) collective-permute-start(bf16[64,1024]{1,0:T(8,128)(2,1)S(1)} %shard_map.54.refs_4_), channel_id=1, source_target_pairs={{0,8},{8,16},{16,24},{24,0},{1,9},{9,17},{17,25},{25,1},{2,10},{10... | collective-permute-start | bytes 393224 | tf_op jit(solution)/shard_map/ppermute | solution.py:19
  33.1 6.0 %collective-permute-start.9 = (bf16[64,1024]{1,0:T(8,128)(2,1)S(1)}, bf16[64,1024]{1,0:T(8,128)(2,1)S(1)}, u32[]{:S(2)}, u32[]{:S(2)}) collective-permute-start(bf16[64,1024]{1,0:T(8,128)(2,1)S(1)} %shard_map.53.refs_0_), channel_id=1, source_target_pairs={{0,2},{1,3},{2,0},{3,1},{4,6},{5,7},{6,4},{7,5},{8,10},{9,11},{10,... | collective-permute-start | bytes 393224 | tf_op jit(solution)/shard_map/ppermute | solution.py:23
  35.8 5.9 %collective-permute-start.10 = (bf16[64,1024]{1,0:T(8,128)(2,1)S(1)}, bf16[64,1024]{1,0:T(8,128)(2,1)S(1)}, u32[]{:S(2)}, u32[]{:S(2)}) collective-permute-start(bf16[64,1024]{1,0:T(8,128)(2,1)S(1)} %shard_map.55.refs_1_), channel_id=1, source_target_pairs={{0,8},{8,16},{16,24},{24,0},{1,9},{9,17},{17,25},{25,1},{2,10},{10... | collective-permute-start | bytes 393224 | tf_op jit(solution)/shard_map/ppermute | solution.py:19
  35.8 5.9 %collective-permute-start.11 = (bf16[64,1024]{1,0:T(8,128)(2,1)S(1)}, bf16[64,1024]{1,0:T(8,128)(2,1)S(1)}, u32[]{:S(2)}, u32[]{:S(2)}) collective-permute-start(bf16[64,1024]{1,0:T(8,128)(2,1)S(1)} %shard_map.54.refs_4_), channel_id=1, source_target_pairs={{0,2},{1,3},{2,0},{3,1},{4,6},{5,7},{6,4},{7,5},{8,10},{9,11},{10,... | collective-permute-start | bytes 393224 | tf_op jit(solution)/shard_map/ppermute | solution.py:23
  40.4 7.3 %collective-permute-start.12 = (bf16[64,1024]{1,0:T(8,128)(2,1)S(1)}, bf16[64,1024]{1,0:T(8,128)(2,1)S(1)}, u32[]{:S(2)}, u32[]{:S(2)}) collective-permute-start(bf16[64,1024]{1,0:T(8,128)(2,1)S(1)} %shard_map.56.refs_5_), channel_id=1, source_target_pairs={{0,8},{8,16},{16,24},{24,0},{1,9},{9,17},{17,25},{25,1},{2,10},{10... | collective-permute-start | bytes 393224 | tf_op jit(solution)/shard_map/ppermute | solution.py:19
  40.5 7.2 %collective-permute-start.13 = (bf16[64,1024]{1,0:T(8,128)(2,1)S(1)}, bf16[64,1024]{1,0:T(8,128)(2,1)S(1)}, u32[]{:S(2)}, u32[]{:S(2)}) collective-permute-start(bf16[64,1024]{1,0:T(8,128)(2,1)S(1)} %shard_map.55.refs_1_), channel_id=1, source_target_pairs={{0,2},{1,3},{2,0},{3,1},{4,6},{5,7},{6,4},{7,5},{8,10},{9,11},{10,... | collective-permute-start | bytes 393224 | tf_op jit(solution)/shard_map/ppermute | solution.py:23
  43.0 6.1 %collective-permute-start.14 = (bf16[64,1024]{1,0:T(8,128)(2,1)S(1)}, bf16[64,1024]{1,0:T(8,128)(2,1)S(1)}, u32[]{:S(2)}, u32[]{:S(2)}) collective-permute-start(bf16[64,1024]{1,0:T(8,128)(2,1)S(1)} %shard_map.57.refs_2_), channel_id=1, source_target_pairs={{0,8},{8,16},{16,24},{24,0},{1,9},{9,17},{17,25},{25,1},{2,10},{10... | collective-permute-start | bytes 393224 | tf_op jit(solution)/shard_map/ppermute | solution.py:19
  43.9 5.3 %collective-permute-start.15 = (bf16[64,1024]{1,0:T(8,128)(2,1)S(1)}, bf16[64,1024]{1,0:T(8,128)(2,1)S(1)}, u32[]{:S(2)}, u32[]{:S(2)}) collective-permute-start(bf16[64,1024]{1,0:T(8,128)(2,1)S(1)} %shard_map.56.refs_5_), channel_id=1, source_target_pairs={{0,2},{1,3},{2,0},{3,1},{4,6},{5,7},{6,4},{7,5},{8,10},{9,11},{10,... | collective-permute-start | bytes 393224 | tf_op jit(solution)/shard_map/ppermute | solution.py:23
  49.0 5.9 %collective-permute-start.16 = (bf16[64,1024]{1,0:T(8,128)(2,1)S(1)}, bf16[64,1024]{1,0:T(8,128)(2,1)S(1)}, u32[]{:S(2)}, u32[]{:S(2)}) collective-permute-start(bf16[64,1024]{1,0:T(8,128)(2,1)S(1)} %shard_map.58.refs_6_), channel_id=1, source_target_pairs={{0,8},{8,16},{16,24},{24,0},{1,9},{9,17},{17,25},{25,1},{2,10},{10... | collective-permute-start | bytes 393224 | tf_op jit(solution)/shard_map/ppermute | solution.py:19
  49.2 7.8 %collective-permute-start.17 = (bf16[64,1024]{1,0:T(8,128)(2,1)S(1)}, bf16[64,1024]{1,0:T(8,128)(2,1)S(1)}, u32[]{:S(2)}, u32[]{:S(2)}) collective-permute-start(bf16[64,1024]{1,0:T(8,128)(2,1)S(1)} %shard_map.57.refs_2_), channel_id=1, source_target_pairs={{0,2},{1,3},{2,0},{3,1},{4,6},{5,7},{6,4},{7,5},{8,10},{9,11},{10,... | collective-permute-start | bytes 393224 | tf_op jit(solution)/shard_map/ppermute | solution.py:23
  54.9 5.0 %collective-permute-start.18 = (bf16[64,1024]{1,0:T(8,128)(2,1)S(1)}, bf16[64,1024]{1,0:T(8,128)(2,1)S(1)}, u32[]{:S(2)}, u32[]{:S(2)}) collective-permute-start(bf16[64,1024]{1,0:T(8,128)(2,1)S(1)} %shard_map.59.refs_3_), channel_id=1, source_target_pairs={{0,2},{1,3},{2,0},{3,1},{4,6},{5,7},{6,4},{7,5},{8,10},{9,11},{10,... | collective-permute-start | bytes 393224 | tf_op jit(solution)/shard_map/ppermute | solution.py:23
  55.5 6.3 %collective-permute-start.19 = (bf16[64,1024]{1,0:T(8,128)(2,1)S(1)}, bf16[64,1024]{1,0:T(8,128)(2,1)S(1)}, u32[]{:S(2)}, u32[]{:S(2)}) collective-permute-start(bf16[64,1024]{1,0:T(8,128)(2,1)S(1)} %shard_map.58.refs_6_), channel_id=1, source_target_pairs={{0,2},{1,3},{2,0},{3,1},{4,6},{5,7},{6,4},{7,5},{8,10},{9,11},{10,... | collective-permute-start | bytes 393224 | tf_op jit(solution)/shard_map/ppermute | solution.py:23
  58.3 5.0 %collective-permute-start.20 = (bf16[64,1024]{1,0:T(8,128)(2,1)S(1)}, bf16[64,1024]{1,0:T(8,128)(2,1)S(1)}, u32[]{:S(2)}, u32[]{:S(2)}) collective-permute-start(bf16[64,1024]{1,0:T(8,128)(2,1)S(1)} %shard_map.60.refs_7_), channel_id=1, source_target_pairs={{0,2},{1,3},{2,0},{3,1},{4,6},{5,7},{6,4},{7,5},{8,10},{9,11},{10,... | collective-permute-start | bytes 393224 | tf_op jit(solution)/shard_map/ppermute | solution.py:23
  64.1 2.7 %collective-permute-start.21 = (bf16[2,2,128,1024]{3,2,1,0:T(8,128)(2,1)S(1)}, bf16[2,2,128,1024]{3,2,1,0:T(8,128)(2,1)S(1)}, u32[]{:S(2)}, u32[]{:S(2)}) collective-permute-start(bf16[2,2,128,1024]{3,2,1,0:T(8,128)(2,1)S(1)} %get-tuple-element.82), channel_id=1, source_target_pairs={{0,1},{1,0},{2,3},{3,2},{4,5},{5,4},{6,7},{7,6},{8,9},{9,8},{10,11... | collective-permute-start | bytes 3145736 | tf_op jit(solution)/shard_map/ppermute | solution.py:23
  67.0 26.2 %collective-permute-start.22 = (bf16[1,2,128,1024]{3,2,1,0:T(8,128)(2,1)S(1)}, bf16[1,2,128,1024]{3,2,1,0:T(8,128)(2,1)S(1)}, u32[]{:S(2)}, u32[]{:S(2)}) collective-permute-start(bf16[1,2,128,1024]{3,2,1,0:T(8,128)(2,1)S(1)} %add_convert_fusion), channel_id=1, source_target_pairs={{0,4},{1,5},{2,6},{3,7},{4,0},{5,1},{6,2},{7,3},{8,12},{9,13},{10,... | collective-permute-start | bytes 1572872 | tf_op jit(solution)/shard_map/ppermute | solution.py:19
  (1 other events, 3.9 us)

commit v12 on v11

--- a/solution.py
+++ b/solution.py
@@ -10,7 +10,7 @@
 
 STEPS = 4
 STREAMS = 2
-BEHIND = 2
+BEHIND = 3
 LIMIT = 16 * 1024 * 1024
 
 
@@ -143,7 +143,9 @@
     return whole_call(functools.partial(second_kernel, part), (joined, right, factor), outs, 4 * width * width * shots)
 
 
-def advance_kernel(level_ref, arrived_ref, ready_ref, joined_ref, factor_ref, out_ref, both):
+def advance_kernel(level_ref, arrived_ref, ready_ref, joined_ref, factor_ref, *refs):
+    *mates, both = refs
+    out_ref = mates[0] if len(mates) == 1 else mates[1]
     part = arrived_ref.shape[0] // 2
     width = arrived_ref.shape[1]
     wide = width // 4
@@ -164,21 +166,21 @@
             )
             out_ref[:, columns] = (out.T * factor_ref[:, columns]).astype(jnp.bfloat16)
 
-
-def advance(level, arrived, ready, joined, factor):
+    if len(mates) > 1:
+        mates[2][: 2 * part] = mates[0][...]
+        mates[2][2 * part :] = out_ref[...]
+
+
+def advance(level, arrived, ready, joined, factor, mate=None):
     rows, width = arrived.shape
-    whole = pl.BlockSpec(memory_space=pltpu.VMEM)
-    return pl.pallas_call(
-        advance_kernel,
-        in_specs=[pl.BlockSpec(memory_space=pltpu.SMEM)] + [whole] * 4,
-        out_specs=whole,
-        out_shape=jax.ShapeDtypeStruct((rows, width), jnp.bfloat16),
-        scratch_shapes=[pltpu.VMEM((rows, 2 * width), jnp.bfloat16)],
-        compiler_params=pltpu.CompilerParams(vmem_limit_bytes=LIMIT),
-        cost_estimate=pl.CostEstimate(
-            flops=4 * rows * width * width, bytes_accessed=4 * width * width + 6 * rows * width, transcendentals=0
-        ),
-    )(level, arrived, ready, pltpu.with_memory_space_constraint(joined, pltpu.VMEM), factor)
+    joined = pltpu.with_memory_space_constraint(joined, pltpu.VMEM)
+    outs = [jax.ShapeDtypeStruct((rows, width), jnp.bfloat16)]
+    args = [arrived, ready, joined, factor]
+    if mate is not None:
+        outs.append(jax.ShapeDtypeStruct((2 * rows, width), jnp.bfloat16))
+        args.append(mate)
+    scratch = [pltpu.VMEM((rows, 2 * width), jnp.bfloat16)]
+    return whole_call(advance_kernel, args, outs, 4 * rows * width * width, (level,), scratch)
 
 
 def operand_kernel(own_ref, got_ref, out_ref):
@@ -225,19 +227,26 @@
 
 
 def gather(levels, level_ref, panels, joined):
-    part = panels[0].shape[0] // 2
+    part = joined.shape[0] // len(panels) // 2
     half = STEPS * part
     first = lax.rem(levels - 1 - level_ref[0], STEPS)
-    for at, panel in enumerate(panels):
+    for at, (ref, top) in enumerate(panels):
         base = at // STEPS * 2 * half
         row = pl.multiple_of(lax.rem(first + at, STEPS) * part, part)
-        joined[pl.ds(base + row, part)] = panel[:part]
-        joined[pl.ds(base + half + row, part)] = panel[part:]
+        joined[pl.ds(base + row, part)] = ref[top : top + part]
+        joined[pl.ds(base + half + row, part)] = ref[top + part : top + 2 * part]
+
+
+def crossed(refs, stream):
+    *pairs, last = refs
+    rows = last.shape[0]
+    return [(pair, stream * rows) for pair in pairs] + [(last, 0)]
 
 
 def early_kernel(levels, level_ref, left_ref, *refs):
     *panels, out_ref, joined = refs
-    gather(levels, level_ref, panels, joined)
+    own, other = panels[: STREAMS * STEPS], panels[STREAMS * STEPS :]
+    gather(levels, level_ref, [(ref, 0) for ref in own] + crossed(other, 0), joined)
     deep = joined.shape[0]
     wide = out_ref.shape[1] // 4
     for n in range(4):
@@ -247,7 +256,7 @@
 
 def late_kernel(levels, level_ref, left_ref, early_ref, *refs):
     *panels, keep_ref, send_ref, joined = refs
-    gather(levels, level_ref, panels, joined)
+    gather(levels, level_ref, crossed(panels, 1), joined)
     start = left_ref.shape[1] - joined.shape[0]
     groups, _, rows, width = keep_ref.shape
     wide = width // 4
@@ -280,7 +289,7 @@
 
 def early_terms(level, left, panels, levels):
     width = panels[0].shape[1]
-    deep = sum(panel.shape[0] for panel in panels)
+    deep = left.shape[1] - panels[-1].shape[0] * STEPS
     out = jax.ShapeDtypeStruct((left.shape[0], width), jnp.float32)
     kernel = functools.partial(early_kernel, levels)
     scratch = [pltpu.VMEM((deep, width), jnp.bfloat16)]
@@ -289,7 +298,7 @@
 
 def late_terms(level, left, early, panels, rows, levels):
     width = early.shape[1]
-    deep = sum(panel.shape[0] for panel in panels)
+    deep = panels[-1].shape[0] * STEPS
     shape = (left.shape[0] // (4 * rows), 2, rows, width)
     outs = [jax.ShapeDtypeStruct(shape, jnp.float32), jax.ShapeDtypeStruct(shape, jnp.bfloat16)]
     kernel = functools.partial(late_kernel, levels)
@@ -331,7 +340,6 @@
     steps = STEPS + levels - 1
     flying = [None] * STREAMS
     own = [[] for _ in range(STREAMS)]
-    other = [[] for _ in range(STREAMS)]
     waiting = []
     crossing = []
     for event in range(STREAMS * steps):
@@ -342,23 +350,23 @@
             if event == steps:
                 arrived, left = lax.optimization_barrier((arrived, left))
             if waiting:
-                which, panel = waiting.pop()
-                panel, arrived = lax.optimization_barrier((panel, arrived))
-                crossing.append((which, len(other[which])))
-                other[which].append(swapped(panel, "freq", 2))
-            if len(crossing) > BEHIND:
-                which, at = crossing.pop(0)
-                arrived, other[which][at] = lax.optimization_barrier((arrived, other[which][at]))
-            out = advance(level, arrived, out, joined, factor)
+                panel, arrived = lax.optimization_barrier((waiting.pop(), arrived))
+                crossing.append((event, swapped(panel, "freq", 2)))
+            for at, (sent, panel) in enumerate(crossing):
+                if event == sent + BEHIND:
+                    arrived, panel = lax.optimization_barrier((arrived, panel))
+                    crossing[at] = (sent, panel)
+            pair = stream > 0 and levels - 1 <= step < steps - 1
+            out, *both = advance(level, arrived, out, joined, factor, own[0][-1] if pair else None)
+            if step >= levels - 1 and (pair or step == steps - 1):
+                waiting.append(both[0] if pair else out)
         if step + 1 < steps:
             flying[stream] = ring(out, "depth", 1)
         if step >= levels - 1:
             own[stream].append(out)
-            waiting.append((stream, out))
-    which, panel = waiting.pop()
-    other[which].append(swapped(panel, "freq", 2))
-    early = early_terms(level, left, own[0] + own[1] + other[0], levels)
-    keep, send = late_terms(level, left, early, other[1], rows, levels)
+    other = [panel for _, panel in crossing] + [swapped(waiting.pop(), "freq", 2)]
+    early = early_terms(level, left, own[0] + own[1] + other[:-1], levels)
+    keep, send = late_terms(level, left, early, other[:-2] + other[-1:], rows, levels)
     near = swapped(send, "freq", 1)
     parts = [keep, near]
     for k in range(1, groups):

time: 95.6 us -> 96 us (level)
  waiting for transfers between devices: 51.6 us -> 52.6 us
    pallas_call x4 -> x16, Pallas kernels: 5.33 us -> 21.1 us  [whole_call(): pl.pallas_call(kernel, in_specs=[pl.BlockSpec(memory_space=pltpu.SMEM)] *...]
    pallas_call x12 -> x0, Pallas kernels: 15.7 us -> none  [advance(): pl.pallas_call(advance_kernel, in_specs=[pl.BlockSpec(memory_space=pltpu....]
    ppermute x10 -> x7, starting transfers between devices: 8.81 us -> 9.65 us  [swapped(): lax.ppermute(block, axis, [(i, i ^ bit) for i in range(lax.axis_size(axis...]
    ppermute x10 -> x7, waiting for transfers between devices: 5.19 us -> 5.72 us  [swapped(): lax.ppermute(block, axis, [(i, i ^ bit) for i in range(lax.axis_size(axis...]
  transfers between devices with their start and end apart: 23 -> 20, of which waited for: 16 -> 15; matrix products, arithmetic and copies ran while one was open for 0% -> 0% of each run, Pallas kernels for 21% -> 21%
where the time goes in v12:
time: 96 us; the launch traced here: 95.7 us
  waiting for transfers between devices  52.6 us (55%)
  Pallas kernels  26.6 us (28%)
  starting transfers between devices  16.1 us (17%)
    ppermute x13, waiting for transfers between devices, ring(): lax.ppermute(block, axis, [(i, (i + distance) % size) for i in range(size)])  46.9 us
    pallas_call x16, Pallas kernels, whole_call(): pl.pallas_call(kernel, in_specs=[pl.BlockSpec(memory_space=pltpu.SMEM)] *...  21.1 us
    ppermute x7, starting transfers between devices, swapped(): lax.ppermute(block, axis, [(i, i ^ bit) for i in range(lax.axis_size(axis...  9.65 us
    ppermute x13, starting transfers between devices, ring(): lax.ppermute(block, axis, [(i, (i + distance) % size) for i in range(size)])  6.44 us
    ppermute x7, waiting for transfers between devices, swapped(): lax.ppermute(block, axis, [(i, i ^ bit) for i in range(lax.axis_size(axis...  5.72 us
    pallas_call x1, Pallas kernels, first_advance(): pl.pallas_call(functools.partial(first_kernel, part), in_specs=[pl.BlockS...  4.72 us
  transfers between devices with their start and end apart: 20, of which 15 were waited for; matrix products, arithmetic and copies ran while one was open for 0% of the time, Pallas kernels for 21%

profile of v12, /device:TPU:4, one launch (start us, length us, event | category | flops | bytes accessed | tf_op | source)
XLA Modules:
  0.0 95.7 jit_solution(6099813498293808701)
XLA Ops:
  0.0 4.7 %shard_map.46 = (bf16[64,1024]{1,0:T(8,128)(2,1)S(1)}, bf16[64,1024]{1,0:T(8,128)(2,1)S(1)}, bf16[64,1024]{1,0:T(8,128)(2,1)S(1)}, bf16[64,1024]{1,0:T(8,128)(2,...) custom-call(s32[1]{0:T(128)} %bitcast.level_ref, ...), custom_call_target="tpu_custom_call" | custom-call | flops 1073741824 | bytes 6291456 | tf_op jit(solution)/shard_map/pallas_call | solution.py:106
  4.7 1.5 %collective-permute-start.4 = (bf16[64,1024]{1,0:T(8,128)(2,1)S(1)}, bf16[64,1024]{1,0:T(8,128)(2,1)S(1)}, u32[]{:S(2)}, u32[]{:S(2)}) collective-permute-start(bf16[64,1024]{1,0:T(8,128)(2,1)S(1)} %get-tuple-element.45.ready_ref), channel_id=1, source_target_pairs={{0,8},{8,16},{16,24},{24,0},{1,9},{9,17},{17,25},{25,1},{2,10},{10... | collective-permute-start | bytes 393224 | tf_op jit(solution)/shard_map/ppermute | solution.py:19
  6.3 1.6 %collective-permute-start.3 = (bf16[2,512,256]{2,1,0:T(8,128)(2,1)S(1)}, bf16[2,512,256]{2,1,0:T(8,128)(2,1)S(1)}, u32[]{:S(2)}, u32[]{:S(2)}) collective-permute-start(bf16[2,512,256]{2,1,0:T(8,128)(2,1)S(1)} %get-tuple-element.43), channel_id=1, source_target_pairs={{0,2},{1,3},{2,0},{3,1},{4,6},{5,7},{6,4},{7,5},{8,10},{9,11},{10,... | collective-permute-start | bytes 1572872 | tf_op jit(solution)/shard_map/ppermute | solution.py:23
  7.9 1.4 %shard_map.47 = (bf16[64,1024]{1,0:T(8,128)(2,1)S(1)}, bf16[64,1024]{1,0:T(8,128)(2,1)S(1)}, bf16[64,1024]{1,0:T(8,128)(2,1)S(1)}, bf16[64,1024]{1,0:T(8,128)(2,1)S(1)}) custom-call(bf16[1024,2048]{1,0:T(8,128)(2,1)S(1)} %get-tuple-element.38.joined_ref, bf16[1024,256]{1,0:T(8,128)(2,1)S(1)} %get-tuple-element.39.right_ref, f32[1,1024]{1,0:T(1,128)S(1)} %bitcast.5), custom_call_target="tpu_custom_call" | custom-call | flops 1073741824 | bytes 5246976 | tf_op jit(solution)/shard_map/pallas_call | solution.py:279
  12.9 2.7 %collective-permute-done.arrived_ref = bf16[64,1024]{1,0:T(8,128)(2,1)S(1)} collective-permute-done((bf16[64,1024]{1,0:T(8,128)(2,1)S(1)}, bf16[64,1024]{1,0:T(8,128)(2,1)S(1)}, u32[]{:S(2)}, u32[]{:S(2)}) %collective-permute-start) | collective-permute-done | bytes 131104 | tf_op jit(solution)/shard_map/ppermute | solution.py:19
  15.6 1.3 %shard_map.48 = bf16[64,1024]{1,0:T(8,128)(2,1)S(1)} custom-call(s32[1]{0:T(128)} %bitcast.level_ref, bf16[64,1024]{1,0:T(8,128)(2,1)S(1)} %collective-permute-done.arrived_ref, bf16[64,1024]{1,0:T(8,128)(2,1)S(1)} %get-tuple-element.41.ready_ref, bf16[1024,2048]{1,0:T(8,128)(2,1)S(1)} %get-tuple-element.38.joined_ref, f32[1,1024]{1,0:T(1,128)S(1)} %bitcast.7), custom_call_target="tpu_custom_call" | custom-call | flops 268435456 | bytes 4591616 | tf_op jit(solution)/shard_map/pallas_call | solution.py:279
  19.9 4.2 %collective-permute-done.1.arrived_ref = bf16[64,1024]{1,0:T(8,128)(2,1)S(1)} collective-permute-done((bf16[64,1024]{1,0:T(8,128)(2,1)S(1)}, bf16[64,1024]{1,0:T(8,128)(2,1)S(1)}, u32[]{:S(2)}, u32[]{:S(2)}) %collective-permute-start.1) | collective-permute-done | bytes 131104 | tf_op jit(solution)/shard_map/ppermute | solution.py:19
  28.8 2.9 %collective-permute-done.2.arrived_ref = bf16[64,1024]{1,0:T(8,128)(2,1)S(1)} collective-permute-done((bf16[64,1024]{1,0:T(8,128)(2,1)S(1)}, bf16[64,1024]{1,0:T(8,128)(2,1)S(1)}, u32[]{:S(2)}, u32[]{:S(2)}) %collective-permute-start.2) | collective-permute-done | bytes 131104 | tf_op jit(solution)/shard_map/ppermute | solution.py:19
  31.7 1.3 %shard_map.54 = (bf16[64,1024]{1,0:T(8,128)(2,1)S(1)}, bf16[128,1024]{1,0:T(8,128)(2,1)S(1)}) custom-call(s32[1]{0:T(128)} %bitcast.level_ref, bf16[64,1024]{1,0:T(8,128)(2,1)S(1)} %collective-permute-done.2.arrived_ref, bf16[64,1024]{1,0:T(8,128)(2,1)S(1)} %get-tuple-element.50.ready_ref, bf16[1024,2048]{1,0:T(8,128)(2,1)S(1)} %get-tuple-element.38.joined_ref, ...), custom_call_target="tpu_custom_call" | custom-call | flops 268435456 | bytes 4984832 | tf_op jit(solution)/shard_map/pallas_call | solution.py:279
  33.8 2.9 %collective-permute-start.11 = (bf16[128,1024]{1,0:T(8,128)(2,1)S(1)}, bf16[128,1024]{1,0:T(8,128)(2,1)S(1)}, u32[]{:S(2)}, u32[]{:S(2)}) collective-permute-start(bf16[128,1024]{1,0:T(8,128)(2,1)S(1)} %get-tuple-element.57), channel_id=1, source_target_pairs={{0,2},{1,3},{2,0},{3,1},{4,6},{5,7},{6,4},{7,5},{8,10},{9,11},{10,... | collective-permute-start | bytes 786440 | tf_op jit(solution)/shard_map/ppermute | solution.py:23
  38.1 1.6 %collective-permute-done.8.arrived_ref = bf16[64,1024]{1,0:T(8,128)(2,1)S(1)} collective-permute-done((bf16[64,1024]{1,0:T(8,128)(2,1)S(1)}, bf16[64,1024]{1,0:T(8,128)(2,1)S(1)}, u32[]{:S(2)}, u32[]{:S(2)}) %collective-permute-start.8) | collective-permute-done | bytes 131104 | tf_op jit(solution)/shard_map/ppermute | solution.py:19
  39.7 1.3 %shard_map.56 = (bf16[64,1024]{1,0:T(8,128)(2,1)S(1)}, bf16[128,1024]{1,0:T(8,128)(2,1)S(1)}) custom-call(s32[1]{0:T(128)} %bitcast.level_ref, bf16[64,1024]{1,0:T(8,128)(2,1)S(1)} %collective-permute-done.8.arrived_ref, bf16[64,1024]{1,0:T(8,128)(2,1)S(1)} %get-tuple-element.40.ready_ref, bf16[1024,2048]{1,0:T(8,128)(2,1)S(1)} %get-tuple-element.38.joined_ref, ...), custom_call_target="tpu_custom_call" | custom-call | flops 268435456 | bytes 4984832 | tf_op jit(solution)/shard_map/pallas_call | solution.py:279
  41.1 4.0 %collective-permute-done.9.arrived_ref = bf16[64,1024]{1,0:T(8,128)(2,1)S(1)} collective-permute-done((bf16[64,1024]{1,0:T(8,128)(2,1)S(1)}, bf16[64,1024]{1,0:T(8,128)(2,1)S(1)}, u32[]{:S(2)}, u32[]{:S(2)}) %collective-permute-start.9) | collective-permute-done | bytes 131104 | tf_op jit(solution)/shard_map/ppermute | solution.py:19
  47.4 1.3 %shard_map.58 = (bf16[64,1024]{1,0:T(8,128)(2,1)S(1)}, bf16[128,1024]{1,0:T(8,128)(2,1)S(1)}) custom-call(s32[1]{0:T(128)} %bitcast.level_ref, bf16[64,1024]{1,0:T(8,128)(2,1)S(1)} %collective-permute-done.10.arrived_ref, bf16[64,1024]{1,0:T(8,128)(2,1)S(1)} %get-tuple-element.41.ready_ref, bf16[1024,2048]{1,0:T(8,128)(2,1)S(1)} %get-tuple-element.38.joined_ref, ...), custom_call_target="tpu_custom_call" | custom-call | flops 268435456 | bytes 4984832 | tf_op jit(solution)/shard_map/pallas_call | solution.py:279
  49.0 3.4 %collective-permute-done.12.arrived_ref = bf16[64,1024]{1,0:T(8,128)(2,1)S(1)} collective-permute-done((bf16[64,1024]{1,0:T(8,128)(2,1)S(1)}, bf16[64,1024]{1,0:T(8,128)(2,1)S(1)}, u32[]{:S(2)}, u32[]{:S(2)}) %collective-permute-start.12) | collective-permute-done | bytes 131104 | tf_op jit(solution)/shard_map/ppermute | solution.py:19
  54.8 3.4 %collective-permute-start.16 = (bf16[64,1024]{1,0:T(8,128)(2,1)S(1)}, bf16[64,1024]{1,0:T(8,128)(2,1)S(1)}, u32[]{:S(2)}, u32[]{:S(2)}) collective-permute-start(bf16[64,1024]{1,0:T(8,128)(2,1)S(1)} %shard_map.59.refs_3_), channel_id=1, source_target_pairs={{0,2},{1,3},{2,0},{3,1},{4,6},{5,7},{6,4},{7,5},{8,10},{9,11},{10,... | collective-permute-start | bytes 393224 | tf_op jit(solution)/shard_map/ppermute | solution.py:23
  58.2 1.3 %shard_map.60.refs_7_ = bf16[64,1024]{1,0:T(8,128)(2,1)S(1)} custom-call(s32[1]{0:T(128)} %bitcast.level_ref, bf16[64,1024]{1,0:T(8,128)(2,1)S(1)} %collective-permute-done.13.arrived_ref, bf16[64,1024]{1,0:T(8,128)(2,1)S(1)} %get-tuple-element.42.ready_ref, bf16[1024,2048]{1,0:T(8,128)(2,1)S(1)} %get-tuple-element.38.joined_ref, f32[1,1024]{1,0:T(1,128)S(1)} %bitcast.17), custom_call_target="tpu_custom_call" | custom-call | flops 268435456 | bytes 4591616 | tf_op jit(solution)/shard_map/pallas_call | solution.py:279
  59.6 1.5 %collective-permute-done.16.refs_11_ = bf16[64,1024]{1,0:T(8,128)(2,1)S(1)} collective-permute-done((bf16[64,1024]{1,0:T(8,128)(2,1)S(1)}, bf16[64,1024]{1,0:T(8,128)(2,1)S(1)}, u32[]{:S(2)}, u32[]{:S(2)}) %collective-permute-start.16) | collective-permute-done | bytes 131104 | tf_op jit(solution)/shard_map/ppermute | solution.py:23
  61.2 1.9 %shard_map.61.early_ref = f32[1024,1024]{1,0:T(8,128)S(1)} custom-call(s32[1]{0:T(128)} %bitcast.level_ref, bf16[1024,1024]{1,0:T(8,128)(2,1)S(1)} %shard_map.50.left_ref, bf16[64,1024]{1,0:T(8,128)(2,1)S(1)} %shard_map.53.refs_0_, bf16[64,1024]{1,0:T(8,128)(2,1)S(1)} %shard_map.55.refs_0_.refs_1_, bf16[64,1024]{1,0:T(8,128)(2,1)S(1)} %shard_map.57.refs_0_.refs_2_, ...), custom_call_target="tpu_custom_call" | custom-call | flops 1610612736 | bytes 8257536 | tf_op jit(solution)/shard_map/pallas_call | solution.py:279
  63.1 1.5 %collective-permute-done.17.refs_3_ = bf16[64,1024]{1,0:T(8,128)(2,1)S(1)} collective-permute-done((bf16[64,1024]{1,0:T(8,128)(2,1)S(1)}, bf16[64,1024]{1,0:T(8,128)(2,1)S(1)}, u32[]{:S(2)}, u32[]{:S(2)}) %collective-permute-start.17) | collective-permute-done | bytes 131104 | tf_op jit(solution)/shard_map/ppermute | solution.py:23
  65.4 2.6 %collective-permute-done.18.refs_1_ = bf16[2,2,128,1024]{3,2,1,0:T(8,128)(2,1)S(1)} collective-permute-done((bf16[2,2,128,1024]{3,2,1,0:T(8,128)(2,1)S(1)}, bf16[2,2,128,1024]{3,2,1,0:T(8,128)(2,1)S(1)}, u32[]{:S(2)}, u32[]{:S(2)}) %collective-permute-start.18) | collective-permute-done | bytes 1048608 | tf_op jit(solution)/shard_map/ppermute | solution.py:23
  68.3 2.7 %collective-permute-start.19 = (bf16[1,2,128,1024]{3,2,1,0:T(8,128)(2,1)S(1)}, bf16[1,2,128,1024]{3,2,1,0:T(8,128)(2,1)S(1)}, u32[]{:S(2)}, u32[]{:S(2)}) collective-permute-start(bf16[1,2,128,1024]{3,2,1,0:T(8,128)(2,1)S(1)} %add_convert_fusion), channel_id=1, source_target_pairs={{0,4},{1,5},{2,6},{3,7},{4,0},{5,1},{6,2},{7,3},{8,12},{9,13},{10,... | collective-permute-start | bytes 1572872 | tf_op jit(solution)/shard_map/ppermute | solution.py:19
  71.0 23.4 %collective-permute-done.19.refs_2_ = bf16[1,2,128,1024]{3,2,1,0:T(8,128)(2,1)S(1)} collective-permute-done((bf16[1,2,128,1024]{3,2,1,0:T(8,128)(2,1)S(1)}, bf16[1,2,128,1024]{3,2,1,0:T(8,128)(2,1)S(1)}, u32[]{:S(2)}, u32[]{:S(2)}) %collective-permute-start.19) | collective-permute-done | bytes 524320 | tf_op jit(solution)/shard_map/ppermute | solution.py:19
  94.4 1.3 %shard_map.63 = f32[1,128,2,1024]{3,2,1,0:T(2,128)} custom-call(f32[2,2,128,1024]{3,2,1,0:T(8,128)S(1)} %get-tuple-element.69.refs_0_, bf16[2,2,128,1024]{3,2,1,0:T(8,128)(2,1)S(1)} %collective-permute-done.18.refs_1_, bf16[1,2,128,1024]{3,2,1,0:T(8,128)(2,1)S(1)} %collective-permute-done.19.refs_2_), custom_call_target="tpu_custom_call" | custom-call | flops 786432 | bytes 4718592 | tf_op jit(solution)/shard_map/pallas_call | solution.py:279
  (39 shorter events, 19.5 us)
Async XLA Ops:
  0.0 7.9 %copy-start.1 = (f32[1,1,1024]{2,1,0:T(1,128)S(1)}, f32[1,1,1024]{2,1,0:T(1,128)}, u32[]{:S(2)}) copy-start(f32[1,1,1024]{2,1,0:T(1,128)} %factor_ref.1) | copy-start | bytes 12292
  4.7 6.2 %collective-permute-start.4 = (bf16[64,1024]{1,0:T(8,128)(2,1)S(1)}, bf16[64,1024]{1,0:T(8,128)(2,1)S(1)}, u32[]{:S(2)}, u32[]{:S(2)}) collective-permute-start(bf16[64,1024]{1,0:T(8,128)(2,1)S(1)} %get-tuple-element.45.ready_ref), channel_id=1, source_target_pairs={{0,8},{8,16},{16,24},{24,0},{1,9},{9,17},{17,25},{25,1},{2,10},{10... | collective-permute-start | bytes 393224 | tf_op jit(solution)/shard_map/ppermute | solution.py:19
  6.3 21.7 %collective-permute-start.3 = (bf16[2,512,256]{2,1,0:T(8,128)(2,1)S(1)}, bf16[2,512,256]{2,1,0:T(8,128)(2,1)S(1)}, u32[]{:S(2)}, u32[]{:S(2)}) collective-permute-start(bf16[2,512,256]{2,1,0:T(8,128)(2,1)S(1)} %get-tuple-element.43), channel_id=1, source_target_pairs={{0,2},{1,3},{2,0},{3,1},{4,6},{5,7},{6,4},{7,5},{8,10},{9,11},{10,... | collective-permute-start | bytes 1572872 | tf_op jit(solution)/shard_map/ppermute | solution.py:23
  9.2 6.3 %collective-permute-start = (bf16[64,1024]{1,0:T(8,128)(2,1)S(1)}, bf16[64,1024]{1,0:T(8,128)(2,1)S(1)}, u32[]{:S(2)}, u32[]{:S(2)}) collective-permute-start(bf16[64,1024]{1,0:T(8,128)(2,1)S(1)} %get-tuple-element.40.ready_ref), channel_id=1, source_target_pairs={{0,8},{8,16},{16,24},{24,0},{1,9},{9,17},{17,25},{25,1},{2,10},{10... | collective-permute-start | bytes 393224 | tf_op jit(solution)/shard_map/ppermute | solution.py:19
  12.2 5.9 %collective-permute-start.5 = (bf16[64,1024]{1,0:T(8,128)(2,1)S(1)}, bf16[64,1024]{1,0:T(8,128)(2,1)S(1)}, u32[]{:S(2)}, u32[]{:S(2)}) collective-permute-start(bf16[64,1024]{1,0:T(8,128)(2,1)S(1)} %shard_map.51), channel_id=1, source_target_pairs={{0,8},{8,16},{16,24},{24,0},{1,9},{9,17},{17,25},{25,1},{2,10},{10... | collective-permute-start | bytes 393224 | tf_op jit(solution)/shard_map/ppermute | solution.py:19
  16.9 7.1 %collective-permute-start.1 = (bf16[64,1024]{1,0:T(8,128)(2,1)S(1)}, bf16[64,1024]{1,0:T(8,128)(2,1)S(1)}, u32[]{:S(2)}, u32[]{:S(2)}) collective-permute-start(bf16[64,1024]{1,0:T(8,128)(2,1)S(1)} %shard_map.48), channel_id=1, source_target_pairs={{0,8},{8,16},{16,24},{24,0},{1,9},{9,17},{17,25},{25,1},{2,10},{10... | collective-permute-start | bytes 393224 | tf_op jit(solution)/shard_map/ppermute | solution.py:19
  19.5 7.1 %collective-permute-start.6 = (bf16[64,1024]{1,0:T(8,128)(2,1)S(1)}, bf16[64,1024]{1,0:T(8,128)(2,1)S(1)}, u32[]{:S(2)}, u32[]{:S(2)}) collective-permute-start(bf16[64,1024]{1,0:T(8,128)(2,1)S(1)} %shard_map.52), channel_id=1, source_target_pairs={{0,8},{8,16},{16,24},{24,0},{1,9},{9,17},{17,25},{25,1},{2,10},{10... | collective-permute-start | bytes 393224 | tf_op jit(solution)/shard_map/ppermute | solution.py:19
  24.0 3.9 %copy-start = (bf16[1,1,2,1024,256]{4,3,2,1,0:T(8,128)(2,1)S(1)}, bf16[1,1,2,1024,256]{4,3,2,1,0:T(8,128)(2,1)}, u32[]{:S(2)}) copy-start(bf16[1,1,2,1024,256]{4,3,2,1,0:T(8,128)(2,1)} %upward_ref.1) | copy-start | bytes 3145732
  25.4 6.3 %collective-permute-start.2 = (bf16[64,1024]{1,0:T(8,128)(2,1)S(1)}, bf16[64,1024]{1,0:T(8,128)(2,1)S(1)}, u32[]{:S(2)}, u32[]{:S(2)}) collective-permute-start(bf16[64,1024]{1,0:T(8,128)(2,1)S(1)} %shard_map.49), channel_id=1, source_target_pairs={{0,8},{8,16},{16,24},{24,0},{1,9},{9,17},{17,25},{25,1},{2,10},{10... | collective-permute-start | bytes 393224 | tf_op jit(solution)/shard_map/ppermute | solution.py:19
  27.9 5.9 %collective-permute-start.7 = (bf16[64,1024]{1,0:T(8,128)(2,1)S(1)}, bf16[64,1024]{1,0:T(8,128)(2,1)S(1)}, u32[]{:S(2)}, u32[]{:S(2)}) collective-permute-start(bf16[64,1024]{1,0:T(8,128)(2,1)S(1)} %shard_map.53.refs_0_), channel_id=1, source_target_pairs={{0,8},{8,16},{16,24},{24,0},{1,9},{9,17},{17,25},{25,1},{2,10},{10... | collective-permute-start | bytes 393224 | tf_op jit(solution)/shard_map/ppermute | solution.py:19
  33.8 5.9 %collective-permute-start.8 = (bf16[64,1024]{1,0:T(8,128)(2,1)S(1)}, bf16[64,1024]{1,0:T(8,128)(2,1)S(1)}, u32[]{:S(2)}, u32[]{:S(2)}) collective-permute-start(bf16[64,1024]{1,0:T(8,128)(2,1)S(1)} %get-tuple-element.53.refs_4_), channel_id=1, source_target_pairs={{0,8},{8,16},{16,24},{24,0},{1,9},{9,17},{17,25},{25,1},{2,10},{10... | collective-permute-start | bytes 393224 | tf_op jit(solution)/shard_map/ppermute | solution.py:19
  33.8 13.5 %collective-permute-start.11 = (bf16[128,1024]{1,0:T(8,128)(2,1)S(1)}, bf16[128,1024]{1,0:T(8,128)(2,1)S(1)}, u32[]{:S(2)}, u32[]{:S(2)}) collective-permute-start(bf16[128,1024]{1,0:T(8,128)(2,1)S(1)} %get-tuple-element.57), channel_id=1, source_target_pairs={{0,2},{1,3},{2,0},{3,1},{4,6},{5,7},{6,4},{7,5},{8,10},{9,11},{10,... | collective-permute-start | bytes 786440 | tf_op jit(solution)/shard_map/ppermute | solution.py:23
  38.0 7.1 %collective-permute-start.9 = (bf16[64,1024]{1,0:T(8,128)(2,1)S(1)}, bf16[64,1024]{1,0:T(8,128)(2,1)S(1)}, u32[]{:S(2)}, u32[]{:S(2)}) collective-permute-start(bf16[64,1024]{1,0:T(8,128)(2,1)S(1)} %shard_map.55.refs_0_.refs_1_), channel_id=1, source_target_pairs={{0,8},{8,16},{16,24},{24,0},{1,9},{9,17},{17,25},{25,1},{2,10},{10... | collective-permute-start | bytes 393224 | tf_op jit(solution)/shard_map/ppermute | solution.py:19
  41.0 6.3 %collective-permute-start.10 = (bf16[64,1024]{1,0:T(8,128)(2,1)S(1)}, bf16[64,1024]{1,0:T(8,128)(2,1)S(1)}, u32[]{:S(2)}, u32[]{:S(2)}) collective-permute-start(bf16[64,1024]{1,0:T(8,128)(2,1)S(1)} %get-tuple-element.56.refs_5_), channel_id=1, source_target_pairs={{0,8},{8,16},{16,24},{24,0},{1,9},{9,17},{17,25},{25,1},{2,10},{10... | collective-permute-start | bytes 393224 | tf_op jit(solution)/shard_map/ppermute | solution.py:19
  46.5 5.9 %collective-permute-start.12 = (bf16[64,1024]{1,0:T(8,128)(2,1)S(1)}, bf16[64,1024]{1,0:T(8,128)(2,1)S(1)}, u32[]{:S(2)}, u32[]{:S(2)}) collective-permute-start(bf16[64,1024]{1,0:T(8,128)(2,1)S(1)} %shard_map.57.refs_0_.refs_2_), channel_id=1, source_target_pairs={{0,8},{8,16},{16,24},{24,0},{1,9},{9,17},{17,25},{25,1},{2,10},{10... | collective-permute-start | bytes 393224 | tf_op jit(solution)/shard_map/ppermute | solution.py:19
  46.5 11.7 %collective-permute-start.14 = (bf16[128,1024]{1,0:T(8,128)(2,1)S(1)}, bf16[128,1024]{1,0:T(8,128)(2,1)S(1)}, u32[]{:S(2)}, u32[]{:S(2)}) collective-permute-start(bf16[128,1024]{1,0:T(8,128)(2,1)S(1)} %get-tuple-element.63), channel_id=1, source_target_pairs={{0,2},{1,3},{2,0},{3,1},{4,6},{5,7},{6,4},{7,5},{8,10},{9,11},{10,... | collective-permute-start | bytes 786440 | tf_op jit(solution)/shard_map/ppermute | solution.py:23
  48.7 6.1 %collective-permute-start.13 = (bf16[64,1024]{1,0:T(8,128)(2,1)S(1)}, bf16[64,1024]{1,0:T(8,128)(2,1)S(1)}, u32[]{:S(2)}, u32[]{:S(2)}) collective-permute-start(bf16[64,1024]{1,0:T(8,128)(2,1)S(1)} %get-tuple-element.61.refs_6_), channel_id=1, source_target_pairs={{0,8},{8,16},{16,24},{24,0},{1,9},{9,17},{17,25},{25,1},{2,10},{10... | collective-permute-start | bytes 393224 | tf_op jit(solution)/shard_map/ppermute | solution.py:19
  52.4 8.8 %collective-permute-start.15 = (bf16[128,1024]{1,0:T(8,128)(2,1)S(1)}, bf16[128,1024]{1,0:T(8,128)(2,1)S(1)}, u32[]{:S(2)}, u32[]{:S(2)}) collective-permute-start(bf16[128,1024]{1,0:T(8,128)(2,1)S(1)} %get-tuple-element.67), channel_id=1, source_target_pairs={{0,2},{1,3},{2,0},{3,1},{4,6},{5,7},{6,4},{7,5},{8,10},{9,11},{10,... | collective-permute-start | bytes 786440 | tf_op jit(solution)/shard_map/ppermute | solution.py:23
  54.8 6.4 %collective-permute-start.16 = (bf16[64,1024]{1,0:T(8,128)(2,1)S(1)}, bf16[64,1024]{1,0:T(8,128)(2,1)S(1)}, u32[]{:S(2)}, u32[]{:S(2)}) collective-permute-start(bf16[64,1024]{1,0:T(8,128)(2,1)S(1)} %shard_map.59.refs_3_), channel_id=1, source_target_pairs={{0,2},{1,3},{2,0},{3,1},{4,6},{5,7},{6,4},{7,5},{8,10},{9,11},{10,... | collective-permute-start | bytes 393224 | tf_op jit(solution)/shard_map/ppermute | solution.py:23
  59.6 5.0 %collective-permute-start.17 = (bf16[64,1024]{1,0:T(8,128)(2,1)S(1)}, bf16[64,1024]{1,0:T(8,128)(2,1)S(1)}, u32[]{:S(2)}, u32[]{:S(2)}) collective-permute-start(bf16[64,1024]{1,0:T(8,128)(2,1)S(1)} %shard_map.60.refs_7_), channel_id=1, source_target_pairs={{0,2},{1,3},{2,0},{3,1},{4,6},{5,7},{6,4},{7,5},{8,10},{9,11},{10,... | collective-permute-start | bytes 393224 | tf_op jit(solution)/shard_map/ppermute | solution.py:23
  65.4 2.7 %collective-permute-start.18 = (bf16[2,2,128,1024]{3,2,1,0:T(8,128)(2,1)S(1)}, bf16[2,2,128,1024]{3,2,1,0:T(8,128)(2,1)S(1)}, u32[]{:S(2)}, u32[]{:S(2)}) collective-permute-start(bf16[2,2,128,1024]{3,2,1,0:T(8,128)(2,1)S(1)} %get-tuple-element.70), channel_id=1, source_target_pairs={{0,1},{1,0},{2,3},{3,2},{4,5},{5,4},{6,7},{7,6},{8,9},{9,8},{10,11... | collective-permute-start | bytes 3145736 | tf_op jit(solution)/shard_map/ppermute | solution.py:23
  68.3 26.1 %collective-permute-start.19 = (bf16[1,2,128,1024]{3,2,1,0:T(8,128)(2,1)S(1)}, bf16[1,2,128,1024]{3,2,1,0:T(8,128)(2,1)S(1)}, u32[]{:S(2)}, u32[]{:S(2)}) collective-permute-start(bf16[1,2,128,1024]{3,2,1,0:T(8,128)(2,1)S(1)} %add_convert_fusion), channel_id=1, source_target_pairs={{0,4},{1,5},{2,6},{3,7},{4,0},{5,1},{6,2},{7,3},{8,12},{9,13},{10,... | collective-permute-start | bytes 1572872 | tf_op jit(solution)/shard_map/ppermute | solution.py:19

commit v13 on v12

--- a/solution.py
+++ b/solution.py
@@ -340,7 +340,6 @@
     steps = STEPS + levels - 1
     flying = [None] * STREAMS
     own = [[] for _ in range(STREAMS)]
-    waiting = []
     crossing = []
     for event in range(STREAMS * steps):
         step, stream = divmod(event, STREAMS)
@@ -349,9 +348,6 @@
             arrived = flying[stream]
             if event == steps:
                 arrived, left = lax.optimization_barrier((arrived, left))
-            if waiting:
-                panel, arrived = lax.optimization_barrier((waiting.pop(), arrived))
-                crossing.append((event, swapped(panel, "freq", 2)))
             for at, (sent, panel) in enumerate(crossing):
                 if event == sent + BEHIND:
                     arrived, panel = lax.optimization_barrier((arrived, panel))
@@ -359,12 +355,12 @@
             pair = stream > 0 and levels - 1 <= step < steps - 1
             out, *both = advance(level, arrived, out, joined, factor, own[0][-1] if pair else None)
             if step >= levels - 1 and (pair or step == steps - 1):
-                waiting.append(both[0] if pair else out)
+                crossing.append((event, swapped(both[0] if pair else out, "freq", 2)))
         if step + 1 < steps:
             flying[stream] = ring(out, "depth", 1)
         if step >= levels - 1:
             own[stream].append(out)
-    other = [panel for _, panel in crossing] + [swapped(waiting.pop(), "freq", 2)]
+    other = [panel for _, panel in crossing]
     early = early_terms(level, left, own[0] + own[1] + other[:-1], levels)
     keep, send = late_terms(level, left, early, other[:-2] + other[-1:], rows, levels)
     near = swapped(send, "freq", 1)

time: 96 us -> 93.5 us (0.974)
  starting transfers between devices: 16.1 us -> 12.5 us
  waiting for transfers between devices: 52.6 us -> 53.6 us
    ppermute x7, starting transfers between devices: 9.65 us -> 6.37 us  [swapped(): lax.ppermute(block, axis, [(i, i ^ bit) for i in range(lax.axis_size(axis...]
    ppermute x13, waiting for transfers between devices: 46.9 us -> 49.8 us  [ring(): lax.ppermute(block, axis, [(i, (i + distance) % size) for i in range(size)])]
    ppermute x7, waiting for transfers between devices: 5.72 us -> 3.77 us  [swapped(): lax.ppermute(block, axis, [(i, i ^ bit) for i in range(lax.axis_size(axis...]
where the time goes in v13:
time: 93.5 us; the launch traced here: 93.2 us
  waiting for transfers between devices  53.6 us (57%)
  Pallas kernels  26.7 us (29%)
  starting transfers between devices  12.5 us (13%)
    ppermute x13, waiting for transfers between devices, ring(): lax.ppermute(block, axis, [(i, (i + distance) % size) for i in range(size)])  49.8 us
    pallas_call x16, Pallas kernels, whole_call(): pl.pallas_call(kernel, in_specs=[pl.BlockSpec(memory_space=pltpu.SMEM)] *...  21.2 us
    ppermute x7, starting transfers between devices, swapped(): lax.ppermute(block, axis, [(i, i ^ bit) for i in range(lax.axis_size(axis...  6.37 us
    ppermute x13, starting transfers between devices, ring(): lax.ppermute(block, axis, [(i, (i + distance) % size) for i in range(size)])  6.13 us
    pallas_call x1, Pallas kernels, first_advance(): pl.pallas_call(functools.partial(first_kernel, part), in_specs=[pl.BlockS...  4.72 us
    ppermute x7, waiting for transfers between devices, swapped(): lax.ppermute(block, axis, [(i, i ^ bit) for i in range(lax.axis_size(axis...  3.77 us
  transfers between devices with their start and end apart: 20, of which 15 were waited for; matrix products, arithmetic and copies ran while one was open for 0% of the time, Pallas kernels for 21%

profile of v13, /device:TPU:4, one launch (start us, length us, event | category | flops | bytes accessed | tf_op | source)
XLA Modules:
  0.0 93.2 jit_solution(2000331990619035843)
XLA Ops:
  0.0 4.7 %shard_map.46 = (bf16[64,1024]{1,0:T(8,128)(2,1)S(1)}, bf16[64,1024]{1,0:T(8,128)(2,1)S(1)}, bf16[64,1024]{1,0:T(8,128)(2,1)S(1)}, bf16[64,1024]{1,0:T(8,128)(2,...) custom-call(s32[1]{0:T(128)} %bitcast.level_ref, ...), custom_call_target="tpu_custom_call" | custom-call | flops 1073741824 | bytes 6291456 | tf_op jit(solution)/shard_map/pallas_call | solution.py:106
  4.7 1.5 %collective-permute-start.4 = (bf16[64,1024]{1,0:T(8,128)(2,1)S(1)}, bf16[64,1024]{1,0:T(8,128)(2,1)S(1)}, u32[]{:S(2)}, u32[]{:S(2)}) collective-permute-start(bf16[64,1024]{1,0:T(8,128)(2,1)S(1)} %get-tuple-element.37.ready_ref), channel_id=1, source_target_pairs={{0,8},{8,16},{16,24},{24,0},{1,9},{9,17},{17,25},{25,1},{2,10},{10... | collective-permute-start | bytes 393224 | tf_op jit(solution)/shard_map/ppermute | solution.py:19
  6.3 1.6 %collective-permute-start.3 = (bf16[2,512,256]{2,1,0:T(8,128)(2,1)S(1)}, bf16[2,512,256]{2,1,0:T(8,128)(2,1)S(1)}, u32[]{:S(2)}, u32[]{:S(2)}) collective-permute-start(bf16[2,512,256]{2,1,0:T(8,128)(2,1)S(1)} %get-tuple-element.35), channel_id=1, source_target_pairs={{0,2},{1,3},{2,0},{3,1},{4,6},{5,7},{6,4},{7,5},{8,10},{9,11},{10,... | collective-permute-start | bytes 1572872 | tf_op jit(solution)/shard_map/ppermute | solution.py:23
  7.9 1.4 %shard_map.47 = (bf16[64,1024]{1,0:T(8,128)(2,1)S(1)}, bf16[64,1024]{1,0:T(8,128)(2,1)S(1)}, bf16[64,1024]{1,0:T(8,128)(2,1)S(1)}, bf16[64,1024]{1,0:T(8,128)(2,1)S(1)}) custom-call(bf16[1024,2048]{1,0:T(8,128)(2,1)S(1)} %get-tuple-element.30.joined_ref, bf16[1024,256]{1,0:T(8,128)(2,1)S(1)} %get-tuple-element.31.right_ref, f32[1,1024]{1,0:T(1,128)S(1)} %bitcast.5), custom_call_target="tpu_custom_call" | custom-call | flops 1073741824 | bytes 5246976 | tf_op jit(solution)/shard_map/pallas_call | solution.py:279
  12.9 2.6 %collective-permute-done.arrived_ref = bf16[64,1024]{1,0:T(8,128)(2,1)S(1)} collective-permute-done((bf16[64,1024]{1,0:T(8,128)(2,1)S(1)}, bf16[64,1024]{1,0:T(8,128)(2,1)S(1)}, u32[]{:S(2)}, u32[]{:S(2)}) %collective-permute-start) | collective-permute-done | bytes 131104 | tf_op jit(solution)/shard_map/ppermute | solution.py:19
  15.5 1.3 %shard_map.48 = bf16[64,1024]{1,0:T(8,128)(2,1)S(1)} custom-call(s32[1]{0:T(128)} %bitcast.level_ref, bf16[64,1024]{1,0:T(8,128)(2,1)S(1)} %collective-permute-done.arrived_ref, bf16[64,1024]{1,0:T(8,128)(2,1)S(1)} %get-tuple-element.33.ready_ref, bf16[1024,2048]{1,0:T(8,128)(2,1)S(1)} %get-tuple-element.30.joined_ref, f32[1,1024]{1,0:T(1,128)S(1)} %bitcast.7), custom_call_target="tpu_custom_call" | custom-call | flops 268435456 | bytes 4591616 | tf_op jit(solution)/shard_map/pallas_call | solution.py:279
  19.9 4.1 %collective-permute-done.1.arrived_ref = bf16[64,1024]{1,0:T(8,128)(2,1)S(1)} collective-permute-done((bf16[64,1024]{1,0:T(8,128)(2,1)S(1)}, bf16[64,1024]{1,0:T(8,128)(2,1)S(1)}, u32[]{:S(2)}, u32[]{:S(2)}) %collective-permute-start.1) | collective-permute-done | bytes 131104 | tf_op jit(solution)/shard_map/ppermute | solution.py:19
  28.7 2.9 %collective-permute-done.2.arrived_ref = bf16[64,1024]{1,0:T(8,128)(2,1)S(1)} collective-permute-done((bf16[64,1024]{1,0:T(8,128)(2,1)S(1)}, bf16[64,1024]{1,0:T(8,128)(2,1)S(1)}, u32[]{:S(2)}, u32[]{:S(2)}) %collective-permute-start.2) | collective-permute-done | bytes 131104 | tf_op jit(solution)/shard_map/ppermute | solution.py:19
  31.7 1.3 %shard_map.55 = (bf16[64,1024]{1,0:T(8,128)(2,1)S(1)}, bf16[128,1024]{1,0:T(8,128)(2,1)S(1)}) custom-call(s32[1]{0:T(128)} %bitcast.level_ref, bf16[64,1024]{1,0:T(8,128)(2,1)S(1)} %collective-permute-done.2.arrived_ref, bf16[64,1024]{1,0:T(8,128)(2,1)S(1)} %get-tuple-element.42.ready_ref, bf16[1024,2048]{1,0:T(8,128)(2,1)S(1)} %get-tuple-element.30.joined_ref, ...), custom_call_target="tpu_custom_call" | custom-call | flops 268435456 | bytes 4984832 | tf_op jit(solution)/shard_map/pallas_call | solution.py:279
  33.1 1.9 %collective-permute-done.7.arrived_ref = bf16[64,1024]{1,0:T(8,128)(2,1)S(1)} collective-permute-done((bf16[64,1024]{1,0:T(8,128)(2,1)S(1)}, bf16[64,1024]{1,0:T(8,128)(2,1)S(1)}, u32[]{:S(2)}, u32[]{:S(2)}) %collective-permute-start.7) | collective-permute-done | bytes 131104 | tf_op jit(solution)/shard_map/ppermute | solution.py:19
  36.4 2.6 %collective-permute-done.11.arrived_ref = bf16[64,1024]{1,0:T(8,128)(2,1)S(1)} collective-permute-done((bf16[64,1024]{1,0:T(8,128)(2,1)S(1)}, bf16[64,1024]{1,0:T(8,128)(2,1)S(1)}, u32[]{:S(2)}, u32[]{:S(2)}) %collective-permute-start.11) | collective-permute-done | bytes 131104 | tf_op jit(solution)/shard_map/ppermute | solution.py:19
  39.0 1.3 %shard_map.57 = (bf16[64,1024]{1,0:T(8,128)(2,1)S(1)}, bf16[128,1024]{1,0:T(8,128)(2,1)S(1)}) custom-call(s32[1]{0:T(128)} %bitcast.level_ref, bf16[64,1024]{1,0:T(8,128)(2,1)S(1)} %collective-permute-done.11.arrived_ref, bf16[64,1024]{1,0:T(8,128)(2,1)S(1)} %get-tuple-element.32.ready_ref, bf16[1024,2048]{1,0:T(8,128)(2,1)S(1)} %get-tuple-element.30.joined_ref, ...), custom_call_target="tpu_custom_call" | custom-call | flops 268435456 | bytes 4984832 | tf_op jit(solution)/shard_map/pallas_call | solution.py:279
  40.3 2.0 %collective-permute-start.12 = (bf16[128,1024]{1,0:T(8,128)(2,1)S(1)}, bf16[128,1024]{1,0:T(8,128)(2,1)S(1)}, u32[]{:S(2)}, u32[]{:S(2)}) collective-permute-start(bf16[128,1024]{1,0:T(8,128)(2,1)S(1)} %get-tuple-element.46), channel_id=1, source_target_pairs={{0,2},{1,3},{2,0},{3,1},{4,6},{5,7},{6,4},{7,5},{8,10},{9,11},{10,... | collective-permute-start | bytes 786440 | tf_op jit(solution)/shard_map/ppermute | solution.py:23
  45.0 3.2 %collective-permute-done.13.arrived_ref = bf16[64,1024]{1,0:T(8,128)(2,1)S(1)} collective-permute-done((bf16[64,1024]{1,0:T(8,128)(2,1)S(1)}, bf16[64,1024]{1,0:T(8,128)(2,1)S(1)}, u32[]{:S(2)}, u32[]{:S(2)}) %collective-permute-start.13) | collective-permute-done | bytes 131104 | tf_op jit(solution)/shard_map/ppermute | solution.py:19
  48.2 1.5 %shard_map.59 = (bf16[64,1024]{1,0:T(8,128)(2,1)S(1)}, bf16[128,1024]{1,0:T(8,128)(2,1)S(1)}) custom-call(s32[1]{0:T(128)} %bitcast.level_ref, bf16[64,1024]{1,0:T(8,128)(2,1)S(1)} %collective-permute-done.13.arrived_ref, bf16[64,1024]{1,0:T(8,128)(2,1)S(1)} %get-tuple-element.33.ready_ref, bf16[1024,2048]{1,0:T(8,128)(2,1)S(1)} %get-tuple-element.30.joined_ref, ...), custom_call_target="tpu_custom_call" | custom-call | flops 268435456 | bytes 4984832 | tf_op jit(solution)/shard_map/pallas_call | solution.py:279
  49.9 2.3 %collective-permute-done.10.arrived_ref = bf16[64,1024]{1,0:T(8,128)(2,1)S(1)} collective-permute-done((bf16[64,1024]{1,0:T(8,128)(2,1)S(1)}, bf16[64,1024]{1,0:T(8,128)(2,1)S(1)}, u32[]{:S(2)}, u32[]{:S(2)}) %collective-permute-start.10) | collective-permute-done | bytes 131104 | tf_op jit(solution)/shard_map/ppermute | solution.py:19
  52.1 1.3 %shard_map.58.refs_3_ = bf16[64,1024]{1,0:T(8,128)(2,1)S(1)} custom-call(s32[1]{0:T(128)} %bitcast.level_ref, bf16[64,1024]{1,0:T(8,128)(2,1)S(1)} %collective-permute-done.10.arrived_ref, bf16[64,1024]{1,0:T(8,128)(2,1)S(1)} %get-tuple-element.39.ready_ref, bf16[1024,2048]{1,0:T(8,128)(2,1)S(1)} %get-tuple-element.30.joined_ref, f32[1,1024]{1,0:T(1,128)S(1)} %bitcast.16), custom_call_target="tpu_custom_call" | custom-call | flops 268435456 | bytes 4591616 | tf_op jit(solution)/shard_map/pallas_call | solution.py:279
  53.9 1.9 %collective-permute-done.14.arrived_ref = bf16[64,1024]{1,0:T(8,128)(2,1)S(1)} collective-permute-done((bf16[64,1024]{1,0:T(8,128)(2,1)S(1)}, bf16[64,1024]{1,0:T(8,128)(2,1)S(1)}, u32[]{:S(2)}, u32[]{:S(2)}) %collective-permute-start.14) | collective-permute-done | bytes 131104 | tf_op jit(solution)/shard_map/ppermute | solution.py:19
  57.0 2.0 %collective-permute-start.17 = (bf16[64,1024]{1,0:T(8,128)(2,1)S(1)}, bf16[64,1024]{1,0:T(8,128)(2,1)S(1)}, u32[]{:S(2)}, u32[]{:S(2)}) collective-permute-start(bf16[64,1024]{1,0:T(8,128)(2,1)S(1)} %shard_map.60.refs_7_), channel_id=1, source_target_pairs={{0,2},{1,3},{2,0},{3,1},{4,6},{5,7},{6,4},{7,5},{8,10},{9,11},{10,... | collective-permute-start | bytes 393224 | tf_op jit(solution)/shard_map/ppermute | solution.py:23
  59.1 1.9 %shard_map.61.early_ref = f32[1024,1024]{1,0:T(8,128)S(1)} custom-call(s32[1]{0:T(128)} %bitcast.level_ref, bf16[1024,1024]{1,0:T(8,128)(2,1)S(1)} %shard_map.50.left_ref, bf16[64,1024]{1,0:T(8,128)(2,1)S(1)} %shard_map.53.refs_0_, bf16[64,1024]{1,0:T(8,128)(2,1)S(1)} %shard_map.54.refs_0_.refs_1_, bf16[64,1024]{1,0:T(8,128)(2,1)S(1)} %shard_map.56.refs_0_.refs_2_, ...), custom_call_target="tpu_custom_call" | custom-call | flops 1610612736 | bytes 8257536 | tf_op jit(solution)/shard_map/pallas_call | solution.py:279
  62.9 2.6 %collective-permute-done.18.refs_1_ = bf16[2,2,128,1024]{3,2,1,0:T(8,128)(2,1)S(1)} collective-permute-done((bf16[2,2,128,1024]{3,2,1,0:T(8,128)(2,1)S(1)}, bf16[2,2,128,1024]{3,2,1,0:T(8,128)(2,1)S(1)}, u32[]{:S(2)}, u32[]{:S(2)}) %collective-permute-start.18) | collective-permute-done | bytes 1048608 | tf_op jit(solution)/shard_map/ppermute | solution.py:23
  65.7 2.7 %collective-permute-start.19 = (bf16[1,2,128,1024]{3,2,1,0:T(8,128)(2,1)S(1)}, bf16[1,2,128,1024]{3,2,1,0:T(8,128)(2,1)S(1)}, u32[]{:S(2)}, u32[]{:S(2)}) collective-permute-start(bf16[1,2,128,1024]{3,2,1,0:T(8,128)(2,1)S(1)} %add_convert_fusion), channel_id=1, source_target_pairs={{0,4},{1,5},{2,6},{3,7},{4,0},{5,1},{6,2},{7,3},{8,12},{9,13},{10,... | collective-permute-start | bytes 1572872 | tf_op jit(solution)/shard_map/ppermute | solution.py:19
  68.4 23.5 %collective-permute-done.19.refs_2_ = bf16[1,2,128,1024]{3,2,1,0:T(8,128)(2,1)S(1)} collective-permute-done((bf16[1,2,128,1024]{3,2,1,0:T(8,128)(2,1)S(1)}, bf16[1,2,128,1024]{3,2,1,0:T(8,128)(2,1)S(1)}, u32[]{:S(2)}, u32[]{:S(2)}) %collective-permute-start.19) | collective-permute-done | bytes 524320 | tf_op jit(solution)/shard_map/ppermute | solution.py:19
  91.9 1.3 %shard_map.63 = f32[1,128,2,1024]{3,2,1,0:T(2,128)} custom-call(f32[2,2,128,1024]{3,2,1,0:T(8,128)S(1)} %get-tuple-element.53.refs_0_, bf16[2,2,128,1024]{3,2,1,0:T(8,128)(2,1)S(1)} %collective-permute-done.18.refs_1_, bf16[1,2,128,1024]{3,2,1,0:T(8,128)(2,1)S(1)} %collective-permute-done.19.refs_2_), custom_call_target="tpu_custom_call" | custom-call | flops 786432 | bytes 4718592 | tf_op jit(solution)/shard_map/pallas_call | solution.py:279
  (39 shorter events, 19.4 us)
Async XLA Ops:
  0.0 7.9 %copy-start.1 = (f32[1,1,1024]{2,1,0:T(1,128)S(1)}, f32[1,1,1024]{2,1,0:T(1,128)}, u32[]{:S(2)}) copy-start(f32[1,1,1024]{2,1,0:T(1,128)} %factor_ref.1) | copy-start | bytes 12292
  4.7 6.2 %collective-permute-start.4 = (bf16[64,1024]{1,0:T(8,128)(2,1)S(1)}, bf16[64,1024]{1,0:T(8,128)(2,1)S(1)}, u32[]{:S(2)}, u32[]{:S(2)}) collective-permute-start(bf16[64,1024]{1,0:T(8,128)(2,1)S(1)} %get-tuple-element.37.ready_ref), channel_id=1, source_target_pairs={{0,8},{8,16},{16,24},{24,0},{1,9},{9,17},{17,25},{25,1},{2,10},{10... | collective-permute-start | bytes 393224 | tf_op jit(solution)/shard_map/ppermute | solution.py:19
  6.3 21.7 %collective-permute-start.3 = (bf16[2,512,256]{2,1,0:T(8,128)(2,1)S(1)}, bf16[2,512,256]{2,1,0:T(8,128)(2,1)S(1)}, u32[]{:S(2)}, u32[]{:S(2)}) collective-permute-start(bf16[2,512,256]{2,1,0:T(8,128)(2,1)S(1)} %get-tuple-element.35), channel_id=1, source_target_pairs={{0,2},{1,3},{2,0},{3,1},{4,6},{5,7},{6,4},{7,5},{8,10},{9,11},{10,... | collective-permute-start | bytes 1572872 | tf_op jit(solution)/shard_map/ppermute | solution.py:23
  9.2 6.3 %collective-permute-start = (bf16[64,1024]{1,0:T(8,128)(2,1)S(1)}, bf16[64,1024]{1,0:T(8,128)(2,1)S(1)}, u32[]{:S(2)}, u32[]{:S(2)}) collective-permute-start(bf16[64,1024]{1,0:T(8,128)(2,1)S(1)} %get-tuple-element.32.ready_ref), channel_id=1, source_target_pairs={{0,8},{8,16},{16,24},{24,0},{1,9},{9,17},{17,25},{25,1},{2,10},{10... | collective-permute-start | bytes 393224 | tf_op jit(solution)/shard_map/ppermute | solution.py:19
  12.2 5.9 %collective-permute-start.5 = (bf16[64,1024]{1,0:T(8,128)(2,1)S(1)}, bf16[64,1024]{1,0:T(8,128)(2,1)S(1)}, u32[]{:S(2)}, u32[]{:S(2)}) collective-permute-start(bf16[64,1024]{1,0:T(8,128)(2,1)S(1)} %shard_map.51), channel_id=1, source_target_pairs={{0,8},{8,16},{16,24},{24,0},{1,9},{9,17},{17,25},{25,1},{2,10},{10... | collective-permute-start | bytes 393224 | tf_op jit(solution)/shard_map/ppermute | solution.py:19
  16.9 7.2 %collective-permute-start.1 = (bf16[64,1024]{1,0:T(8,128)(2,1)S(1)}, bf16[64,1024]{1,0:T(8,128)(2,1)S(1)}, u32[]{:S(2)}, u32[]{:S(2)}) collective-permute-start(bf16[64,1024]{1,0:T(8,128)(2,1)S(1)} %shard_map.48), channel_id=1, source_target_pairs={{0,8},{8,16},{16,24},{24,0},{1,9},{9,17},{17,25},{25,1},{2,10},{10... | collective-permute-start | bytes 393224 | tf_op jit(solution)/shard_map/ppermute | solution.py:19
  19.5 7.1 %collective-permute-start.6 = (bf16[64,1024]{1,0:T(8,128)(2,1)S(1)}, bf16[64,1024]{1,0:T(8,128)(2,1)S(1)}, u32[]{:S(2)}, u32[]{:S(2)}) collective-permute-start(bf16[64,1024]{1,0:T(8,128)(2,1)S(1)} %shard_map.52), channel_id=1, source_target_pairs={{0,8},{8,16},{16,24},{24,0},{1,9},{9,17},{17,25},{25,1},{2,10},{10... | collective-permute-start | bytes 393224 | tf_op jit(solution)/shard_map/ppermute | solution.py:19
  24.0 3.9 %copy-start = (bf16[1,1,2,1024,256]{4,3,2,1,0:T(8,128)(2,1)S(1)}, bf16[1,1,2,1024,256]{4,3,2,1,0:T(8,128)(2,1)}, u32[]{:S(2)}) copy-start(bf16[1,1,2,1024,256]{4,3,2,1,0:T(8,128)(2,1)} %upward_ref.1) | copy-start | bytes 3145732
  25.3 6.3 %collective-permute-start.2 = (bf16[64,1024]{1,0:T(8,128)(2,1)S(1)}, bf16[64,1024]{1,0:T(8,128)(2,1)S(1)}, u32[]{:S(2)}, u32[]{:S(2)}) collective-permute-start(bf16[64,1024]{1,0:T(8,128)(2,1)S(1)} %shard_map.49), channel_id=1, source_target_pairs={{0,8},{8,16},{16,24},{24,0},{1,9},{9,17},{17,25},{25,1},{2,10},{10... | collective-permute-start | bytes 393224 | tf_op jit(solution)/shard_map/ppermute | solution.py:19
  27.9 7.1 %collective-permute-start.7 = (bf16[64,1024]{1,0:T(8,128)(2,1)S(1)}, bf16[64,1024]{1,0:T(8,128)(2,1)S(1)}, u32[]{:S(2)}, u32[]{:S(2)}) collective-permute-start(bf16[64,1024]{1,0:T(8,128)(2,1)S(1)} %shard_map.53.refs_0_), channel_id=1, source_target_pairs={{0,8},{8,16},{16,24},{24,0},{1,9},{9,17},{17,25},{25,1},{2,10},{10... | collective-permute-start | bytes 393224 | tf_op jit(solution)/shard_map/ppermute | solution.py:19
  33.0 10.6 %collective-permute-start.9 = (bf16[128,1024]{1,0:T(8,128)(2,1)S(1)}, bf16[128,1024]{1,0:T(8,128)(2,1)S(1)}, u32[]{:S(2)}, u32[]{:S(2)}) collective-permute-start(bf16[128,1024]{1,0:T(8,128)(2,1)S(1)} %get-tuple-element.43), channel_id=1, source_target_pairs={{0,2},{1,3},{2,0},{3,1},{4,6},{5,7},{6,4},{7,5},{8,10},{9,11},{10,... | collective-permute-start | bytes 786440 | tf_op jit(solution)/shard_map/ppermute | solution.py:23
  33.1 5.9 %collective-permute-start.11 = (bf16[64,1024]{1,0:T(8,128)(2,1)S(1)}, bf16[64,1024]{1,0:T(8,128)(2,1)S(1)}, u32[]{:S(2)}, u32[]{:S(2)}) collective-permute-start(bf16[64,1024]{1,0:T(8,128)(2,1)S(1)} %get-tuple-element.45.refs_4_), channel_id=1, source_target_pairs={{0,8},{8,16},{16,24},{24,0},{1,9},{9,17},{17,25},{25,1},{2,10},{10... | collective-permute-start | bytes 393224 | tf_op jit(solution)/shard_map/ppermute | solution.py:19
  36.3 7.3 %collective-permute-start.8 = (bf16[64,1024]{1,0:T(8,128)(2,1)S(1)}, bf16[64,1024]{1,0:T(8,128)(2,1)S(1)}, u32[]{:S(2)}, u32[]{:S(2)}) collective-permute-start(bf16[64,1024]{1,0:T(8,128)(2,1)S(1)} %shard_map.54.refs_0_.refs_1_), channel_id=1, source_target_pairs={{0,8},{8,16},{16,24},{24,0},{1,9},{9,17},{17,25},{25,1},{2,10},{10... | collective-permute-start | bytes 393224 | tf_op jit(solution)/shard_map/ppermute | solution.py:19
  40.3 11.8 %collective-permute-start.12 = (bf16[128,1024]{1,0:T(8,128)(2,1)S(1)}, bf16[128,1024]{1,0:T(8,128)(2,1)S(1)}, u32[]{:S(2)}, u32[]{:S(2)}) collective-permute-start(bf16[128,1024]{1,0:T(8,128)(2,1)S(1)} %get-tuple-element.46), channel_id=1, source_target_pairs={{0,2},{1,3},{2,0},{3,1},{4,6},{5,7},{6,4},{7,5},{8,10},{9,11},{10,... | collective-permute-start | bytes 786440 | tf_op jit(solution)/shard_map/ppermute | solution.py:23
  42.3 5.9 %collective-permute-start.13 = (bf16[64,1024]{1,0:T(8,128)(2,1)S(1)}, bf16[64,1024]{1,0:T(8,128)(2,1)S(1)}, u32[]{:S(2)}, u32[]{:S(2)}) collective-permute-start(bf16[64,1024]{1,0:T(8,128)(2,1)S(1)} %get-tuple-element.48.refs_5_), channel_id=1, source_target_pairs={{0,8},{8,16},{16,24},{24,0},{1,9},{9,17},{17,25},{25,1},{2,10},{10... | collective-permute-start | bytes 393224 | tf_op jit(solution)/shard_map/ppermute | solution.py:19
  44.9 7.2 %collective-permute-start.10 = (bf16[64,1024]{1,0:T(8,128)(2,1)S(1)}, bf16[64,1024]{1,0:T(8,128)(2,1)S(1)}, u32[]{:S(2)}, u32[]{:S(2)}) collective-permute-start(bf16[64,1024]{1,0:T(8,128)(2,1)S(1)} %shard_map.56.refs_0_.refs_2_), channel_id=1, source_target_pairs={{0,8},{8,16},{16,24},{24,0},{1,9},{9,17},{17,25},{25,1},{2,10},{10... | collective-permute-start | bytes 393224 | tf_op jit(solution)/shard_map/ppermute | solution.py:19
  49.7 9.4 %collective-permute-start.15 = (bf16[128,1024]{1,0:T(8,128)(2,1)S(1)}, bf16[128,1024]{1,0:T(8,128)(2,1)S(1)}, u32[]{:S(2)}, u32[]{:S(2)}) collective-permute-start(bf16[128,1024]{1,0:T(8,128)(2,1)S(1)} %get-tuple-element.52), channel_id=1, source_target_pairs={{0,2},{1,3},{2,0},{3,1},{4,6},{5,7},{6,4},{7,5},{8,10},{9,11},{10,... | collective-permute-start | bytes 786440 | tf_op jit(solution)/shard_map/ppermute | solution.py:23
  49.9 5.9 %collective-permute-start.14 = (bf16[64,1024]{1,0:T(8,128)(2,1)S(1)}, bf16[64,1024]{1,0:T(8,128)(2,1)S(1)}, u32[]{:S(2)}, u32[]{:S(2)}) collective-permute-start(bf16[64,1024]{1,0:T(8,128)(2,1)S(1)} %get-tuple-element.49.refs_6_), channel_id=1, source_target_pairs={{0,8},{8,16},{16,24},{24,0},{1,9},{9,17},{17,25},{25,1},{2,10},{10... | collective-permute-start | bytes 393224 | tf_op jit(solution)/shard_map/ppermute | solution.py:19
  53.4 5.6 %collective-permute-start.16 = (bf16[64,1024]{1,0:T(8,128)(2,1)S(1)}, bf16[64,1024]{1,0:T(8,128)(2,1)S(1)}, u32[]{:S(2)}, u32[]{:S(2)}) collective-permute-start(bf16[64,1024]{1,0:T(8,128)(2,1)S(1)} %shard_map.58.refs_3_), channel_id=1, source_target_pairs={{0,2},{1,3},{2,0},{3,1},{4,6},{5,7},{6,4},{7,5},{8,10},{9,11},{10,... | collective-permute-start | bytes 393224 | tf_op jit(solution)/shard_map/ppermute | solution.py:23
  57.0 5.0 %collective-permute-start.17 = (bf16[64,1024]{1,0:T(8,128)(2,1)S(1)}, bf16[64,1024]{1,0:T(8,128)(2,1)S(1)}, u32[]{:S(2)}, u32[]{:S(2)}) collective-permute-start(bf16[64,1024]{1,0:T(8,128)(2,1)S(1)} %shard_map.60.refs_7_), channel_id=1, source_target_pairs={{0,2},{1,3},{2,0},{3,1},{4,6},{5,7},{6,4},{7,5},{8,10},{9,11},{10,... | collective-permute-start | bytes 393224 | tf_op jit(solution)/shard_map/ppermute | solution.py:23
  62.8 2.7 %collective-permute-start.18 = (bf16[2,2,128,1024]{3,2,1,0:T(8,128)(2,1)S(1)}, bf16[2,2,128,1024]{3,2,1,0:T(8,128)(2,1)S(1)}, u32[]{:S(2)}, u32[]{:S(2)}) collective-permute-start(bf16[2,2,128,1024]{3,2,1,0:T(8,128)(2,1)S(1)} %get-tuple-element.54), channel_id=1, source_target_pairs={{0,1},{1,0},{2,3},{3,2},{4,5},{5,4},{6,7},{7,6},{8,9},{9,8},{10,11... | collective-permute-start | bytes 3145736 | tf_op jit(solution)/shard_map/ppermute | solution.py:23
  65.7 26.2 %collective-permute-start.19 = (bf16[1,2,128,1024]{3,2,1,0:T(8,128)(2,1)S(1)}, bf16[1,2,128,1024]{3,2,1,0:T(8,128)(2,1)S(1)}, u32[]{:S(2)}, u32[]{:S(2)}) collective-permute-start(bf16[1,2,128,1024]{3,2,1,0:T(8,128)(2,1)S(1)} %add_convert_fusion), channel_id=1, source_target_pairs={{0,4},{1,5},{2,6},{3,7},{4,0},{5,1},{6,2},{7,3},{8,12},{9,13},{10,... | collective-permute-start | bytes 1572872 | tf_op jit(solution)/shard_map/ppermute | solution.py:19

commit v14 on v13

--- a/solution.py
+++ b/solution.py
@@ -143,9 +143,7 @@
     return whole_call(functools.partial(second_kernel, part), (joined, right, factor), outs, 4 * width * width * shots)
 
 
-def advance_kernel(level_ref, arrived_ref, ready_ref, joined_ref, factor_ref, *refs):
-    *mates, both = refs
-    out_ref = mates[0] if len(mates) == 1 else mates[1]
+def advance_kernel(level_ref, arrived_ref, ready_ref, joined_ref, factor_ref, out_ref, both):
     part = arrived_ref.shape[0] // 2
     width = arrived_ref.shape[1]
     wide = width // 4
@@ -166,21 +164,25 @@
             )
             out_ref[:, columns] = (out.T * factor_ref[:, columns]).astype(jnp.bfloat16)
 
-    if len(mates) > 1:
-        mates[2][: 2 * part] = mates[0][...]
-        mates[2][2 * part :] = out_ref[...]
-
-
-def advance(level, arrived, ready, joined, factor, mate=None):
+
+def advance(level, arrived, ready, joined, factor):
     rows, width = arrived.shape
     joined = pltpu.with_memory_space_constraint(joined, pltpu.VMEM)
-    outs = [jax.ShapeDtypeStruct((rows, width), jnp.bfloat16)]
-    args = [arrived, ready, joined, factor]
-    if mate is not None:
-        outs.append(jax.ShapeDtypeStruct((2 * rows, width), jnp.bfloat16))
-        args.append(mate)
+    out = jax.ShapeDtypeStruct((rows, width), jnp.bfloat16)
+    args = (arrived, ready, joined, factor)
     scratch = [pltpu.VMEM((rows, 2 * width), jnp.bfloat16)]
-    return whole_call(advance_kernel, args, outs, 4 * rows * width * width, (level,), scratch)
+    return whole_call(advance_kernel, args, [out], 4 * rows * width * width, (level,), scratch)[0]
+
+
+def pair_kernel(first_ref, second_ref, out_ref):
+    rows = first_ref.shape[0]
+    out_ref[:rows] = first_ref[...]
+    out_ref[rows:] = second_ref[...]
+
+
+def paired(first, second):
+    out = jax.ShapeDtypeStruct((2 * first.shape[0], first.shape[1]), first.dtype)
+    return whole_call(pair_kernel, (first, second), [out], 0)[0]
 
 
 def operand_kernel(own_ref, got_ref, out_ref):
@@ -349,17 +351,18 @@
             if event == steps:
                 arrived, left = lax.optimization_barrier((arrived, left))
             for at, (sent, panel) in enumerate(crossing):
-                if event == sent + BEHIND:
+                if event == sent + BEHIND + (at == 0):
                     arrived, panel = lax.optimization_barrier((arrived, panel))
                     crossing[at] = (sent, panel)
-            pair = stream > 0 and levels - 1 <= step < steps - 1
-            out, *both = advance(level, arrived, out, joined, factor, own[0][-1] if pair else None)
-            if step >= levels - 1 and (pair or step == steps - 1):
-                crossing.append((event, swapped(both[0] if pair else out, "freq", 2)))
+            out = advance(level, arrived, out, joined, factor)
         if step + 1 < steps:
             flying[stream] = ring(out, "depth", 1)
         if step >= levels - 1:
             own[stream].append(out)
+            if step == steps - 1:
+                crossing.append((event, swapped(out, "freq", 2)))
+            elif stream > 0:
+                crossing.append((event, swapped(paired(own[0][-1], out), "freq", 2)))
     other = [panel for _, panel in crossing]
     early = early_terms(level, left, own[0] + own[1] + other[:-1], levels)
     keep, send = late_terms(level, left, early, other[:-2] + other[-1:], rows, levels)

time: 93.5 us -> 92.8 us (level)
    ppermute x13, waiting for transfers between devices: 49.8 us -> 48.6 us  [ring(): lax.ppermute(block, axis, [(i, (i + distance) % size) for i in range(size)])]
    pallas_call x16 -> x19, Pallas kernels: 21.2 us -> 21.2 us  [whole_call(): pl.pallas_call(kernel, in_specs=[pl.BlockSpec(memory_space=pltpu.SMEM)] *...]
  transfers between devices with their start and end apart: 20 -> 20, of which waited for: 15 -> 16; matrix products, arithmetic and copies ran while one was open for 0% -> 0% of each run, Pallas kernels for 21% -> 22%
where the time goes in v14:
time: 92.8 us; the launch traced here: 92.5 us
  waiting for transfers between devices  52.8 us (57%)
  Pallas kernels  26.7 us (29%)
  starting transfers between devices  12.5 us (13%)
    ppermute x13, waiting for transfers between devices, ring(): lax.ppermute(block, axis, [(i, (i + distance) % size) for i in range(size)])  48.6 us
    pallas_call x19, Pallas kernels, whole_call(): pl.pallas_call(kernel, in_specs=[pl.BlockSpec(memory_space=pltpu.SMEM)] *...  21.2 us
    ppermute x13, starting transfers between devices, ring(): lax.ppermute(block, axis, [(i, (i + distance) % size) for i in range(size)])  6.42 us
    ppermute x7, starting transfers between devices, swapped(): lax.ppermute(block, axis, [(i, i ^ bit) for i in range(lax.axis_size(axis...  6.11 us
    pallas_call x1, Pallas kernels, first_advance(): pl.pallas_call(functools.partial(first_kernel, part), in_specs=[pl.BlockS...  4.72 us
    ppermute x7, waiting for transfers between devices, swapped(): lax.ppermute(block, axis, [(i, i ^ bit) for i in range(lax.axis_size(axis...  4.19 us
  transfers between devices with their start and end apart: 20, of which 16 were waited for; matrix products, arithmetic and copies ran while one was open for 0% of the time, Pallas kernels for 22%

profile of v14, /device:TPU:4, one launch (start us, length us, event | category | flops | bytes accessed | tf_op | source)
XLA Modules:
  0.0 92.5 jit_solution(13488509403452555436)
XLA Ops:
  0.0 4.7 %shard_map.46 = (bf16[64,1024]{1,0:T(8,128)(2,1)S(1)}, bf16[64,1024]{1,0:T(8,128)(2,1)S(1)}, bf16[64,1024]{1,0:T(8,128)(2,1)S(1)}, bf16[64,1024]{1,0:T(8,128)(2,...) custom-call(s32[1]{0:T(128)} %bitcast.level_ref, ...), custom_call_target="tpu_custom_call" | custom-call | flops 1073741824 | bytes 6291456 | tf_op jit(solution)/shard_map/pallas_call | solution.py:106
  4.7 1.5 %collective-permute-start.4 = (bf16[64,1024]{1,0:T(8,128)(2,1)S(1)}, bf16[64,1024]{1,0:T(8,128)(2,1)S(1)}, u32[]{:S(2)}, u32[]{:S(2)}) collective-permute-start(bf16[64,1024]{1,0:T(8,128)(2,1)S(1)} %get-tuple-element.31.ready_ref), channel_id=1, source_target_pairs={{0,8},{8,16},{16,24},{24,0},{1,9},{9,17},{17,25},{25,1},{2,10},{10... | collective-permute-start | bytes 393224 | tf_op jit(solution)/shard_map/ppermute | solution.py:19
  6.3 1.6 %collective-permute-start.3 = (bf16[2,512,256]{2,1,0:T(8,128)(2,1)S(1)}, bf16[2,512,256]{2,1,0:T(8,128)(2,1)S(1)}, u32[]{:S(2)}, u32[]{:S(2)}) collective-permute-start(bf16[2,512,256]{2,1,0:T(8,128)(2,1)S(1)} %get-tuple-element.29), channel_id=1, source_target_pairs={{0,2},{1,3},{2,0},{3,1},{4,6},{5,7},{6,4},{7,5},{8,10},{9,11},{10,... | collective-permute-start | bytes 1572872 | tf_op jit(solution)/shard_map/ppermute | solution.py:23
  7.9 1.4 %shard_map.47 = (bf16[64,1024]{1,0:T(8,128)(2,1)S(1)}, bf16[64,1024]{1,0:T(8,128)(2,1)S(1)}, bf16[64,1024]{1,0:T(8,128)(2,1)S(1)}, bf16[64,1024]{1,0:T(8,128)(2,1)S(1)}) custom-call(bf16[1024,2048]{1,0:T(8,128)(2,1)S(1)} %get-tuple-element.24.joined_ref, bf16[1024,256]{1,0:T(8,128)(2,1)S(1)} %get-tuple-element.25.right_ref, f32[1,1024]{1,0:T(1,128)S(1)} %bitcast.5), custom_call_target="tpu_custom_call" | custom-call | flops 1073741824 | bytes 5246976 | tf_op jit(solution)/shard_map/pallas_call | solution.py:281
  10.9 1.3 %shard_map.51 = bf16[64,1024]{1,0:T(8,128)(2,1)S(1)} custom-call(s32[1]{0:T(128)} %bitcast.level_ref, bf16[64,1024]{1,0:T(8,128)(2,1)S(1)} %collective-permute-done.4.arrived_ref, bf16[64,1024]{1,0:T(8,128)(2,1)S(1)} %get-tuple-element.32.ready_ref, bf16[1024,2048]{1,0:T(8,128)(2,1)S(1)} %get-tuple-element.24.joined_ref, f32[1,1024]{1,0:T(1,128)S(1)} %bitcast.6), custom_call_target="tpu_custom_call" | custom-call | flops 268435456 | bytes 4591616 | tf_op jit(solution)/shard_map/pallas_call | solution.py:281
  12.9 2.7 %collective-permute-done.arrived_ref = bf16[64,1024]{1,0:T(8,128)(2,1)S(1)} collective-permute-done((bf16[64,1024]{1,0:T(8,128)(2,1)S(1)}, bf16[64,1024]{1,0:T(8,128)(2,1)S(1)}, u32[]{:S(2)}, u32[]{:S(2)}) %collective-permute-start) | collective-permute-done | bytes 131104 | tf_op jit(solution)/shard_map/ppermute | solution.py:19
  15.6 1.3 %shard_map.48 = bf16[64,1024]{1,0:T(8,128)(2,1)S(1)} custom-call(s32[1]{0:T(128)} %bitcast.level_ref, bf16[64,1024]{1,0:T(8,128)(2,1)S(1)} %collective-permute-done.arrived_ref, bf16[64,1024]{1,0:T(8,128)(2,1)S(1)} %get-tuple-element.27.ready_ref, bf16[1024,2048]{1,0:T(8,128)(2,1)S(1)} %get-tuple-element.24.joined_ref, f32[1,1024]{1,0:T(1,128)S(1)} %bitcast.7), custom_call_target="tpu_custom_call" | custom-call | flops 268435456 | bytes 4591616 | tf_op jit(solution)/shard_map/pallas_call | solution.py:281
  19.9 4.2 %collective-permute-done.1.arrived_ref = bf16[64,1024]{1,0:T(8,128)(2,1)S(1)} collective-permute-done((bf16[64,1024]{1,0:T(8,128)(2,1)S(1)}, bf16[64,1024]{1,0:T(8,128)(2,1)S(1)}, u32[]{:S(2)}, u32[]{:S(2)}) %collective-permute-start.1) | collective-permute-done | bytes 131104 | tf_op jit(solution)/shard_map/ppermute | solution.py:19
  28.8 2.9 %collective-permute-done.2.arrived_ref = bf16[64,1024]{1,0:T(8,128)(2,1)S(1)} collective-permute-done((bf16[64,1024]{1,0:T(8,128)(2,1)S(1)}, bf16[64,1024]{1,0:T(8,128)(2,1)S(1)}, u32[]{:S(2)}, u32[]{:S(2)}) %collective-permute-start.2) | collective-permute-done | bytes 131104 | tf_op jit(solution)/shard_map/ppermute | solution.py:19
  31.7 1.3 %shard_map.56.second_ref.refs_4_ = bf16[64,1024]{1,0:T(8,128)(2,1)S(1)} custom-call(s32[1]{0:T(128)} %bitcast.level_ref, bf16[64,1024]{1,0:T(8,128)(2,1)S(1)} %collective-permute-done.2.arrived_ref, bf16[64,1024]{1,0:T(8,128)(2,1)S(1)} %get-tuple-element.36.ready_ref, bf16[1024,2048]{1,0:T(8,128)(2,1)S(1)} %get-tuple-element.24.joined_ref, ...), custom_call_target="tpu_custom_call" | custom-call | flops 268435456 | bytes 4591616 | tf_op jit(solution)/shard_map/pallas_call | solution.py:281
  34.5 1.3 %shard_map.54.first_ref.refs_1_ = bf16[64,1024]{1,0:T(8,128)(2,1)S(1)} custom-call(s32[1]{0:T(128)} %bitcast.level_ref, bf16[64,1024]{1,0:T(8,128)(2,1)S(1)} %collective-permute-done.7.arrived_ref, bf16[64,1024]{1,0:T(8,128)(2,1)S(1)} %get-tuple-element.31.ready_ref, bf16[1024,2048]{1,0:T(8,128)(2,1)S(1)} %get-tuple-element.24.joined_ref, f32[1,1024]{1,0:T(1,128)S(1)} %bitcast.12), custom_call_target="tpu_custom_call" | custom-call | flops 268435456 | bytes 4591616 | tf_op jit(solution)/shard_map/pallas_call | solution.py:281
  35.8 3.2 %collective-permute-done.10.arrived_ref = bf16[64,1024]{1,0:T(8,128)(2,1)S(1)} collective-permute-done((bf16[64,1024]{1,0:T(8,128)(2,1)S(1)}, bf16[64,1024]{1,0:T(8,128)(2,1)S(1)}, u32[]{:S(2)}, u32[]{:S(2)}) %collective-permute-start.10) | collective-permute-done | bytes 131104 | tf_op jit(solution)/shard_map/ppermute | solution.py:19
  39.1 1.3 %shard_map.57.second_ref.refs_5_ = bf16[64,1024]{1,0:T(8,128)(2,1)S(1)} custom-call(s32[1]{0:T(128)} %bitcast.level_ref, bf16[64,1024]{1,0:T(8,128)(2,1)S(1)} %collective-permute-done.10.arrived_ref, bf16[64,1024]{1,0:T(8,128)(2,1)S(1)} %get-tuple-element.26.ready_ref, bf16[1024,2048]{1,0:T(8,128)(2,1)S(1)} %get-tuple-element.24.joined_ref, ...), custom_call_target="tpu_custom_call" | custom-call | flops 268435456 | bytes 4591616 | tf_op jit(solution)/shard_map/pallas_call | solution.py:281
  43.1 4.3 %collective-permute-done.12.arrived_ref = bf16[64,1024]{1,0:T(8,128)(2,1)S(1)} collective-permute-done((bf16[64,1024]{1,0:T(8,128)(2,1)S(1)}, bf16[64,1024]{1,0:T(8,128)(2,1)S(1)}, u32[]{:S(2)}, u32[]{:S(2)}) %collective-permute-start.12) | collective-permute-done | bytes 131104 | tf_op jit(solution)/shard_map/ppermute | solution.py:19
  47.4 1.5 %shard_map.61.second_ref.refs_6_ = bf16[64,1024]{1,0:T(8,128)(2,1)S(1)} custom-call(s32[1]{0:T(128)} %bitcast.level_ref, bf16[64,1024]{1,0:T(8,128)(2,1)S(1)} %collective-permute-done.12.arrived_ref, bf16[64,1024]{1,0:T(8,128)(2,1)S(1)} %get-tuple-element.27.ready_ref, bf16[1024,2048]{1,0:T(8,128)(2,1)S(1)} %get-tuple-element.24.joined_ref, ...), custom_call_target="tpu_custom_call" | custom-call | flops 268435456 | bytes 4591616 | tf_op jit(solution)/shard_map/pallas_call | solution.py:281
  50.9 1.5 %collective-permute-start.16 = (bf16[64,1024]{1,0:T(8,128)(2,1)S(1)}, bf16[64,1024]{1,0:T(8,128)(2,1)S(1)}, u32[]{:S(2)}, u32[]{:S(2)}) collective-permute-start(bf16[64,1024]{1,0:T(8,128)(2,1)S(1)} %shard_map.59.refs_3_), channel_id=1, source_target_pairs={{0,2},{1,3},{2,0},{3,1},{4,6},{5,7},{6,4},{7,5},{8,10},{9,11},{10,... | collective-permute-start | bytes 393224 | tf_op jit(solution)/shard_map/ppermute | solution.py:23
  52.4 2.5 %collective-permute-done.14.arrived_ref = bf16[64,1024]{1,0:T(8,128)(2,1)S(1)} collective-permute-done((bf16[64,1024]{1,0:T(8,128)(2,1)S(1)}, bf16[64,1024]{1,0:T(8,128)(2,1)S(1)}, u32[]{:S(2)}, u32[]{:S(2)}) %collective-permute-start.14) | collective-permute-done | bytes 131104 | tf_op jit(solution)/shard_map/ppermute | solution.py:19
  54.9 1.3 %shard_map.62.refs_7_ = bf16[64,1024]{1,0:T(8,128)(2,1)S(1)} custom-call(s32[1]{0:T(128)} %bitcast.level_ref, bf16[64,1024]{1,0:T(8,128)(2,1)S(1)} %collective-permute-done.14.arrived_ref, bf16[64,1024]{1,0:T(8,128)(2,1)S(1)} %get-tuple-element.28.ready_ref, bf16[1024,2048]{1,0:T(8,128)(2,1)S(1)} %get-tuple-element.24.joined_ref, f32[1,1024]{1,0:T(1,128)S(1)} %bitcast.17), custom_call_target="tpu_custom_call" | custom-call | flops 268435456 | bytes 4591616 | tf_op jit(solution)/shard_map/pallas_call | solution.py:281
  56.2 2.0 %collective-permute-start.17 = (bf16[64,1024]{1,0:T(8,128)(2,1)S(1)}, bf16[64,1024]{1,0:T(8,128)(2,1)S(1)}, u32[]{:S(2)}, u32[]{:S(2)}) collective-permute-start(bf16[64,1024]{1,0:T(8,128)(2,1)S(1)} %shard_map.62.refs_7_), channel_id=1, source_target_pairs={{0,2},{1,3},{2,0},{3,1},{4,6},{5,7},{6,4},{7,5},{8,10},{9,11},{10,... | collective-permute-start | bytes 393224 | tf_op jit(solution)/shard_map/ppermute | solution.py:23
  58.3 1.9 %shard_map.64.early_ref = f32[1024,1024]{1,0:T(8,128)S(1)} custom-call(s32[1]{0:T(128)} %bitcast.level_ref, bf16[1024,1024]{1,0:T(8,128)(2,1)S(1)} %shard_map.50.left_ref, bf16[64,1024]{1,0:T(8,128)(2,1)S(1)} %shard_map.53.first_ref.refs_0_, bf16[64,1024]{1,0:T(8,128)(2,1)S(1)} %shard_map.54.first_ref.refs_1_, ...), custom_call_target="tpu_custom_call" | custom-call | flops 1610612736 | bytes 8257536 | tf_op jit(solution)/shard_map/pallas_call | solution.py:281
  62.1 2.6 %collective-permute-done.18.refs_1_ = bf16[2,2,128,1024]{3,2,1,0:T(8,128)(2,1)S(1)} collective-permute-done((bf16[2,2,128,1024]{3,2,1,0:T(8,128)(2,1)S(1)}, bf16[2,2,128,1024]{3,2,1,0:T(8,128)(2,1)S(1)}, u32[]{:S(2)}, u32[]{:S(2)}) %collective-permute-start.18) | collective-permute-done | bytes 1048608 | tf_op jit(solution)/shard_map/ppermute | solution.py:23
  64.9 2.8 %collective-permute-start.19 = (bf16[1,2,128,1024]{3,2,1,0:T(8,128)(2,1)S(1)}, bf16[1,2,128,1024]{3,2,1,0:T(8,128)(2,1)S(1)}, u32[]{:S(2)}, u32[]{:S(2)}) collective-permute-start(bf16[1,2,128,1024]{3,2,1,0:T(8,128)(2,1)S(1)} %add_convert_fusion), channel_id=1, source_target_pairs={{0,4},{1,5},{2,6},{3,7},{4,0},{5,1},{6,2},{7,3},{8,12},{9,13},{10,... | collective-permute-start | bytes 1572872 | tf_op jit(solution)/shard_map/ppermute | solution.py:19
  67.7 23.5 %collective-permute-done.19.refs_2_ = bf16[1,2,128,1024]{3,2,1,0:T(8,128)(2,1)S(1)} collective-permute-done((bf16[1,2,128,1024]{3,2,1,0:T(8,128)(2,1)S(1)}, bf16[1,2,128,1024]{3,2,1,0:T(8,128)(2,1)S(1)}, u32[]{:S(2)}, u32[]{:S(2)}) %collective-permute-start.19) | collective-permute-done | bytes 524320 | tf_op jit(solution)/shard_map/ppermute | solution.py:19
  91.2 1.3 %shard_map.66 = f32[1,128,2,1024]{3,2,1,0:T(2,128)} custom-call(f32[2,2,128,1024]{3,2,1,0:T(8,128)S(1)} %get-tuple-element.41.refs_0_, bf16[2,2,128,1024]{3,2,1,0:T(8,128)(2,1)S(1)} %collective-permute-done.18.refs_1_, bf16[1,2,128,1024]{3,2,1,0:T(8,128)(2,1)S(1)} %collective-permute-done.19.refs_2_), custom_call_target="tpu_custom_call" | custom-call | flops 786432 | bytes 4718592 | tf_op jit(solution)/shard_map/pallas_call | solution.py:281
  (42 shorter events, 18.2 us)
Async XLA Ops:
  0.0 7.9 %copy-start.1 = (f32[1,1,1024]{2,1,0:T(1,128)S(1)}, f32[1,1,1024]{2,1,0:T(1,128)}, u32[]{:S(2)}) copy-start(f32[1,1,1024]{2,1,0:T(1,128)} %factor_ref.1) | copy-start | bytes 12292
  4.7 6.2 %collective-permute-start.4 = (bf16[64,1024]{1,0:T(8,128)(2,1)S(1)}, bf16[64,1024]{1,0:T(8,128)(2,1)S(1)}, u32[]{:S(2)}, u32[]{:S(2)}) collective-permute-start(bf16[64,1024]{1,0:T(8,128)(2,1)S(1)} %get-tuple-element.31.ready_ref), channel_id=1, source_target_pairs={{0,8},{8,16},{16,24},{24,0},{1,9},{9,17},{17,25},{25,1},{2,10},{10... | collective-permute-start | bytes 393224 | tf_op jit(solution)/shard_map/ppermute | solution.py:19
  6.3 21.7 %collective-permute-start.3 = (bf16[2,512,256]{2,1,0:T(8,128)(2,1)S(1)}, bf16[2,512,256]{2,1,0:T(8,128)(2,1)S(1)}, u32[]{:S(2)}, u32[]{:S(2)}) collective-permute-start(bf16[2,512,256]{2,1,0:T(8,128)(2,1)S(1)} %get-tuple-element.29), channel_id=1, source_target_pairs={{0,2},{1,3},{2,0},{3,1},{4,6},{5,7},{6,4},{7,5},{8,10},{9,11},{10,... | collective-permute-start | bytes 1572872 | tf_op jit(solution)/shard_map/ppermute | solution.py:23
  9.2 6.3 %collective-permute-start = (bf16[64,1024]{1,0:T(8,128)(2,1)S(1)}, bf16[64,1024]{1,0:T(8,128)(2,1)S(1)}, u32[]{:S(2)}, u32[]{:S(2)}) collective-permute-start(bf16[64,1024]{1,0:T(8,128)(2,1)S(1)} %get-tuple-element.26.ready_ref), channel_id=1, source_target_pairs={{0,8},{8,16},{16,24},{24,0},{1,9},{9,17},{17,25},{25,1},{2,10},{10... | collective-permute-start | bytes 393224 | tf_op jit(solution)/shard_map/ppermute | solution.py:19
  12.2 5.9 %collective-permute-start.5 = (bf16[64,1024]{1,0:T(8,128)(2,1)S(1)}, bf16[64,1024]{1,0:T(8,128)(2,1)S(1)}, u32[]{:S(2)}, u32[]{:S(2)}) collective-permute-start(bf16[64,1024]{1,0:T(8,128)(2,1)S(1)} %shard_map.51), channel_id=1, source_target_pairs={{0,8},{8,16},{16,24},{24,0},{1,9},{9,17},{17,25},{25,1},{2,10},{10... | collective-permute-start | bytes 393224 | tf_op jit(solution)/shard_map/ppermute | solution.py:19
  16.9 7.1 %collective-permute-start.1 = (bf16[64,1024]{1,0:T(8,128)(2,1)S(1)}, bf16[64,1024]{1,0:T(8,128)(2,1)S(1)}, u32[]{:S(2)}, u32[]{:S(2)}) collective-permute-start(bf16[64,1024]{1,0:T(8,128)(2,1)S(1)} %shard_map.48), channel_id=1, source_target_pairs={{0,8},{8,16},{16,24},{24,0},{1,9},{9,17},{17,25},{25,1},{2,10},{10... | collective-permute-start | bytes 393224 | tf_op jit(solution)/shard_map/ppermute | solution.py:19
  19.5 7.1 %collective-permute-start.6 = (bf16[64,1024]{1,0:T(8,128)(2,1)S(1)}, bf16[64,1024]{1,0:T(8,128)(2,1)S(1)}, u32[]{:S(2)}, u32[]{:S(2)}) collective-permute-start(bf16[64,1024]{1,0:T(8,128)(2,1)S(1)} %shard_map.52), channel_id=1, source_target_pairs={{0,8},{8,16},{16,24},{24,0},{1,9},{9,17},{17,25},{25,1},{2,10},{10... | collective-permute-start | bytes 393224 | tf_op jit(solution)/shard_map/ppermute | solution.py:19
  24.0 3.9 %copy-start = (bf16[1,1,2,1024,256]{4,3,2,1,0:T(8,128)(2,1)S(1)}, bf16[1,1,2,1024,256]{4,3,2,1,0:T(8,128)(2,1)}, u32[]{:S(2)}) copy-start(bf16[1,1,2,1024,256]{4,3,2,1,0:T(8,128)(2,1)} %upward_ref.1) | copy-start | bytes 3145732
  25.4 6.3 %collective-permute-start.2 = (bf16[64,1024]{1,0:T(8,128)(2,1)S(1)}, bf16[64,1024]{1,0:T(8,128)(2,1)S(1)}, u32[]{:S(2)}, u32[]{:S(2)}) collective-permute-start(bf16[64,1024]{1,0:T(8,128)(2,1)S(1)} %shard_map.49), channel_id=1, source_target_pairs={{0,8},{8,16},{16,24},{24,0},{1,9},{9,17},{17,25},{25,1},{2,10},{10... | collective-permute-start | bytes 393224 | tf_op jit(solution)/shard_map/ppermute | solution.py:19
  27.9 6.6 %collective-permute-start.7 = (bf16[64,1024]{1,0:T(8,128)(2,1)S(1)}, bf16[64,1024]{1,0:T(8,128)(2,1)S(1)}, u32[]{:S(2)}, u32[]{:S(2)}) collective-permute-start(bf16[64,1024]{1,0:T(8,128)(2,1)S(1)} %shard_map.53.first_ref.refs_0_), channel_id=1, source_target_pairs={{0,8},{8,16},{16,24},{24,0},{1,9},{9,17},{17,25},{25,1},{2,10},{10... | collective-permute-start | bytes 393224 | tf_op jit(solution)/shard_map/ppermute | solution.py:19
  33.0 6.1 %collective-permute-start.10 = (bf16[64,1024]{1,0:T(8,128)(2,1)S(1)}, bf16[64,1024]{1,0:T(8,128)(2,1)S(1)}, u32[]{:S(2)}, u32[]{:S(2)}) collective-permute-start(bf16[64,1024]{1,0:T(8,128)(2,1)S(1)} %shard_map.56.second_ref.refs_4_), channel_id=1, source_target_pairs={{0,8},{8,16},{16,24},{24,0},{1,9},{9,17},{17,25},{25,1},{2,10},{10... | collective-permute-start | bytes 393224 | tf_op jit(solution)/shard_map/ppermute | solution.py:19
  33.1 10.0 %collective-permute-start.13 = (bf16[128,1024]{1,0:T(8,128)(2,1)S(1)}, bf16[128,1024]{1,0:T(8,128)(2,1)S(1)}, u32[]{:S(2)}, u32[]{:S(2)}) collective-permute-start(bf16[128,1024]{1,0:T(8,128)(2,1)S(1)} %shard_map.60), channel_id=1, source_target_pairs={{0,2},{1,3},{2,0},{3,1},{4,6},{5,7},{6,4},{7,5},{8,10},{9,11},{10,... | collective-permute-start | bytes 786440 | tf_op jit(solution)/shard_map/ppermute | solution.py:23
  35.8 5.9 %collective-permute-start.8 = (bf16[64,1024]{1,0:T(8,128)(2,1)S(1)}, bf16[64,1024]{1,0:T(8,128)(2,1)S(1)}, u32[]{:S(2)}, u32[]{:S(2)}) collective-permute-start(bf16[64,1024]{1,0:T(8,128)(2,1)S(1)} %shard_map.54.first_ref.refs_1_), channel_id=1, source_target_pairs={{0,8},{8,16},{16,24},{24,0},{1,9},{9,17},{17,25},{25,1},{2,10},{10... | collective-permute-start | bytes 393224 | tf_op jit(solution)/shard_map/ppermute | solution.py:19
  40.4 7.0 %collective-permute-start.12 = (bf16[64,1024]{1,0:T(8,128)(2,1)S(1)}, bf16[64,1024]{1,0:T(8,128)(2,1)S(1)}, u32[]{:S(2)}, u32[]{:S(2)}) collective-permute-start(bf16[64,1024]{1,0:T(8,128)(2,1)S(1)} %shard_map.57.second_ref.refs_5_), channel_id=1, source_target_pairs={{0,8},{8,16},{16,24},{24,0},{1,9},{9,17},{17,25},{25,1},{2,10},{10... | collective-permute-start | bytes 393224 | tf_op jit(solution)/shard_map/ppermute | solution.py:19
  40.5 9.1 %collective-permute-start.11 = (bf16[128,1024]{1,0:T(8,128)(2,1)S(1)}, bf16[128,1024]{1,0:T(8,128)(2,1)S(1)}, u32[]{:S(2)}, u32[]{:S(2)}) collective-permute-start(bf16[128,1024]{1,0:T(8,128)(2,1)S(1)} %shard_map.58), channel_id=1, source_target_pairs={{0,2},{1,3},{2,0},{3,1},{4,6},{5,7},{6,4},{7,5},{8,10},{9,11},{10,... | collective-permute-start | bytes 786440 | tf_op jit(solution)/shard_map/ppermute | solution.py:23
  43.0 6.1 %collective-permute-start.9 = (bf16[64,1024]{1,0:T(8,128)(2,1)S(1)}, bf16[64,1024]{1,0:T(8,128)(2,1)S(1)}, u32[]{:S(2)}, u32[]{:S(2)}) collective-permute-start(bf16[64,1024]{1,0:T(8,128)(2,1)S(1)} %shard_map.55.first_ref.refs_2_), channel_id=1, source_target_pairs={{0,8},{8,16},{16,24},{24,0},{1,9},{9,17},{17,25},{25,1},{2,10},{10... | collective-permute-start | bytes 393224 | tf_op jit(solution)/shard_map/ppermute | solution.py:19
  48.9 9.4 %collective-permute-start.15 = (bf16[128,1024]{1,0:T(8,128)(2,1)S(1)}, bf16[128,1024]{1,0:T(8,128)(2,1)S(1)}, u32[]{:S(2)}, u32[]{:S(2)}) collective-permute-start(bf16[128,1024]{1,0:T(8,128)(2,1)S(1)} %shard_map.63), channel_id=1, source_target_pairs={{0,2},{1,3},{2,0},{3,1},{4,6},{5,7},{6,4},{7,5},{8,10},{9,11},{10,... | collective-permute-start | bytes 786440 | tf_op jit(solution)/shard_map/ppermute | solution.py:23
  49.0 5.9 %collective-permute-start.14 = (bf16[64,1024]{1,0:T(8,128)(2,1)S(1)}, bf16[64,1024]{1,0:T(8,128)(2,1)S(1)}, u32[]{:S(2)}, u32[]{:S(2)}) collective-permute-start(bf16[64,1024]{1,0:T(8,128)(2,1)S(1)} %shard_map.61.second_ref.refs_6_), channel_id=1, source_target_pairs={{0,8},{8,16},{16,24},{24,0},{1,9},{9,17},{17,25},{25,1},{2,10},{10... | collective-permute-start | bytes 393224 | tf_op jit(solution)/shard_map/ppermute | solution.py:19
  50.9 7.4 %collective-permute-start.16 = (bf16[64,1024]{1,0:T(8,128)(2,1)S(1)}, bf16[64,1024]{1,0:T(8,128)(2,1)S(1)}, u32[]{:S(2)}, u32[]{:S(2)}) collective-permute-start(bf16[64,1024]{1,0:T(8,128)(2,1)S(1)} %shard_map.59.refs_3_), channel_id=1, source_target_pairs={{0,2},{1,3},{2,0},{3,1},{4,6},{5,7},{6,4},{7,5},{8,10},{9,11},{10,... | collective-permute-start | bytes 393224 | tf_op jit(solution)/shard_map/ppermute | solution.py:23
  56.2 5.0 %collective-permute-start.17 = (bf16[64,1024]{1,0:T(8,128)(2,1)S(1)}, bf16[64,1024]{1,0:T(8,128)(2,1)S(1)}, u32[]{:S(2)}, u32[]{:S(2)}) collective-permute-start(bf16[64,1024]{1,0:T(8,128)(2,1)S(1)} %shard_map.62.refs_7_), channel_id=1, source_target_pairs={{0,2},{1,3},{2,0},{3,1},{4,6},{5,7},{6,4},{7,5},{8,10},{9,11},{10,... | collective-permute-start | bytes 393224 | tf_op jit(solution)/shard_map/ppermute | solution.py:23
  62.0 2.7 %collective-permute-start.18 = (bf16[2,2,128,1024]{3,2,1,0:T(8,128)(2,1)S(1)}, bf16[2,2,128,1024]{3,2,1,0:T(8,128)(2,1)S(1)}, u32[]{:S(2)}, u32[]{:S(2)}) collective-permute-start(bf16[2,2,128,1024]{3,2,1,0:T(8,128)(2,1)S(1)} %get-tuple-element.42), channel_id=1, source_target_pairs={{0,1},{1,0},{2,3},{3,2},{4,5},{5,4},{6,7},{7,6},{8,9},{9,8},{10,11... | collective-permute-start | bytes 3145736 | tf_op jit(solution)/shard_map/ppermute | solution.py:23
  64.9 26.3 %collective-permute-start.19 = (bf16[1,2,128,1024]{3,2,1,0:T(8,128)(2,1)S(1)}, bf16[1,2,128,1024]{3,2,1,0:T(8,128)(2,1)S(1)}, u32[]{:S(2)}, u32[]{:S(2)}) collective-permute-start(bf16[1,2,128,1024]{3,2,1,0:T(8,128)(2,1)S(1)} %add_convert_fusion), channel_id=1, source_target_pairs={{0,4},{1,5},{2,6},{3,7},{4,0},{5,1},{6,2},{7,3},{8,12},{9,13},{10,... | collective-permute-start | bytes 1572872 | tf_op jit(solution)/shard_map/ppermute | solution.py:19

commit v15 on v14

--- a/solution.py
+++ b/solution.py
@@ -11,6 +11,7 @@
 STEPS = 4
 STREAMS = 2
 BEHIND = 3
+TOGETHER = 2
 LIMIT = 16 * 1024 * 1024
 
 
@@ -174,15 +175,17 @@
     return whole_call(advance_kernel, args, [out], 4 * rows * width * width, (level,), scratch)[0]
 
 
-def pair_kernel(first_ref, second_ref, out_ref):
-    rows = first_ref.shape[0]
-    out_ref[:rows] = first_ref[...]
-    out_ref[rows:] = second_ref[...]
-
-
-def paired(first, second):
-    out = jax.ShapeDtypeStruct((2 * first.shape[0], first.shape[1]), first.dtype)
-    return whole_call(pair_kernel, (first, second), [out], 0)[0]
+def stack_kernel(*refs):
+    *panels, out_ref = refs
+    rows = panels[0].shape[0]
+    for at, panel in enumerate(panels):
+        out_ref[at * rows : (at + 1) * rows] = panel[...]
+
+
+def stacked(panels):
+    rows, width = panels[0].shape
+    out = jax.ShapeDtypeStruct((len(panels) * rows, width), panels[0].dtype)
+    return whole_call(stack_kernel, panels, [out], 0)[0]
 
 
 def operand_kernel(own_ref, got_ref, out_ref):
@@ -239,16 +242,16 @@
         joined[pl.ds(base + half + row, part)] = ref[top + part : top + 2 * part]
 
 
-def crossed(refs, stream):
-    *pairs, last = refs
-    rows = last.shape[0]
-    return [(pair, stream * rows) for pair in pairs] + [(last, 0)]
-
-
-def early_kernel(levels, level_ref, left_ref, *refs):
+def crossed(refs, counts, stream):
+    rows = refs[0].shape[0] // counts[0]
+    panels = [(ref, at * rows) for ref, count in zip(refs, counts) for at in range(count)]
+    return panels[stream::STREAMS]
+
+
+def early_kernel(levels, counts, level_ref, left_ref, *refs):
     *panels, out_ref, joined = refs
     own, other = panels[: STREAMS * STEPS], panels[STREAMS * STEPS :]
-    gather(levels, level_ref, [(ref, 0) for ref in own] + crossed(other, 0), joined)
+    gather(levels, level_ref, [(ref, 0) for ref in own] + crossed(other, counts, 0), joined)
     deep = joined.shape[0]
     wide = out_ref.shape[1] // 4
     for n in range(4):
@@ -256,9 +259,9 @@
         out_ref[:, columns] = jnp.dot(left_ref[:, :deep], joined[:, columns], preferred_element_type=jnp.float32)
 
 
-def late_kernel(levels, level_ref, left_ref, early_ref, *refs):
-    *panels, keep_ref, send_ref, joined = refs
-    gather(levels, level_ref, crossed(panels, 1), joined)
+def late_kernel(levels, counts, level_ref, left_ref, early_ref, *refs):
+    *panels, keep_ref, own_ref, send_ref, joined = refs
+    gather(levels, level_ref, crossed(panels[:-1], counts[:-1], 1) + [(panels[-1], 0)], joined)
     start = left_ref.shape[1] - joined.shape[0]
     groups, _, rows, width = keep_ref.shape
     wide = width // 4
@@ -272,7 +275,8 @@
                 lo = (2 * k + part) * rows
                 keep_ref[k, part, :, columns] = out[lo : lo + rows]
                 lo += 2 * groups * rows
-                send_ref[k, part, :, columns] = out[lo : lo + rows].astype(jnp.bfloat16)
+                to_ref, at = (send_ref, k - 1) if k else (own_ref, 0)
+                to_ref[at, part, :, columns] = out[lo : lo + rows].astype(jnp.bfloat16)
 
 
 def whole_call(kernel, args, outs, flops, scalars=(), scratch=()):
@@ -289,21 +293,23 @@
     )(*scalars, *args)
 
 
-def early_terms(level, left, panels, levels):
+def early_terms(level, left, panels, levels, counts):
     width = panels[0].shape[1]
     deep = left.shape[1] - panels[-1].shape[0] * STEPS
     out = jax.ShapeDtypeStruct((left.shape[0], width), jnp.float32)
-    kernel = functools.partial(early_kernel, levels)
+    kernel = functools.partial(early_kernel, levels, counts)
     scratch = [pltpu.VMEM((deep, width), jnp.bfloat16)]
     return whole_call(kernel, (left, *panels), [out], 2 * deep * left.shape[0] * width, (level,), scratch)[0]
 
 
-def late_terms(level, left, early, panels, rows, levels):
+def late_terms(level, left, early, panels, rows, levels, counts):
     width = early.shape[1]
     deep = panels[-1].shape[0] * STEPS
-    shape = (left.shape[0] // (4 * rows), 2, rows, width)
-    outs = [jax.ShapeDtypeStruct(shape, jnp.float32), jax.ShapeDtypeStruct(shape, jnp.bfloat16)]
-    kernel = functools.partial(late_kernel, levels)
+    groups = left.shape[0] // (4 * rows)
+    outs = [jax.ShapeDtypeStruct((groups, 2, rows, width), jnp.float32)] + [
+        jax.ShapeDtypeStruct((count, 2, rows, width), jnp.bfloat16) for count in (1, groups - 1)
+    ]
+    kernel = functools.partial(late_kernel, levels, counts)
     scratch = [pltpu.VMEM((deep, width), jnp.bfloat16)]
     return whole_call(kernel, (left, early, *panels), outs, 2 * deep * left.shape[0] * width, (level,), scratch)
 
@@ -342,6 +348,7 @@
     steps = STEPS + levels - 1
     flying = [None] * STREAMS
     own = [[] for _ in range(STREAMS)]
+    waiting = []
     crossing = []
     for event in range(STREAMS * steps):
         step, stream = divmod(event, STREAMS)
@@ -361,15 +368,21 @@
             own[stream].append(out)
             if step == steps - 1:
                 crossing.append((event, swapped(out, "freq", 2)))
-            elif stream > 0:
-                crossing.append((event, swapped(paired(own[0][-1], out), "freq", 2)))
+            else:
+                waiting.append(out)
+                if len(waiting) == TOGETHER:
+                    crossing.append((event, swapped(stacked(waiting), "freq", 2)))
+                    waiting = []
     other = [panel for _, panel in crossing]
-    early = early_terms(level, left, own[0] + own[1] + other[:-1], levels)
-    keep, send = late_terms(level, left, early, other[:-2] + other[-1:], rows, levels)
+    counts = [panel.shape[0] // out.shape[0] for panel in other]
+    early = early_terms(level, left, own[0] + own[1] + other[:-1], levels, counts[:-1])
+    late = late_terms(level, left, early, other[:-2] + other[-1:], rows, levels, counts[:-2] + counts[-1:])
+    keep, send_own, send = late
     near = swapped(send, "freq", 1)
-    parts = [keep, near]
+    send_own, near = lax.optimization_barrier((send_own, near))
+    parts = [keep, swapped(send_own, "freq", 1)]
     for k in range(1, groups):
-        total = (keep[k : k + 1] + near[k : k + 1].astype(jnp.float32)).astype(jnp.bfloat16)
+        total = (keep[k : k + 1] + near[k - 1 : k].astype(jnp.float32)).astype(jnp.bfloat16)
         parts.append(ring(total, "freq", 4 * k))
     return last_sum(parts, (2.0 * shots * freqs) ** (-0.5))
 

time: 92.8 us -> 92.1 us (level)
    ppermute x7 -> x8, waiting for transfers between devices: 4.19 us -> 3.44 us  [swapped(): lax.ppermute(block, axis, [(i, i ^ bit) for i in range(lax.axis_size(axis...]
    ppermute x7 -> x8, starting transfers between devices: 6.11 us -> 6.11 us  [swapped(): lax.ppermute(block, axis, [(i, i ^ bit) for i in range(lax.axis_size(axis...]
  transfers between devices with their start and end apart: 20 -> 21, of which waited for: 16 -> 16; matrix products, arithmetic and copies ran while one was open for 0% -> 0% of each run, Pallas kernels for 22% -> 22%
where the time goes in v15:
time: 92.1 us; the launch traced here: 91.8 us
  waiting for transfers between devices  52.1 us (57%)
  Pallas kernels  26.7 us (29%)
  starting transfers between devices  12.5 us (14%)
    ppermute x13, waiting for transfers between devices, ring(): lax.ppermute(block, axis, [(i, (i + distance) % size) for i in range(size)])  48.6 us
    pallas_call x19, Pallas kernels, whole_call(): pl.pallas_call(kernel, in_specs=[pl.BlockSpec(memory_space=pltpu.SMEM)] *...  21.2 us
    ppermute x13, starting transfers between devices, ring(): lax.ppermute(block, axis, [(i, (i + distance) % size) for i in range(size)])  6.42 us
    ppermute x8, starting transfers between devices, swapped(): lax.ppermute(block, axis, [(i, i ^ bit) for i in range(lax.axis_size(axis...  6.11 us
    pallas_call x1, Pallas kernels, first_advance(): pl.pallas_call(functools.partial(first_kernel, part), in_specs=[pl.BlockS...  4.72 us
    ppermute x8, waiting for transfers between devices, swapped(): lax.ppermute(block, axis, [(i, i ^ bit) for i in range(lax.axis_size(axis...  3.44 us
  transfers between devices with their start and end apart: 21, of which 16 were waited for; matrix products, arithmetic and copies ran while one was open for 0% of the time, Pallas kernels for 22%

profile of v15, /device:TPU:4, one launch (start us, length us, event | category | flops | bytes accessed | tf_op | source)
XLA Modules:
  0.0 91.8 jit_solution(4128921355323274706)
XLA Ops:
  0.0 4.7 %shard_map.46 = (bf16[64,1024]{1,0:T(8,128)(2,1)S(1)}, bf16[64,1024]{1,0:T(8,128)(2,1)S(1)}, bf16[64,1024]{1,0:T(8,128)(2,1)S(1)}, bf16[64,1024]{1,0:T(8,128)(2,...) custom-call(s32[1]{0:T(128)} %bitcast.level_ref, ...), custom_call_target="tpu_custom_call" | custom-call | flops 1073741824 | bytes 6291456 | tf_op jit(solution)/shard_map/pallas_call | solution.py:107
  4.7 1.5 %collective-permute-start.4 = (bf16[64,1024]{1,0:T(8,128)(2,1)S(1)}, bf16[64,1024]{1,0:T(8,128)(2,1)S(1)}, u32[]{:S(2)}, u32[]{:S(2)}) collective-permute-start(bf16[64,1024]{1,0:T(8,128)(2,1)S(1)} %get-tuple-element.34.ready_ref), channel_id=1, source_target_pairs={{0,8},{8,16},{16,24},{24,0},{1,9},{9,17},{17,25},{25,1},{2,10},{10... | collective-permute-start | bytes 393224 | tf_op jit(solution)/shard_map/ppermute | solution.py:20
  6.3 1.6 %collective-permute-start.3 = (bf16[2,512,256]{2,1,0:T(8,128)(2,1)S(1)}, bf16[2,512,256]{2,1,0:T(8,128)(2,1)S(1)}, u32[]{:S(2)}, u32[]{:S(2)}) collective-permute-start(bf16[2,512,256]{2,1,0:T(8,128)(2,1)S(1)} %get-tuple-element.32), channel_id=1, source_target_pairs={{0,2},{1,3},{2,0},{3,1},{4,6},{5,7},{6,4},{7,5},{8,10},{9,11},{10,... | collective-permute-start | bytes 1572872 | tf_op jit(solution)/shard_map/ppermute | solution.py:24
  7.9 1.4 %shard_map.47 = (bf16[64,1024]{1,0:T(8,128)(2,1)S(1)}, bf16[64,1024]{1,0:T(8,128)(2,1)S(1)}, bf16[64,1024]{1,0:T(8,128)(2,1)S(1)}, bf16[64,1024]{1,0:T(8,128)(2,1)S(1)}) custom-call(bf16[1024,2048]{1,0:T(8,128)(2,1)S(1)} %get-tuple-element.27.joined_ref, bf16[1024,256]{1,0:T(8,128)(2,1)S(1)} %get-tuple-element.28.right_ref, f32[1,1024]{1,0:T(1,128)S(1)} %bitcast.5), custom_call_target="tpu_custom_call" | custom-call | flops 1073741824 | bytes 5246976 | tf_op jit(solution)/shard_map/pallas_call | solution.py:285
  10.9 1.3 %shard_map.51 = bf16[64,1024]{1,0:T(8,128)(2,1)S(1)} custom-call(s32[1]{0:T(128)} %bitcast.level_ref, bf16[64,1024]{1,0:T(8,128)(2,1)S(1)} %collective-permute-done.4.arrived_ref, bf16[64,1024]{1,0:T(8,128)(2,1)S(1)} %get-tuple-element.35.ready_ref, bf16[1024,2048]{1,0:T(8,128)(2,1)S(1)} %get-tuple-element.27.joined_ref, f32[1,1024]{1,0:T(1,128)S(1)} %bitcast.6), custom_call_target="tpu_custom_call" | custom-call | flops 268435456 | bytes 4591616 | tf_op jit(solution)/shard_map/pallas_call | solution.py:285
  12.9 2.7 %collective-permute-done.arrived_ref = bf16[64,1024]{1,0:T(8,128)(2,1)S(1)} collective-permute-done((bf16[64,1024]{1,0:T(8,128)(2,1)S(1)}, bf16[64,1024]{1,0:T(8,128)(2,1)S(1)}, u32[]{:S(2)}, u32[]{:S(2)}) %collective-permute-start) | collective-permute-done | bytes 131104 | tf_op jit(solution)/shard_map/ppermute | solution.py:20
  15.6 1.3 %shard_map.48 = bf16[64,1024]{1,0:T(8,128)(2,1)S(1)} custom-call(s32[1]{0:T(128)} %bitcast.level_ref, bf16[64,1024]{1,0:T(8,128)(2,1)S(1)} %collective-permute-done.arrived_ref, bf16[64,1024]{1,0:T(8,128)(2,1)S(1)} %get-tuple-element.30.ready_ref, bf16[1024,2048]{1,0:T(8,128)(2,1)S(1)} %get-tuple-element.27.joined_ref, f32[1,1024]{1,0:T(1,128)S(1)} %bitcast.7), custom_call_target="tpu_custom_call" | custom-call | flops 268435456 | bytes 4591616 | tf_op jit(solution)/shard_map/pallas_call | solution.py:285
  19.9 4.2 %collective-permute-done.1.arrived_ref = bf16[64,1024]{1,0:T(8,128)(2,1)S(1)} collective-permute-done((bf16[64,1024]{1,0:T(8,128)(2,1)S(1)}, bf16[64,1024]{1,0:T(8,128)(2,1)S(1)}, u32[]{:S(2)}, u32[]{:S(2)}) %collective-permute-start.1) | collective-permute-done | bytes 131104 | tf_op jit(solution)/shard_map/ppermute | solution.py:20
  28.8 2.9 %collective-permute-done.2.arrived_ref = bf16[64,1024]{1,0:T(8,128)(2,1)S(1)} collective-permute-done((bf16[64,1024]{1,0:T(8,128)(2,1)S(1)}, bf16[64,1024]{1,0:T(8,128)(2,1)S(1)}, u32[]{:S(2)}, u32[]{:S(2)}) %collective-permute-start.2) | collective-permute-done | bytes 131104 | tf_op jit(solution)/shard_map/ppermute | solution.py:20
  31.7 1.3 %shard_map.56.refs_1_.refs_4_ = bf16[64,1024]{1,0:T(8,128)(2,1)S(1)} custom-call(s32[1]{0:T(128)} %bitcast.level_ref, bf16[64,1024]{1,0:T(8,128)(2,1)S(1)} %collective-permute-done.2.arrived_ref, bf16[64,1024]{1,0:T(8,128)(2,1)S(1)} %get-tuple-element.39.ready_ref, bf16[1024,2048]{1,0:T(8,128)(2,1)S(1)} %get-tuple-element.27.joined_ref, f32[1,1024]{1,0:T(1,128)S(1)} %bitcast.11), custom_call_target="tpu_custom_call" | custom-call | flops 268435456 | bytes 4591616 | tf_op jit(solution)/shard_map/pallas_call | solution.py:285
  34.5 1.3 %shard_map.54.refs_0_.refs_1_ = bf16[64,1024]{1,0:T(8,128)(2,1)S(1)} custom-call(s32[1]{0:T(128)} %bitcast.level_ref, bf16[64,1024]{1,0:T(8,128)(2,1)S(1)} %collective-permute-done.7.arrived_ref, bf16[64,1024]{1,0:T(8,128)(2,1)S(1)} %get-tuple-element.34.ready_ref, bf16[1024,2048]{1,0:T(8,128)(2,1)S(1)} %get-tuple-element.27.joined_ref, f32[1,1024]{1,0:T(1,128)S(1)} %bitcast.12), custom_call_target="tpu_custom_call" | custom-call | flops 268435456 | bytes 4591616 | tf_op jit(solution)/shard_map/pallas_call | solution.py:285
  35.8 3.2 %collective-permute-done.10.arrived_ref = bf16[64,1024]{1,0:T(8,128)(2,1)S(1)} collective-permute-done((bf16[64,1024]{1,0:T(8,128)(2,1)S(1)}, bf16[64,1024]{1,0:T(8,128)(2,1)S(1)}, u32[]{:S(2)}, u32[]{:S(2)}) %collective-permute-start.10) | collective-permute-done | bytes 131104 | tf_op jit(solution)/shard_map/ppermute | solution.py:20
  39.1 1.3 %shard_map.57.refs_1_.refs_5_ = bf16[64,1024]{1,0:T(8,128)(2,1)S(1)} custom-call(s32[1]{0:T(128)} %bitcast.level_ref, bf16[64,1024]{1,0:T(8,128)(2,1)S(1)} %collective-permute-done.10.arrived_ref, bf16[64,1024]{1,0:T(8,128)(2,1)S(1)} %get-tuple-element.29.ready_ref, bf16[1024,2048]{1,0:T(8,128)(2,1)S(1)} %get-tuple-element.27.joined_ref, f32[1,1024]{1,0:T(1,128)S(1)} %bitcast.13), custom_call_target="tpu_custom_call" | custom-call | flops 268435456 | bytes 4591616 | tf_op jit(solution)/shard_map/pallas_call | solution.py:285
  43.1 4.3 %collective-permute-done.12.arrived_ref = bf16[64,1024]{1,0:T(8,128)(2,1)S(1)} collective-permute-done((bf16[64,1024]{1,0:T(8,128)(2,1)S(1)}, bf16[64,1024]{1,0:T(8,128)(2,1)S(1)}, u32[]{:S(2)}, u32[]{:S(2)}) %collective-permute-start.12) | collective-permute-done | bytes 131104 | tf_op jit(solution)/shard_map/ppermute | solution.py:20
  47.4 1.5 %shard_map.61.refs_1_.refs_6_ = bf16[64,1024]{1,0:T(8,128)(2,1)S(1)} custom-call(s32[1]{0:T(128)} %bitcast.level_ref, bf16[64,1024]{1,0:T(8,128)(2,1)S(1)} %collective-permute-done.12.arrived_ref, bf16[64,1024]{1,0:T(8,128)(2,1)S(1)} %get-tuple-element.30.ready_ref, bf16[1024,2048]{1,0:T(8,128)(2,1)S(1)} %get-tuple-element.27.joined_ref, f32[1,1024]{1,0:T(1,128)S(1)} %bitcast.15), custom_call_target="tpu_custom_call" | custom-call | flops 268435456 | bytes 4591616 | tf_op jit(solution)/shard_map/pallas_call | solution.py:285
  50.9 1.5 %collective-permute-start.16 = (bf16[64,1024]{1,0:T(8,128)(2,1)S(1)}, bf16[64,1024]{1,0:T(8,128)(2,1)S(1)}, u32[]{:S(2)}, u32[]{:S(2)}) collective-permute-start(bf16[64,1024]{1,0:T(8,128)(2,1)S(1)} %shard_map.59.refs_3_), channel_id=1, source_target_pairs={{0,2},{1,3},{2,0},{3,1},{4,6},{5,7},{6,4},{7,5},{8,10},{9,11},{10,... | collective-permute-start | bytes 393224 | tf_op jit(solution)/shard_map/ppermute | solution.py:24
  52.4 2.5 %collective-permute-done.14.arrived_ref = bf16[64,1024]{1,0:T(8,128)(2,1)S(1)} collective-permute-done((bf16[64,1024]{1,0:T(8,128)(2,1)S(1)}, bf16[64,1024]{1,0:T(8,128)(2,1)S(1)}, u32[]{:S(2)}, u32[]{:S(2)}) %collective-permute-start.14) | collective-permute-done | bytes 131104 | tf_op jit(solution)/shard_map/ppermute | solution.py:20
  54.9 1.3 %shard_map.62.refs_7_ = bf16[64,1024]{1,0:T(8,128)(2,1)S(1)} custom-call(s32[1]{0:T(128)} %bitcast.level_ref, bf16[64,1024]{1,0:T(8,128)(2,1)S(1)} %collective-permute-done.14.arrived_ref, bf16[64,1024]{1,0:T(8,128)(2,1)S(1)} %get-tuple-element.31.ready_ref, bf16[1024,2048]{1,0:T(8,128)(2,1)S(1)} %get-tuple-element.27.joined_ref, f32[1,1024]{1,0:T(1,128)S(1)} %bitcast.17), custom_call_target="tpu_custom_call" | custom-call | flops 268435456 | bytes 4591616 | tf_op jit(solution)/shard_map/pallas_call | solution.py:285
  56.2 2.0 %collective-permute-start.17 = (bf16[64,1024]{1,0:T(8,128)(2,1)S(1)}, bf16[64,1024]{1,0:T(8,128)(2,1)S(1)}, u32[]{:S(2)}, u32[]{:S(2)}) collective-permute-start(bf16[64,1024]{1,0:T(8,128)(2,1)S(1)} %shard_map.62.refs_7_), channel_id=1, source_target_pairs={{0,2},{1,3},{2,0},{3,1},{4,6},{5,7},{6,4},{7,5},{8,10},{9,11},{10,... | collective-permute-start | bytes 393224 | tf_op jit(solution)/shard_map/ppermute | solution.py:24
  58.3 1.9 %shard_map.64.early_ref = f32[1024,1024]{1,0:T(8,128)S(1)} custom-call(s32[1]{0:T(128)} %bitcast.level_ref, bf16[1024,1024]{1,0:T(8,128)(2,1)S(1)} %shard_map.50.left_ref, bf16[64,1024]{1,0:T(8,128)(2,1)S(1)} %shard_map.53.refs_0_, bf16[64,1024]{1,0:T(8,128)(2,1)S(1)} %shard_map.54.refs_0_.refs_1_, bf16[64,1024]{1,0:T(8,128)(2,1)S(1)} %shard_map.55.refs_0_.refs_2_, ...), custom_call_target="tpu_custom_call" | custom-call | flops 1610612736 | bytes 8257536 | tf_op jit(solution)/shard_map/pallas_call | solution.py:285
  62.1 1.9 %collective-permute-done.18 = bf16[1,2,128,1024]{3,2,1,0:T(8,128)(2,1)S(1)} collective-permute-done((bf16[1,2,128,1024]{3,2,1,0:T(8,128)(2,1)S(1)}, bf16[1,2,128,1024]{3,2,1,0:T(8,128)(2,1)S(1)}, u32[]{:S(2)}, u32[]{:S(2)}) %collective-permute-start.18) | collective-permute-done | bytes 524320 | tf_op jit(solution)/shard_map/ppermute | solution.py:24
  64.2 2.8 %collective-permute-start.20 = (bf16[1,2,128,1024]{3,2,1,0:T(8,128)(2,1)S(1)}, bf16[1,2,128,1024]{3,2,1,0:T(8,128)(2,1)S(1)}, u32[]{:S(2)}, u32[]{:S(2)}) collective-permute-start(bf16[1,2,128,1024]{3,2,1,0:T(8,128)(2,1)S(1)} %add_convert_fusion), channel_id=1, source_target_pairs={{0,4},{1,5},{2,6},{3,7},{4,0},{5,1},{6,2},{7,3},{8,12},{9,13},{10,... | collective-permute-start | bytes 1572872 | tf_op jit(solution)/shard_map/ppermute | solution.py:20
  67.0 23.5 %collective-permute-done.20.refs_2_ = bf16[1,2,128,1024]{3,2,1,0:T(8,128)(2,1)S(1)} collective-permute-done((bf16[1,2,128,1024]{3,2,1,0:T(8,128)(2,1)S(1)}, bf16[1,2,128,1024]{3,2,1,0:T(8,128)(2,1)S(1)}, u32[]{:S(2)}, u32[]{:S(2)}) %collective-permute-start.20) | collective-permute-done | bytes 524320 | tf_op jit(solution)/shard_map/ppermute | solution.py:20
  90.4 1.3 %shard_map.66 = f32[1,128,2,1024]{3,2,1,0:T(2,128)} custom-call(f32[2,2,128,1024]{3,2,1,0:T(8,128)S(1)} %get-tuple-element.44.refs_0_, bf16[1,2,128,1024]{3,2,1,0:T(8,128)(2,1)S(1)} %collective-permute-done.19.refs_1_, bf16[1,2,128,1024]{3,2,1,0:T(8,128)(2,1)S(1)} %collective-permute-done.20.refs_2_), custom_call_target="tpu_custom_call" | custom-call | flops 786432 | bytes 4194304 | tf_op jit(solution)/shard_map/pallas_call | solution.py:285
  (44 shorter events, 18.2 us)
Async XLA Ops:
  0.0 7.9 %copy-start.1 = (f32[1,1,1024]{2,1,0:T(1,128)S(1)}, f32[1,1,1024]{2,1,0:T(1,128)}, u32[]{:S(2)}) copy-start(f32[1,1,1024]{2,1,0:T(1,128)} %factor_ref.1) | copy-start | bytes 12292
  4.7 6.2 %collective-permute-start.4 = (bf16[64,1024]{1,0:T(8,128)(2,1)S(1)}, bf16[64,1024]{1,0:T(8,128)(2,1)S(1)}, u32[]{:S(2)}, u32[]{:S(2)}) collective-permute-start(bf16[64,1024]{1,0:T(8,128)(2,1)S(1)} %get-tuple-element.34.ready_ref), channel_id=1, source_target_pairs={{0,8},{8,16},{16,24},{24,0},{1,9},{9,17},{17,25},{25,1},{2,10},{10... | collective-permute-start | bytes 393224 | tf_op jit(solution)/shard_map/ppermute | solution.py:20
  6.3 21.7 %collective-permute-start.3 = (bf16[2,512,256]{2,1,0:T(8,128)(2,1)S(1)}, bf16[2,512,256]{2,1,0:T(8,128)(2,1)S(1)}, u32[]{:S(2)}, u32[]{:S(2)}) collective-permute-start(bf16[2,512,256]{2,1,0:T(8,128)(2,1)S(1)} %get-tuple-element.32), channel_id=1, source_target_pairs={{0,2},{1,3},{2,0},{3,1},{4,6},{5,7},{6,4},{7,5},{8,10},{9,11},{10,... | collective-permute-start | bytes 1572872 | tf_op jit(solution)/shard_map/ppermute | solution.py:24
  9.2 6.3 %collective-permute-start = (bf16[64,1024]{1,0:T(8,128)(2,1)S(1)}, bf16[64,1024]{1,0:T(8,128)(2,1)S(1)}, u32[]{:S(2)}, u32[]{:S(2)}) collective-permute-start(bf16[64,1024]{1,0:T(8,128)(2,1)S(1)} %get-tuple-element.29.ready_ref), channel_id=1, source_target_pairs={{0,8},{8,16},{16,24},{24,0},{1,9},{9,17},{17,25},{25,1},{2,10},{10... | collective-permute-start | bytes 393224 | tf_op jit(solution)/shard_map/ppermute | solution.py:20
  12.2 5.9 %collective-permute-start.5 = (bf16[64,1024]{1,0:T(8,128)(2,1)S(1)}, bf16[64,1024]{1,0:T(8,128)(2,1)S(1)}, u32[]{:S(2)}, u32[]{:S(2)}) collective-permute-start(bf16[64,1024]{1,0:T(8,128)(2,1)S(1)} %shard_map.51), channel_id=1, source_target_pairs={{0,8},{8,16},{16,24},{24,0},{1,9},{9,17},{17,25},{25,1},{2,10},{10... | collective-permute-start | bytes 393224 | tf_op jit(solution)/shard_map/ppermute | solution.py:20
  16.9 7.1 %collective-permute-start.1 = (bf16[64,1024]{1,0:T(8,128)(2,1)S(1)}, bf16[64,1024]{1,0:T(8,128)(2,1)S(1)}, u32[]{:S(2)}, u32[]{:S(2)}) collective-permute-start(bf16[64,1024]{1,0:T(8,128)(2,1)S(1)} %shard_map.48), channel_id=1, source_target_pairs={{0,8},{8,16},{16,24},{24,0},{1,9},{9,17},{17,25},{25,1},{2,10},{10... | collective-permute-start | bytes 393224 | tf_op jit(solution)/shard_map/ppermute | solution.py:20
  19.5 7.1 %collective-permute-start.6 = (bf16[64,1024]{1,0:T(8,128)(2,1)S(1)}, bf16[64,1024]{1,0:T(8,128)(2,1)S(1)}, u32[]{:S(2)}, u32[]{:S(2)}) collective-permute-start(bf16[64,1024]{1,0:T(8,128)(2,1)S(1)} %shard_map.52), channel_id=1, source_target_pairs={{0,8},{8,16},{16,24},{24,0},{1,9},{9,17},{17,25},{25,1},{2,10},{10... | collective-permute-start | bytes 393224 | tf_op jit(solution)/shard_map/ppermute | solution.py:20
  24.0 3.9 %copy-start = (bf16[1,1,2,1024,256]{4,3,2,1,0:T(8,128)(2,1)S(1)}, bf16[1,1,2,1024,256]{4,3,2,1,0:T(8,128)(2,1)}, u32[]{:S(2)}) copy-start(bf16[1,1,2,1024,256]{4,3,2,1,0:T(8,128)(2,1)} %upward_ref.1) | copy-start | bytes 3145732
  25.4 6.3 %collective-permute-start.2 = (bf16[64,1024]{1,0:T(8,128)(2,1)S(1)}, bf16[64,1024]{1,0:T(8,128)(2,1)S(1)}, u32[]{:S(2)}, u32[]{:S(2)}) collective-permute-start(bf16[64,1024]{1,0:T(8,128)(2,1)S(1)} %shard_map.49), channel_id=1, source_target_pairs={{0,8},{8,16},{16,24},{24,0},{1,9},{9,17},{17,25},{25,1},{2,10},{10... | collective-permute-start | bytes 393224 | tf_op jit(solution)/shard_map/ppermute | solution.py:20
  27.9 6.6 %collective-permute-start.7 = (bf16[64,1024]{1,0:T(8,128)(2,1)S(1)}, bf16[64,1024]{1,0:T(8,128)(2,1)S(1)}, u32[]{:S(2)}, u32[]{:S(2)}) collective-permute-start(bf16[64,1024]{1,0:T(8,128)(2,1)S(1)} %shard_map.53.refs_0_), channel_id=1, source_target_pairs={{0,8},{8,16},{16,24},{24,0},{1,9},{9,17},{17,25},{25,1},{2,10},{10... | collective-permute-start | bytes 393224 | tf_op jit(solution)/shard_map/ppermute | solution.py:20
  33.0 6.1 %collective-permute-start.10 = (bf16[64,1024]{1,0:T(8,128)(2,1)S(1)}, bf16[64,1024]{1,0:T(8,128)(2,1)S(1)}, u32[]{:S(2)}, u32[]{:S(2)}) collective-permute-start(bf16[64,1024]{1,0:T(8,128)(2,1)S(1)} %shard_map.56.refs_1_.refs_4_), channel_id=1, source_target_pairs={{0,8},{8,16},{16,24},{24,0},{1,9},{9,17},{17,25},{25,1},{2,10},{10... | collective-permute-start | bytes 393224 | tf_op jit(solution)/shard_map/ppermute | solution.py:20
  33.1 10.0 %collective-permute-start.13 = (bf16[128,1024]{1,0:T(8,128)(2,1)S(1)}, bf16[128,1024]{1,0:T(8,128)(2,1)S(1)}, u32[]{:S(2)}, u32[]{:S(2)}) collective-permute-start(bf16[128,1024]{1,0:T(8,128)(2,1)S(1)} %shard_map.60), channel_id=1, source_target_pairs={{0,2},{1,3},{2,0},{3,1},{4,6},{5,7},{6,4},{7,5},{8,10},{9,11},{10,... | collective-permute-start | bytes 786440 | tf_op jit(solution)/shard_map/ppermute | solution.py:24
  35.8 5.9 %collective-permute-start.8 = (bf16[64,1024]{1,0:T(8,128)(2,1)S(1)}, bf16[64,1024]{1,0:T(8,128)(2,1)S(1)}, u32[]{:S(2)}, u32[]{:S(2)}) collective-permute-start(bf16[64,1024]{1,0:T(8,128)(2,1)S(1)} %shard_map.54.refs_0_.refs_1_), channel_id=1, source_target_pairs={{0,8},{8,16},{16,24},{24,0},{1,9},{9,17},{17,25},{25,1},{2,10},{10... | collective-permute-start | bytes 393224 | tf_op jit(solution)/shard_map/ppermute | solution.py:20
  40.4 7.0 %collective-permute-start.12 = (bf16[64,1024]{1,0:T(8,128)(2,1)S(1)}, bf16[64,1024]{1,0:T(8,128)(2,1)S(1)}, u32[]{:S(2)}, u32[]{:S(2)}) collective-permute-start(bf16[64,1024]{1,0:T(8,128)(2,1)S(1)} %shard_map.57.refs_1_.refs_5_), channel_id=1, source_target_pairs={{0,8},{8,16},{16,24},{24,0},{1,9},{9,17},{17,25},{25,1},{2,10},{10... | collective-permute-start | bytes 393224 | tf_op jit(solution)/shard_map/ppermute | solution.py:20
  40.5 9.1 %collective-permute-start.11 = (bf16[128,1024]{1,0:T(8,128)(2,1)S(1)}, bf16[128,1024]{1,0:T(8,128)(2,1)S(1)}, u32[]{:S(2)}, u32[]{:S(2)}) collective-permute-start(bf16[128,1024]{1,0:T(8,128)(2,1)S(1)} %shard_map.58), channel_id=1, source_target_pairs={{0,2},{1,3},{2,0},{3,1},{4,6},{5,7},{6,4},{7,5},{8,10},{9,11},{10,... | collective-permute-start | bytes 786440 | tf_op jit(solution)/shard_map/ppermute | solution.py:24
  43.0 6.1 %collective-permute-start.9 = (bf16[64,1024]{1,0:T(8,128)(2,1)S(1)}, bf16[64,1024]{1,0:T(8,128)(2,1)S(1)}, u32[]{:S(2)}, u32[]{:S(2)}) collective-permute-start(bf16[64,1024]{1,0:T(8,128)(2,1)S(1)} %shard_map.55.refs_0_.refs_2_), channel_id=1, source_target_pairs={{0,8},{8,16},{16,24},{24,0},{1,9},{9,17},{17,25},{25,1},{2,10},{10... | collective-permute-start | bytes 393224 | tf_op jit(solution)/shard_map/ppermute | solution.py:20
  48.9 9.4 %collective-permute-start.15 = (bf16[128,1024]{1,0:T(8,128)(2,1)S(1)}, bf16[128,1024]{1,0:T(8,128)(2,1)S(1)}, u32[]{:S(2)}, u32[]{:S(2)}) collective-permute-start(bf16[128,1024]{1,0:T(8,128)(2,1)S(1)} %shard_map.63), channel_id=1, source_target_pairs={{0,2},{1,3},{2,0},{3,1},{4,6},{5,7},{6,4},{7,5},{8,10},{9,11},{10,... | collective-permute-start | bytes 786440 | tf_op jit(solution)/shard_map/ppermute | solution.py:24
  49.0 5.9 %collective-permute-start.14 = (bf16[64,1024]{1,0:T(8,128)(2,1)S(1)}, bf16[64,1024]{1,0:T(8,128)(2,1)S(1)}, u32[]{:S(2)}, u32[]{:S(2)}) collective-permute-start(bf16[64,1024]{1,0:T(8,128)(2,1)S(1)} %shard_map.61.refs_1_.refs_6_), channel_id=1, source_target_pairs={{0,8},{8,16},{16,24},{24,0},{1,9},{9,17},{17,25},{25,1},{2,10},{10... | collective-permute-start | bytes 393224 | tf_op jit(solution)/shard_map/ppermute | solution.py:20
  50.9 7.4 %collective-permute-start.16 = (bf16[64,1024]{1,0:T(8,128)(2,1)S(1)}, bf16[64,1024]{1,0:T(8,128)(2,1)S(1)}, u32[]{:S(2)}, u32[]{:S(2)}) collective-permute-start(bf16[64,1024]{1,0:T(8,128)(2,1)S(1)} %shard_map.59.refs_3_), channel_id=1, source_target_pairs={{0,2},{1,3},{2,0},{3,1},{4,6},{5,7},{6,4},{7,5},{8,10},{9,11},{10,... | collective-permute-start | bytes 393224 | tf_op jit(solution)/shard_map/ppermute | solution.py:24
  56.2 5.0 %collective-permute-start.17 = (bf16[64,1024]{1,0:T(8,128)(2,1)S(1)}, bf16[64,1024]{1,0:T(8,128)(2,1)S(1)}, u32[]{:S(2)}, u32[]{:S(2)}) collective-permute-start(bf16[64,1024]{1,0:T(8,128)(2,1)S(1)} %shard_map.62.refs_7_), channel_id=1, source_target_pairs={{0,2},{1,3},{2,0},{3,1},{4,6},{5,7},{6,4},{7,5},{8,10},{9,11},{10,... | collective-permute-start | bytes 393224 | tf_op jit(solution)/shard_map/ppermute | solution.py:24
  62.0 2.0 %collective-permute-start.18 = (bf16[1,2,128,1024]{3,2,1,0:T(8,128)(2,1)S(1)}, bf16[1,2,128,1024]{3,2,1,0:T(8,128)(2,1)S(1)}, u32[]{:S(2)}, u32[]{:S(2)}) collective-permute-start(bf16[1,2,128,1024]{3,2,1,0:T(8,128)(2,1)S(1)} %get-tuple-element.46), channel_id=1, source_target_pairs={{0,1},{1,0},{2,3},{3,2},{4,5},{5,4},{6,7},{7,6},{8,9},{9,8},{10,11... | collective-permute-start | bytes 1572872 | tf_op jit(solution)/shard_map/ppermute | solution.py:24
  64.2 26.3 %collective-permute-start.20 = (bf16[1,2,128,1024]{3,2,1,0:T(8,128)(2,1)S(1)}, bf16[1,2,128,1024]{3,2,1,0:T(8,128)(2,1)S(1)}, u32[]{:S(2)}, u32[]{:S(2)}) collective-permute-start(bf16[1,2,128,1024]{3,2,1,0:T(8,128)(2,1)S(1)} %add_convert_fusion), channel_id=1, source_target_pairs={{0,4},{1,5},{2,6},{3,7},{4,0},{5,1},{6,2},{7,3},{8,12},{9,13},{10,... | collective-permute-start | bytes 1572872 | tf_op jit(solution)/shard_map/ppermute | solution.py:20
  67.0 23.5 %collective-permute-start.19 = (bf16[1,2,128,1024]{3,2,1,0:T(8,128)(2,1)S(1)}, bf16[1,2,128,1024]{3,2,1,0:T(8,128)(2,1)S(1)}, u32[]{:S(2)}, u32[]{:S(2)}) collective-permute-start(bf16[1,2,128,1024]{3,2,1,0:T(8,128)(2,1)S(1)} %get-tuple-element.47), channel_id=1, source_target_pairs={{0,1},{1,0},{2,3},{3,2},{4,5},{5,4},{6,7},{7,6},{8,9},{9,8},{10,11... | collective-permute-start | bytes 1572872 | tf_op jit(solution)/shard_map/ppermute | solution.py:24

commit v16 on v15

--- a/solution.py
+++ b/solution.py
@@ -358,7 +358,7 @@
             if event == steps:
                 arrived, left = lax.optimization_barrier((arrived, left))
             for at, (sent, panel) in enumerate(crossing):
-                if event == sent + BEHIND + (at == 0):
+                if event == sent + BEHIND + (at <= 1) - (at == 3):
                     arrived, panel = lax.optimization_barrier((arrived, panel))
                     crossing[at] = (sent, panel)
             out = advance(level, arrived, out, joined, factor)
@@ -370,8 +370,8 @@
                 crossing.append((event, swapped(out, "freq", 2)))
             else:
                 waiting.append(out)
-                if len(waiting) == TOGETHER:
-                    crossing.append((event, swapped(stacked(waiting), "freq", 2)))
+                if len(waiting) == TOGETHER or step >= steps - 2:
+                    crossing.append((event, swapped(stacked(waiting) if len(waiting) > 1 else waiting[0], "freq", 2)))
                     waiting = []
     other = [panel for _, panel in crossing]
     counts = [panel.shape[0] // out.shape[0] for panel in other]

time: 92.1 us -> 95.2 us (1.034); the launches traced: 91.8 us -> 93.7 us
  waiting for transfers between devices: 52.1 us -> 53.8 us
    ppermute x8 -> x9, waiting for transfers between devices: 3.44 us -> 6.14 us  [swapped(): lax.ppermute(block, axis, [(i, i ^ bit) for i in range(lax.axis_size(axis...]
    ppermute x8 -> x9, starting transfers between devices: 6.11 us -> 6.35 us  [swapped(): lax.ppermute(block, axis, [(i, i ^ bit) for i in range(lax.axis_size(axis...]
    pallas_call x19 -> x18, Pallas kernels: 21.2 us -> 21.1 us  [whole_call(): pl.pallas_call(kernel, in_specs=[pl.BlockSpec(memory_space=pltpu.SMEM)] *...]
  transfers between devices with their start and end apart: 21 -> 22, of which waited for: 16 -> 15; matrix products, arithmetic and copies ran while one was open for 0% -> 0% of each run, Pallas kernels for 22% -> 21%
where the time goes in v16:
time: 95.2 us; the launch traced here: 93.7 us
  waiting for transfers between devices  53.8 us (57%)
  Pallas kernels  26.5 us (28%)
  starting transfers between devices  12.9 us (14%)
    ppermute x13, waiting for transfers between devices, ring(): lax.ppermute(block, axis, [(i, (i + distance) % size) for i in range(size)])  47.7 us
    pallas_call x18, Pallas kernels, whole_call(): pl.pallas_call(kernel, in_specs=[pl.BlockSpec(memory_space=pltpu.SMEM)] *...  21.1 us
    ppermute x13, starting transfers between devices, ring(): lax.ppermute(block, axis, [(i, (i + distance) % size) for i in range(size)])  6.53 us
    ppermute x9, starting transfers between devices, swapped(): lax.ppermute(block, axis, [(i, i ^ bit) for i in range(lax.axis_size(axis...  6.35 us
    ppermute x9, waiting for transfers between devices, swapped(): lax.ppermute(block, axis, [(i, i ^ bit) for i in range(lax.axis_size(axis...  6.14 us
    pallas_call x1, Pallas kernels, first_advance(): pl.pallas_call(functools.partial(first_kernel, part), in_specs=[pl.BlockS...  4.72 us
  transfers between devices with their start and end apart: 22, of which 15 were waited for; matrix products, arithmetic and copies ran while one was open for 0% of the time, Pallas kernels for 21%

profile of v16, /device:TPU:4, one launch (start us, length us, event | category | flops | bytes accessed | tf_op | source)
XLA Modules:
  0.0 93.7 jit_solution(7757098869936473896)
XLA Ops:
  0.0 4.7 %shard_map.46 = (bf16[64,1024]{1,0:T(8,128)(2,1)S(1)}, bf16[64,1024]{1,0:T(8,128)(2,1)S(1)}, bf16[64,1024]{1,0:T(8,128)(2,1)S(1)}, bf16[64,1024]{1,0:T(8,128)(2,...) custom-call(s32[1]{0:T(128)} %bitcast.level_ref, ...), custom_call_target="tpu_custom_call" | custom-call | flops 1073741824 | bytes 6291456 | tf_op jit(solution)/shard_map/pallas_call | solution.py:107
  4.7 1.5 %collective-permute-start.4 = (bf16[64,1024]{1,0:T(8,128)(2,1)S(1)}, bf16[64,1024]{1,0:T(8,128)(2,1)S(1)}, u32[]{:S(2)}, u32[]{:S(2)}) collective-permute-start(bf16[64,1024]{1,0:T(8,128)(2,1)S(1)} %get-tuple-element.38.ready_ref), channel_id=1, source_target_pairs={{0,8},{8,16},{16,24},{24,0},{1,9},{9,17},{17,25},{25,1},{2,10},{10... | collective-permute-start | bytes 393224 | tf_op jit(solution)/shard_map/ppermute | solution.py:20
  6.3 1.6 %collective-permute-start.3 = (bf16[2,512,256]{2,1,0:T(8,128)(2,1)S(1)}, bf16[2,512,256]{2,1,0:T(8,128)(2,1)S(1)}, u32[]{:S(2)}, u32[]{:S(2)}) collective-permute-start(bf16[2,512,256]{2,1,0:T(8,128)(2,1)S(1)} %get-tuple-element.36), channel_id=1, source_target_pairs={{0,2},{1,3},{2,0},{3,1},{4,6},{5,7},{6,4},{7,5},{8,10},{9,11},{10,... | collective-permute-start | bytes 1572872 | tf_op jit(solution)/shard_map/ppermute | solution.py:24
  7.9 1.4 %shard_map.47 = (bf16[64,1024]{1,0:T(8,128)(2,1)S(1)}, bf16[64,1024]{1,0:T(8,128)(2,1)S(1)}, bf16[64,1024]{1,0:T(8,128)(2,1)S(1)}, bf16[64,1024]{1,0:T(8,128)(2,1)S(1)}) custom-call(bf16[1024,2048]{1,0:T(8,128)(2,1)S(1)} %get-tuple-element.31.joined_ref, bf16[1024,256]{1,0:T(8,128)(2,1)S(1)} %get-tuple-element.32.right_ref, f32[1,1024]{1,0:T(1,128)S(1)} %bitcast.5), custom_call_target="tpu_custom_call" | custom-call | flops 1073741824 | bytes 5246976 | tf_op jit(solution)/shard_map/pallas_call | solution.py:285
  10.9 1.3 %shard_map.51 = bf16[64,1024]{1,0:T(8,128)(2,1)S(1)} custom-call(s32[1]{0:T(128)} %bitcast.level_ref, bf16[64,1024]{1,0:T(8,128)(2,1)S(1)} %collective-permute-done.4.arrived_ref, bf16[64,1024]{1,0:T(8,128)(2,1)S(1)} %get-tuple-element.39.ready_ref, bf16[1024,2048]{1,0:T(8,128)(2,1)S(1)} %get-tuple-element.31.joined_ref, f32[1,1024]{1,0:T(1,128)S(1)} %bitcast.6), custom_call_target="tpu_custom_call" | custom-call | flops 268435456 | bytes 4591616 | tf_op jit(solution)/shard_map/pallas_call | solution.py:285
  12.9 2.7 %collective-permute-done.arrived_ref = bf16[64,1024]{1,0:T(8,128)(2,1)S(1)} collective-permute-done((bf16[64,1024]{1,0:T(8,128)(2,1)S(1)}, bf16[64,1024]{1,0:T(8,128)(2,1)S(1)}, u32[]{:S(2)}, u32[]{:S(2)}) %collective-permute-start) | collective-permute-done | bytes 131104 | tf_op jit(solution)/shard_map/ppermute | solution.py:20
  15.6 1.3 %shard_map.48 = bf16[64,1024]{1,0:T(8,128)(2,1)S(1)} custom-call(s32[1]{0:T(128)} %bitcast.level_ref, bf16[64,1024]{1,0:T(8,128)(2,1)S(1)} %collective-permute-done.arrived_ref, bf16[64,1024]{1,0:T(8,128)(2,1)S(1)} %get-tuple-element.34.ready_ref, bf16[1024,2048]{1,0:T(8,128)(2,1)S(1)} %get-tuple-element.31.joined_ref, f32[1,1024]{1,0:T(1,128)S(1)} %bitcast.7), custom_call_target="tpu_custom_call" | custom-call | flops 268435456 | bytes 4591616 | tf_op jit(solution)/shard_map/pallas_call | solution.py:285
  19.9 4.2 %collective-permute-done.1.arrived_ref = bf16[64,1024]{1,0:T(8,128)(2,1)S(1)} collective-permute-done((bf16[64,1024]{1,0:T(8,128)(2,1)S(1)}, bf16[64,1024]{1,0:T(8,128)(2,1)S(1)}, u32[]{:S(2)}, u32[]{:S(2)}) %collective-permute-start.1) | collective-permute-done | bytes 131104 | tf_op jit(solution)/shard_map/ppermute | solution.py:20
  28.8 2.9 %collective-permute-done.2.arrived_ref = bf16[64,1024]{1,0:T(8,128)(2,1)S(1)} collective-permute-done((bf16[64,1024]{1,0:T(8,128)(2,1)S(1)}, bf16[64,1024]{1,0:T(8,128)(2,1)S(1)}, u32[]{:S(2)}, u32[]{:S(2)}) %collective-permute-start.2) | collective-permute-done | bytes 131104 | tf_op jit(solution)/shard_map/ppermute | solution.py:20
  31.7 1.3 %shard_map.57.refs_1_.refs_4_ = bf16[64,1024]{1,0:T(8,128)(2,1)S(1)} custom-call(s32[1]{0:T(128)} %bitcast.level_ref, bf16[64,1024]{1,0:T(8,128)(2,1)S(1)} %collective-permute-done.2.arrived_ref, bf16[64,1024]{1,0:T(8,128)(2,1)S(1)} %get-tuple-element.43.ready_ref, bf16[1024,2048]{1,0:T(8,128)(2,1)S(1)} %get-tuple-element.31.joined_ref, f32[1,1024]{1,0:T(1,128)S(1)} %bitcast.11), custom_call_target="tpu_custom_call" | custom-call | flops 268435456 | bytes 4591616 | tf_op jit(solution)/shard_map/pallas_call | solution.py:285
  34.5 1.3 %shard_map.54.refs_0_.refs_1_ = bf16[64,1024]{1,0:T(8,128)(2,1)S(1)} custom-call(s32[1]{0:T(128)} %bitcast.level_ref, bf16[64,1024]{1,0:T(8,128)(2,1)S(1)} %collective-permute-done.7.arrived_ref, bf16[64,1024]{1,0:T(8,128)(2,1)S(1)} %get-tuple-element.38.ready_ref, bf16[1024,2048]{1,0:T(8,128)(2,1)S(1)} %get-tuple-element.31.joined_ref, f32[1,1024]{1,0:T(1,128)S(1)} %bitcast.12), custom_call_target="tpu_custom_call" | custom-call | flops 268435456 | bytes 4591616 | tf_op jit(solution)/shard_map/pallas_call | solution.py:285
  35.8 3.2 %collective-permute-done.10.arrived_ref = bf16[64,1024]{1,0:T(8,128)(2,1)S(1)} collective-permute-done((bf16[64,1024]{1,0:T(8,128)(2,1)S(1)}, bf16[64,1024]{1,0:T(8,128)(2,1)S(1)}, u32[]{:S(2)}, u32[]{:S(2)}) %collective-permute-start.10) | collective-permute-done | bytes 131104 | tf_op jit(solution)/shard_map/ppermute | solution.py:20
  39.1 1.3 %shard_map.58.refs_1_.refs_5_ = bf16[64,1024]{1,0:T(8,128)(2,1)S(1)} custom-call(s32[1]{0:T(128)} %bitcast.level_ref, bf16[64,1024]{1,0:T(8,128)(2,1)S(1)} %collective-permute-done.10.arrived_ref, bf16[64,1024]{1,0:T(8,128)(2,1)S(1)} %get-tuple-element.33.ready_ref, bf16[1024,2048]{1,0:T(8,128)(2,1)S(1)} %get-tuple-element.31.joined_ref, f32[1,1024]{1,0:T(1,128)S(1)} %bitcast.13), custom_call_target="tpu_custom_call" | custom-call | flops 268435456 | bytes 4591616 | tf_op jit(solution)/shard_map/pallas_call | solution.py:285
  43.1 4.4 %collective-permute-done.11.arrived_ref = bf16[64,1024]{1,0:T(8,128)(2,1)S(1)} collective-permute-done((bf16[64,1024]{1,0:T(8,128)(2,1)S(1)}, bf16[64,1024]{1,0:T(8,128)(2,1)S(1)}, u32[]{:S(2)}, u32[]{:S(2)}) %collective-permute-start.11) | collective-permute-done | bytes 131104 | tf_op jit(solution)/shard_map/ppermute | solution.py:20
  47.5 1.3 %shard_map.60.refs_6_ = bf16[64,1024]{1,0:T(8,128)(2,1)S(1)} custom-call(s32[1]{0:T(128)} %bitcast.level_ref, bf16[64,1024]{1,0:T(8,128)(2,1)S(1)} %collective-permute-done.11.arrived_ref, bf16[64,1024]{1,0:T(8,128)(2,1)S(1)} %get-tuple-element.34.ready_ref, bf16[1024,2048]{1,0:T(8,128)(2,1)S(1)} %get-tuple-element.31.joined_ref, f32[1,1024]{1,0:T(1,128)S(1)} %bitcast.15), custom_call_target="tpu_custom_call" | custom-call | flops 268435456 | bytes 4591616 | tf_op jit(solution)/shard_map/pallas_call | solution.py:285
  53.4 1.5 %collective-permute-done.13.arrived_ref = bf16[64,1024]{1,0:T(8,128)(2,1)S(1)} collective-permute-done((bf16[64,1024]{1,0:T(8,128)(2,1)S(1)}, bf16[64,1024]{1,0:T(8,128)(2,1)S(1)}, u32[]{:S(2)}, u32[]{:S(2)}) %collective-permute-start.13) | collective-permute-done | bytes 131104 | tf_op jit(solution)/shard_map/ppermute | solution.py:20
  54.9 2.0 %collective-permute-done.16.refs_11_.refs_3_ = bf16[64,1024]{1,0:T(8,128)(2,1)S(1)} collective-permute-done((bf16[64,1024]{1,0:T(8,128)(2,1)S(1)}, bf16[64,1024]{1,0:T(8,128)(2,1)S(1)}, u32[]{:S(2)}, u32[]{:S(2)}) %collective-permute-start.16) | collective-permute-done | bytes 131104 | tf_op jit(solution)/shard_map/ppermute | solution.py:24
  56.9 1.3 %shard_map.62.refs_7_ = bf16[64,1024]{1,0:T(8,128)(2,1)S(1)} custom-call(s32[1]{0:T(128)} %bitcast.level_ref, bf16[64,1024]{1,0:T(8,128)(2,1)S(1)} %collective-permute-done.13.arrived_ref, bf16[64,1024]{1,0:T(8,128)(2,1)S(1)} %get-tuple-element.35.ready_ref, bf16[1024,2048]{1,0:T(8,128)(2,1)S(1)} %get-tuple-element.31.joined_ref, f32[1,1024]{1,0:T(1,128)S(1)} %bitcast.17), custom_call_target="tpu_custom_call" | custom-call | flops 268435456 | bytes 4591616 | tf_op jit(solution)/shard_map/pallas_call | solution.py:285
  59.1 1.9 %shard_map.63.early_ref = f32[1024,1024]{1,0:T(8,128)S(1)} custom-call(s32[1]{0:T(128)} %bitcast.level_ref, bf16[1024,1024]{1,0:T(8,128)(2,1)S(1)} %shard_map.50.left_ref, bf16[64,1024]{1,0:T(8,128)(2,1)S(1)} %shard_map.53.refs_0_, bf16[64,1024]{1,0:T(8,128)(2,1)S(1)} %shard_map.54.refs_0_.refs_1_, bf16[64,1024]{1,0:T(8,128)(2,1)S(1)} %shard_map.55.refs_2_, ...), custom_call_target="tpu_custom_call" | custom-call | flops 1610612736 | bytes 8257536 | tf_op jit(solution)/shard_map/pallas_call | solution.py:285
  61.0 2.2 %collective-permute-done.18.refs_4_ = bf16[64,1024]{1,0:T(8,128)(2,1)S(1)} collective-permute-done((bf16[64,1024]{1,0:T(8,128)(2,1)S(1)}, bf16[64,1024]{1,0:T(8,128)(2,1)S(1)}, u32[]{:S(2)}, u32[]{:S(2)}) %collective-permute-start.18) | collective-permute-done | bytes 131104 | tf_op jit(solution)/shard_map/ppermute | solution.py:24
  64.1 1.9 %collective-permute-done.19 = bf16[1,2,128,1024]{3,2,1,0:T(8,128)(2,1)S(1)} collective-permute-done((bf16[1,2,128,1024]{3,2,1,0:T(8,128)(2,1)S(1)}, bf16[1,2,128,1024]{3,2,1,0:T(8,128)(2,1)S(1)}, u32[]{:S(2)}, u32[]{:S(2)}) %collective-permute-start.19) | collective-permute-done | bytes 524320 | tf_op jit(solution)/shard_map/ppermute | solution.py:24
  66.2 2.7 %collective-permute-start.21 = (bf16[1,2,128,1024]{3,2,1,0:T(8,128)(2,1)S(1)}, bf16[1,2,128,1024]{3,2,1,0:T(8,128)(2,1)S(1)}, u32[]{:S(2)}, u32[]{:S(2)}) collective-permute-start(bf16[1,2,128,1024]{3,2,1,0:T(8,128)(2,1)S(1)} %add_convert_fusion), channel_id=1, source_target_pairs={{0,4},{1,5},{2,6},{3,7},{4,0},{5,1},{6,2},{7,3},{8,12},{9,13},{10,... | collective-permute-start | bytes 1572872 | tf_op jit(solution)/shard_map/ppermute | solution.py:20
  68.9 23.5 %collective-permute-done.21.refs_2_ = bf16[1,2,128,1024]{3,2,1,0:T(8,128)(2,1)S(1)} collective-permute-done((bf16[1,2,128,1024]{3,2,1,0:T(8,128)(2,1)S(1)}, bf16[1,2,128,1024]{3,2,1,0:T(8,128)(2,1)S(1)}, u32[]{:S(2)}, u32[]{:S(2)}) %collective-permute-start.21) | collective-permute-done | bytes 524320 | tf_op jit(solution)/shard_map/ppermute | solution.py:20
  92.4 1.3 %shard_map.65 = f32[1,128,2,1024]{3,2,1,0:T(2,128)} custom-call(f32[2,2,128,1024]{3,2,1,0:T(8,128)S(1)} %get-tuple-element.52.refs_0_, bf16[1,2,128,1024]{3,2,1,0:T(8,128)(2,1)S(1)} %collective-permute-done.20.refs_1_, bf16[1,2,128,1024]{3,2,1,0:T(8,128)(2,1)S(1)} %collective-permute-done.21.refs_2_), custom_call_target="tpu_custom_call" | custom-call | flops 786432 | bytes 4194304 | tf_op jit(solution)/shard_map/pallas_call | solution.py:285
  (45 shorter events, 20.6 us)
Async XLA Ops:
  0.0 7.9 %copy-start.1 = (f32[1,1,1024]{2,1,0:T(1,128)S(1)}, f32[1,1,1024]{2,1,0:T(1,128)}, u32[]{:S(2)}) copy-start(f32[1,1,1024]{2,1,0:T(1,128)} %factor_ref.1) | copy-start | bytes 12292
  4.7 6.2 %collective-permute-start.4 = (bf16[64,1024]{1,0:T(8,128)(2,1)S(1)}, bf16[64,1024]{1,0:T(8,128)(2,1)S(1)}, u32[]{:S(2)}, u32[]{:S(2)}) collective-permute-start(bf16[64,1024]{1,0:T(8,128)(2,1)S(1)} %get-tuple-element.38.ready_ref), channel_id=1, source_target_pairs={{0,8},{8,16},{16,24},{24,0},{1,9},{9,17},{17,25},{25,1},{2,10},{10... | collective-permute-start | bytes 393224 | tf_op jit(solution)/shard_map/ppermute | solution.py:20
  6.3 21.7 %collective-permute-start.3 = (bf16[2,512,256]{2,1,0:T(8,128)(2,1)S(1)}, bf16[2,512,256]{2,1,0:T(8,128)(2,1)S(1)}, u32[]{:S(2)}, u32[]{:S(2)}) collective-permute-start(bf16[2,512,256]{2,1,0:T(8,128)(2,1)S(1)} %get-tuple-element.36), channel_id=1, source_target_pairs={{0,2},{1,3},{2,0},{3,1},{4,6},{5,7},{6,4},{7,5},{8,10},{9,11},{10,... | collective-permute-start | bytes 1572872 | tf_op jit(solution)/shard_map/ppermute | solution.py:24
  9.2 6.3 %collective-permute-start = (bf16[64,1024]{1,0:T(8,128)(2,1)S(1)}, bf16[64,1024]{1,0:T(8,128)(2,1)S(1)}, u32[]{:S(2)}, u32[]{:S(2)}) collective-permute-start(bf16[64,1024]{1,0:T(8,128)(2,1)S(1)} %get-tuple-element.33.ready_ref), channel_id=1, source_target_pairs={{0,8},{8,16},{16,24},{24,0},{1,9},{9,17},{17,25},{25,1},{2,10},{10... | collective-permute-start | bytes 393224 | tf_op jit(solution)/shard_map/ppermute | solution.py:20
  12.2 5.9 %collective-permute-start.5 = (bf16[64,1024]{1,0:T(8,128)(2,1)S(1)}, bf16[64,1024]{1,0:T(8,128)(2,1)S(1)}, u32[]{:S(2)}, u32[]{:S(2)}) collective-permute-start(bf16[64,1024]{1,0:T(8,128)(2,1)S(1)} %shard_map.51), channel_id=1, source_target_pairs={{0,8},{8,16},{16,24},{24,0},{1,9},{9,17},{17,25},{25,1},{2,10},{10... | collective-permute-start | bytes 393224 | tf_op jit(solution)/shard_map/ppermute | solution.py:20
  16.9 7.1 %collective-permute-start.1 = (bf16[64,1024]{1,0:T(8,128)(2,1)S(1)}, bf16[64,1024]{1,0:T(8,128)(2,1)S(1)}, u32[]{:S(2)}, u32[]{:S(2)}) collective-permute-start(bf16[64,1024]{1,0:T(8,128)(2,1)S(1)} %shard_map.48), channel_id=1, source_target_pairs={{0,8},{8,16},{16,24},{24,0},{1,9},{9,17},{17,25},{25,1},{2,10},{10... | collective-permute-start | bytes 393224 | tf_op jit(solution)/shard_map/ppermute | solution.py:20
  19.5 7.1 %collective-permute-start.6 = (bf16[64,1024]{1,0:T(8,128)(2,1)S(1)}, bf16[64,1024]{1,0:T(8,128)(2,1)S(1)}, u32[]{:S(2)}, u32[]{:S(2)}) collective-permute-start(bf16[64,1024]{1,0:T(8,128)(2,1)S(1)} %shard_map.52), channel_id=1, source_target_pairs={{0,8},{8,16},{16,24},{24,0},{1,9},{9,17},{17,25},{25,1},{2,10},{10... | collective-permute-start | bytes 393224 | tf_op jit(solution)/shard_map/ppermute | solution.py:20
  24.0 3.9 %copy-start = (bf16[1,1,2,1024,256]{4,3,2,1,0:T(8,128)(2,1)S(1)}, bf16[1,1,2,1024,256]{4,3,2,1,0:T(8,128)(2,1)}, u32[]{:S(2)}) copy-start(bf16[1,1,2,1024,256]{4,3,2,1,0:T(8,128)(2,1)} %upward_ref.1) | copy-start | bytes 3145732
  25.4 6.3 %collective-permute-start.2 = (bf16[64,1024]{1,0:T(8,128)(2,1)S(1)}, bf16[64,1024]{1,0:T(8,128)(2,1)S(1)}, u32[]{:S(2)}, u32[]{:S(2)}) collective-permute-start(bf16[64,1024]{1,0:T(8,128)(2,1)S(1)} %shard_map.49), channel_id=1, source_target_pairs={{0,8},{8,16},{16,24},{24,0},{1,9},{9,17},{17,25},{25,1},{2,10},{10... | collective-permute-start | bytes 393224 | tf_op jit(solution)/shard_map/ppermute | solution.py:20
  27.9 6.6 %collective-permute-start.7 = (bf16[64,1024]{1,0:T(8,128)(2,1)S(1)}, bf16[64,1024]{1,0:T(8,128)(2,1)S(1)}, u32[]{:S(2)}, u32[]{:S(2)}) collective-permute-start(bf16[64,1024]{1,0:T(8,128)(2,1)S(1)} %shard_map.53.refs_0_), channel_id=1, source_target_pairs={{0,8},{8,16},{16,24},{24,0},{1,9},{9,17},{17,25},{25,1},{2,10},{10... | collective-permute-start | bytes 393224 | tf_op jit(solution)/shard_map/ppermute | solution.py:20
  33.0 6.1 %collective-permute-start.10 = (bf16[64,1024]{1,0:T(8,128)(2,1)S(1)}, bf16[64,1024]{1,0:T(8,128)(2,1)S(1)}, u32[]{:S(2)}, u32[]{:S(2)}) collective-permute-start(bf16[64,1024]{1,0:T(8,128)(2,1)S(1)} %shard_map.57.refs_1_.refs_4_), channel_id=1, source_target_pairs={{0,8},{8,16},{16,24},{24,0},{1,9},{9,17},{17,25},{25,1},{2,10},{10... | collective-permute-start | bytes 393224 | tf_op jit(solution)/shard_map/ppermute | solution.py:20
  33.1 10.0 %collective-permute-start.12 = (bf16[128,1024]{1,0:T(8,128)(2,1)S(1)}, bf16[128,1024]{1,0:T(8,128)(2,1)S(1)}, u32[]{:S(2)}, u32[]{:S(2)}) collective-permute-start(bf16[128,1024]{1,0:T(8,128)(2,1)S(1)} %shard_map.59), channel_id=1, source_target_pairs={{0,2},{1,3},{2,0},{3,1},{4,6},{5,7},{6,4},{7,5},{8,10},{9,11},{10,... | collective-permute-start | bytes 786440 | tf_op jit(solution)/shard_map/ppermute | solution.py:24
  35.8 5.9 %collective-permute-start.8 = (bf16[64,1024]{1,0:T(8,128)(2,1)S(1)}, bf16[64,1024]{1,0:T(8,128)(2,1)S(1)}, u32[]{:S(2)}, u32[]{:S(2)}) collective-permute-start(bf16[64,1024]{1,0:T(8,128)(2,1)S(1)} %shard_map.54.refs_0_.refs_1_), channel_id=1, source_target_pairs={{0,8},{8,16},{16,24},{24,0},{1,9},{9,17},{17,25},{25,1},{2,10},{10... | collective-permute-start | bytes 393224 | tf_op jit(solution)/shard_map/ppermute | solution.py:20
  40.4 7.1 %collective-permute-start.11 = (bf16[64,1024]{1,0:T(8,128)(2,1)S(1)}, bf16[64,1024]{1,0:T(8,128)(2,1)S(1)}, u32[]{:S(2)}, u32[]{:S(2)}) collective-permute-start(bf16[64,1024]{1,0:T(8,128)(2,1)S(1)} %shard_map.58.refs_1_.refs_5_), channel_id=1, source_target_pairs={{0,8},{8,16},{16,24},{24,0},{1,9},{9,17},{17,25},{25,1},{2,10},{10... | collective-permute-start | bytes 393224 | tf_op jit(solution)/shard_map/ppermute | solution.py:20
  40.5 14.4 %collective-permute-start.14 = (bf16[128,1024]{1,0:T(8,128)(2,1)S(1)}, bf16[128,1024]{1,0:T(8,128)(2,1)S(1)}, u32[]{:S(2)}, u32[]{:S(2)}) collective-permute-start(bf16[128,1024]{1,0:T(8,128)(2,1)S(1)} %shard_map.61), channel_id=1, source_target_pairs={{0,2},{1,3},{2,0},{3,1},{4,6},{5,7},{6,4},{7,5},{8,10},{9,11},{10,... | collective-permute-start | bytes 786440 | tf_op jit(solution)/shard_map/ppermute | solution.py:24
  43.0 8.1 %collective-permute-start.9 = (bf16[64,1024]{1,0:T(8,128)(2,1)S(1)}, bf16[64,1024]{1,0:T(8,128)(2,1)S(1)}, u32[]{:S(2)}, u32[]{:S(2)}) collective-permute-start(bf16[64,1024]{1,0:T(8,128)(2,1)S(1)} %shard_map.55.refs_2_), channel_id=1, source_target_pairs={{0,8},{8,16},{16,24},{24,0},{1,9},{9,17},{17,25},{25,1},{2,10},{10... | collective-permute-start | bytes 393224 | tf_op jit(solution)/shard_map/ppermute | solution.py:20
  48.8 6.1 %collective-permute-start.13 = (bf16[64,1024]{1,0:T(8,128)(2,1)S(1)}, bf16[64,1024]{1,0:T(8,128)(2,1)S(1)}, u32[]{:S(2)}, u32[]{:S(2)}) collective-permute-start(bf16[64,1024]{1,0:T(8,128)(2,1)S(1)} %shard_map.60.refs_6_), channel_id=1, source_target_pairs={{0,8},{8,16},{16,24},{24,0},{1,9},{9,17},{17,25},{25,1},{2,10},{10... | collective-permute-start | bytes 393224 | tf_op jit(solution)/shard_map/ppermute | solution.py:20
  49.0 5.9 %collective-permute-start.15 = (bf16[64,1024]{1,0:T(8,128)(2,1)S(1)}, bf16[64,1024]{1,0:T(8,128)(2,1)S(1)}, u32[]{:S(2)}, u32[]{:S(2)}) collective-permute-start(bf16[64,1024]{1,0:T(8,128)(2,1)S(1)} %shard_map.55.refs_2_), channel_id=1, source_target_pairs={{0,2},{1,3},{2,0},{3,1},{4,6},{5,7},{6,4},{7,5},{8,10},{9,11},{10,... | collective-permute-start | bytes 393224 | tf_op jit(solution)/shard_map/ppermute | solution.py:24
  49.9 6.9 %collective-permute-start.16 = (bf16[64,1024]{1,0:T(8,128)(2,1)S(1)}, bf16[64,1024]{1,0:T(8,128)(2,1)S(1)}, u32[]{:S(2)}, u32[]{:S(2)}) collective-permute-start(bf16[64,1024]{1,0:T(8,128)(2,1)S(1)} %shard_map.60.refs_6_), channel_id=1, source_target_pairs={{0,2},{1,3},{2,0},{3,1},{4,6},{5,7},{6,4},{7,5},{8,10},{9,11},{10,... | collective-permute-start | bytes 393224 | tf_op jit(solution)/shard_map/ppermute | solution.py:24
  52.5 6.7 %collective-permute-start.17 = (bf16[64,1024]{1,0:T(8,128)(2,1)S(1)}, bf16[64,1024]{1,0:T(8,128)(2,1)S(1)}, u32[]{:S(2)}, u32[]{:S(2)}) collective-permute-start(bf16[64,1024]{1,0:T(8,128)(2,1)S(1)} %shard_map.56.refs_3_), channel_id=1, source_target_pairs={{0,2},{1,3},{2,0},{3,1},{4,6},{5,7},{6,4},{7,5},{8,10},{9,11},{10,... | collective-permute-start | bytes 393224 | tf_op jit(solution)/shard_map/ppermute | solution.py:24
  58.2 5.0 %collective-permute-start.18 = (bf16[64,1024]{1,0:T(8,128)(2,1)S(1)}, bf16[64,1024]{1,0:T(8,128)(2,1)S(1)}, u32[]{:S(2)}, u32[]{:S(2)}) collective-permute-start(bf16[64,1024]{1,0:T(8,128)(2,1)S(1)} %shard_map.62.refs_7_), channel_id=1, source_target_pairs={{0,2},{1,3},{2,0},{3,1},{4,6},{5,7},{6,4},{7,5},{8,10},{9,11},{10,... | collective-permute-start | bytes 393224 | tf_op jit(solution)/shard_map/ppermute | solution.py:24
  64.0 2.0 %collective-permute-start.19 = (bf16[1,2,128,1024]{3,2,1,0:T(8,128)(2,1)S(1)}, bf16[1,2,128,1024]{3,2,1,0:T(8,128)(2,1)S(1)}, u32[]{:S(2)}, u32[]{:S(2)}) collective-permute-start(bf16[1,2,128,1024]{3,2,1,0:T(8,128)(2,1)S(1)} %get-tuple-element.54), channel_id=1, source_target_pairs={{0,1},{1,0},{2,3},{3,2},{4,5},{5,4},{6,7},{7,6},{8,9},{9,8},{10,11... | collective-permute-start | bytes 1572872 | tf_op jit(solution)/shard_map/ppermute | solution.py:24
  66.2 26.2 %collective-permute-start.21 = (bf16[1,2,128,1024]{3,2,1,0:T(8,128)(2,1)S(1)}, bf16[1,2,128,1024]{3,2,1,0:T(8,128)(2,1)S(1)}, u32[]{:S(2)}, u32[]{:S(2)}) collective-permute-start(bf16[1,2,128,1024]{3,2,1,0:T(8,128)(2,1)S(1)} %add_convert_fusion), channel_id=1, source_target_pairs={{0,4},{1,5},{2,6},{3,7},{4,0},{5,1},{6,2},{7,3},{8,12},{9,13},{10,... | collective-permute-start | bytes 1572872 | tf_op jit(solution)/shard_map/ppermute | solution.py:20
  68.9 23.5 %collective-permute-start.20 = (bf16[1,2,128,1024]{3,2,1,0:T(8,128)(2,1)S(1)}, bf16[1,2,128,1024]{3,2,1,0:T(8,128)(2,1)S(1)}, u32[]{:S(2)}, u32[]{:S(2)}) collective-permute-start(bf16[1,2,128,1024]{3,2,1,0:T(8,128)(2,1)S(1)} %get-tuple-element.55), channel_id=1, source_target_pairs={{0,1},{1,0},{2,3},{3,2},{4,5},{5,4},{6,7},{7,6},{8,9},{9,8},{10,11... | collective-permute-start | bytes 1572872 | tf_op jit(solution)/shard_map/ppermute | solution.py:24

commit v17 on v15

--- a/solution.py
+++ b/solution.py
@@ -315,18 +315,37 @@
 
 
 def last_kernel(scale, *refs):
-    *parts, out_ref = refs
-    for part in range(2):
-        total = parts[0][0, part]
-        for ref in parts[1:]:
-            total += ref[0, part].astype(jnp.float32)
-        out_ref[0, :, part] = total * scale
+    *parts, out_ref, total, sems = refs
+    pieces = sems.shape[0]
+    tall = total.shape[0] // pieces
+    copies = []
+    for piece in range(pieces):
+        rows = slice(piece * tall, (piece + 1) * tall)
+        for part in range(2):
+            out = parts[0][0, part, rows]
+            for ref in parts[1:]:
+                out += ref[0, part, rows].astype(jnp.float32)
+            total[rows, part] = out * scale
+        span = pl.ds(piece * tall, tall)
+        copies.append(pltpu.make_async_copy(total.at[span], out_ref.at[0, span], sems.at[piece]))
+        copies[-1].start()
+    for copy in copies:
+        copy.wait()
 
 
 def last_sum(parts, scale):
     rows, width = parts[0].shape[2:]
-    out = jax.ShapeDtypeStruct((1, rows, 2, width), jnp.float32)
-    return whole_call(functools.partial(last_kernel, scale), parts, [out], 2 * len(parts) * rows * width)[0]
+    return pl.pallas_call(
+        functools.partial(last_kernel, scale),
+        in_specs=[pl.BlockSpec(memory_space=pltpu.VMEM)] * len(parts),
+        out_specs=pl.BlockSpec(memory_space=pltpu.HBM),
+        out_shape=jax.ShapeDtypeStruct((1, rows, 2, width), jnp.float32),
+        scratch_shapes=[pltpu.VMEM((rows, 2, width), jnp.float32), pltpu.SemaphoreType.DMA((4,))],
+        compiler_params=pltpu.CompilerParams(vmem_limit_bytes=LIMIT),
+        cost_estimate=pl.CostEstimate(
+            flops=2 * len(parts) * rows * width, bytes_accessed=16 * rows * width, transcendentals=0
+        ),
+    )(*parts)
 
 
 def shards(source, propagator, transmission, upgoing):

time: 92.1 us -> 92 us (level)
    pallas_call x19 -> x18, Pallas kernels: 21.2 us -> 19.9 us  [whole_call(): pl.pallas_call(kernel, in_specs=[pl.BlockSpec(memory_space=pltpu.SMEM)] *...]
    pallas_call x0 -> x1, Pallas kernels: none -> 1.09 us  [last_sum(): pl.pallas_call(functools.partial(last_kernel, scale), in_specs=[pl.BlockS...]
where the time goes in v17:
time: 92 us; the launch traced here: 91.7 us
  waiting for transfers between devices  52.1 us (57%)
  Pallas kernels  26.5 us (29%)
  starting transfers between devices  12.5 us (14%)
    ppermute x13, waiting for transfers between devices, ring(): lax.ppermute(block, axis, [(i, (i + distance) % size) for i in range(size)])  48.6 us
    pallas_call x18, Pallas kernels, whole_call(): pl.pallas_call(kernel, in_specs=[pl.BlockSpec(memory_space=pltpu.SMEM)] *...  19.9 us
    ppermute x13, starting transfers between devices, ring(): lax.ppermute(block, axis, [(i, (i + distance) % size) for i in range(size)])  6.42 us
    ppermute x8, starting transfers between devices, swapped(): lax.ppermute(block, axis, [(i, i ^ bit) for i in range(lax.axis_size(axis...  6.11 us
    pallas_call x1, Pallas kernels, first_advance(): pl.pallas_call(functools.partial(first_kernel, part), in_specs=[pl.BlockS...  4.72 us
    ppermute x8, waiting for transfers between devices, swapped(): lax.ppermute(block, axis, [(i, i ^ bit) for i in range(lax.axis_size(axis...  3.44 us
  transfers between devices with their start and end apart: 21, of which 16 were waited for; matrix products, arithmetic and copies ran while one was open for 0% of the time, Pallas kernels for 22%

profile of v17, /device:TPU:4, one launch (start us, length us, event | category | flops | bytes accessed | tf_op | source)
XLA Modules:
  0.0 91.7 jit_solution(8637058134457420254)
XLA Ops:
  0.0 4.7 %shard_map.46 = (bf16[64,1024]{1,0:T(8,128)(2,1)S(1)}, bf16[64,1024]{1,0:T(8,128)(2,1)S(1)}, bf16[64,1024]{1,0:T(8,128)(2,1)S(1)}, bf16[64,1024]{1,0:T(8,128)(2,...) custom-call(s32[1]{0:T(128)} %bitcast.level_ref, ...), custom_call_target="tpu_custom_call" | custom-call | flops 1073741824 | bytes 6291456 | tf_op jit(solution)/shard_map/pallas_call | solution.py:107
  4.7 1.5 %collective-permute-start.4 = (bf16[64,1024]{1,0:T(8,128)(2,1)S(1)}, bf16[64,1024]{1,0:T(8,128)(2,1)S(1)}, u32[]{:S(2)}, u32[]{:S(2)}) collective-permute-start(bf16[64,1024]{1,0:T(8,128)(2,1)S(1)} %get-tuple-element.34.ready_ref), channel_id=1, source_target_pairs={{0,8},{8,16},{16,24},{24,0},{1,9},{9,17},{17,25},{25,1},{2,10},{10... | collective-permute-start | bytes 393224 | tf_op jit(solution)/shard_map/ppermute | solution.py:20
  6.3 1.6 %collective-permute-start.3 = (bf16[2,512,256]{2,1,0:T(8,128)(2,1)S(1)}, bf16[2,512,256]{2,1,0:T(8,128)(2,1)S(1)}, u32[]{:S(2)}, u32[]{:S(2)}) collective-permute-start(bf16[2,512,256]{2,1,0:T(8,128)(2,1)S(1)} %get-tuple-element.32), channel_id=1, source_target_pairs={{0,2},{1,3},{2,0},{3,1},{4,6},{5,7},{6,4},{7,5},{8,10},{9,11},{10,... | collective-permute-start | bytes 1572872 | tf_op jit(solution)/shard_map/ppermute | solution.py:24
  7.9 1.4 %shard_map.47 = (bf16[64,1024]{1,0:T(8,128)(2,1)S(1)}, bf16[64,1024]{1,0:T(8,128)(2,1)S(1)}, bf16[64,1024]{1,0:T(8,128)(2,1)S(1)}, bf16[64,1024]{1,0:T(8,128)(2,1)S(1)}) custom-call(bf16[1024,2048]{1,0:T(8,128)(2,1)S(1)} %get-tuple-element.27.joined_ref, bf16[1024,256]{1,0:T(8,128)(2,1)S(1)} %get-tuple-element.28.right_ref, f32[1,1024]{1,0:T(1,128)S(1)} %bitcast.5), custom_call_target="tpu_custom_call" | custom-call | flops 1073741824 | bytes 5246976 | tf_op jit(solution)/shard_map/pallas_call | solution.py:285
  10.9 1.3 %shard_map.51 = bf16[64,1024]{1,0:T(8,128)(2,1)S(1)} custom-call(s32[1]{0:T(128)} %bitcast.level_ref, bf16[64,1024]{1,0:T(8,128)(2,1)S(1)} %collective-permute-done.4.arrived_ref, bf16[64,1024]{1,0:T(8,128)(2,1)S(1)} %get-tuple-element.35.ready_ref, bf16[1024,2048]{1,0:T(8,128)(2,1)S(1)} %get-tuple-element.27.joined_ref, f32[1,1024]{1,0:T(1,128)S(1)} %bitcast.6), custom_call_target="tpu_custom_call" | custom-call | flops 268435456 | bytes 4591616 | tf_op jit(solution)/shard_map/pallas_call | solution.py:285
  12.9 2.7 %collective-permute-done.arrived_ref = bf16[64,1024]{1,0:T(8,128)(2,1)S(1)} collective-permute-done((bf16[64,1024]{1,0:T(8,128)(2,1)S(1)}, bf16[64,1024]{1,0:T(8,128)(2,1)S(1)}, u32[]{:S(2)}, u32[]{:S(2)}) %collective-permute-start) | collective-permute-done | bytes 131104 | tf_op jit(solution)/shard_map/ppermute | solution.py:20
  15.6 1.3 %shard_map.48 = bf16[64,1024]{1,0:T(8,128)(2,1)S(1)} custom-call(s32[1]{0:T(128)} %bitcast.level_ref, bf16[64,1024]{1,0:T(8,128)(2,1)S(1)} %collective-permute-done.arrived_ref, bf16[64,1024]{1,0:T(8,128)(2,1)S(1)} %get-tuple-element.30.ready_ref, bf16[1024,2048]{1,0:T(8,128)(2,1)S(1)} %get-tuple-element.27.joined_ref, f32[1,1024]{1,0:T(1,128)S(1)} %bitcast.7), custom_call_target="tpu_custom_call" | custom-call | flops 268435456 | bytes 4591616 | tf_op jit(solution)/shard_map/pallas_call | solution.py:285
  19.9 4.2 %collective-permute-done.1.arrived_ref = bf16[64,1024]{1,0:T(8,128)(2,1)S(1)} collective-permute-done((bf16[64,1024]{1,0:T(8,128)(2,1)S(1)}, bf16[64,1024]{1,0:T(8,128)(2,1)S(1)}, u32[]{:S(2)}, u32[]{:S(2)}) %collective-permute-start.1) | collective-permute-done | bytes 131104 | tf_op jit(solution)/shard_map/ppermute | solution.py:20
  26.6 1.3 %shard_map.53.refs_0_ = bf16[64,1024]{1,0:T(8,128)(2,1)S(1)} custom-call(s32[1]{0:T(128)} %bitcast.level_ref, bf16[64,1024]{1,0:T(8,128)(2,1)S(1)} %collective-permute-done.6.arrived_ref, bf16[64,1024]{1,0:T(8,128)(2,1)S(1)} %get-tuple-element.37.ready_ref, bf16[1024,2048]{1,0:T(8,128)(2,1)S(1)} %get-tuple-element.27.joined_ref, f32[1,1024]{1,0:T(1,128)S(1)} %bitcast.10), custom_call_target="tpu_custom_call" | custom-call | flops 268435456 | bytes 4591616 | tf_op jit(solution)/shard_map/pallas_call | solution.py:285
  28.8 2.9 %collective-permute-done.2.arrived_ref = bf16[64,1024]{1,0:T(8,128)(2,1)S(1)} collective-permute-done((bf16[64,1024]{1,0:T(8,128)(2,1)S(1)}, bf16[64,1024]{1,0:T(8,128)(2,1)S(1)}, u32[]{:S(2)}, u32[]{:S(2)}) %collective-permute-start.2) | collective-permute-done | bytes 131104 | tf_op jit(solution)/shard_map/ppermute | solution.py:20
  31.7 1.3 %shard_map.56.refs_1_.refs_4_ = bf16[64,1024]{1,0:T(8,128)(2,1)S(1)} custom-call(s32[1]{0:T(128)} %bitcast.level_ref, bf16[64,1024]{1,0:T(8,128)(2,1)S(1)} %collective-permute-done.2.arrived_ref, bf16[64,1024]{1,0:T(8,128)(2,1)S(1)} %get-tuple-element.39.ready_ref, bf16[1024,2048]{1,0:T(8,128)(2,1)S(1)} %get-tuple-element.27.joined_ref, f32[1,1024]{1,0:T(1,128)S(1)} %bitcast.11), custom_call_target="tpu_custom_call" | custom-call | flops 268435456 | bytes 4591616 | tf_op jit(solution)/shard_map/pallas_call | solution.py:285
  34.5 1.3 %shard_map.54.refs_0_.refs_1_ = bf16[64,1024]{1,0:T(8,128)(2,1)S(1)} custom-call(s32[1]{0:T(128)} %bitcast.level_ref, bf16[64,1024]{1,0:T(8,128)(2,1)S(1)} %collective-permute-done.7.arrived_ref, bf16[64,1024]{1,0:T(8,128)(2,1)S(1)} %get-tuple-element.34.ready_ref, bf16[1024,2048]{1,0:T(8,128)(2,1)S(1)} %get-tuple-element.27.joined_ref, f32[1,1024]{1,0:T(1,128)S(1)} %bitcast.12), custom_call_target="tpu_custom_call" | custom-call | flops 268435456 | bytes 4591616 | tf_op jit(solution)/shard_map/pallas_call | solution.py:285
  35.8 3.2 %collective-permute-done.10.arrived_ref = bf16[64,1024]{1,0:T(8,128)(2,1)S(1)} collective-permute-done((bf16[64,1024]{1,0:T(8,128)(2,1)S(1)}, bf16[64,1024]{1,0:T(8,128)(2,1)S(1)}, u32[]{:S(2)}, u32[]{:S(2)}) %collective-permute-start.10) | collective-permute-done | bytes 131104 | tf_op jit(solution)/shard_map/ppermute | solution.py:20
  39.1 1.3 %shard_map.57.refs_1_.refs_5_ = bf16[64,1024]{1,0:T(8,128)(2,1)S(1)} custom-call(s32[1]{0:T(128)} %bitcast.level_ref, bf16[64,1024]{1,0:T(8,128)(2,1)S(1)} %collective-permute-done.10.arrived_ref, bf16[64,1024]{1,0:T(8,128)(2,1)S(1)} %get-tuple-element.29.ready_ref, bf16[1024,2048]{1,0:T(8,128)(2,1)S(1)} %get-tuple-element.27.joined_ref, f32[1,1024]{1,0:T(1,128)S(1)} %bitcast.13), custom_call_target="tpu_custom_call" | custom-call | flops 268435456 | bytes 4591616 | tf_op jit(solution)/shard_map/pallas_call | solution.py:285
  43.1 4.3 %collective-permute-done.12.arrived_ref = bf16[64,1024]{1,0:T(8,128)(2,1)S(1)} collective-permute-done((bf16[64,1024]{1,0:T(8,128)(2,1)S(1)}, bf16[64,1024]{1,0:T(8,128)(2,1)S(1)}, u32[]{:S(2)}, u32[]{:S(2)}) %collective-permute-start.12) | collective-permute-done | bytes 131104 | tf_op jit(solution)/shard_map/ppermute | solution.py:20
  47.4 1.5 %shard_map.61.refs_1_.refs_6_ = bf16[64,1024]{1,0:T(8,128)(2,1)S(1)} custom-call(s32[1]{0:T(128)} %bitcast.level_ref, bf16[64,1024]{1,0:T(8,128)(2,1)S(1)} %collective-permute-done.12.arrived_ref, bf16[64,1024]{1,0:T(8,128)(2,1)S(1)} %get-tuple-element.30.ready_ref, bf16[1024,2048]{1,0:T(8,128)(2,1)S(1)} %get-tuple-element.27.joined_ref, f32[1,1024]{1,0:T(1,128)S(1)} %bitcast.15), custom_call_target="tpu_custom_call" | custom-call | flops 268435456 | bytes 4591616 | tf_op jit(solution)/shard_map/pallas_call | solution.py:285
  50.9 1.5 %collective-permute-start.16 = (bf16[64,1024]{1,0:T(8,128)(2,1)S(1)}, bf16[64,1024]{1,0:T(8,128)(2,1)S(1)}, u32[]{:S(2)}, u32[]{:S(2)}) collective-permute-start(bf16[64,1024]{1,0:T(8,128)(2,1)S(1)} %shard_map.59.refs_3_), channel_id=1, source_target_pairs={{0,2},{1,3},{2,0},{3,1},{4,6},{5,7},{6,4},{7,5},{8,10},{9,11},{10,... | collective-permute-start | bytes 393224 | tf_op jit(solution)/shard_map/ppermute | solution.py:24
  52.4 2.5 %collective-permute-done.14.arrived_ref = bf16[64,1024]{1,0:T(8,128)(2,1)S(1)} collective-permute-done((bf16[64,1024]{1,0:T(8,128)(2,1)S(1)}, bf16[64,1024]{1,0:T(8,128)(2,1)S(1)}, u32[]{:S(2)}, u32[]{:S(2)}) %collective-permute-start.14) | collective-permute-done | bytes 131104 | tf_op jit(solution)/shard_map/ppermute | solution.py:20
  54.9 1.3 %shard_map.62.refs_7_ = bf16[64,1024]{1,0:T(8,128)(2,1)S(1)} custom-call(s32[1]{0:T(128)} %bitcast.level_ref, bf16[64,1024]{1,0:T(8,128)(2,1)S(1)} %collective-permute-done.14.arrived_ref, bf16[64,1024]{1,0:T(8,128)(2,1)S(1)} %get-tuple-element.31.ready_ref, bf16[1024,2048]{1,0:T(8,128)(2,1)S(1)} %get-tuple-element.27.joined_ref, f32[1,1024]{1,0:T(1,128)S(1)} %bitcast.17), custom_call_target="tpu_custom_call" | custom-call | flops 268435456 | bytes 4591616 | tf_op jit(solution)/shard_map/pallas_call | solution.py:285
  56.2 2.0 %collective-permute-start.17 = (bf16[64,1024]{1,0:T(8,128)(2,1)S(1)}, bf16[64,1024]{1,0:T(8,128)(2,1)S(1)}, u32[]{:S(2)}, u32[]{:S(2)}) collective-permute-start(bf16[64,1024]{1,0:T(8,128)(2,1)S(1)} %shard_map.62.refs_7_), channel_id=1, source_target_pairs={{0,2},{1,3},{2,0},{3,1},{4,6},{5,7},{6,4},{7,5},{8,10},{9,11},{10,... | collective-permute-start | bytes 393224 | tf_op jit(solution)/shard_map/ppermute | solution.py:24
  58.3 1.9 %shard_map.64.early_ref = f32[1024,1024]{1,0:T(8,128)S(1)} custom-call(s32[1]{0:T(128)} %bitcast.level_ref, bf16[1024,1024]{1,0:T(8,128)(2,1)S(1)} %shard_map.50.left_ref, bf16[64,1024]{1,0:T(8,128)(2,1)S(1)} %shard_map.53.refs_0_, bf16[64,1024]{1,0:T(8,128)(2,1)S(1)} %shard_map.54.refs_0_.refs_1_, bf16[64,1024]{1,0:T(8,128)(2,1)S(1)} %shard_map.55.refs_0_.refs_2_, ...), custom_call_target="tpu_custom_call" | custom-call | flops 1610612736 | bytes 8257536 | tf_op jit(solution)/shard_map/pallas_call | solution.py:285
  62.1 1.9 %collective-permute-done.18 = bf16[1,2,128,1024]{3,2,1,0:T(8,128)(2,1)S(1)} collective-permute-done((bf16[1,2,128,1024]{3,2,1,0:T(8,128)(2,1)S(1)}, bf16[1,2,128,1024]{3,2,1,0:T(8,128)(2,1)S(1)}, u32[]{:S(2)}, u32[]{:S(2)}) %collective-permute-start.18) | collective-permute-done | bytes 524320 | tf_op jit(solution)/shard_map/ppermute | solution.py:24
  64.2 2.8 %collective-permute-start.20 = (bf16[1,2,128,1024]{3,2,1,0:T(8,128)(2,1)S(1)}, bf16[1,2,128,1024]{3,2,1,0:T(8,128)(2,1)S(1)}, u32[]{:S(2)}, u32[]{:S(2)}) collective-permute-start(bf16[1,2,128,1024]{3,2,1,0:T(8,128)(2,1)S(1)} %add_convert_fusion), channel_id=1, source_target_pairs={{0,4},{1,5},{2,6},{3,7},{4,0},{5,1},{6,2},{7,3},{8,12},{9,13},{10,... | collective-permute-start | bytes 1572872 | tf_op jit(solution)/shard_map/ppermute | solution.py:20
  67.0 23.5 %collective-permute-done.20.refs_2_ = bf16[1,2,128,1024]{3,2,1,0:T(8,128)(2,1)S(1)} collective-permute-done((bf16[1,2,128,1024]{3,2,1,0:T(8,128)(2,1)S(1)}, bf16[1,2,128,1024]{3,2,1,0:T(8,128)(2,1)S(1)}, u32[]{:S(2)}, u32[]{:S(2)}) %collective-permute-start.20) | collective-permute-done | bytes 524320 | tf_op jit(solution)/shard_map/ppermute | solution.py:20
  (44 shorter events, 18.0 us)
Async XLA Ops:
  0.0 7.9 %copy-start.1 = (f32[1,1,1024]{2,1,0:T(1,128)S(1)}, f32[1,1,1024]{2,1,0:T(1,128)}, u32[]{:S(2)}) copy-start(f32[1,1,1024]{2,1,0:T(1,128)} %factor_ref.1) | copy-start | bytes 12292
  4.7 6.2 %collective-permute-start.4 = (bf16[64,1024]{1,0:T(8,128)(2,1)S(1)}, bf16[64,1024]{1,0:T(8,128)(2,1)S(1)}, u32[]{:S(2)}, u32[]{:S(2)}) collective-permute-start(bf16[64,1024]{1,0:T(8,128)(2,1)S(1)} %get-tuple-element.34.ready_ref), channel_id=1, source_target_pairs={{0,8},{8,16},{16,24},{24,0},{1,9},{9,17},{17,25},{25,1},{2,10},{10... | collective-permute-start | bytes 393224 | tf_op jit(solution)/shard_map/ppermute | solution.py:20
  6.3 21.7 %collective-permute-start.3 = (bf16[2,512,256]{2,1,0:T(8,128)(2,1)S(1)}, bf16[2,512,256]{2,1,0:T(8,128)(2,1)S(1)}, u32[]{:S(2)}, u32[]{:S(2)}) collective-permute-start(bf16[2,512,256]{2,1,0:T(8,128)(2,1)S(1)} %get-tuple-element.32), channel_id=1, source_target_pairs={{0,2},{1,3},{2,0},{3,1},{4,6},{5,7},{6,4},{7,5},{8,10},{9,11},{10,... | collective-permute-start | bytes 1572872 | tf_op jit(solution)/shard_map/ppermute | solution.py:24
  9.2 6.3 %collective-permute-start = (bf16[64,1024]{1,0:T(8,128)(2,1)S(1)}, bf16[64,1024]{1,0:T(8,128)(2,1)S(1)}, u32[]{:S(2)}, u32[]{:S(2)}) collective-permute-start(bf16[64,1024]{1,0:T(8,128)(2,1)S(1)} %get-tuple-element.29.ready_ref), channel_id=1, source_target_pairs={{0,8},{8,16},{16,24},{24,0},{1,9},{9,17},{17,25},{25,1},{2,10},{10... | collective-permute-start | bytes 393224 | tf_op jit(solution)/shard_map/ppermute | solution.py:20
  12.2 5.9 %collective-permute-start.5 = (bf16[64,1024]{1,0:T(8,128)(2,1)S(1)}, bf16[64,1024]{1,0:T(8,128)(2,1)S(1)}, u32[]{:S(2)}, u32[]{:S(2)}) collective-permute-start(bf16[64,1024]{1,0:T(8,128)(2,1)S(1)} %shard_map.51), channel_id=1, source_target_pairs={{0,8},{8,16},{16,24},{24,0},{1,9},{9,17},{17,25},{25,1},{2,10},{10... | collective-permute-start | bytes 393224 | tf_op jit(solution)/shard_map/ppermute | solution.py:20
  16.9 7.1 %collective-permute-start.1 = (bf16[64,1024]{1,0:T(8,128)(2,1)S(1)}, bf16[64,1024]{1,0:T(8,128)(2,1)S(1)}, u32[]{:S(2)}, u32[]{:S(2)}) collective-permute-start(bf16[64,1024]{1,0:T(8,128)(2,1)S(1)} %shard_map.48), channel_id=1, source_target_pairs={{0,8},{8,16},{16,24},{24,0},{1,9},{9,17},{17,25},{25,1},{2,10},{10... | collective-permute-start | bytes 393224 | tf_op jit(solution)/shard_map/ppermute | solution.py:20
  19.5 7.1 %collective-permute-start.6 = (bf16[64,1024]{1,0:T(8,128)(2,1)S(1)}, bf16[64,1024]{1,0:T(8,128)(2,1)S(1)}, u32[]{:S(2)}, u32[]{:S(2)}) collective-permute-start(bf16[64,1024]{1,0:T(8,128)(2,1)S(1)} %shard_map.52), channel_id=1, source_target_pairs={{0,8},{8,16},{16,24},{24,0},{1,9},{9,17},{17,25},{25,1},{2,10},{10... | collective-permute-start | bytes 393224 | tf_op jit(solution)/shard_map/ppermute | solution.py:20
  24.0 3.9 %copy-start = (bf16[1,1,2,1024,256]{4,3,2,1,0:T(8,128)(2,1)S(1)}, bf16[1,1,2,1024,256]{4,3,2,1,0:T(8,128)(2,1)}, u32[]{:S(2)}) copy-start(bf16[1,1,2,1024,256]{4,3,2,1,0:T(8,128)(2,1)} %upward_ref.1) | copy-start | bytes 3145732
  25.4 6.3 %collective-permute-start.2 = (bf16[64,1024]{1,0:T(8,128)(2,1)S(1)}, bf16[64,1024]{1,0:T(8,128)(2,1)S(1)}, u32[]{:S(2)}, u32[]{:S(2)}) collective-permute-start(bf16[64,1024]{1,0:T(8,128)(2,1)S(1)} %shard_map.49), channel_id=1, source_target_pairs={{0,8},{8,16},{16,24},{24,0},{1,9},{9,17},{17,25},{25,1},{2,10},{10... | collective-permute-start | bytes 393224 | tf_op jit(solution)/shard_map/ppermute | solution.py:20
  27.9 6.6 %collective-permute-start.7 = (bf16[64,1024]{1,0:T(8,128)(2,1)S(1)}, bf16[64,1024]{1,0:T(8,128)(2,1)S(1)}, u32[]{:S(2)}, u32[]{:S(2)}) collective-permute-start(bf16[64,1024]{1,0:T(8,128)(2,1)S(1)} %shard_map.53.refs_0_), channel_id=1, source_target_pairs={{0,8},{8,16},{16,24},{24,0},{1,9},{9,17},{17,25},{25,1},{2,10},{10... | collective-permute-start | bytes 393224 | tf_op jit(solution)/shard_map/ppermute | solution.py:20
  33.0 6.1 %collective-permute-start.10 = (bf16[64,1024]{1,0:T(8,128)(2,1)S(1)}, bf16[64,1024]{1,0:T(8,128)(2,1)S(1)}, u32[]{:S(2)}, u32[]{:S(2)}) collective-permute-start(bf16[64,1024]{1,0:T(8,128)(2,1)S(1)} %shard_map.56.refs_1_.refs_4_), channel_id=1, source_target_pairs={{0,8},{8,16},{16,24},{24,0},{1,9},{9,17},{17,25},{25,1},{2,10},{10... | collective-permute-start | bytes 393224 | tf_op jit(solution)/shard_map/ppermute | solution.py:20
  33.1 10.0 %collective-permute-start.13 = (bf16[128,1024]{1,0:T(8,128)(2,1)S(1)}, bf16[128,1024]{1,0:T(8,128)(2,1)S(1)}, u32[]{:S(2)}, u32[]{:S(2)}) collective-permute-start(bf16[128,1024]{1,0:T(8,128)(2,1)S(1)} %shard_map.60), channel_id=1, source_target_pairs={{0,2},{1,3},{2,0},{3,1},{4,6},{5,7},{6,4},{7,5},{8,10},{9,11},{10,... | collective-permute-start | bytes 786440 | tf_op jit(solution)/shard_map/ppermute | solution.py:24
  35.8 5.9 %collective-permute-start.8 = (bf16[64,1024]{1,0:T(8,128)(2,1)S(1)}, bf16[64,1024]{1,0:T(8,128)(2,1)S(1)}, u32[]{:S(2)}, u32[]{:S(2)}) collective-permute-start(bf16[64,1024]{1,0:T(8,128)(2,1)S(1)} %shard_map.54.refs_0_.refs_1_), channel_id=1, source_target_pairs={{0,8},{8,16},{16,24},{24,0},{1,9},{9,17},{17,25},{25,1},{2,10},{10... | collective-permute-start | bytes 393224 | tf_op jit(solution)/shard_map/ppermute | solution.py:20
  40.4 7.0 %collective-permute-start.12 = (bf16[64,1024]{1,0:T(8,128)(2,1)S(1)}, bf16[64,1024]{1,0:T(8,128)(2,1)S(1)}, u32[]{:S(2)}, u32[]{:S(2)}) collective-permute-start(bf16[64,1024]{1,0:T(8,128)(2,1)S(1)} %shard_map.57.refs_1_.refs_5_), channel_id=1, source_target_pairs={{0,8},{8,16},{16,24},{24,0},{1,9},{9,17},{17,25},{25,1},{2,10},{10... | collective-permute-start | bytes 393224 | tf_op jit(solution)/shard_map/ppermute | solution.py:20
  40.5 9.1 %collective-permute-start.11 = (bf16[128,1024]{1,0:T(8,128)(2,1)S(1)}, bf16[128,1024]{1,0:T(8,128)(2,1)S(1)}, u32[]{:S(2)}, u32[]{:S(2)}) collective-permute-start(bf16[128,1024]{1,0:T(8,128)(2,1)S(1)} %shard_map.58), channel_id=1, source_target_pairs={{0,2},{1,3},{2,0},{3,1},{4,6},{5,7},{6,4},{7,5},{8,10},{9,11},{10,... | collective-permute-start | bytes 786440 | tf_op jit(solution)/shard_map/ppermute | solution.py:24
  43.0 6.1 %collective-permute-start.9 = (bf16[64,1024]{1,0:T(8,128)(2,1)S(1)}, bf16[64,1024]{1,0:T(8,128)(2,1)S(1)}, u32[]{:S(2)}, u32[]{:S(2)}) collective-permute-start(bf16[64,1024]{1,0:T(8,128)(2,1)S(1)} %shard_map.55.refs_0_.refs_2_), channel_id=1, source_target_pairs={{0,8},{8,16},{16,24},{24,0},{1,9},{9,17},{17,25},{25,1},{2,10},{10... | collective-permute-start | bytes 393224 | tf_op jit(solution)/shard_map/ppermute | solution.py:20
  48.9 9.4 %collective-permute-start.15 = (bf16[128,1024]{1,0:T(8,128)(2,1)S(1)}, bf16[128,1024]{1,0:T(8,128)(2,1)S(1)}, u32[]{:S(2)}, u32[]{:S(2)}) collective-permute-start(bf16[128,1024]{1,0:T(8,128)(2,1)S(1)} %shard_map.63), channel_id=1, source_target_pairs={{0,2},{1,3},{2,0},{3,1},{4,6},{5,7},{6,4},{7,5},{8,10},{9,11},{10,... | collective-permute-start | bytes 786440 | tf_op jit(solution)/shard_map/ppermute | solution.py:24
  49.0 5.9 %collective-permute-start.14 = (bf16[64,1024]{1,0:T(8,128)(2,1)S(1)}, bf16[64,1024]{1,0:T(8,128)(2,1)S(1)}, u32[]{:S(2)}, u32[]{:S(2)}) collective-permute-start(bf16[64,1024]{1,0:T(8,128)(2,1)S(1)} %shard_map.61.refs_1_.refs_6_), channel_id=1, source_target_pairs={{0,8},{8,16},{16,24},{24,0},{1,9},{9,17},{17,25},{25,1},{2,10},{10... | collective-permute-start | bytes 393224 | tf_op jit(solution)/shard_map/ppermute | solution.py:20
  50.9 7.4 %collective-permute-start.16 = (bf16[64,1024]{1,0:T(8,128)(2,1)S(1)}, bf16[64,1024]{1,0:T(8,128)(2,1)S(1)}, u32[]{:S(2)}, u32[]{:S(2)}) collective-permute-start(bf16[64,1024]{1,0:T(8,128)(2,1)S(1)} %shard_map.59.refs_3_), channel_id=1, source_target_pairs={{0,2},{1,3},{2,0},{3,1},{4,6},{5,7},{6,4},{7,5},{8,10},{9,11},{10,... | collective-permute-start | bytes 393224 | tf_op jit(solution)/shard_map/ppermute | solution.py:24
  56.2 5.0 %collective-permute-start.17 = (bf16[64,1024]{1,0:T(8,128)(2,1)S(1)}, bf16[64,1024]{1,0:T(8,128)(2,1)S(1)}, u32[]{:S(2)}, u32[]{:S(2)}) collective-permute-start(bf16[64,1024]{1,0:T(8,128)(2,1)S(1)} %shard_map.62.refs_7_), channel_id=1, source_target_pairs={{0,2},{1,3},{2,0},{3,1},{4,6},{5,7},{6,4},{7,5},{8,10},{9,11},{10,... | collective-permute-start | bytes 393224 | tf_op jit(solution)/shard_map/ppermute | solution.py:24
  62.0 2.0 %collective-permute-start.18 = (bf16[1,2,128,1024]{3,2,1,0:T(8,128)(2,1)S(1)}, bf16[1,2,128,1024]{3,2,1,0:T(8,128)(2,1)S(1)}, u32[]{:S(2)}, u32[]{:S(2)}) collective-permute-start(bf16[1,2,128,1024]{3,2,1,0:T(8,128)(2,1)S(1)} %get-tuple-element.46), channel_id=1, source_target_pairs={{0,1},{1,0},{2,3},{3,2},{4,5},{5,4},{6,7},{7,6},{8,9},{9,8},{10,11... | collective-permute-start | bytes 1572872 | tf_op jit(solution)/shard_map/ppermute | solution.py:24
  64.2 26.3 %collective-permute-start.20 = (bf16[1,2,128,1024]{3,2,1,0:T(8,128)(2,1)S(1)}, bf16[1,2,128,1024]{3,2,1,0:T(8,128)(2,1)S(1)}, u32[]{:S(2)}, u32[]{:S(2)}) collective-permute-start(bf16[1,2,128,1024]{3,2,1,0:T(8,128)(2,1)S(1)} %add_convert_fusion), channel_id=1, source_target_pairs={{0,4},{1,5},{2,6},{3,7},{4,0},{5,1},{6,2},{7,3},{8,12},{9,13},{10,... | collective-permute-start | bytes 1572872 | tf_op jit(solution)/shard_map/ppermute | solution.py:20
  67.0 23.5 %collective-permute-start.19 = (bf16[1,2,128,1024]{3,2,1,0:T(8,128)(2,1)S(1)}, bf16[1,2,128,1024]{3,2,1,0:T(8,128)(2,1)S(1)}, u32[]{:S(2)}, u32[]{:S(2)}) collective-permute-start(bf16[1,2,128,1024]{3,2,1,0:T(8,128)(2,1)S(1)} %get-tuple-element.47), channel_id=1, source_target_pairs={{0,1},{1,0},{2,3},{3,2},{4,5},{5,4},{6,7},{7,6},{8,9},{9,8},{10,11... | collective-permute-start | bytes 1572872 | tf_op jit(solution)/shard_map/ppermute | solution.py:24

commit v18 on v17

--- a/solution.py
+++ b/solution.py
@@ -147,7 +147,6 @@
 def advance_kernel(level_ref, arrived_ref, ready_ref, joined_ref, factor_ref, out_ref, both):
     part = arrived_ref.shape[0] // 2
     width = arrived_ref.shape[1]
-    wide = width // 4
 
     @pl.when(level_ref[0] == 0)
     def _():
@@ -158,12 +157,10 @@
         both[:, :width] = arrived_ref[...]
         both[:part, width:] = -arrived_ref[part:]
         both[part:, width:] = arrived_ref[:part]
-        for n in range(4):
-            columns = slice(n * wide, (n + 1) * wide)
-            out = lax.dot_general(
-                joined_ref[columns], both[...], (((1,), (1,)), ((), ())), preferred_element_type=jnp.float32
-            )
-            out_ref[:, columns] = (out.T * factor_ref[:, columns]).astype(jnp.bfloat16)
+        out = lax.dot_general(
+            joined_ref[...], both[...], (((1,), (1,)), ((), ())), preferred_element_type=jnp.float32
+        )
+        out_ref[...] = (out.T * factor_ref[...]).astype(jnp.bfloat16)
 
 
 def advance(level, arrived, ready, joined, factor):

time: 92 us -> 91.6 us (level)
  transfers between devices with their start and end apart: 21 -> 21, of which waited for: 16 -> 16; matrix products, arithmetic and copies ran while one was open for 0% -> 0% of each run, Pallas kernels for 22% -> 21%
where the time goes in v18:
time: 91.6 us; the launch traced here: 91.4 us
  waiting for transfers between devices  52.5 us (57%)
  Pallas kernels  26.1 us (28%)
  starting transfers between devices  12.2 us (13%)
    ppermute x13, waiting for transfers between devices, ring(): lax.ppermute(block, axis, [(i, (i + distance) % size) for i in range(size)])  48.9 us
    pallas_call x18, Pallas kernels, whole_call(): pl.pallas_call(kernel, in_specs=[pl.BlockSpec(memory_space=pltpu.SMEM)] *...  19.5 us
    ppermute x13, starting transfers between devices, ring(): lax.ppermute(block, axis, [(i, (i + distance) % size) for i in range(size)])  6.3 us
    ppermute x8, starting transfers between devices, swapped(): lax.ppermute(block, axis, [(i, i ^ bit) for i in range(lax.axis_size(axis...  5.85 us
    pallas_call x1, Pallas kernels, first_advance(): pl.pallas_call(functools.partial(first_kernel, part), in_specs=[pl.BlockS...  4.72 us
    ppermute x8, waiting for transfers between devices, swapped(): lax.ppermute(block, axis, [(i, i ^ bit) for i in range(lax.axis_size(axis...  3.64 us
  transfers between devices with their start and end apart: 21, of which 16 were waited for; matrix products, arithmetic and copies ran while one was open for 0% of the time, Pallas kernels for 21%

profile of v18, /device:TPU:4, one launch (start us, length us, event | category | flops | bytes accessed | tf_op | source)
XLA Modules:
  0.0 91.4 jit_solution(7719713635574691033)
XLA Ops:
  0.0 4.7 %shard_map.46 = (bf16[64,1024]{1,0:T(8,128)(2,1)S(1)}, bf16[64,1024]{1,0:T(8,128)(2,1)S(1)}, bf16[64,1024]{1,0:T(8,128)(2,1)S(1)}, bf16[64,1024]{1,0:T(8,128)(2,...) custom-call(s32[1]{0:T(128)} %bitcast.level_ref, ...), custom_call_target="tpu_custom_call" | custom-call | flops 1073741824 | bytes 6291456 | tf_op jit(solution)/shard_map/pallas_call | solution.py:107
  4.7 1.5 %collective-permute-start.4 = (bf16[64,1024]{1,0:T(8,128)(2,1)S(1)}, bf16[64,1024]{1,0:T(8,128)(2,1)S(1)}, u32[]{:S(2)}, u32[]{:S(2)}) collective-permute-start(bf16[64,1024]{1,0:T(8,128)(2,1)S(1)} %get-tuple-element.34.ready_ref), channel_id=1, source_target_pairs={{0,8},{8,16},{16,24},{24,0},{1,9},{9,17},{17,25},{25,1},{2,10},{10... | collective-permute-start | bytes 393224 | tf_op jit(solution)/shard_map/ppermute | solution.py:20
  6.3 1.6 %collective-permute-start.3 = (bf16[2,512,256]{2,1,0:T(8,128)(2,1)S(1)}, bf16[2,512,256]{2,1,0:T(8,128)(2,1)S(1)}, u32[]{:S(2)}, u32[]{:S(2)}) collective-permute-start(bf16[2,512,256]{2,1,0:T(8,128)(2,1)S(1)} %get-tuple-element.32), channel_id=1, source_target_pairs={{0,2},{1,3},{2,0},{3,1},{4,6},{5,7},{6,4},{7,5},{8,10},{9,11},{10,... | collective-permute-start | bytes 1572872 | tf_op jit(solution)/shard_map/ppermute | solution.py:24
  7.9 1.4 %shard_map.47 = (bf16[64,1024]{1,0:T(8,128)(2,1)S(1)}, bf16[64,1024]{1,0:T(8,128)(2,1)S(1)}, bf16[64,1024]{1,0:T(8,128)(2,1)S(1)}, bf16[64,1024]{1,0:T(8,128)(2,1)S(1)}) custom-call(bf16[1024,2048]{1,0:T(8,128)(2,1)S(1)} %get-tuple-element.27.joined_ref, bf16[1024,256]{1,0:T(8,128)(2,1)S(1)} %get-tuple-element.28.right_ref, f32[1,1024]{1,0:T(1,128)S(1)} %bitcast.5), custom_call_target="tpu_custom_call" | custom-call | flops 1073741824 | bytes 5246976 | tf_op jit(solution)/shard_map/pallas_call | solution.py:282
  12.9 2.7 %collective-permute-done.arrived_ref = bf16[64,1024]{1,0:T(8,128)(2,1)S(1)} collective-permute-done((bf16[64,1024]{1,0:T(8,128)(2,1)S(1)}, bf16[64,1024]{1,0:T(8,128)(2,1)S(1)}, u32[]{:S(2)}, u32[]{:S(2)}) %collective-permute-start) | collective-permute-done | bytes 131104 | tf_op jit(solution)/shard_map/ppermute | solution.py:20
  15.6 1.3 %shard_map.48 = bf16[64,1024]{1,0:T(8,128)(2,1)S(1)} custom-call(s32[1]{0:T(128)} %bitcast.level_ref, bf16[64,1024]{1,0:T(8,128)(2,1)S(1)} %collective-permute-done.arrived_ref, bf16[64,1024]{1,0:T(8,128)(2,1)S(1)} %get-tuple-element.30.ready_ref, bf16[1024,2048]{1,0:T(8,128)(2,1)S(1)} %get-tuple-element.27.joined_ref, f32[1,1024]{1,0:T(1,128)S(1)} %bitcast.7), custom_call_target="tpu_custom_call" | custom-call | flops 268435456 | bytes 4591616 | tf_op jit(solution)/shard_map/pallas_call | solution.py:282
  18.1 1.3 %shard_map.52 = bf16[64,1024]{1,0:T(8,128)(2,1)S(1)} custom-call(s32[1]{0:T(128)} %bitcast.level_ref, bf16[64,1024]{1,0:T(8,128)(2,1)S(1)} %collective-permute-done.5.arrived_ref, bf16[64,1024]{1,0:T(8,128)(2,1)S(1)} %get-tuple-element.36.ready_ref, bf16[1024,2048]{1,0:T(8,128)(2,1)S(1)} %get-tuple-element.27.joined_ref, f32[1,1024]{1,0:T(1,128)S(1)} %bitcast.8), custom_call_target="tpu_custom_call" | custom-call | flops 268435456 | bytes 4591616 | tf_op jit(solution)/shard_map/pallas_call | solution.py:282
  19.8 4.2 %collective-permute-done.1.arrived_ref = bf16[64,1024]{1,0:T(8,128)(2,1)S(1)} collective-permute-done((bf16[64,1024]{1,0:T(8,128)(2,1)S(1)}, bf16[64,1024]{1,0:T(8,128)(2,1)S(1)}, u32[]{:S(2)}, u32[]{:S(2)}) %collective-permute-start.1) | collective-permute-done | bytes 131104 | tf_op jit(solution)/shard_map/ppermute | solution.py:20
  24.0 1.3 %shard_map.49 = bf16[64,1024]{1,0:T(8,128)(2,1)S(1)} custom-call(s32[1]{0:T(128)} %bitcast.level_ref, bf16[64,1024]{1,0:T(8,128)(2,1)S(1)} %collective-permute-done.1.arrived_ref, bf16[64,1024]{1,0:T(8,128)(2,1)S(1)} %get-tuple-element.31.ready_ref, bf16[1024,2048]{1,0:T(8,128)(2,1)S(1)} %get-tuple-element.27.joined_ref, f32[1,1024]{1,0:T(1,128)S(1)} %bitcast.9), custom_call_target="tpu_custom_call" | custom-call | flops 268435456 | bytes 4591616 | tf_op jit(solution)/shard_map/pallas_call | solution.py:282
  28.7 2.9 %collective-permute-done.2.arrived_ref = bf16[64,1024]{1,0:T(8,128)(2,1)S(1)} collective-permute-done((bf16[64,1024]{1,0:T(8,128)(2,1)S(1)}, bf16[64,1024]{1,0:T(8,128)(2,1)S(1)}, u32[]{:S(2)}, u32[]{:S(2)}) %collective-permute-start.2) | collective-permute-done | bytes 131104 | tf_op jit(solution)/shard_map/ppermute | solution.py:20
  31.6 1.3 %shard_map.56.refs_1_.refs_4_ = bf16[64,1024]{1,0:T(8,128)(2,1)S(1)} custom-call(s32[1]{0:T(128)} %bitcast.level_ref, bf16[64,1024]{1,0:T(8,128)(2,1)S(1)} %collective-permute-done.2.arrived_ref, bf16[64,1024]{1,0:T(8,128)(2,1)S(1)} %get-tuple-element.39.ready_ref, bf16[1024,2048]{1,0:T(8,128)(2,1)S(1)} %get-tuple-element.27.joined_ref, f32[1,1024]{1,0:T(1,128)S(1)} %bitcast.11), custom_call_target="tpu_custom_call" | custom-call | flops 268435456 | bytes 4591616 | tf_op jit(solution)/shard_map/pallas_call | solution.py:282
  34.4 1.3 %shard_map.54.refs_0_.refs_1_ = bf16[64,1024]{1,0:T(8,128)(2,1)S(1)} custom-call(s32[1]{0:T(128)} %bitcast.level_ref, bf16[64,1024]{1,0:T(8,128)(2,1)S(1)} %collective-permute-done.7.arrived_ref, bf16[64,1024]{1,0:T(8,128)(2,1)S(1)} %get-tuple-element.34.ready_ref, bf16[1024,2048]{1,0:T(8,128)(2,1)S(1)} %get-tuple-element.27.joined_ref, f32[1,1024]{1,0:T(1,128)S(1)} %bitcast.12), custom_call_target="tpu_custom_call" | custom-call | flops 268435456 | bytes 4591616 | tf_op jit(solution)/shard_map/pallas_call | solution.py:282
  35.8 3.3 %collective-permute-done.10.arrived_ref = bf16[64,1024]{1,0:T(8,128)(2,1)S(1)} collective-permute-done((bf16[64,1024]{1,0:T(8,128)(2,1)S(1)}, bf16[64,1024]{1,0:T(8,128)(2,1)S(1)}, u32[]{:S(2)}, u32[]{:S(2)}) %collective-permute-start.10) | collective-permute-done | bytes 131104 | tf_op jit(solution)/shard_map/ppermute | solution.py:20
  39.0 1.3 %shard_map.57.refs_1_.refs_5_ = bf16[64,1024]{1,0:T(8,128)(2,1)S(1)} custom-call(s32[1]{0:T(128)} %bitcast.level_ref, bf16[64,1024]{1,0:T(8,128)(2,1)S(1)} %collective-permute-done.10.arrived_ref, bf16[64,1024]{1,0:T(8,128)(2,1)S(1)} %get-tuple-element.29.ready_ref, bf16[1024,2048]{1,0:T(8,128)(2,1)S(1)} %get-tuple-element.27.joined_ref, f32[1,1024]{1,0:T(1,128)S(1)} %bitcast.13), custom_call_target="tpu_custom_call" | custom-call | flops 268435456 | bytes 4591616 | tf_op jit(solution)/shard_map/pallas_call | solution.py:282
  41.6 1.3 %shard_map.55.refs_0_.refs_2_ = bf16[64,1024]{1,0:T(8,128)(2,1)S(1)} custom-call(s32[1]{0:T(128)} %bitcast.level_ref, bf16[64,1024]{1,0:T(8,128)(2,1)S(1)} %collective-permute-done.8.arrived_ref, bf16[64,1024]{1,0:T(8,128)(2,1)S(1)} %get-tuple-element.35.ready_ref, bf16[1024,2048]{1,0:T(8,128)(2,1)S(1)} %get-tuple-element.27.joined_ref, f32[1,1024]{1,0:T(1,128)S(1)} %bitcast.14), custom_call_target="tpu_custom_call" | custom-call | flops 268435456 | bytes 4591616 | tf_op jit(solution)/shard_map/pallas_call | solution.py:282
  43.0 4.4 %collective-permute-done.12.arrived_ref = bf16[64,1024]{1,0:T(8,128)(2,1)S(1)} collective-permute-done((bf16[64,1024]{1,0:T(8,128)(2,1)S(1)}, bf16[64,1024]{1,0:T(8,128)(2,1)S(1)}, u32[]{:S(2)}, u32[]{:S(2)}) %collective-permute-start.12) | collective-permute-done | bytes 131104 | tf_op jit(solution)/shard_map/ppermute | solution.py:20
  49.7 1.3 %shard_map.59.refs_3_ = bf16[64,1024]{1,0:T(8,128)(2,1)S(1)} custom-call(s32[1]{0:T(128)} %bitcast.level_ref, bf16[64,1024]{1,0:T(8,128)(2,1)S(1)} %collective-permute-done.9.arrived_ref, bf16[64,1024]{1,0:T(8,128)(2,1)S(1)} %get-tuple-element.36.ready_ref, bf16[1024,2048]{1,0:T(8,128)(2,1)S(1)} %get-tuple-element.27.joined_ref, f32[1,1024]{1,0:T(1,128)S(1)} %bitcast.16), custom_call_target="tpu_custom_call" | custom-call | flops 268435456 | bytes 4591616 | tf_op jit(solution)/shard_map/pallas_call | solution.py:282
  52.2 2.5 %collective-permute-done.14.arrived_ref = bf16[64,1024]{1,0:T(8,128)(2,1)S(1)} collective-permute-done((bf16[64,1024]{1,0:T(8,128)(2,1)S(1)}, bf16[64,1024]{1,0:T(8,128)(2,1)S(1)}, u32[]{:S(2)}, u32[]{:S(2)}) %collective-permute-start.14) | collective-permute-done | bytes 131104 | tf_op jit(solution)/shard_map/ppermute | solution.py:20
  54.7 1.3 %shard_map.62.refs_7_ = bf16[64,1024]{1,0:T(8,128)(2,1)S(1)} custom-call(s32[1]{0:T(128)} %bitcast.level_ref, bf16[64,1024]{1,0:T(8,128)(2,1)S(1)} %collective-permute-done.14.arrived_ref, bf16[64,1024]{1,0:T(8,128)(2,1)S(1)} %get-tuple-element.31.ready_ref, bf16[1024,2048]{1,0:T(8,128)(2,1)S(1)} %get-tuple-element.27.joined_ref, f32[1,1024]{1,0:T(1,128)S(1)} %bitcast.17), custom_call_target="tpu_custom_call" | custom-call | flops 268435456 | bytes 4591616 | tf_op jit(solution)/shard_map/pallas_call | solution.py:282
  56.0 2.0 %collective-permute-start.17 = (bf16[64,1024]{1,0:T(8,128)(2,1)S(1)}, bf16[64,1024]{1,0:T(8,128)(2,1)S(1)}, u32[]{:S(2)}, u32[]{:S(2)}) collective-permute-start(bf16[64,1024]{1,0:T(8,128)(2,1)S(1)} %shard_map.62.refs_7_), channel_id=1, source_target_pairs={{0,2},{1,3},{2,0},{3,1},{4,6},{5,7},{6,4},{7,5},{8,10},{9,11},{10,... | collective-permute-start | bytes 393224 | tf_op jit(solution)/shard_map/ppermute | solution.py:24
  58.0 1.9 %shard_map.64.early_ref = f32[1024,1024]{1,0:T(8,128)S(1)} custom-call(s32[1]{0:T(128)} %bitcast.level_ref, bf16[1024,1024]{1,0:T(8,128)(2,1)S(1)} %shard_map.50.left_ref, bf16[64,1024]{1,0:T(8,128)(2,1)S(1)} %shard_map.53.refs_0_, bf16[64,1024]{1,0:T(8,128)(2,1)S(1)} %shard_map.54.refs_0_.refs_1_, bf16[64,1024]{1,0:T(8,128)(2,1)S(1)} %shard_map.55.refs_0_.refs_2_, ...), custom_call_target="tpu_custom_call" | custom-call | flops 1610612736 | bytes 8257536 | tf_op jit(solution)/shard_map/pallas_call | solution.py:282
  61.9 1.9 %collective-permute-done.18 = bf16[1,2,128,1024]{3,2,1,0:T(8,128)(2,1)S(1)} collective-permute-done((bf16[1,2,128,1024]{3,2,1,0:T(8,128)(2,1)S(1)}, bf16[1,2,128,1024]{3,2,1,0:T(8,128)(2,1)S(1)}, u32[]{:S(2)}, u32[]{:S(2)}) %collective-permute-start.18) | collective-permute-done | bytes 524320 | tf_op jit(solution)/shard_map/ppermute | solution.py:24
  64.0 2.7 %collective-permute-start.20 = (bf16[1,2,128,1024]{3,2,1,0:T(8,128)(2,1)S(1)}, bf16[1,2,128,1024]{3,2,1,0:T(8,128)(2,1)S(1)}, u32[]{:S(2)}, u32[]{:S(2)}) collective-permute-start(bf16[1,2,128,1024]{3,2,1,0:T(8,128)(2,1)S(1)} %add_convert_fusion), channel_id=1, source_target_pairs={{0,4},{1,5},{2,6},{3,7},{4,0},{5,1},{6,2},{7,3},{8,12},{9,13},{10,... | collective-permute-start | bytes 1572872 | tf_op jit(solution)/shard_map/ppermute | solution.py:20
  66.7 23.5 %collective-permute-done.20.refs_2_ = bf16[1,2,128,1024]{3,2,1,0:T(8,128)(2,1)S(1)} collective-permute-done((bf16[1,2,128,1024]{3,2,1,0:T(8,128)(2,1)S(1)}, bf16[1,2,128,1024]{3,2,1,0:T(8,128)(2,1)S(1)}, u32[]{:S(2)}, u32[]{:S(2)}) %collective-permute-start.20) | collective-permute-done | bytes 524320 | tf_op jit(solution)/shard_map/ppermute | solution.py:20
  (44 shorter events, 18.3 us)
Async XLA Ops:
  0.0 7.9 %copy-start.1 = (f32[1,1,1024]{2,1,0:T(1,128)S(1)}, f32[1,1,1024]{2,1,0:T(1,128)}, u32[]{:S(2)}) copy-start(f32[1,1,1024]{2,1,0:T(1,128)} %factor_ref.1) | copy-start | bytes 12292
  4.7 6.2 %collective-permute-start.4 = (bf16[64,1024]{1,0:T(8,128)(2,1)S(1)}, bf16[64,1024]{1,0:T(8,128)(2,1)S(1)}, u32[]{:S(2)}, u32[]{:S(2)}) collective-permute-start(bf16[64,1024]{1,0:T(8,128)(2,1)S(1)} %get-tuple-element.34.ready_ref), channel_id=1, source_target_pairs={{0,8},{8,16},{16,24},{24,0},{1,9},{9,17},{17,25},{25,1},{2,10},{10... | collective-permute-start | bytes 393224 | tf_op jit(solution)/shard_map/ppermute | solution.py:20
  6.3 21.7 %collective-permute-start.3 = (bf16[2,512,256]{2,1,0:T(8,128)(2,1)S(1)}, bf16[2,512,256]{2,1,0:T(8,128)(2,1)S(1)}, u32[]{:S(2)}, u32[]{:S(2)}) collective-permute-start(bf16[2,512,256]{2,1,0:T(8,128)(2,1)S(1)} %get-tuple-element.32), channel_id=1, source_target_pairs={{0,2},{1,3},{2,0},{3,1},{4,6},{5,7},{6,4},{7,5},{8,10},{9,11},{10,... | collective-permute-start | bytes 1572872 | tf_op jit(solution)/shard_map/ppermute | solution.py:24
  9.2 6.4 %collective-permute-start = (bf16[64,1024]{1,0:T(8,128)(2,1)S(1)}, bf16[64,1024]{1,0:T(8,128)(2,1)S(1)}, u32[]{:S(2)}, u32[]{:S(2)}) collective-permute-start(bf16[64,1024]{1,0:T(8,128)(2,1)S(1)} %get-tuple-element.29.ready_ref), channel_id=1, source_target_pairs={{0,8},{8,16},{16,24},{24,0},{1,9},{9,17},{17,25},{25,1},{2,10},{10... | collective-permute-start | bytes 393224 | tf_op jit(solution)/shard_map/ppermute | solution.py:20
  12.2 5.9 %collective-permute-start.5 = (bf16[64,1024]{1,0:T(8,128)(2,1)S(1)}, bf16[64,1024]{1,0:T(8,128)(2,1)S(1)}, u32[]{:S(2)}, u32[]{:S(2)}) collective-permute-start(bf16[64,1024]{1,0:T(8,128)(2,1)S(1)} %shard_map.51), channel_id=1, source_target_pairs={{0,8},{8,16},{16,24},{24,0},{1,9},{9,17},{17,25},{25,1},{2,10},{10... | collective-permute-start | bytes 393224 | tf_op jit(solution)/shard_map/ppermute | solution.py:20
  16.9 7.1 %collective-permute-start.1 = (bf16[64,1024]{1,0:T(8,128)(2,1)S(1)}, bf16[64,1024]{1,0:T(8,128)(2,1)S(1)}, u32[]{:S(2)}, u32[]{:S(2)}) collective-permute-start(bf16[64,1024]{1,0:T(8,128)(2,1)S(1)} %shard_map.48), channel_id=1, source_target_pairs={{0,8},{8,16},{16,24},{24,0},{1,9},{9,17},{17,25},{25,1},{2,10},{10... | collective-permute-start | bytes 393224 | tf_op jit(solution)/shard_map/ppermute | solution.py:20
  19.4 7.2 %collective-permute-start.6 = (bf16[64,1024]{1,0:T(8,128)(2,1)S(1)}, bf16[64,1024]{1,0:T(8,128)(2,1)S(1)}, u32[]{:S(2)}, u32[]{:S(2)}) collective-permute-start(bf16[64,1024]{1,0:T(8,128)(2,1)S(1)} %shard_map.52), channel_id=1, source_target_pairs={{0,8},{8,16},{16,24},{24,0},{1,9},{9,17},{17,25},{25,1},{2,10},{10... | collective-permute-start | bytes 393224 | tf_op jit(solution)/shard_map/ppermute | solution.py:20
  24.0 3.9 %copy-start = (bf16[1,1,2,1024,256]{4,3,2,1,0:T(8,128)(2,1)S(1)}, bf16[1,1,2,1024,256]{4,3,2,1,0:T(8,128)(2,1)}, u32[]{:S(2)}) copy-start(bf16[1,1,2,1024,256]{4,3,2,1,0:T(8,128)(2,1)} %upward_ref.1) | copy-start | bytes 3145732
  25.3 6.3 %collective-permute-start.2 = (bf16[64,1024]{1,0:T(8,128)(2,1)S(1)}, bf16[64,1024]{1,0:T(8,128)(2,1)S(1)}, u32[]{:S(2)}, u32[]{:S(2)}) collective-permute-start(bf16[64,1024]{1,0:T(8,128)(2,1)S(1)} %shard_map.49), channel_id=1, source_target_pairs={{0,8},{8,16},{16,24},{24,0},{1,9},{9,17},{17,25},{25,1},{2,10},{10... | collective-permute-start | bytes 393224 | tf_op jit(solution)/shard_map/ppermute | solution.py:20
  27.9 6.5 %collective-permute-start.7 = (bf16[64,1024]{1,0:T(8,128)(2,1)S(1)}, bf16[64,1024]{1,0:T(8,128)(2,1)S(1)}, u32[]{:S(2)}, u32[]{:S(2)}) collective-permute-start(bf16[64,1024]{1,0:T(8,128)(2,1)S(1)} %shard_map.53.refs_0_), channel_id=1, source_target_pairs={{0,8},{8,16},{16,24},{24,0},{1,9},{9,17},{17,25},{25,1},{2,10},{10... | collective-permute-start | bytes 393224 | tf_op jit(solution)/shard_map/ppermute | solution.py:20
  32.9 6.1 %collective-permute-start.10 = (bf16[64,1024]{1,0:T(8,128)(2,1)S(1)}, bf16[64,1024]{1,0:T(8,128)(2,1)S(1)}, u32[]{:S(2)}, u32[]{:S(2)}) collective-permute-start(bf16[64,1024]{1,0:T(8,128)(2,1)S(1)} %shard_map.56.refs_1_.refs_4_), channel_id=1, source_target_pairs={{0,8},{8,16},{16,24},{24,0},{1,9},{9,17},{17,25},{25,1},{2,10},{10... | collective-permute-start | bytes 393224 | tf_op jit(solution)/shard_map/ppermute | solution.py:20
  33.0 10.0 %collective-permute-start.13 = (bf16[128,1024]{1,0:T(8,128)(2,1)S(1)}, bf16[128,1024]{1,0:T(8,128)(2,1)S(1)}, u32[]{:S(2)}, u32[]{:S(2)}) collective-permute-start(bf16[128,1024]{1,0:T(8,128)(2,1)S(1)} %shard_map.60), channel_id=1, source_target_pairs={{0,2},{1,3},{2,0},{3,1},{4,6},{5,7},{6,4},{7,5},{8,10},{9,11},{10,... | collective-permute-start | bytes 786440 | tf_op jit(solution)/shard_map/ppermute | solution.py:24
  35.7 5.9 %collective-permute-start.8 = (bf16[64,1024]{1,0:T(8,128)(2,1)S(1)}, bf16[64,1024]{1,0:T(8,128)(2,1)S(1)}, u32[]{:S(2)}, u32[]{:S(2)}) collective-permute-start(bf16[64,1024]{1,0:T(8,128)(2,1)S(1)} %shard_map.54.refs_0_.refs_1_), channel_id=1, source_target_pairs={{0,8},{8,16},{16,24},{24,0},{1,9},{9,17},{17,25},{25,1},{2,10},{10... | collective-permute-start | bytes 393224 | tf_op jit(solution)/shard_map/ppermute | solution.py:20
  40.3 7.1 %collective-permute-start.12 = (bf16[64,1024]{1,0:T(8,128)(2,1)S(1)}, bf16[64,1024]{1,0:T(8,128)(2,1)S(1)}, u32[]{:S(2)}, u32[]{:S(2)}) collective-permute-start(bf16[64,1024]{1,0:T(8,128)(2,1)S(1)} %shard_map.57.refs_1_.refs_5_), channel_id=1, source_target_pairs={{0,8},{8,16},{16,24},{24,0},{1,9},{9,17},{17,25},{25,1},{2,10},{10... | collective-permute-start | bytes 393224 | tf_op jit(solution)/shard_map/ppermute | solution.py:20
  40.4 9.2 %collective-permute-start.11 = (bf16[128,1024]{1,0:T(8,128)(2,1)S(1)}, bf16[128,1024]{1,0:T(8,128)(2,1)S(1)}, u32[]{:S(2)}, u32[]{:S(2)}) collective-permute-start(bf16[128,1024]{1,0:T(8,128)(2,1)S(1)} %shard_map.58), channel_id=1, source_target_pairs={{0,2},{1,3},{2,0},{3,1},{4,6},{5,7},{6,4},{7,5},{8,10},{9,11},{10,... | collective-permute-start | bytes 786440 | tf_op jit(solution)/shard_map/ppermute | solution.py:24
  42.9 6.1 %collective-permute-start.9 = (bf16[64,1024]{1,0:T(8,128)(2,1)S(1)}, bf16[64,1024]{1,0:T(8,128)(2,1)S(1)}, u32[]{:S(2)}, u32[]{:S(2)}) collective-permute-start(bf16[64,1024]{1,0:T(8,128)(2,1)S(1)} %shard_map.55.refs_0_.refs_2_), channel_id=1, source_target_pairs={{0,8},{8,16},{16,24},{24,0},{1,9},{9,17},{17,25},{25,1},{2,10},{10... | collective-permute-start | bytes 393224 | tf_op jit(solution)/shard_map/ppermute | solution.py:20
  48.7 9.3 %collective-permute-start.15 = (bf16[128,1024]{1,0:T(8,128)(2,1)S(1)}, bf16[128,1024]{1,0:T(8,128)(2,1)S(1)}, u32[]{:S(2)}, u32[]{:S(2)}) collective-permute-start(bf16[128,1024]{1,0:T(8,128)(2,1)S(1)} %shard_map.63), channel_id=1, source_target_pairs={{0,2},{1,3},{2,0},{3,1},{4,6},{5,7},{6,4},{7,5},{8,10},{9,11},{10,... | collective-permute-start | bytes 786440 | tf_op jit(solution)/shard_map/ppermute | solution.py:24
  48.8 5.9 %collective-permute-start.14 = (bf16[64,1024]{1,0:T(8,128)(2,1)S(1)}, bf16[64,1024]{1,0:T(8,128)(2,1)S(1)}, u32[]{:S(2)}, u32[]{:S(2)}) collective-permute-start(bf16[64,1024]{1,0:T(8,128)(2,1)S(1)} %shard_map.61.refs_1_.refs_6_), channel_id=1, source_target_pairs={{0,8},{8,16},{16,24},{24,0},{1,9},{9,17},{17,25},{25,1},{2,10},{10... | collective-permute-start | bytes 393224 | tf_op jit(solution)/shard_map/ppermute | solution.py:20
  50.9 7.1 %collective-permute-start.16 = (bf16[64,1024]{1,0:T(8,128)(2,1)S(1)}, bf16[64,1024]{1,0:T(8,128)(2,1)S(1)}, u32[]{:S(2)}, u32[]{:S(2)}) collective-permute-start(bf16[64,1024]{1,0:T(8,128)(2,1)S(1)} %shard_map.59.refs_3_), channel_id=1, source_target_pairs={{0,2},{1,3},{2,0},{3,1},{4,6},{5,7},{6,4},{7,5},{8,10},{9,11},{10,... | collective-permute-start | bytes 393224 | tf_op jit(solution)/shard_map/ppermute | solution.py:24
  56.0 5.0 %collective-permute-start.17 = (bf16[64,1024]{1,0:T(8,128)(2,1)S(1)}, bf16[64,1024]{1,0:T(8,128)(2,1)S(1)}, u32[]{:S(2)}, u32[]{:S(2)}) collective-permute-start(bf16[64,1024]{1,0:T(8,128)(2,1)S(1)} %shard_map.62.refs_7_), channel_id=1, source_target_pairs={{0,2},{1,3},{2,0},{3,1},{4,6},{5,7},{6,4},{7,5},{8,10},{9,11},{10,... | collective-permute-start | bytes 393224 | tf_op jit(solution)/shard_map/ppermute | solution.py:24
  61.8 2.0 %collective-permute-start.18 = (bf16[1,2,128,1024]{3,2,1,0:T(8,128)(2,1)S(1)}, bf16[1,2,128,1024]{3,2,1,0:T(8,128)(2,1)S(1)}, u32[]{:S(2)}, u32[]{:S(2)}) collective-permute-start(bf16[1,2,128,1024]{3,2,1,0:T(8,128)(2,1)S(1)} %get-tuple-element.46), channel_id=1, source_target_pairs={{0,1},{1,0},{2,3},{3,2},{4,5},{5,4},{6,7},{7,6},{8,9},{9,8},{10,11... | collective-permute-start | bytes 1572872 | tf_op jit(solution)/shard_map/ppermute | solution.py:24
  64.0 26.2 %collective-permute-start.20 = (bf16[1,2,128,1024]{3,2,1,0:T(8,128)(2,1)S(1)}, bf16[1,2,128,1024]{3,2,1,0:T(8,128)(2,1)S(1)}, u32[]{:S(2)}, u32[]{:S(2)}) collective-permute-start(bf16[1,2,128,1024]{3,2,1,0:T(8,128)(2,1)S(1)} %add_convert_fusion), channel_id=1, source_target_pairs={{0,4},{1,5},{2,6},{3,7},{4,0},{5,1},{6,2},{7,3},{8,12},{9,13},{10,... | collective-permute-start | bytes 1572872 | tf_op jit(solution)/shard_map/ppermute | solution.py:20
  66.7 23.5 %collective-permute-start.19 = (bf16[1,2,128,1024]{3,2,1,0:T(8,128)(2,1)S(1)}, bf16[1,2,128,1024]{3,2,1,0:T(8,128)(2,1)S(1)}, u32[]{:S(2)}, u32[]{:S(2)}) collective-permute-start(bf16[1,2,128,1024]{3,2,1,0:T(8,128)(2,1)S(1)} %get-tuple-element.47), channel_id=1, source_target_pairs={{0,1},{1,0},{2,3},{3,2},{4,5},{5,4},{6,7},{7,6},{8,9},{9,8},{10,11... | collective-permute-start | bytes 1572872 | tf_op jit(solution)/shard_map/ppermute | solution.py:24

commit v19 on v18

--- a/solution.py
+++ b/solution.py
@@ -79,18 +79,15 @@
                 upward_ref.at[0, 0, :, pl.ds(row, tall)], asked_ref.at[:, pl.ds(k * tall, tall)], asked_sems.at[k]
             )
         )
-    for copy in begin:
-        copy.start()
-    for n in range(blocks):
-        for copy in copies(n):
-            copy.start()
-    for copy in rest:
+    for copy in begin + copies(0) + copies(1):
         copy.start()
     for copy in begin:
         copy.wait()
     for n in range(blocks):
         for copy in copies(n):
             copy.wait()
+        for copy in copies(n + 2) if n + 2 < blocks else rest if n + 2 == blocks else []:
+            copy.start()
         columns = slice(n * wide, (n + 1) * wide)
         real, imag = joined_ref[columns, :width], joined_ref[columns, width:]
         start_panels(part, real, imag, right[...], factor[:, columns], outs, columns)

time: 91.6 us -> 91.1 us (level)
  transfers between devices with their start and end apart: 21 -> 21, of which waited for: 16 -> 16; matrix products, arithmetic and copies ran while one was open for 0% -> 0% of each run, Pallas kernels for 21% -> 22%
where the time goes in v19:
time: 91.1 us; the launch traced here: 90.8 us
  waiting for transfers between devices  52.7 us (58%)
  Pallas kernels  25.5 us (28%)
  starting transfers between devices  12.1 us (13%)
    ppermute x13, waiting for transfers between devices, ring(): lax.ppermute(block, axis, [(i, (i + distance) % size) for i in range(size)])  49 us
    pallas_call x18, Pallas kernels, whole_call(): pl.pallas_call(kernel, in_specs=[pl.BlockSpec(memory_space=pltpu.SMEM)] *...  19.5 us
    ppermute x13, starting transfers between devices, ring(): lax.ppermute(block, axis, [(i, (i + distance) % size) for i in range(size)])  6.23 us
    ppermute x8, starting transfers between devices, swapped(): lax.ppermute(block, axis, [(i, i ^ bit) for i in range(lax.axis_size(axis...  5.82 us
    pallas_call x1, Pallas kernels, first_advance(): pl.pallas_call(functools.partial(first_kernel, part), in_specs=[pl.BlockS...  4.14 us
    ppermute x8, waiting for transfers between devices, swapped(): lax.ppermute(block, axis, [(i, i ^ bit) for i in range(lax.axis_size(axis...  3.63 us
  transfers between devices with their start and end apart: 21, of which 16 were waited for; matrix products, arithmetic and copies ran while one was open for 0% of the time, Pallas kernels for 22%

profile of v19, /device:TPU:4, one launch (start us, length us, event | category | flops | bytes accessed | tf_op | source)
XLA Modules:
  0.0 90.8 jit_solution(5621428899696172113)
XLA Ops:
  0.0 4.1 %shard_map.46 = (bf16[64,1024]{1,0:T(8,128)(2,1)S(1)}, bf16[64,1024]{1,0:T(8,128)(2,1)S(1)}, bf16[64,1024]{1,0:T(8,128)(2,1)S(1)}, bf16[64,1024]{1,0:T(8,128)(2,...) custom-call(s32[1]{0:T(128)} %bitcast.level_ref, ...), custom_call_target="tpu_custom_call" | custom-call | flops 1073741824 | bytes 6291456 | tf_op jit(solution)/shard_map/pallas_call | solution.py:104
  4.2 1.5 %collective-permute-start.4 = (bf16[64,1024]{1,0:T(8,128)(2,1)S(1)}, bf16[64,1024]{1,0:T(8,128)(2,1)S(1)}, u32[]{:S(2)}, u32[]{:S(2)}) collective-permute-start(bf16[64,1024]{1,0:T(8,128)(2,1)S(1)} %get-tuple-element.34.ready_ref), channel_id=1, source_target_pairs={{0,8},{8,16},{16,24},{24,0},{1,9},{9,17},{17,25},{25,1},{2,10},{10... | collective-permute-start | bytes 393224 | tf_op jit(solution)/shard_map/ppermute | solution.py:20
  5.7 1.6 %collective-permute-start.3 = (bf16[2,512,256]{2,1,0:T(8,128)(2,1)S(1)}, bf16[2,512,256]{2,1,0:T(8,128)(2,1)S(1)}, u32[]{:S(2)}, u32[]{:S(2)}) collective-permute-start(bf16[2,512,256]{2,1,0:T(8,128)(2,1)S(1)} %get-tuple-element.32), channel_id=1, source_target_pairs={{0,2},{1,3},{2,0},{3,1},{4,6},{5,7},{6,4},{7,5},{8,10},{9,11},{10,... | collective-permute-start | bytes 1572872 | tf_op jit(solution)/shard_map/ppermute | solution.py:24
  7.3 1.4 %shard_map.47 = (bf16[64,1024]{1,0:T(8,128)(2,1)S(1)}, bf16[64,1024]{1,0:T(8,128)(2,1)S(1)}, bf16[64,1024]{1,0:T(8,128)(2,1)S(1)}, bf16[64,1024]{1,0:T(8,128)(2,1)S(1)}) custom-call(bf16[1024,2048]{1,0:T(8,128)(2,1)S(1)} %get-tuple-element.27.joined_ref, bf16[1024,256]{1,0:T(8,128)(2,1)S(1)} %get-tuple-element.28.right_ref, f32[1,1024]{1,0:T(1,128)S(1)} %bitcast.5), custom_call_target="tpu_custom_call" | custom-call | flops 1073741824 | bytes 5246976 | tf_op jit(solution)/shard_map/pallas_call | solution.py:279
  10.3 1.3 %shard_map.51 = bf16[64,1024]{1,0:T(8,128)(2,1)S(1)} custom-call(s32[1]{0:T(128)} %bitcast.level_ref, bf16[64,1024]{1,0:T(8,128)(2,1)S(1)} %collective-permute-done.4.arrived_ref, bf16[64,1024]{1,0:T(8,128)(2,1)S(1)} %get-tuple-element.35.ready_ref, bf16[1024,2048]{1,0:T(8,128)(2,1)S(1)} %get-tuple-element.27.joined_ref, f32[1,1024]{1,0:T(1,128)S(1)} %bitcast.6), custom_call_target="tpu_custom_call" | custom-call | flops 268435456 | bytes 4591616 | tf_op jit(solution)/shard_map/pallas_call | solution.py:279
  12.3 2.7 %collective-permute-done.arrived_ref = bf16[64,1024]{1,0:T(8,128)(2,1)S(1)} collective-permute-done((bf16[64,1024]{1,0:T(8,128)(2,1)S(1)}, bf16[64,1024]{1,0:T(8,128)(2,1)S(1)}, u32[]{:S(2)}, u32[]{:S(2)}) %collective-permute-start) | collective-permute-done | bytes 131104 | tf_op jit(solution)/shard_map/ppermute | solution.py:20
  15.0 1.3 %shard_map.48 = bf16[64,1024]{1,0:T(8,128)(2,1)S(1)} custom-call(s32[1]{0:T(128)} %bitcast.level_ref, bf16[64,1024]{1,0:T(8,128)(2,1)S(1)} %collective-permute-done.arrived_ref, bf16[64,1024]{1,0:T(8,128)(2,1)S(1)} %get-tuple-element.30.ready_ref, bf16[1024,2048]{1,0:T(8,128)(2,1)S(1)} %get-tuple-element.27.joined_ref, f32[1,1024]{1,0:T(1,128)S(1)} %bitcast.7), custom_call_target="tpu_custom_call" | custom-call | flops 268435456 | bytes 4591616 | tf_op jit(solution)/shard_map/pallas_call | solution.py:279
  19.3 4.2 %collective-permute-done.1.arrived_ref = bf16[64,1024]{1,0:T(8,128)(2,1)S(1)} collective-permute-done((bf16[64,1024]{1,0:T(8,128)(2,1)S(1)}, bf16[64,1024]{1,0:T(8,128)(2,1)S(1)}, u32[]{:S(2)}, u32[]{:S(2)}) %collective-permute-start.1) | collective-permute-done | bytes 131104 | tf_op jit(solution)/shard_map/ppermute | solution.py:20
  23.4 1.3 %shard_map.49 = bf16[64,1024]{1,0:T(8,128)(2,1)S(1)} custom-call(s32[1]{0:T(128)} %bitcast.level_ref, bf16[64,1024]{1,0:T(8,128)(2,1)S(1)} %collective-permute-done.1.arrived_ref, bf16[64,1024]{1,0:T(8,128)(2,1)S(1)} %get-tuple-element.31.ready_ref, bf16[1024,2048]{1,0:T(8,128)(2,1)S(1)} %get-tuple-element.27.joined_ref, f32[1,1024]{1,0:T(1,128)S(1)} %bitcast.9), custom_call_target="tpu_custom_call" | custom-call | flops 268435456 | bytes 4591616 | tf_op jit(solution)/shard_map/pallas_call | solution.py:279
  28.2 2.9 %collective-permute-done.2.arrived_ref = bf16[64,1024]{1,0:T(8,128)(2,1)S(1)} collective-permute-done((bf16[64,1024]{1,0:T(8,128)(2,1)S(1)}, bf16[64,1024]{1,0:T(8,128)(2,1)S(1)}, u32[]{:S(2)}, u32[]{:S(2)}) %collective-permute-start.2) | collective-permute-done | bytes 131104 | tf_op jit(solution)/shard_map/ppermute | solution.py:20
  31.0 1.3 %shard_map.56.refs_1_.refs_4_ = bf16[64,1024]{1,0:T(8,128)(2,1)S(1)} custom-call(s32[1]{0:T(128)} %bitcast.level_ref, bf16[64,1024]{1,0:T(8,128)(2,1)S(1)} %collective-permute-done.2.arrived_ref, bf16[64,1024]{1,0:T(8,128)(2,1)S(1)} %get-tuple-element.39.ready_ref, bf16[1024,2048]{1,0:T(8,128)(2,1)S(1)} %get-tuple-element.27.joined_ref, f32[1,1024]{1,0:T(1,128)S(1)} %bitcast.11), custom_call_target="tpu_custom_call" | custom-call | flops 268435456 | bytes 4591616 | tf_op jit(solution)/shard_map/pallas_call | solution.py:279
  33.8 1.3 %shard_map.54.refs_0_.refs_1_ = bf16[64,1024]{1,0:T(8,128)(2,1)S(1)} custom-call(s32[1]{0:T(128)} %bitcast.level_ref, bf16[64,1024]{1,0:T(8,128)(2,1)S(1)} %collective-permute-done.7.arrived_ref, bf16[64,1024]{1,0:T(8,128)(2,1)S(1)} %get-tuple-element.34.ready_ref, bf16[1024,2048]{1,0:T(8,128)(2,1)S(1)} %get-tuple-element.27.joined_ref, f32[1,1024]{1,0:T(1,128)S(1)} %bitcast.12), custom_call_target="tpu_custom_call" | custom-call | flops 268435456 | bytes 4591616 | tf_op jit(solution)/shard_map/pallas_call | solution.py:279
  35.2 3.2 %collective-permute-done.10.arrived_ref = bf16[64,1024]{1,0:T(8,128)(2,1)S(1)} collective-permute-done((bf16[64,1024]{1,0:T(8,128)(2,1)S(1)}, bf16[64,1024]{1,0:T(8,128)(2,1)S(1)}, u32[]{:S(2)}, u32[]{:S(2)}) %collective-permute-start.10) | collective-permute-done | bytes 131104 | tf_op jit(solution)/shard_map/ppermute | solution.py:20
  38.5 1.3 %shard_map.57.refs_1_.refs_5_ = bf16[64,1024]{1,0:T(8,128)(2,1)S(1)} custom-call(s32[1]{0:T(128)} %bitcast.level_ref, bf16[64,1024]{1,0:T(8,128)(2,1)S(1)} %collective-permute-done.10.arrived_ref, bf16[64,1024]{1,0:T(8,128)(2,1)S(1)} %get-tuple-element.29.ready_ref, bf16[1024,2048]{1,0:T(8,128)(2,1)S(1)} %get-tuple-element.27.joined_ref, f32[1,1024]{1,0:T(1,128)S(1)} %bitcast.13), custom_call_target="tpu_custom_call" | custom-call | flops 268435456 | bytes 4591616 | tf_op jit(solution)/shard_map/pallas_call | solution.py:279
  41.1 1.3 %shard_map.55.refs_0_.refs_2_ = bf16[64,1024]{1,0:T(8,128)(2,1)S(1)} custom-call(s32[1]{0:T(128)} %bitcast.level_ref, bf16[64,1024]{1,0:T(8,128)(2,1)S(1)} %collective-permute-done.8.arrived_ref, bf16[64,1024]{1,0:T(8,128)(2,1)S(1)} %get-tuple-element.35.ready_ref, bf16[1024,2048]{1,0:T(8,128)(2,1)S(1)} %get-tuple-element.27.joined_ref, f32[1,1024]{1,0:T(1,128)S(1)} %bitcast.14), custom_call_target="tpu_custom_call" | custom-call | flops 268435456 | bytes 4591616 | tf_op jit(solution)/shard_map/pallas_call | solution.py:279
  42.4 4.4 %collective-permute-done.12.arrived_ref = bf16[64,1024]{1,0:T(8,128)(2,1)S(1)} collective-permute-done((bf16[64,1024]{1,0:T(8,128)(2,1)S(1)}, bf16[64,1024]{1,0:T(8,128)(2,1)S(1)}, u32[]{:S(2)}, u32[]{:S(2)}) %collective-permute-start.12) | collective-permute-done | bytes 131104 | tf_op jit(solution)/shard_map/ppermute | solution.py:20
  46.8 1.3 %shard_map.61.refs_1_.refs_6_ = bf16[64,1024]{1,0:T(8,128)(2,1)S(1)} custom-call(s32[1]{0:T(128)} %bitcast.level_ref, bf16[64,1024]{1,0:T(8,128)(2,1)S(1)} %collective-permute-done.12.arrived_ref, bf16[64,1024]{1,0:T(8,128)(2,1)S(1)} %get-tuple-element.30.ready_ref, bf16[1024,2048]{1,0:T(8,128)(2,1)S(1)} %get-tuple-element.27.joined_ref, f32[1,1024]{1,0:T(1,128)S(1)} %bitcast.15), custom_call_target="tpu_custom_call" | custom-call | flops 268435456 | bytes 4591616 | tf_op jit(solution)/shard_map/pallas_call | solution.py:279
  51.6 2.5 %collective-permute-done.14.arrived_ref = bf16[64,1024]{1,0:T(8,128)(2,1)S(1)} collective-permute-done((bf16[64,1024]{1,0:T(8,128)(2,1)S(1)}, bf16[64,1024]{1,0:T(8,128)(2,1)S(1)}, u32[]{:S(2)}, u32[]{:S(2)}) %collective-permute-start.14) | collective-permute-done | bytes 131104 | tf_op jit(solution)/shard_map/ppermute | solution.py:20
  54.2 1.3 %shard_map.62.refs_7_ = bf16[64,1024]{1,0:T(8,128)(2,1)S(1)} custom-call(s32[1]{0:T(128)} %bitcast.level_ref, bf16[64,1024]{1,0:T(8,128)(2,1)S(1)} %collective-permute-done.14.arrived_ref, bf16[64,1024]{1,0:T(8,128)(2,1)S(1)} %get-tuple-element.31.ready_ref, bf16[1024,2048]{1,0:T(8,128)(2,1)S(1)} %get-tuple-element.27.joined_ref, f32[1,1024]{1,0:T(1,128)S(1)} %bitcast.17), custom_call_target="tpu_custom_call" | custom-call | flops 268435456 | bytes 4591616 | tf_op jit(solution)/shard_map/pallas_call | solution.py:279
  55.5 2.0 %collective-permute-start.17 = (bf16[64,1024]{1,0:T(8,128)(2,1)S(1)}, bf16[64,1024]{1,0:T(8,128)(2,1)S(1)}, u32[]{:S(2)}, u32[]{:S(2)}) collective-permute-start(bf16[64,1024]{1,0:T(8,128)(2,1)S(1)} %shard_map.62.refs_7_), channel_id=1, source_target_pairs={{0,2},{1,3},{2,0},{3,1},{4,6},{5,7},{6,4},{7,5},{8,10},{9,11},{10,... | collective-permute-start | bytes 393224 | tf_op jit(solution)/shard_map/ppermute | solution.py:24
  57.5 1.9 %shard_map.64.early_ref = f32[1024,1024]{1,0:T(8,128)S(1)} custom-call(s32[1]{0:T(128)} %bitcast.level_ref, bf16[1024,1024]{1,0:T(8,128)(2,1)S(1)} %shard_map.50.left_ref, bf16[64,1024]{1,0:T(8,128)(2,1)S(1)} %shard_map.53.refs_0_, bf16[64,1024]{1,0:T(8,128)(2,1)S(1)} %shard_map.54.refs_0_.refs_1_, bf16[64,1024]{1,0:T(8,128)(2,1)S(1)} %shard_map.55.refs_0_.refs_2_, ...), custom_call_target="tpu_custom_call" | custom-call | flops 1610612736 | bytes 8257536 | tf_op jit(solution)/shard_map/pallas_call | solution.py:279
  61.3 1.9 %collective-permute-done.18 = bf16[1,2,128,1024]{3,2,1,0:T(8,128)(2,1)S(1)} collective-permute-done((bf16[1,2,128,1024]{3,2,1,0:T(8,128)(2,1)S(1)}, bf16[1,2,128,1024]{3,2,1,0:T(8,128)(2,1)S(1)}, u32[]{:S(2)}, u32[]{:S(2)}) %collective-permute-start.18) | collective-permute-done | bytes 524320 | tf_op jit(solution)/shard_map/ppermute | solution.py:24
  63.4 2.6 %collective-permute-start.20 = (bf16[1,2,128,1024]{3,2,1,0:T(8,128)(2,1)S(1)}, bf16[1,2,128,1024]{3,2,1,0:T(8,128)(2,1)S(1)}, u32[]{:S(2)}, u32[]{:S(2)}) collective-permute-start(bf16[1,2,128,1024]{3,2,1,0:T(8,128)(2,1)S(1)} %add_convert_fusion), channel_id=1, source_target_pairs={{0,4},{1,5},{2,6},{3,7},{4,0},{5,1},{6,2},{7,3},{8,12},{9,13},{10,... | collective-permute-start | bytes 1572872 | tf_op jit(solution)/shard_map/ppermute | solution.py:20
  66.1 23.5 %collective-permute-done.20.refs_2_ = bf16[1,2,128,1024]{3,2,1,0:T(8,128)(2,1)S(1)} collective-permute-done((bf16[1,2,128,1024]{3,2,1,0:T(8,128)(2,1)S(1)}, bf16[1,2,128,1024]{3,2,1,0:T(8,128)(2,1)S(1)}, u32[]{:S(2)}, u32[]{:S(2)}) %collective-permute-start.20) | collective-permute-done | bytes 524320 | tf_op jit(solution)/shard_map/ppermute | solution.py:20
  (44 shorter events, 18.2 us)
Async XLA Ops:
  0.0 7.3 %copy-start.1 = (f32[1,1,1024]{2,1,0:T(1,128)S(1)}, f32[1,1,1024]{2,1,0:T(1,128)}, u32[]{:S(2)}) copy-start(f32[1,1,1024]{2,1,0:T(1,128)} %factor_ref.1) | copy-start | bytes 12292
  4.2 6.2 %collective-permute-start.4 = (bf16[64,1024]{1,0:T(8,128)(2,1)S(1)}, bf16[64,1024]{1,0:T(8,128)(2,1)S(1)}, u32[]{:S(2)}, u32[]{:S(2)}) collective-permute-start(bf16[64,1024]{1,0:T(8,128)(2,1)S(1)} %get-tuple-element.34.ready_ref), channel_id=1, source_target_pairs={{0,8},{8,16},{16,24},{24,0},{1,9},{9,17},{17,25},{25,1},{2,10},{10... | collective-permute-start | bytes 393224 | tf_op jit(solution)/shard_map/ppermute | solution.py:20
  5.7 21.7 %collective-permute-start.3 = (bf16[2,512,256]{2,1,0:T(8,128)(2,1)S(1)}, bf16[2,512,256]{2,1,0:T(8,128)(2,1)S(1)}, u32[]{:S(2)}, u32[]{:S(2)}) collective-permute-start(bf16[2,512,256]{2,1,0:T(8,128)(2,1)S(1)} %get-tuple-element.32), channel_id=1, source_target_pairs={{0,2},{1,3},{2,0},{3,1},{4,6},{5,7},{6,4},{7,5},{8,10},{9,11},{10,... | collective-permute-start | bytes 1572872 | tf_op jit(solution)/shard_map/ppermute | solution.py:24
  8.7 6.3 %collective-permute-start = (bf16[64,1024]{1,0:T(8,128)(2,1)S(1)}, bf16[64,1024]{1,0:T(8,128)(2,1)S(1)}, u32[]{:S(2)}, u32[]{:S(2)}) collective-permute-start(bf16[64,1024]{1,0:T(8,128)(2,1)S(1)} %get-tuple-element.29.ready_ref), channel_id=1, source_target_pairs={{0,8},{8,16},{16,24},{24,0},{1,9},{9,17},{17,25},{25,1},{2,10},{10... | collective-permute-start | bytes 393224 | tf_op jit(solution)/shard_map/ppermute | solution.py:20
  11.6 5.9 %collective-permute-start.5 = (bf16[64,1024]{1,0:T(8,128)(2,1)S(1)}, bf16[64,1024]{1,0:T(8,128)(2,1)S(1)}, u32[]{:S(2)}, u32[]{:S(2)}) collective-permute-start(bf16[64,1024]{1,0:T(8,128)(2,1)S(1)} %shard_map.51), channel_id=1, source_target_pairs={{0,8},{8,16},{16,24},{24,0},{1,9},{9,17},{17,25},{25,1},{2,10},{10... | collective-permute-start | bytes 393224 | tf_op jit(solution)/shard_map/ppermute | solution.py:20
  16.3 7.2 %collective-permute-start.1 = (bf16[64,1024]{1,0:T(8,128)(2,1)S(1)}, bf16[64,1024]{1,0:T(8,128)(2,1)S(1)}, u32[]{:S(2)}, u32[]{:S(2)}) collective-permute-start(bf16[64,1024]{1,0:T(8,128)(2,1)S(1)} %shard_map.48), channel_id=1, source_target_pairs={{0,8},{8,16},{16,24},{24,0},{1,9},{9,17},{17,25},{25,1},{2,10},{10... | collective-permute-start | bytes 393224 | tf_op jit(solution)/shard_map/ppermute | solution.py:20
  18.9 7.2 %collective-permute-start.6 = (bf16[64,1024]{1,0:T(8,128)(2,1)S(1)}, bf16[64,1024]{1,0:T(8,128)(2,1)S(1)}, u32[]{:S(2)}, u32[]{:S(2)}) collective-permute-start(bf16[64,1024]{1,0:T(8,128)(2,1)S(1)} %shard_map.52), channel_id=1, source_target_pairs={{0,8},{8,16},{16,24},{24,0},{1,9},{9,17},{17,25},{25,1},{2,10},{10... | collective-permute-start | bytes 393224 | tf_op jit(solution)/shard_map/ppermute | solution.py:20
  23.4 3.9 %copy-start = (bf16[1,1,2,1024,256]{4,3,2,1,0:T(8,128)(2,1)S(1)}, bf16[1,1,2,1024,256]{4,3,2,1,0:T(8,128)(2,1)}, u32[]{:S(2)}) copy-start(bf16[1,1,2,1024,256]{4,3,2,1,0:T(8,128)(2,1)} %upward_ref.1) | copy-start | bytes 3145732
  24.7 6.3 %collective-permute-start.2 = (bf16[64,1024]{1,0:T(8,128)(2,1)S(1)}, bf16[64,1024]{1,0:T(8,128)(2,1)S(1)}, u32[]{:S(2)}, u32[]{:S(2)}) collective-permute-start(bf16[64,1024]{1,0:T(8,128)(2,1)S(1)} %shard_map.49), channel_id=1, source_target_pairs={{0,8},{8,16},{16,24},{24,0},{1,9},{9,17},{17,25},{25,1},{2,10},{10... | collective-permute-start | bytes 393224 | tf_op jit(solution)/shard_map/ppermute | solution.py:20
  27.3 6.5 %collective-permute-start.7 = (bf16[64,1024]{1,0:T(8,128)(2,1)S(1)}, bf16[64,1024]{1,0:T(8,128)(2,1)S(1)}, u32[]{:S(2)}, u32[]{:S(2)}) collective-permute-start(bf16[64,1024]{1,0:T(8,128)(2,1)S(1)} %shard_map.53.refs_0_), channel_id=1, source_target_pairs={{0,8},{8,16},{16,24},{24,0},{1,9},{9,17},{17,25},{25,1},{2,10},{10... | collective-permute-start | bytes 393224 | tf_op jit(solution)/shard_map/ppermute | solution.py:20
  32.3 6.1 %collective-permute-start.10 = (bf16[64,1024]{1,0:T(8,128)(2,1)S(1)}, bf16[64,1024]{1,0:T(8,128)(2,1)S(1)}, u32[]{:S(2)}, u32[]{:S(2)}) collective-permute-start(bf16[64,1024]{1,0:T(8,128)(2,1)S(1)} %shard_map.56.refs_1_.refs_4_), channel_id=1, source_target_pairs={{0,8},{8,16},{16,24},{24,0},{1,9},{9,17},{17,25},{25,1},{2,10},{10... | collective-permute-start | bytes 393224 | tf_op jit(solution)/shard_map/ppermute | solution.py:20
  32.4 10.0 %collective-permute-start.13 = (bf16[128,1024]{1,0:T(8,128)(2,1)S(1)}, bf16[128,1024]{1,0:T(8,128)(2,1)S(1)}, u32[]{:S(2)}, u32[]{:S(2)}) collective-permute-start(bf16[128,1024]{1,0:T(8,128)(2,1)S(1)} %shard_map.60), channel_id=1, source_target_pairs={{0,2},{1,3},{2,0},{3,1},{4,6},{5,7},{6,4},{7,5},{8,10},{9,11},{10,... | collective-permute-start | bytes 786440 | tf_op jit(solution)/shard_map/ppermute | solution.py:24
  35.1 5.9 %collective-permute-start.8 = (bf16[64,1024]{1,0:T(8,128)(2,1)S(1)}, bf16[64,1024]{1,0:T(8,128)(2,1)S(1)}, u32[]{:S(2)}, u32[]{:S(2)}) collective-permute-start(bf16[64,1024]{1,0:T(8,128)(2,1)S(1)} %shard_map.54.refs_0_.refs_1_), channel_id=1, source_target_pairs={{0,8},{8,16},{16,24},{24,0},{1,9},{9,17},{17,25},{25,1},{2,10},{10... | collective-permute-start | bytes 393224 | tf_op jit(solution)/shard_map/ppermute | solution.py:20
  39.7 7.1 %collective-permute-start.12 = (bf16[64,1024]{1,0:T(8,128)(2,1)S(1)}, bf16[64,1024]{1,0:T(8,128)(2,1)S(1)}, u32[]{:S(2)}, u32[]{:S(2)}) collective-permute-start(bf16[64,1024]{1,0:T(8,128)(2,1)S(1)} %shard_map.57.refs_1_.refs_5_), channel_id=1, source_target_pairs={{0,8},{8,16},{16,24},{24,0},{1,9},{9,17},{17,25},{25,1},{2,10},{10... | collective-permute-start | bytes 393224 | tf_op jit(solution)/shard_map/ppermute | solution.py:20
  39.8 9.2 %collective-permute-start.11 = (bf16[128,1024]{1,0:T(8,128)(2,1)S(1)}, bf16[128,1024]{1,0:T(8,128)(2,1)S(1)}, u32[]{:S(2)}, u32[]{:S(2)}) collective-permute-start(bf16[128,1024]{1,0:T(8,128)(2,1)S(1)} %shard_map.58), channel_id=1, source_target_pairs={{0,2},{1,3},{2,0},{3,1},{4,6},{5,7},{6,4},{7,5},{8,10},{9,11},{10,... | collective-permute-start | bytes 786440 | tf_op jit(solution)/shard_map/ppermute | solution.py:24
  42.4 6.1 %collective-permute-start.9 = (bf16[64,1024]{1,0:T(8,128)(2,1)S(1)}, bf16[64,1024]{1,0:T(8,128)(2,1)S(1)}, u32[]{:S(2)}, u32[]{:S(2)}) collective-permute-start(bf16[64,1024]{1,0:T(8,128)(2,1)S(1)} %shard_map.55.refs_0_.refs_2_), channel_id=1, source_target_pairs={{0,8},{8,16},{16,24},{24,0},{1,9},{9,17},{17,25},{25,1},{2,10},{10... | collective-permute-start | bytes 393224 | tf_op jit(solution)/shard_map/ppermute | solution.py:20
  48.2 9.3 %collective-permute-start.15 = (bf16[128,1024]{1,0:T(8,128)(2,1)S(1)}, bf16[128,1024]{1,0:T(8,128)(2,1)S(1)}, u32[]{:S(2)}, u32[]{:S(2)}) collective-permute-start(bf16[128,1024]{1,0:T(8,128)(2,1)S(1)} %shard_map.63), channel_id=1, source_target_pairs={{0,2},{1,3},{2,0},{3,1},{4,6},{5,7},{6,4},{7,5},{8,10},{9,11},{10,... | collective-permute-start | bytes 786440 | tf_op jit(solution)/shard_map/ppermute | solution.py:24
  48.2 5.9 %collective-permute-start.14 = (bf16[64,1024]{1,0:T(8,128)(2,1)S(1)}, bf16[64,1024]{1,0:T(8,128)(2,1)S(1)}, u32[]{:S(2)}, u32[]{:S(2)}) collective-permute-start(bf16[64,1024]{1,0:T(8,128)(2,1)S(1)} %shard_map.61.refs_1_.refs_6_), channel_id=1, source_target_pairs={{0,8},{8,16},{16,24},{24,0},{1,9},{9,17},{17,25},{25,1},{2,10},{10... | collective-permute-start | bytes 393224 | tf_op jit(solution)/shard_map/ppermute | solution.py:20
  50.4 7.1 %collective-permute-start.16 = (bf16[64,1024]{1,0:T(8,128)(2,1)S(1)}, bf16[64,1024]{1,0:T(8,128)(2,1)S(1)}, u32[]{:S(2)}, u32[]{:S(2)}) collective-permute-start(bf16[64,1024]{1,0:T(8,128)(2,1)S(1)} %shard_map.59.refs_3_), channel_id=1, source_target_pairs={{0,2},{1,3},{2,0},{3,1},{4,6},{5,7},{6,4},{7,5},{8,10},{9,11},{10,... | collective-permute-start | bytes 393224 | tf_op jit(solution)/shard_map/ppermute | solution.py:24
  55.5 5.0 %collective-permute-start.17 = (bf16[64,1024]{1,0:T(8,128)(2,1)S(1)}, bf16[64,1024]{1,0:T(8,128)(2,1)S(1)}, u32[]{:S(2)}, u32[]{:S(2)}) collective-permute-start(bf16[64,1024]{1,0:T(8,128)(2,1)S(1)} %shard_map.62.refs_7_), channel_id=1, source_target_pairs={{0,2},{1,3},{2,0},{3,1},{4,6},{5,7},{6,4},{7,5},{8,10},{9,11},{10,... | collective-permute-start | bytes 393224 | tf_op jit(solution)/shard_map/ppermute | solution.py:24
  61.3 2.0 %collective-permute-start.18 = (bf16[1,2,128,1024]{3,2,1,0:T(8,128)(2,1)S(1)}, bf16[1,2,128,1024]{3,2,1,0:T(8,128)(2,1)S(1)}, u32[]{:S(2)}, u32[]{:S(2)}) collective-permute-start(bf16[1,2,128,1024]{3,2,1,0:T(8,128)(2,1)S(1)} %get-tuple-element.46), channel_id=1, source_target_pairs={{0,1},{1,0},{2,3},{3,2},{4,5},{5,4},{6,7},{7,6},{8,9},{9,8},{10,11... | collective-permute-start | bytes 1572872 | tf_op jit(solution)/shard_map/ppermute | solution.py:24
  63.4 26.2 %collective-permute-start.20 = (bf16[1,2,128,1024]{3,2,1,0:T(8,128)(2,1)S(1)}, bf16[1,2,128,1024]{3,2,1,0:T(8,128)(2,1)S(1)}, u32[]{:S(2)}, u32[]{:S(2)}) collective-permute-start(bf16[1,2,128,1024]{3,2,1,0:T(8,128)(2,1)S(1)} %add_convert_fusion), channel_id=1, source_target_pairs={{0,4},{1,5},{2,6},{3,7},{4,0},{5,1},{6,2},{7,3},{8,12},{9,13},{10,... | collective-permute-start | bytes 1572872 | tf_op jit(solution)/shard_map/ppermute | solution.py:20
  66.1 23.5 %collective-permute-start.19 = (bf16[1,2,128,1024]{3,2,1,0:T(8,128)(2,1)S(1)}, bf16[1,2,128,1024]{3,2,1,0:T(8,128)(2,1)S(1)}, u32[]{:S(2)}, u32[]{:S(2)}) collective-permute-start(bf16[1,2,128,1024]{3,2,1,0:T(8,128)(2,1)S(1)} %get-tuple-element.47), channel_id=1, source_target_pairs={{0,1},{1,0},{2,3},{3,2},{4,5},{5,4},{6,7},{7,6},{8,9},{9,8},{10,11... | collective-permute-start | bytes 1572872 | tf_op jit(solution)/shard_map/ppermute | solution.py:24

commit v20 on v19

--- a/solution.py
+++ b/solution.py
@@ -127,8 +127,8 @@
 
 def second_kernel(part, joined_ref, right_ref, factor_ref, *outs):
     width = joined_ref.shape[0]
-    wide = width // 4
-    for n in range(4):
+    wide = width // 2
+    for n in range(2):
         columns = slice(n * wide, (n + 1) * wide)
         real, imag = joined_ref[columns, :width], joined_ref[columns, width:]
         start_panels(part, real, imag, right_ref[...], factor_ref[:, columns], outs, columns)

time: 91.1 us -> 91.1 us (level)
  transfers between devices with their start and end apart: 21 -> 21, of which waited for: 16 -> 16; matrix products, arithmetic and copies ran while one was open for 0% -> 0% of each run, Pallas kernels for 22% -> 21%
where the time goes in v20:
time: 91.1 us; the launch traced here: 90.8 us
  waiting for transfers between devices  52.7 us (58%)
  Pallas kernels  25.5 us (28%)
  starting transfers between devices  12.1 us (13%)
    ppermute x13, waiting for transfers between devices, ring(): lax.ppermute(block, axis, [(i, (i + distance) % size) for i in range(size)])  49.1 us
    pallas_call x18, Pallas kernels, whole_call(): pl.pallas_call(kernel, in_specs=[pl.BlockSpec(memory_space=pltpu.SMEM)] *...  19.5 us
    ppermute x13, starting transfers between devices, ring(): lax.ppermute(block, axis, [(i, (i + distance) % size) for i in range(size)])  6.26 us
    ppermute x8, starting transfers between devices, swapped(): lax.ppermute(block, axis, [(i, i ^ bit) for i in range(lax.axis_size(axis...  5.8 us
    pallas_call x1, Pallas kernels, first_advance(): pl.pallas_call(functools.partial(first_kernel, part), in_specs=[pl.BlockS...  4.14 us
    ppermute x8, waiting for transfers between devices, swapped(): lax.ppermute(block, axis, [(i, i ^ bit) for i in range(lax.axis_size(axis...  3.63 us
  transfers between devices with their start and end apart: 21, of which 16 were waited for; matrix products, arithmetic and copies ran while one was open for 0% of the time, Pallas kernels for 21%

profile of v20, /device:TPU:4, one launch (start us, length us, event | category | flops | bytes accessed | tf_op | source)
XLA Modules:
  0.0 90.8 jit_solution(12558508124779600176)
XLA Ops:
  0.0 4.1 %shard_map.46 = (bf16[64,1024]{1,0:T(8,128)(2,1)S(1)}, bf16[64,1024]{1,0:T(8,128)(2,1)S(1)}, bf16[64,1024]{1,0:T(8,128)(2,1)S(1)}, bf16[64,1024]{1,0:T(8,128)(2,...) custom-call(s32[1]{0:T(128)} %bitcast.level_ref, ...), custom_call_target="tpu_custom_call" | custom-call | flops 1073741824 | bytes 6291456 | tf_op jit(solution)/shard_map/pallas_call | solution.py:104
  4.2 1.5 %collective-permute-start.4 = (bf16[64,1024]{1,0:T(8,128)(2,1)S(1)}, bf16[64,1024]{1,0:T(8,128)(2,1)S(1)}, u32[]{:S(2)}, u32[]{:S(2)}) collective-permute-start(bf16[64,1024]{1,0:T(8,128)(2,1)S(1)} %get-tuple-element.34.ready_ref), channel_id=1, source_target_pairs={{0,8},{8,16},{16,24},{24,0},{1,9},{9,17},{17,25},{25,1},{2,10},{10... | collective-permute-start | bytes 393224 | tf_op jit(solution)/shard_map/ppermute | solution.py:20
  5.7 1.6 %collective-permute-start.3 = (bf16[2,512,256]{2,1,0:T(8,128)(2,1)S(1)}, bf16[2,512,256]{2,1,0:T(8,128)(2,1)S(1)}, u32[]{:S(2)}, u32[]{:S(2)}) collective-permute-start(bf16[2,512,256]{2,1,0:T(8,128)(2,1)S(1)} %get-tuple-element.32), channel_id=1, source_target_pairs={{0,2},{1,3},{2,0},{3,1},{4,6},{5,7},{6,4},{7,5},{8,10},{9,11},{10,... | collective-permute-start | bytes 1572872 | tf_op jit(solution)/shard_map/ppermute | solution.py:24
  7.3 1.4 %shard_map.47 = (bf16[64,1024]{1,0:T(8,128)(2,1)S(1)}, bf16[64,1024]{1,0:T(8,128)(2,1)S(1)}, bf16[64,1024]{1,0:T(8,128)(2,1)S(1)}, bf16[64,1024]{1,0:T(8,128)(2,1)S(1)}) custom-call(bf16[1024,2048]{1,0:T(8,128)(2,1)S(1)} %get-tuple-element.27.joined_ref, bf16[1024,256]{1,0:T(8,128)(2,1)S(1)} %get-tuple-element.28.right_ref, f32[1,1024]{1,0:T(1,128)S(1)} %bitcast.5), custom_call_target="tpu_custom_call" | custom-call | flops 1073741824 | bytes 5246976 | tf_op jit(solution)/shard_map/pallas_call | solution.py:279
  10.3 1.3 %shard_map.51 = bf16[64,1024]{1,0:T(8,128)(2,1)S(1)} custom-call(s32[1]{0:T(128)} %bitcast.level_ref, bf16[64,1024]{1,0:T(8,128)(2,1)S(1)} %collective-permute-done.4.arrived_ref, bf16[64,1024]{1,0:T(8,128)(2,1)S(1)} %get-tuple-element.35.ready_ref, bf16[1024,2048]{1,0:T(8,128)(2,1)S(1)} %get-tuple-element.27.joined_ref, f32[1,1024]{1,0:T(1,128)S(1)} %bitcast.6), custom_call_target="tpu_custom_call" | custom-call | flops 268435456 | bytes 4591616 | tf_op jit(solution)/shard_map/pallas_call | solution.py:279
  12.3 2.7 %collective-permute-done.arrived_ref = bf16[64,1024]{1,0:T(8,128)(2,1)S(1)} collective-permute-done((bf16[64,1024]{1,0:T(8,128)(2,1)S(1)}, bf16[64,1024]{1,0:T(8,128)(2,1)S(1)}, u32[]{:S(2)}, u32[]{:S(2)}) %collective-permute-start) | collective-permute-done | bytes 131104 | tf_op jit(solution)/shard_map/ppermute | solution.py:20
  15.0 1.3 %shard_map.48 = bf16[64,1024]{1,0:T(8,128)(2,1)S(1)} custom-call(s32[1]{0:T(128)} %bitcast.level_ref, bf16[64,1024]{1,0:T(8,128)(2,1)S(1)} %collective-permute-done.arrived_ref, bf16[64,1024]{1,0:T(8,128)(2,1)S(1)} %get-tuple-element.30.ready_ref, bf16[1024,2048]{1,0:T(8,128)(2,1)S(1)} %get-tuple-element.27.joined_ref, f32[1,1024]{1,0:T(1,128)S(1)} %bitcast.7), custom_call_target="tpu_custom_call" | custom-call | flops 268435456 | bytes 4591616 | tf_op jit(solution)/shard_map/pallas_call | solution.py:279
  19.3 4.2 %collective-permute-done.1.arrived_ref = bf16[64,1024]{1,0:T(8,128)(2,1)S(1)} collective-permute-done((bf16[64,1024]{1,0:T(8,128)(2,1)S(1)}, bf16[64,1024]{1,0:T(8,128)(2,1)S(1)}, u32[]{:S(2)}, u32[]{:S(2)}) %collective-permute-start.1) | collective-permute-done | bytes 131104 | tf_op jit(solution)/shard_map/ppermute | solution.py:20
  23.4 1.3 %shard_map.49 = bf16[64,1024]{1,0:T(8,128)(2,1)S(1)} custom-call(s32[1]{0:T(128)} %bitcast.level_ref, bf16[64,1024]{1,0:T(8,128)(2,1)S(1)} %collective-permute-done.1.arrived_ref, bf16[64,1024]{1,0:T(8,128)(2,1)S(1)} %get-tuple-element.31.ready_ref, bf16[1024,2048]{1,0:T(8,128)(2,1)S(1)} %get-tuple-element.27.joined_ref, f32[1,1024]{1,0:T(1,128)S(1)} %bitcast.9), custom_call_target="tpu_custom_call" | custom-call | flops 268435456 | bytes 4591616 | tf_op jit(solution)/shard_map/pallas_call | solution.py:279
  28.1 2.9 %collective-permute-done.2.arrived_ref = bf16[64,1024]{1,0:T(8,128)(2,1)S(1)} collective-permute-done((bf16[64,1024]{1,0:T(8,128)(2,1)S(1)}, bf16[64,1024]{1,0:T(8,128)(2,1)S(1)}, u32[]{:S(2)}, u32[]{:S(2)}) %collective-permute-start.2) | collective-permute-done | bytes 131104 | tf_op jit(solution)/shard_map/ppermute | solution.py:20
  31.1 1.3 %shard_map.56.refs_1_.refs_4_ = bf16[64,1024]{1,0:T(8,128)(2,1)S(1)} custom-call(s32[1]{0:T(128)} %bitcast.level_ref, bf16[64,1024]{1,0:T(8,128)(2,1)S(1)} %collective-permute-done.2.arrived_ref, bf16[64,1024]{1,0:T(8,128)(2,1)S(1)} %get-tuple-element.39.ready_ref, bf16[1024,2048]{1,0:T(8,128)(2,1)S(1)} %get-tuple-element.27.joined_ref, f32[1,1024]{1,0:T(1,128)S(1)} %bitcast.11), custom_call_target="tpu_custom_call" | custom-call | flops 268435456 | bytes 4591616 | tf_op jit(solution)/shard_map/pallas_call | solution.py:279
  32.6 1.3 %collective-permute-done.7.arrived_ref = bf16[64,1024]{1,0:T(8,128)(2,1)S(1)} collective-permute-done((bf16[64,1024]{1,0:T(8,128)(2,1)S(1)}, bf16[64,1024]{1,0:T(8,128)(2,1)S(1)}, u32[]{:S(2)}, u32[]{:S(2)}) %collective-permute-start.7) | collective-permute-done | bytes 131104 | tf_op jit(solution)/shard_map/ppermute | solution.py:20
  33.8 1.3 %shard_map.54.refs_0_.refs_1_ = bf16[64,1024]{1,0:T(8,128)(2,1)S(1)} custom-call(s32[1]{0:T(128)} %bitcast.level_ref, bf16[64,1024]{1,0:T(8,128)(2,1)S(1)} %collective-permute-done.7.arrived_ref, bf16[64,1024]{1,0:T(8,128)(2,1)S(1)} %get-tuple-element.34.ready_ref, bf16[1024,2048]{1,0:T(8,128)(2,1)S(1)} %get-tuple-element.27.joined_ref, f32[1,1024]{1,0:T(1,128)S(1)} %bitcast.12), custom_call_target="tpu_custom_call" | custom-call | flops 268435456 | bytes 4591616 | tf_op jit(solution)/shard_map/pallas_call | solution.py:279
  35.2 3.3 %collective-permute-done.10.arrived_ref = bf16[64,1024]{1,0:T(8,128)(2,1)S(1)} collective-permute-done((bf16[64,1024]{1,0:T(8,128)(2,1)S(1)}, bf16[64,1024]{1,0:T(8,128)(2,1)S(1)}, u32[]{:S(2)}, u32[]{:S(2)}) %collective-permute-start.10) | collective-permute-done | bytes 131104 | tf_op jit(solution)/shard_map/ppermute | solution.py:20
  38.5 1.3 %shard_map.57.refs_1_.refs_5_ = bf16[64,1024]{1,0:T(8,128)(2,1)S(1)} custom-call(s32[1]{0:T(128)} %bitcast.level_ref, bf16[64,1024]{1,0:T(8,128)(2,1)S(1)} %collective-permute-done.10.arrived_ref, bf16[64,1024]{1,0:T(8,128)(2,1)S(1)} %get-tuple-element.29.ready_ref, bf16[1024,2048]{1,0:T(8,128)(2,1)S(1)} %get-tuple-element.27.joined_ref, f32[1,1024]{1,0:T(1,128)S(1)} %bitcast.13), custom_call_target="tpu_custom_call" | custom-call | flops 268435456 | bytes 4591616 | tf_op jit(solution)/shard_map/pallas_call | solution.py:279
  42.5 4.4 %collective-permute-done.12.arrived_ref = bf16[64,1024]{1,0:T(8,128)(2,1)S(1)} collective-permute-done((bf16[64,1024]{1,0:T(8,128)(2,1)S(1)}, bf16[64,1024]{1,0:T(8,128)(2,1)S(1)}, u32[]{:S(2)}, u32[]{:S(2)}) %collective-permute-start.12) | collective-permute-done | bytes 131104 | tf_op jit(solution)/shard_map/ppermute | solution.py:20
  46.9 1.3 %shard_map.61.refs_1_.refs_6_ = bf16[64,1024]{1,0:T(8,128)(2,1)S(1)} custom-call(s32[1]{0:T(128)} %bitcast.level_ref, bf16[64,1024]{1,0:T(8,128)(2,1)S(1)} %collective-permute-done.12.arrived_ref, bf16[64,1024]{1,0:T(8,128)(2,1)S(1)} %get-tuple-element.30.ready_ref, bf16[1024,2048]{1,0:T(8,128)(2,1)S(1)} %get-tuple-element.27.joined_ref, f32[1,1024]{1,0:T(1,128)S(1)} %bitcast.15), custom_call_target="tpu_custom_call" | custom-call | flops 268435456 | bytes 4591616 | tf_op jit(solution)/shard_map/pallas_call | solution.py:279
  51.7 2.5 %collective-permute-done.14.arrived_ref = bf16[64,1024]{1,0:T(8,128)(2,1)S(1)} collective-permute-done((bf16[64,1024]{1,0:T(8,128)(2,1)S(1)}, bf16[64,1024]{1,0:T(8,128)(2,1)S(1)}, u32[]{:S(2)}, u32[]{:S(2)}) %collective-permute-start.14) | collective-permute-done | bytes 131104 | tf_op jit(solution)/shard_map/ppermute | solution.py:20
  54.2 1.3 %shard_map.62.refs_7_ = bf16[64,1024]{1,0:T(8,128)(2,1)S(1)} custom-call(s32[1]{0:T(128)} %bitcast.level_ref, bf16[64,1024]{1,0:T(8,128)(2,1)S(1)} %collective-permute-done.14.arrived_ref, bf16[64,1024]{1,0:T(8,128)(2,1)S(1)} %get-tuple-element.31.ready_ref, bf16[1024,2048]{1,0:T(8,128)(2,1)S(1)} %get-tuple-element.27.joined_ref, f32[1,1024]{1,0:T(1,128)S(1)} %bitcast.17), custom_call_target="tpu_custom_call" | custom-call | flops 268435456 | bytes 4591616 | tf_op jit(solution)/shard_map/pallas_call | solution.py:279
  55.5 2.0 %collective-permute-start.17 = (bf16[64,1024]{1,0:T(8,128)(2,1)S(1)}, bf16[64,1024]{1,0:T(8,128)(2,1)S(1)}, u32[]{:S(2)}, u32[]{:S(2)}) collective-permute-start(bf16[64,1024]{1,0:T(8,128)(2,1)S(1)} %shard_map.62.refs_7_), channel_id=1, source_target_pairs={{0,2},{1,3},{2,0},{3,1},{4,6},{5,7},{6,4},{7,5},{8,10},{9,11},{10,... | collective-permute-start | bytes 393224 | tf_op jit(solution)/shard_map/ppermute | solution.py:24
  57.5 1.9 %shard_map.64.early_ref = f32[1024,1024]{1,0:T(8,128)S(1)} custom-call(s32[1]{0:T(128)} %bitcast.level_ref, bf16[1024,1024]{1,0:T(8,128)(2,1)S(1)} %shard_map.50.left_ref, bf16[64,1024]{1,0:T(8,128)(2,1)S(1)} %shard_map.53.refs_0_, bf16[64,1024]{1,0:T(8,128)(2,1)S(1)} %shard_map.54.refs_0_.refs_1_, bf16[64,1024]{1,0:T(8,128)(2,1)S(1)} %shard_map.55.refs_0_.refs_2_, ...), custom_call_target="tpu_custom_call" | custom-call | flops 1610612736 | bytes 8257536 | tf_op jit(solution)/shard_map/pallas_call | solution.py:279
  61.4 1.9 %collective-permute-done.18 = bf16[1,2,128,1024]{3,2,1,0:T(8,128)(2,1)S(1)} collective-permute-done((bf16[1,2,128,1024]{3,2,1,0:T(8,128)(2,1)S(1)}, bf16[1,2,128,1024]{3,2,1,0:T(8,128)(2,1)S(1)}, u32[]{:S(2)}, u32[]{:S(2)}) %collective-permute-start.18) | collective-permute-done | bytes 524320 | tf_op jit(solution)/shard_map/ppermute | solution.py:24
  63.4 2.7 %collective-permute-start.20 = (bf16[1,2,128,1024]{3,2,1,0:T(8,128)(2,1)S(1)}, bf16[1,2,128,1024]{3,2,1,0:T(8,128)(2,1)S(1)}, u32[]{:S(2)}, u32[]{:S(2)}) collective-permute-start(bf16[1,2,128,1024]{3,2,1,0:T(8,128)(2,1)S(1)} %add_convert_fusion), channel_id=1, source_target_pairs={{0,4},{1,5},{2,6},{3,7},{4,0},{5,1},{6,2},{7,3},{8,12},{9,13},{10,... | collective-permute-start | bytes 1572872 | tf_op jit(solution)/shard_map/ppermute | solution.py:20
  66.1 23.5 %collective-permute-done.20.refs_2_ = bf16[1,2,128,1024]{3,2,1,0:T(8,128)(2,1)S(1)} collective-permute-done((bf16[1,2,128,1024]{3,2,1,0:T(8,128)(2,1)S(1)}, bf16[1,2,128,1024]{3,2,1,0:T(8,128)(2,1)S(1)}, u32[]{:S(2)}, u32[]{:S(2)}) %collective-permute-start.20) | collective-permute-done | bytes 524320 | tf_op jit(solution)/shard_map/ppermute | solution.py:20
  (44 shorter events, 18.2 us)
Async XLA Ops:
  0.0 7.3 %copy-start.1 = (f32[1,1,1024]{2,1,0:T(1,128)S(1)}, f32[1,1,1024]{2,1,0:T(1,128)}, u32[]{:S(2)}) copy-start(f32[1,1,1024]{2,1,0:T(1,128)} %factor_ref.1) | copy-start | bytes 12292
  4.2 6.2 %collective-permute-start.4 = (bf16[64,1024]{1,0:T(8,128)(2,1)S(1)}, bf16[64,1024]{1,0:T(8,128)(2,1)S(1)}, u32[]{:S(2)}, u32[]{:S(2)}) collective-permute-start(bf16[64,1024]{1,0:T(8,128)(2,1)S(1)} %get-tuple-element.34.ready_ref), channel_id=1, source_target_pairs={{0,8},{8,16},{16,24},{24,0},{1,9},{9,17},{17,25},{25,1},{2,10},{10... | collective-permute-start | bytes 393224 | tf_op jit(solution)/shard_map/ppermute | solution.py:20
  5.7 21.6 %collective-permute-start.3 = (bf16[2,512,256]{2,1,0:T(8,128)(2,1)S(1)}, bf16[2,512,256]{2,1,0:T(8,128)(2,1)S(1)}, u32[]{:S(2)}, u32[]{:S(2)}) collective-permute-start(bf16[2,512,256]{2,1,0:T(8,128)(2,1)S(1)} %get-tuple-element.32), channel_id=1, source_target_pairs={{0,2},{1,3},{2,0},{3,1},{4,6},{5,7},{6,4},{7,5},{8,10},{9,11},{10,... | collective-permute-start | bytes 1572872 | tf_op jit(solution)/shard_map/ppermute | solution.py:24
  8.6 6.3 %collective-permute-start = (bf16[64,1024]{1,0:T(8,128)(2,1)S(1)}, bf16[64,1024]{1,0:T(8,128)(2,1)S(1)}, u32[]{:S(2)}, u32[]{:S(2)}) collective-permute-start(bf16[64,1024]{1,0:T(8,128)(2,1)S(1)} %get-tuple-element.29.ready_ref), channel_id=1, source_target_pairs={{0,8},{8,16},{16,24},{24,0},{1,9},{9,17},{17,25},{25,1},{2,10},{10... | collective-permute-start | bytes 393224 | tf_op jit(solution)/shard_map/ppermute | solution.py:20
  11.6 5.9 %collective-permute-start.5 = (bf16[64,1024]{1,0:T(8,128)(2,1)S(1)}, bf16[64,1024]{1,0:T(8,128)(2,1)S(1)}, u32[]{:S(2)}, u32[]{:S(2)}) collective-permute-start(bf16[64,1024]{1,0:T(8,128)(2,1)S(1)} %shard_map.51), channel_id=1, source_target_pairs={{0,8},{8,16},{16,24},{24,0},{1,9},{9,17},{17,25},{25,1},{2,10},{10... | collective-permute-start | bytes 393224 | tf_op jit(solution)/shard_map/ppermute | solution.py:20
  16.3 7.2 %collective-permute-start.1 = (bf16[64,1024]{1,0:T(8,128)(2,1)S(1)}, bf16[64,1024]{1,0:T(8,128)(2,1)S(1)}, u32[]{:S(2)}, u32[]{:S(2)}) collective-permute-start(bf16[64,1024]{1,0:T(8,128)(2,1)S(1)} %shard_map.48), channel_id=1, source_target_pairs={{0,8},{8,16},{16,24},{24,0},{1,9},{9,17},{17,25},{25,1},{2,10},{10... | collective-permute-start | bytes 393224 | tf_op jit(solution)/shard_map/ppermute | solution.py:20
  18.9 7.1 %collective-permute-start.6 = (bf16[64,1024]{1,0:T(8,128)(2,1)S(1)}, bf16[64,1024]{1,0:T(8,128)(2,1)S(1)}, u32[]{:S(2)}, u32[]{:S(2)}) collective-permute-start(bf16[64,1024]{1,0:T(8,128)(2,1)S(1)} %shard_map.52), channel_id=1, source_target_pairs={{0,8},{8,16},{16,24},{24,0},{1,9},{9,17},{17,25},{25,1},{2,10},{10... | collective-permute-start | bytes 393224 | tf_op jit(solution)/shard_map/ppermute | solution.py:20
  23.4 3.9 %copy-start = (bf16[1,1,2,1024,256]{4,3,2,1,0:T(8,128)(2,1)S(1)}, bf16[1,1,2,1024,256]{4,3,2,1,0:T(8,128)(2,1)}, u32[]{:S(2)}) copy-start(bf16[1,1,2,1024,256]{4,3,2,1,0:T(8,128)(2,1)} %upward_ref.1) | copy-start | bytes 3145732
  24.7 6.3 %collective-permute-start.2 = (bf16[64,1024]{1,0:T(8,128)(2,1)S(1)}, bf16[64,1024]{1,0:T(8,128)(2,1)S(1)}, u32[]{:S(2)}, u32[]{:S(2)}) collective-permute-start(bf16[64,1024]{1,0:T(8,128)(2,1)S(1)} %shard_map.49), channel_id=1, source_target_pairs={{0,8},{8,16},{16,24},{24,0},{1,9},{9,17},{17,25},{25,1},{2,10},{10... | collective-permute-start | bytes 393224 | tf_op jit(solution)/shard_map/ppermute | solution.py:20
  27.3 6.6 %collective-permute-start.7 = (bf16[64,1024]{1,0:T(8,128)(2,1)S(1)}, bf16[64,1024]{1,0:T(8,128)(2,1)S(1)}, u32[]{:S(2)}, u32[]{:S(2)}) collective-permute-start(bf16[64,1024]{1,0:T(8,128)(2,1)S(1)} %shard_map.53.refs_0_), channel_id=1, source_target_pairs={{0,8},{8,16},{16,24},{24,0},{1,9},{9,17},{17,25},{25,1},{2,10},{10... | collective-permute-start | bytes 393224 | tf_op jit(solution)/shard_map/ppermute | solution.py:20
  32.4 6.1 %collective-permute-start.10 = (bf16[64,1024]{1,0:T(8,128)(2,1)S(1)}, bf16[64,1024]{1,0:T(8,128)(2,1)S(1)}, u32[]{:S(2)}, u32[]{:S(2)}) collective-permute-start(bf16[64,1024]{1,0:T(8,128)(2,1)S(1)} %shard_map.56.refs_1_.refs_4_), channel_id=1, source_target_pairs={{0,8},{8,16},{16,24},{24,0},{1,9},{9,17},{17,25},{25,1},{2,10},{10... | collective-permute-start | bytes 393224 | tf_op jit(solution)/shard_map/ppermute | solution.py:20
  32.5 10.0 %collective-permute-start.13 = (bf16[128,1024]{1,0:T(8,128)(2,1)S(1)}, bf16[128,1024]{1,0:T(8,128)(2,1)S(1)}, u32[]{:S(2)}, u32[]{:S(2)}) collective-permute-start(bf16[128,1024]{1,0:T(8,128)(2,1)S(1)} %shard_map.60), channel_id=1, source_target_pairs={{0,2},{1,3},{2,0},{3,1},{4,6},{5,7},{6,4},{7,5},{8,10},{9,11},{10,... | collective-permute-start | bytes 786440 | tf_op jit(solution)/shard_map/ppermute | solution.py:24
  35.1 6.0 %collective-permute-start.8 = (bf16[64,1024]{1,0:T(8,128)(2,1)S(1)}, bf16[64,1024]{1,0:T(8,128)(2,1)S(1)}, u32[]{:S(2)}, u32[]{:S(2)}) collective-permute-start(bf16[64,1024]{1,0:T(8,128)(2,1)S(1)} %shard_map.54.refs_0_.refs_1_), channel_id=1, source_target_pairs={{0,8},{8,16},{16,24},{24,0},{1,9},{9,17},{17,25},{25,1},{2,10},{10... | collective-permute-start | bytes 393224 | tf_op jit(solution)/shard_map/ppermute | solution.py:20
  39.8 7.1 %collective-permute-start.12 = (bf16[64,1024]{1,0:T(8,128)(2,1)S(1)}, bf16[64,1024]{1,0:T(8,128)(2,1)S(1)}, u32[]{:S(2)}, u32[]{:S(2)}) collective-permute-start(bf16[64,1024]{1,0:T(8,128)(2,1)S(1)} %shard_map.57.refs_1_.refs_5_), channel_id=1, source_target_pairs={{0,8},{8,16},{16,24},{24,0},{1,9},{9,17},{17,25},{25,1},{2,10},{10... | collective-permute-start | bytes 393224 | tf_op jit(solution)/shard_map/ppermute | solution.py:20
  39.9 9.2 %collective-permute-start.11 = (bf16[128,1024]{1,0:T(8,128)(2,1)S(1)}, bf16[128,1024]{1,0:T(8,128)(2,1)S(1)}, u32[]{:S(2)}, u32[]{:S(2)}) collective-permute-start(bf16[128,1024]{1,0:T(8,128)(2,1)S(1)} %shard_map.58), channel_id=1, source_target_pairs={{0,2},{1,3},{2,0},{3,1},{4,6},{5,7},{6,4},{7,5},{8,10},{9,11},{10,... | collective-permute-start | bytes 786440 | tf_op jit(solution)/shard_map/ppermute | solution.py:24
  42.4 6.1 %collective-permute-start.9 = (bf16[64,1024]{1,0:T(8,128)(2,1)S(1)}, bf16[64,1024]{1,0:T(8,128)(2,1)S(1)}, u32[]{:S(2)}, u32[]{:S(2)}) collective-permute-start(bf16[64,1024]{1,0:T(8,128)(2,1)S(1)} %shard_map.55.refs_0_.refs_2_), channel_id=1, source_target_pairs={{0,8},{8,16},{16,24},{24,0},{1,9},{9,17},{17,25},{25,1},{2,10},{10... | collective-permute-start | bytes 393224 | tf_op jit(solution)/shard_map/ppermute | solution.py:20
  48.2 9.3 %collective-permute-start.15 = (bf16[128,1024]{1,0:T(8,128)(2,1)S(1)}, bf16[128,1024]{1,0:T(8,128)(2,1)S(1)}, u32[]{:S(2)}, u32[]{:S(2)}) collective-permute-start(bf16[128,1024]{1,0:T(8,128)(2,1)S(1)} %shard_map.63), channel_id=1, source_target_pairs={{0,2},{1,3},{2,0},{3,1},{4,6},{5,7},{6,4},{7,5},{8,10},{9,11},{10,... | collective-permute-start | bytes 786440 | tf_op jit(solution)/shard_map/ppermute | solution.py:24
  48.3 5.9 %collective-permute-start.14 = (bf16[64,1024]{1,0:T(8,128)(2,1)S(1)}, bf16[64,1024]{1,0:T(8,128)(2,1)S(1)}, u32[]{:S(2)}, u32[]{:S(2)}) collective-permute-start(bf16[64,1024]{1,0:T(8,128)(2,1)S(1)} %shard_map.61.refs_1_.refs_6_), channel_id=1, source_target_pairs={{0,8},{8,16},{16,24},{24,0},{1,9},{9,17},{17,25},{25,1},{2,10},{10... | collective-permute-start | bytes 393224 | tf_op jit(solution)/shard_map/ppermute | solution.py:20
  50.4 7.1 %collective-permute-start.16 = (bf16[64,1024]{1,0:T(8,128)(2,1)S(1)}, bf16[64,1024]{1,0:T(8,128)(2,1)S(1)}, u32[]{:S(2)}, u32[]{:S(2)}) collective-permute-start(bf16[64,1024]{1,0:T(8,128)(2,1)S(1)} %shard_map.59.refs_3_), channel_id=1, source_target_pairs={{0,2},{1,3},{2,0},{3,1},{4,6},{5,7},{6,4},{7,5},{8,10},{9,11},{10,... | collective-permute-start | bytes 393224 | tf_op jit(solution)/shard_map/ppermute | solution.py:24
  55.5 5.0 %collective-permute-start.17 = (bf16[64,1024]{1,0:T(8,128)(2,1)S(1)}, bf16[64,1024]{1,0:T(8,128)(2,1)S(1)}, u32[]{:S(2)}, u32[]{:S(2)}) collective-permute-start(bf16[64,1024]{1,0:T(8,128)(2,1)S(1)} %shard_map.62.refs_7_), channel_id=1, source_target_pairs={{0,2},{1,3},{2,0},{3,1},{4,6},{5,7},{6,4},{7,5},{8,10},{9,11},{10,... | collective-permute-start | bytes 393224 | tf_op jit(solution)/shard_map/ppermute | solution.py:24
  61.3 2.0 %collective-permute-start.18 = (bf16[1,2,128,1024]{3,2,1,0:T(8,128)(2,1)S(1)}, bf16[1,2,128,1024]{3,2,1,0:T(8,128)(2,1)S(1)}, u32[]{:S(2)}, u32[]{:S(2)}) collective-permute-start(bf16[1,2,128,1024]{3,2,1,0:T(8,128)(2,1)S(1)} %get-tuple-element.46), channel_id=1, source_target_pairs={{0,1},{1,0},{2,3},{3,2},{4,5},{5,4},{6,7},{7,6},{8,9},{9,8},{10,11... | collective-permute-start | bytes 1572872 | tf_op jit(solution)/shard_map/ppermute | solution.py:24
  63.4 26.2 %collective-permute-start.20 = (bf16[1,2,128,1024]{3,2,1,0:T(8,128)(2,1)S(1)}, bf16[1,2,128,1024]{3,2,1,0:T(8,128)(2,1)S(1)}, u32[]{:S(2)}, u32[]{:S(2)}) collective-permute-start(bf16[1,2,128,1024]{3,2,1,0:T(8,128)(2,1)S(1)} %add_convert_fusion), channel_id=1, source_target_pairs={{0,4},{1,5},{2,6},{3,7},{4,0},{5,1},{6,2},{7,3},{8,12},{9,13},{10,... | collective-permute-start | bytes 1572872 | tf_op jit(solution)/shard_map/ppermute | solution.py:20
  66.1 23.5 %collective-permute-start.19 = (bf16[1,2,128,1024]{3,2,1,0:T(8,128)(2,1)S(1)}, bf16[1,2,128,1024]{3,2,1,0:T(8,128)(2,1)S(1)}, u32[]{:S(2)}, u32[]{:S(2)}) collective-permute-start(bf16[1,2,128,1024]{3,2,1,0:T(8,128)(2,1)S(1)} %get-tuple-element.47), channel_id=1, source_target_pairs={{0,1},{1,0},{2,3},{3,2},{4,5},{5,4},{6,7},{7,6},{8,9},{9,8},{10,11... | collective-permute-start | bytes 1572872 | tf_op jit(solution)/shard_map/ppermute | solution.py:24
